TPU v7x, 32 devices: a whole 2x2x4 slice. The times are simulated.
32 devices in a mesh: parts: 2 (over x), dp: 8 (over z, y), tp: 2 (over core).
Axes of the slice: x: 2, y: 2, z: 4, core: 2. Of those that a mesh axis runs over, the one named last changes fastest.
Arguments:
- hidden: bfloat16 [768, 4, 5120], P(('parts', 'dp'), None, 'tp'), parts along dimension 0, may hold values from -6 to 6
- base_weight: bfloat16 [5120, 2, 4, 128], P('tp'), may hold values from -0.078125 to 0.078125
- factor_a: bfloat16 [10240, 64], P(('parts', 'tp'), 'dp'), parts along dimension 0, may hold values from -0.078125 to 0.078125
- factor_b: bfloat16 [128, 2, 4, 128], P(('parts', 'dp')), parts along dimension 0, may hold values from -0.75 to 0.75
- queries: bfloat16 [768, 4, 32, 128], P(('parts', 'dp'), None, 'tp'), parts along dimension 0, may hold values from -144 to 144
- cache: bfloat16 [768, 128, 2, 4, 128], P(('parts', 'dp'), None, None, 'tp'), parts along dimension 0, may hold values from -6 to 6
- lengths: int32 [768], P(('parts', 'dp')), parts along dimension 0, may hold values from 8 to 128, as said below
Outputs:
- fresh: bfloat16 [768, 4, 2, 4, 128], P(('parts', 'dp'), None, None, 'tp'), parts along dimension 0
- context: bfloat16 [768, 4, 32, 128], P(('parts', 'dp'), None, 'tp'), parts along dimension 0
There are 2 independent parts, one for each index of `parts`. A program takes and returns all parts, laid end to end along the dimension named above; an argument that names none is the same for every part. Nothing has to cross between parts.
Inputs may be any that keep to these rules, and one draw needn't show every extreme that they name: `lengths`: some row has exactly 128 live slots.
All inputs are finite; a program needn't handle non-finite values.
Results may differ from a plain program's by a relative error of at most 0.0054.
Values may be sent and summed in bfloat16 or wider, within the bound.
No kernel may reach another device: no remote copies, remote signals or barrier semaphores. Data moves between devices by JAX's collectives and lax.ppermute only.
A program may use at most 64 MiB of HBM per device.

v0:
```python
import jax
import jax.numpy as jnp
from jax import lax
from jax.sharding import PartitionSpec as P


def attend(queries, cache, fresh, lengths):
    rows, steps, heads, size = queries.shape
    kvh = cache.shape[3]
    slots = cache.shape[1]
    scale = size ** (-0.5)
    grouped = queries.reshape(rows, steps, kvh, heads // kvh, size)
    s_old = (
        jnp.einsum("rtgqd,rjgd->rtgqj", grouped, cache[:, :, 0], preferred_element_type=jnp.float32)
        * scale
    )
    s_new = (
        jnp.einsum("rtgqd,rjgd->rtgqj", grouped, fresh[:, :, 0], preferred_element_type=jnp.float32)
        * scale
    )
    live_old = (jnp.arange(slots)[None, :] < lengths[:, None])[:, None, None, None, :]
    live_new = (jnp.arange(steps)[None, :] <= jnp.arange(steps)[:, None])[None, :, None, None, :]
    s_old = jnp.where(live_old, s_old, -1e30)
    s_new = jnp.where(live_new, s_new, -1e30)
    top = jnp.maximum(jnp.max(s_old, axis=-1), jnp.max(s_new, axis=-1))[..., None]
    e_old = jnp.where(live_old, jnp.exp(s_old - top), 0.0)
    e_new = jnp.where(live_new, jnp.exp(s_new - top), 0.0)
    total = jnp.sum(e_old, axis=-1) + jnp.sum(e_new, axis=-1)
    w_old = e_old.astype(jnp.bfloat16)
    w_new = e_new.astype(jnp.bfloat16)
    summed = jnp.einsum(
        "rtgqj,rjgd->rtgqd", w_old, cache[:, :, 1], preferred_element_type=jnp.float32
    )
    summed = summed + jnp.einsum(
        "rtgqj,rjgd->rtgqd", w_new, fresh[:, :, 1], preferred_element_type=jnp.float32
    )
    result = summed / total[..., None]
    return result.reshape(rows, steps, heads, size).astype(jnp.bfloat16)


def shards(hidden, base_weight, factor_a, factor_b, queries, cache, lengths):
    width = base_weight.shape[0]
    kvh_all = base_weight.shape[2]
    size = base_weight.shape[3]
    columns = 2 * kvh_all * size
    down_full = lax.all_gather(factor_a, "dp", axis=1, tiled=True)
    up_full = lax.all_gather(factor_b, "dp", axis=0, tiled=True)
    low_rank = jnp.dot(
        down_full, up_full.reshape(up_full.shape[0], columns), preferred_element_type=jnp.float32
    )
    merged = (base_weight.reshape(width, columns).astype(jnp.float32) + low_rank).astype(
        jnp.bfloat16
    )
    rows, steps = (hidden.shape[0], hidden.shape[1])
    partial_value = jnp.dot(
        hidden.reshape(rows * steps, width), merged, preferred_element_type=jnp.float32
    )
    partial_value = partial_value.reshape(rows, steps, 2, kvh_all, size)
    own_heads = cache.shape[3]
    summed_all = lax.psum(partial_value, "tp")
    start = lax.axis_index("tp") * own_heads
    summed = lax.dynamic_slice_in_dim(summed_all, start, own_heads, 3)
    fresh = summed.astype(jnp.bfloat16)
    context = attend(queries, cache, fresh, lengths)
    return (fresh, context)


def solution(mesh):
    return jax.shard_map(
        shards,
        mesh=mesh,
        in_specs=(
            P(("parts", "dp"), None, "tp"),
            P("tp", None, None, None),
            P(("parts", "tp"), "dp"),
            P(("parts", "dp"), None, None, None),
            P(("parts", "dp"), None, "tp", None),
            P(("parts", "dp"), None, None, "tp", None),
            P(("parts", "dp")),
        ),
        out_specs=(
            P(("parts", "dp"), None, None, "tp", None),
            P(("parts", "dp"), None, "tp", None),
        ),
        check_vma=False,
    )
```

profile of v0, /device:TPU:0, one launch (start us, length us, event | category | flops | bytes accessed | tf_op | source)
XLA Modules:
  0.0 106.8 jit_solution(7684407932467065536)
XLA Ops:
  0.6 0.0 copy-start
  0.6 1.8 %reshape.61 = bf16[192,2560]{1,0:T(8,128)(2,1)S(1)} reshape(bf16[48,4,2560]{2,1,0:T(4,128)(2,1)} %param.7) | data formatting | bytes 1966080 | tf_op jit(solution)/shard_map/reshape | solution.py:56
  2.4 0.0 copy-start.1
  2.4 0.0 copy-start.2
  2.4 9.8 %reshape.64 = f32[2560,1024]{1,0:T(8,128)} reshape(bf16[2560,2,4,128]{3,2,1,0:T(4,128)(2,1)} %param.8) | data formatting | bytes 15728640 | tf_op jit(solution)/shard_map/convert_element_type | solution.py:51
  12.2 0.0 copy-done.1
  12.2 32.7 %all_gather.6 = bf16[2560,64]{0,1:T(8,128)(2,1)S(1)} all-gather(bf16[2560,8]{0,1:T(8,128)(2,1)S(1)} %copy-done.1), channel_id=1, replica_groups=mesh['parts'=2,'dp'=8,'tp'=2] {'dp'}, dimensions={1}, use_global_device_ids=true | all-gather | bytes 368640 | tf_op jit(solution)/shard_map/all_gather | solution.py:46
  44.9 0.0 copy-done.2
  44.9 30.5 %all_gather.7 = bf16[64,2,4,128]{3,2,1,0:T(4,128)(2,1)S(1)} all-gather(bf16[8,2,4,128]{3,2,1,0:T(4,128)(2,1)S(1)} %copy-done.2), channel_id=1, replica_groups=mesh['parts'=2,'dp'=8,'tp'=2] {'dp'}, dimensions={0}, use_global_device_ids=true | all-gather | bytes 147456 | tf_op jit(solution)/shard_map/all_gather | solution.py:47
  75.5 0.1 reshape.60
  75.5 6.5 %fusion.7 = f32[192,1024]{1,0:T(8,128)S(1)} fusion(bf16[192,2560]{1,0:T(8,128)(2,1)S(1)} %reshape.61, f32[2560,1024]{1,0:T(8,128)} %reshape.64, bf16[2560,64]{0,1:T(8,128)(2,1)S(1)} %all_gather.6, bf16[64,1024]{1,0:T(8,128)(2,1)S(1)} %reshape.60), kind=kOutput, calls=%fused_computation.14 | convolution fusion | flops 1347420160 | bytes 12713984 | tf_op jit(solution)/shard_map/dot_general | solution.py:55
  82.1 0.4 reshape.62
  82.5 0.2 copy.22
  82.7 5.7 %all-reduce.1 = bf16[48,4,2,4,128]{4,1,3,0,2:T(4,128)(2,1)S(1)} all-reduce(f32[48,4,2,4,128]{4,1,3,0,2:T(4,128)S(1)} %copy.22), channel_id=1, replica_groups=mesh['parts'=2,'dp'=8,'tp'=2] {'tp'}, use_global_device_ids=true, to_apply=%region_0.0 | all-reduce | flops 196608 | bytes 1179648 | tf_op jit(solution)/shard_map/psum | solution.py:60
  88.4 0.1 dynamic-slice_convert_fusion
  88.5 0.8 copy.28
  89.3 0.0 copy-start.3
  89.3 6.9 %fusion.26 = (bf16[48,128,1,2,128]{4,3,2,1,0:T(2,128)(2,1)S(1)}, bf16[48,128,1,2,128]{4,3,2,1,0:T(2,128)(2,1)S(1)}) fusion(bf16[48,128,2,2,128]{4,3,2,1,0:T(2,128)(2,1)} %param.12), kind=kLoop, calls=%fused_computation.39 | loop fusion | bytes 12582912 | tf_op jit(solution)/shard_map/slice | solution.py:14
  96.2 0.0 copy-done.3
  96.2 0.1 iota_compare_fusion
  96.3 0.0 copy-done
  96.3 1.9 %bitcast_reduce_fusion = (f32[48,4,2,8]{3,1,2,0:T(4,128)S(1)}, f32[48,2,128,4,8]{2,4,3,1,0:T(8,128)S(1)}) fusion(bf16[48,128,1,2,128]{4,3,2,1,0:T(2,128)(2,1)S(1)} %get-tuple-element.8, pred[48,128]{1,0:T(8,128)(4,1)S(1)} %iota_compare_fusion, bf16[48,4,16,128]{3,2,1,0:T(8,128)(2,1)S(1)} %copy-done), kind=kOutput, calls=%fused_computation.10 | convolution fusion | flops 101839872 | bytes 5523456 | tf_op jit(solution)/shard_map/rtgqd,rjgd->rtgqj/dot_general | solution.py:14
  98.2 3.6 %fusion.27 = (f32[48,4,2,8]{3,1,2,0:T(4,128)S(1)}, f32[48,4,2,8,4]{3,4,1,2,0:T(4,128)S(1)}) fusion(bf16[48,4,2,2,128]{4,1,3,0,2:T(4,128)(2,1)S(1)} %dynamic-slice_convert_fusion, pred[4,4]{1,0:T(4,128)(4,1)S(1)} %iota_compare_fusion.1, bf16[48,4,16,128]{3,2,1,0:T(8,128)(2,1)S(1)} %copy-done), kind=kOutput, calls=%fused_computation.40 | convolution fusion | flops 3179520 | bytes 946688 | tf_op jit(solution)/shard_map/rtgqd,rjgd->rtgqj/dot_general | solution.py:18
  101.8 0.1 max.7
  101.8 1.0 fusion
  102.8 1.1 %fusion.10 = f32[48,4,2,8]{3,1,2,0:T(4,128)S(1)} fusion(f32[48,2,128,4,8]{2,4,3,1,0:T(8,128)S(1)} %get-tuple-element.11, f32[48,4,2,8]{3,1,2,0:T(4,128)S(1)} %max.7, pred[48,128]{1,0:T(8,128)(4,1)S(1)} %iota_compare_fusion), kind=kLoop, calls=%fused_computation.18 | loop fusion | flops 1176576 | bytes 1603584 | tf_op jit(solution)/shard_map/reduce_sum | solution.py:28
  104.0 0.8 fusion.18
  104.7 0.1 add.21
  104.8 1.0 fusion.4
  105.8 1.0 copy.52
  (1 shorter events, 0.0 us)
Async XLA Ops:
  0.6 95.6 %copy-start = (bf16[48,4,16,128]{3,2,1,0:T(8,128)(2,1)S(1)}, bf16[48,4,16,128]{3,2,1,0:T(8,128)(2,1)}, u32[]{:S(2)}) copy-start(bf16[48,4,16,128]{3,2,1,0:T(8,128)(2,1)} %param.11) | copy-start | bytes 2359300
  2.4 9.8 %copy-start.1 = (bf16[2560,8]{0,1:T(8,128)(2,1)S(1)}, bf16[2560,8]{0,1:T(8,128)(2,1)}, u32[]{:S(2)}) copy-start(bf16[2560,8]{0,1:T(8,128)(2,1)} %param.9) | copy-start | bytes 122884
  2.4 42.5 %copy-start.2 = (bf16[8,2,4,128]{3,2,1,0:T(4,128)(2,1)S(1)}, bf16[8,2,4,128]{3,2,1,0:T(4,128)(2,1)}, u32[]{:S(2)}) copy-start(bf16[8,2,4,128]{3,2,1,0:T(4,128)(2,1)} %param.10) | copy-start | bytes 49156
  89.3 6.9 %copy-start.3 = (s32[48]{0:T(128)S(1)}, s32[48]{0:T(128)}, u32[]{:S(2)}) copy-start(s32[48]{0:T(128)} %param.13) | copy-start | bytes 580
where the time goes:
time: 107 us
  blocking collectives  68.9 us (64%)
  local copies, waits for them, and re-layouts  21 us (20%)
  matrix products  14 us (13%)
  other arithmetic  2.09 us (2%)
    all_gather x1, blocking collectives, shards(): down_full = lax.all_gather(factor_a, 'dp', axis=1, tiled=True)  32.7 us
    all_gather x1, blocking collectives, shards(): up_full = lax.all_gather(factor_b, 'dp', axis=0, tiled=True)  30.5 us
    convert_element_type x1, local copies, waits for them, and re-layouts, shards(): base_weight.reshape(width, columns).astype(jnp.float32) + low_rank  9.78 us
    slice x1, local copies, waits for them, and re-layouts, attend(): cache[:, :, 0]  6.89 us
    dot_general x1, matrix products, shards(): jnp.dot(hidden.reshape(rows * steps, width), merged, preferred_element_ty...  6.54 us
    psum x1, blocking collectives, shards(): summed_all = lax.psum(partial_value, 'tp')  5.69 us
    dot_general x1, matrix products, attend(): jnp.einsum('rtgqd,rjgd->rtgqj', grouped, fresh[:, :, 0], preferred_elemen...  3.58 us

commit v1 on v0

v1 whole, which is shorter than its diff:
```python
import jax
import jax.numpy as jnp
from jax import lax
from jax.sharding import PartitionSpec as P


def gather_blocks(x, count):
    blocks = [x]
    for k in range(1, count):
        blocks.append(lax.ppermute(x, "dp", [(i, i ^ k) for i in range(count)]))
    return blocks


def attend_cached(queries, cache, lengths):
    rows, steps, heads, size = queries.shape
    slots, kvh = cache.shape[1], cache.shape[3]
    grouped = queries.reshape(rows, steps, kvh, heads // kvh, size)
    scores = (
        jnp.einsum("rtgqd,rjgd->rtgqj", grouped, cache[:, :, 0], preferred_element_type=jnp.float32)
        * size ** (-0.5)
    )
    live = (jnp.arange(slots)[None, :] < lengths[:, None])[:, None, None, None, :]
    scores = jnp.where(live, scores, -1e30)
    top = jnp.max(scores, axis=-1, keepdims=True)
    expo = jnp.where(live, jnp.exp(scores - top), 0.0)
    total = jnp.sum(expo, axis=-1, keepdims=True)
    summed = jnp.einsum(
        "rtgqj,rjgd->rtgqd", expo.astype(jnp.bfloat16), cache[:, :, 1], preferred_element_type=jnp.float32
    )
    return top, total, summed


def attend_new(queries, fresh, top_old, total_old, summed_old):
    rows, steps, heads, size = queries.shape
    kvh = fresh.shape[3]
    grouped = queries.reshape(rows, steps, kvh, heads // kvh, size)
    scores = (
        jnp.einsum("rtgqd,rjgd->rtgqj", grouped, fresh[:, :, 0], preferred_element_type=jnp.float32)
        * size ** (-0.5)
    )
    live = (jnp.arange(steps)[None, :] <= jnp.arange(steps)[:, None])[None, :, None, None, :]
    scores = jnp.where(live, scores, -1e30)
    top = jnp.maximum(top_old, jnp.max(scores, axis=-1, keepdims=True))
    expo = jnp.where(live, jnp.exp(scores - top), 0.0)
    back = jnp.exp(top_old - top)
    total = back * total_old + jnp.sum(expo, axis=-1, keepdims=True)
    summed = back * summed_old + jnp.einsum(
        "rtgqj,rjgd->rtgqd", expo.astype(jnp.bfloat16), fresh[:, :, 1], preferred_element_type=jnp.float32
    )
    return (summed / total).reshape(rows, steps, heads, size).astype(jnp.bfloat16)


def shards(dp, tp, hidden, base_weight, factor_a, factor_b, queries, cache, lengths):
    width, _, kvh_all, size = base_weight.shape
    columns = 2 * kvh_all * size
    own = cache.shape[3]
    rows, steps = hidden.shape[:2]
    if dp & (dp - 1) == 0 and dp <= 8:
        down = jnp.concatenate(gather_blocks(factor_a.T, dp), axis=0)
        up = jnp.concatenate(gather_blocks(factor_b, dp), axis=0)
    else:
        down = lax.all_gather(factor_a.T, "dp", axis=0, tiled=True)
        up = lax.all_gather(factor_b, "dp", axis=0, tiled=True)
    top, total, summed = attend_cached(queries, cache, lengths)
    low_rank = lax.dot_general(
        down, up.reshape(up.shape[0], columns), (((0,), (0,)), ((), ())), preferred_element_type=jnp.float32
    )
    merged = (base_weight.reshape(width, columns).astype(jnp.float32) + low_rank).astype(jnp.bfloat16)
    part = jnp.dot(hidden.reshape(rows * steps, width), merged, preferred_element_type=jnp.float32)
    part = part.reshape(rows, steps, 2, tp, own, size)
    me = lax.axis_index("tp")
    mine = lax.dynamic_index_in_dim(part, me, 3, keepdims=False)
    for k in range(1, tp):
        other = lax.dynamic_index_in_dim(part, me ^ k, 3, keepdims=False)
        mine = mine + lax.ppermute(other, "tp", [(i, i ^ k) for i in range(tp)])
    fresh = mine.astype(jnp.bfloat16)
    return fresh, attend_new(queries, fresh, top, total, summed)


def solution(mesh):
    dp, tp = mesh.shape["dp"], mesh.shape["tp"]

    def body(*args):
        return shards(dp, tp, *args)

    return jax.shard_map(
        body,
        mesh=mesh,
        in_specs=(
            P(("parts", "dp"), None, "tp"),
            P("tp", None, None, None),
            P(("parts", "tp"), "dp"),
            P(("parts", "dp"), None, None, None),
            P(("parts", "dp"), None, "tp", None),
            P(("parts", "dp"), None, None, "tp", None),
            P(("parts", "dp")),
        ),
        out_specs=(
            P(("parts", "dp"), None, None, "tp", None),
            P(("parts", "dp"), None, "tp", None),
        ),
        check_vma=False,
    )
```

time: 107 us -> 98.8 us (0.923)
  blocking collectives: 68.9 us -> 0 us
  waiting for transfers between devices: 0 us -> 24.8 us
  starting transfers between devices: 0 us -> 18.6 us
  local copies, waits for them, and re-layouts: 21 us -> 33.5 us
  matrix products: 14 us -> 16.7 us
  other arithmetic: 2.09 us -> 3.33 us
    all_gather x2 -> x0, blocking collectives: 63.2 us -> none  [the longest x1 32.7 us: shards(): down_full = lax.all_gather(factor_a, 'dp', axis=1, tiled=True)]
    ppermute x0 -> x15, waiting for transfers between devices: none -> 24.8 us  [the longest x14 24.8 us: gather_blocks(): blocks.append(lax.ppermute(x, 'dp', [(i, i ^ k) for i in range(count)]))]
    ppermute x0 -> x15, starting transfers between devices: none -> 18.6 us  [the longest x14 18.6 us: gather_blocks(): blocks.append(lax.ppermute(x, 'dp', [(i, i ^ k) for i in range(count)]))]
    unnamed x9 -> x31, local copies, waits for them, and re-layouts: 0.85 us -> 11.7 us
    psum x1 -> x0, blocking collectives: 5.69 us -> none  [shards(): summed_all = lax.psum(partial_value, 'tp')]
    dot_general x4, matrix products: 7.43 us -> 10.2 us  [the longest x1 3.58 us: attend_new(): jnp.einsum('rtgqd,rjgd->rtgqj', grouped, fresh[:, :, 0], preferred_elemen...]
    reshape x1, local copies, waits for them, and re-layouts: 1.76 us -> 0.22 us  [shards(): hidden.reshape(rows * steps, width)]
    slice x1, local copies, waits for them, and re-layouts: 6.89 us -> 8.07 us  [attend_cached(): cache[:, :, 0]]
  transfers between devices with their start and end apart: 0 -> 15, of which waited for: 0 -> 7; matrix products, arithmetic and copies ran while one was open for 0% -> 37% of each run, Pallas kernels for 0% -> 0%
where the time goes in v1:
time: 98.8 us; the launch traced here: 97.9 us
  local copies, waits for them, and re-layouts  33.5 us (34%)
  waiting for transfers between devices  24.8 us (25%)
  starting transfers between devices  18.6 us (19%)
  matrix products  16.7 us (17%)
  other arithmetic  3.33 us (3%)
    ppermute x14, waiting for transfers between devices, gather_blocks(): blocks.append(lax.ppermute(x, 'dp', [(i, i ^ k) for i in range(count)]))  24.8 us
    ppermute x14, starting transfers between devices, gather_blocks(): blocks.append(lax.ppermute(x, 'dp', [(i, i ^ k) for i in range(count)]))  18.6 us
    unnamed x31, local copies, waits for them, and re-layouts  11.7 us
    convert_element_type x1, local copies, waits for them, and re-layouts, shards(): base_weight.reshape(width, columns).astype(jnp.float32) + low_rank  9.84 us
    slice x1, local copies, waits for them, and re-layouts, attend_cached(): cache[:, :, 0]  8.07 us
    dot_general x1, matrix products, shards(): jnp.dot(hidden.reshape(rows * steps, width), merged, preferred_element_ty...  6.54 us
    dot_general x1, matrix products, attend_new(): jnp.einsum('rtgqd,rjgd->rtgqj', grouped, fresh[:, :, 0], preferred_elemen...  3.58 us
    dot_general x1, matrix products, attend_cached(): jnp.einsum('rtgqj,rjgd->rtgqd', expo.astype(jnp.bfloat16), cache[:, :, 1]...  3.22 us
  transfers between devices with their start and end apart: 15, of which 7 were waited for; matrix products, arithmetic and copies ran while one was open for 37% of the time, Pallas kernels for 0%

profile of v1, /device:TPU:0, one launch (start us, length us, event | category | flops | bytes accessed | tf_op | source)
XLA Modules:
  0.0 97.9 jit_solution(3283656222939142043)
XLA Ops:
  0.6 0.0 copy-start
  0.6 3.0 %collective-permute-start = (bf16[8,2560]{1,0:T(8,128)(2,1)}, bf16[8,2560]{1,0:T(8,128)(2,1)}, u32[]{:S(2)}, u32[]{:S(2)}) collective-permute-start(bf16[8,2560]{1,0:T(8,128)(2,1)} %bitcast.94), channel_id=1, source_target_pairs={{0,2},{2,0},{4,6},{6,4},{8,10},{10,8},{12,14},{14,12},{1,3},{3,1},... | collective-permute-start | bytes 122888 | tf_op jit(solution)/shard_map/ppermute | solution.py:10
  3.7 1.6 %collective-permute-start.1 = (bf16[8,2560]{1,0:T(8,128)(2,1)}, bf16[8,2560]{1,0:T(8,128)(2,1)}, u32[]{:S(2)}, u32[]{:S(2)}) collective-permute-start(bf16[8,2560]{1,0:T(8,128)(2,1)} %bitcast.95), channel_id=1, source_target_pairs={{0,4},{2,6},{4,0},{6,2},{8,12},{10,14},{12,8},{14,10},{1,5},{3,7},... | collective-permute-start | bytes 122888 | tf_op jit(solution)/shard_map/ppermute | solution.py:10
  5.3 0.0 collective-permute-start.2
  5.3 3.0 %collective-permute-start.3 = (bf16[8,2560]{1,0:T(8,128)(2,1)}, bf16[8,2560]{1,0:T(8,128)(2,1)S(1)}, u32[]{:S(2)}, u32[]{:S(2)}) collective-permute-start(bf16[8,2560]{1,0:T(8,128)(2,1)} %bitcast.97), channel_id=1, source_target_pairs={{0,8},{2,10},{4,12},{6,14},{8,0},{10,2},{12,4},{14,6},{1,9},{3,11}... | collective-permute-start | bytes 122888 | tf_op jit(solution)/shard_map/ppermute | solution.py:10
  8.2 1.5 %collective-permute-start.7 = (bf16[8,2,4,128]{3,2,1,0:T(4,128)(2,1)}, bf16[8,2,4,128]{3,2,1,0:T(4,128)(2,1)}, u32[]{:S(2)}, u32[]{:S(2)}) collective-permute-start(bf16[8,2,4,128]{3,2,1,0:T(4,128)(2,1)} %param.10), channel_id=1, source_target_pairs={{0,2},{2,0},{4,6},{6,4},{8,10},{10,8},{12,14},{14,12},{1,3},{3,1},... | collective-permute-start | bytes 49160 | tf_op jit(solution)/shard_map/ppermute | solution.py:10
  9.8 0.8 constant_dynamic-update-slice_fusion.7
  10.5 1.3 %constant_dynamic-update-slice_fusion.15 = bf16[64,2,4,128]{3,2,1,0:T(4,128)(2,1)} fusion(bf16[8,2,4,128]{3,2,1,0:T(4,128)(2,1)} %param.10), kind=kLoop, calls=%fused_computation.55 | loop fusion | bytes 32768
  11.9 0.7 iota_compare_fusion
  12.6 8.1 %fusion.27 = (bf16[48,128,1,2,128]{4,3,2,1,0:T(2,128)(2,1)S(1)}, bf16[48,128,1,2,128]{4,3,2,1,0:T(2,128)(2,1)}) fusion(bf16[48,128,2,2,128]{4,3,2,1,0:T(2,128)(2,1)} %param.12), kind=kLoop, calls=%fused_computation.62 | loop fusion | bytes 12582912 | tf_op jit(solution)/shard_map/slice | solution.py:19
  20.7 1.9 %bitcast_reduce_fusion = (f32[48,4,2,8]{3,1,2,0:T(4,128)S(1)}, f32[48,2,128,4,8]{2,4,3,1,0:T(8,128)S(1)}) fusion(bf16[48,128,1,2,128]{4,3,2,1,0:T(2,128)(2,1)S(1)} %get-tuple-element.8, pred[48,128]{1,0:T(8,128)(4,1)S(1)} %iota_compare_fusion, bf16[48,4,16,128]{3,2,1,0:T(8,128)(2,1)S(1)} %copy-done), kind=kOutput, calls=%fused_computation.11 | convolution fusion | flops 101839872 | bytes 5523456 | tf_op jit(solution)/shard_map/rtgqd,rjgd->rtgqj/dot_general | solution.py:19
  22.6 1.1 %copy-done.1 = f32[48,2,128,4,8]{2,4,3,1,0:T(8,128)} copy-done((f32[48,2,128,4,8]{2,4,3,1,0:T(8,128)}, f32[48,2,128,4,8]{2,4,3,1,0:T(8,128)S(1)}, u32[]{:S(2)}) %copy-start.1) | copy-done | bytes 1572888
  23.7 1.1 %fusion.10 = f32[48,4,2,8]{3,1,2,0:T(4,128)S(1)} fusion(f32[48,2,128,4,8]{2,4,3,1,0:T(8,128)S(1)} %get-tuple-element.13, f32[48,4,2,8]{3,1,2,0:T(4,128)S(1)} %get-tuple-element.12, pred[48,128]{1,0:T(8,128)(4,1)S(1)} %iota_compare_fusion), kind=kLoop, calls=%fused_computation.19 | loop fusion | flops 1176576 | bytes 1603584 | tf_op jit(solution)/shard_map/reduce_sum | solution.py:26
  24.8 0.5 iota_compare_fusion.1
  25.3 9.8 %reshape.82 = f32[2560,1024]{1,0:T(8,128)} reshape(bf16[2560,2,4,128]{3,2,1,0:T(4,128)(2,1)} %param.8) | data formatting | bytes 15728640 | tf_op jit(solution)/shard_map/convert_element_type | solution.py:68
  35.1 0.2 reshape.79
  35.4 0.0 collective-permute-done.7
  35.4 1.6 %collective-permute-start.8 = (bf16[8,2,4,128]{3,2,1,0:T(4,128)(2,1)}, bf16[8,2,4,128]{3,2,1,0:T(4,128)(2,1)S(1)}, u32[]{:S(2)}, u32[]{:S(2)}) collective-permute-start(bf16[8,2,4,128]{3,2,1,0:T(4,128)(2,1)} %param.10), channel_id=1, source_target_pairs={{0,4},{2,6},{4,0},{6,2},{8,12},{10,14},{12,8},{14,10},{1,5},{3,7},... | collective-permute-start | bytes 49160 | tf_op jit(solution)/shard_map/ppermute | solution.py:10
  37.0 1.3 %constant_dynamic-update-slice_fusion.14 = bf16[64,2,4,128]{3,2,1,0:T(4,128)(2,1)} fusion(bf16[64,2,4,128]{3,2,1,0:T(4,128)(2,1)} %constant_dynamic-update-slice_fusion.15, bf16[8,2,4,128]{3,2,1,0:T(4,128)(2,1)} %collective-permute-done.7), kind=kLoop, calls=%fused_computation.54 | loop fusion | bytes 32768
  38.4 1.0 %collective-permute-done.8 = bf16[8,2,4,128]{3,2,1,0:T(4,128)(2,1)S(1)} collective-permute-done((bf16[8,2,4,128]{3,2,1,0:T(4,128)(2,1)}, bf16[8,2,4,128]{3,2,1,0:T(4,128)(2,1)S(1)}, u32[]{:S(2)}, u32[]{:S(2)}) %collective-permute-start.8) | collective-permute-done | bytes 16416 | tf_op jit(solution)/shard_map/ppermute | solution.py:10
  39.4 1.5 %collective-permute-start.9 = (bf16[8,2,4,128]{3,2,1,0:T(4,128)(2,1)}, bf16[8,2,4,128]{3,2,1,0:T(4,128)(2,1)S(1)}, u32[]{:S(2)}, u32[]{:S(2)}) collective-permute-start(bf16[8,2,4,128]{3,2,1,0:T(4,128)(2,1)} %param.10), channel_id=1, source_target_pairs={{0,6},{2,4},{4,2},{6,0},{8,14},{10,12},{12,10},{14,8},{1,7},{3,5},... | collective-permute-start | bytes 49160 | tf_op jit(solution)/shard_map/ppermute | solution.py:10
  40.9 0.6 constant_dynamic-update-slice_fusion.13
  41.5 2.9 %collective-permute-done.9 = bf16[8,2,4,128]{3,2,1,0:T(4,128)(2,1)S(1)} collective-permute-done((bf16[8,2,4,128]{3,2,1,0:T(4,128)(2,1)}, bf16[8,2,4,128]{3,2,1,0:T(4,128)(2,1)S(1)}, u32[]{:S(2)}, u32[]{:S(2)}) %collective-permute-start.9) | collective-permute-done | bytes 16416 | tf_op jit(solution)/shard_map/ppermute | solution.py:10
  44.4 0.2 collective-permute-start.10
  44.6 0.6 constant_dynamic-update-slice_fusion.12
  45.2 4.2 %collective-permute-done.10 = bf16[8,2,4,128]{3,2,1,0:T(4,128)(2,1)S(1)} collective-permute-done((bf16[8,2,4,128]{3,2,1,0:T(4,128)(2,1)}, bf16[8,2,4,128]{3,2,1,0:T(4,128)(2,1)S(1)}, u32[]{:S(2)}, u32[]{:S(2)}) %collective-permute-start.10) | collective-permute-done | bytes 16416 | tf_op jit(solution)/shard_map/ppermute | solution.py:10
  49.4 0.6 constant_dynamic-update-slice_fusion.11
  50.0 5.1 %collective-permute-done.11 = bf16[8,2,4,128]{3,2,1,0:T(4,128)(2,1)S(1)} collective-permute-done((bf16[8,2,4,128]{3,2,1,0:T(4,128)(2,1)}, bf16[8,2,4,128]{3,2,1,0:T(4,128)(2,1)S(1)}, u32[]{:S(2)}, u32[]{:S(2)}) %collective-permute-start.11) | collective-permute-done | bytes 16416 | tf_op jit(solution)/shard_map/ppermute | solution.py:10
  55.1 1.2 %collective-permute-start.12 = (bf16[8,2,4,128]{3,2,1,0:T(4,128)(2,1)}, bf16[8,2,4,128]{3,2,1,0:T(4,128)(2,1)S(1)}, u32[]{:S(2)}, u32[]{:S(2)}) collective-permute-start(bf16[8,2,4,128]{3,2,1,0:T(4,128)(2,1)} %param.10), channel_id=1, source_target_pairs={{0,12},{2,14},{4,8},{6,10},{8,4},{10,6},{12,0},{14,2},{1,13},{3,15... | collective-permute-start | bytes 49160 | tf_op jit(solution)/shard_map/ppermute | solution.py:10
  56.4 0.6 constant_dynamic-update-slice_fusion.10
  57.0 3.9 %collective-permute-done.12 = bf16[8,2,4,128]{3,2,1,0:T(4,128)(2,1)S(1)} collective-permute-done((bf16[8,2,4,128]{3,2,1,0:T(4,128)(2,1)}, bf16[8,2,4,128]{3,2,1,0:T(4,128)(2,1)S(1)}, u32[]{:S(2)}, u32[]{:S(2)}) %collective-permute-start.12) | collective-permute-done | bytes 16416 | tf_op jit(solution)/shard_map/ppermute | solution.py:10
  60.9 1.3 %collective-permute-start.13 = (bf16[8,2,4,128]{3,2,1,0:T(4,128)(2,1)}, bf16[8,2,4,128]{3,2,1,0:T(4,128)(2,1)S(1)}, u32[]{:S(2)}, u32[]{:S(2)}) collective-permute-start(bf16[8,2,4,128]{3,2,1,0:T(4,128)(2,1)} %param.10), channel_id=1, source_target_pairs={{0,14},{2,12},{4,10},{6,8},{8,6},{10,4},{12,2},{14,0},{1,15},{3,13... | collective-permute-start | bytes 49160 | tf_op jit(solution)/shard_map/ppermute | solution.py:10
  62.2 0.6 constant_dynamic-update-slice_fusion.9
  62.8 4.8 %collective-permute-done.13 = bf16[8,2,4,128]{3,2,1,0:T(4,128)(2,1)S(1)} collective-permute-done((bf16[8,2,4,128]{3,2,1,0:T(4,128)(2,1)}, bf16[8,2,4,128]{3,2,1,0:T(4,128)(2,1)S(1)}, u32[]{:S(2)}, u32[]{:S(2)}) %collective-permute-start.13) | collective-permute-done | bytes 16416 | tf_op jit(solution)/shard_map/ppermute | solution.py:10
  67.6 0.0 collective-permute-start.4
  67.6 0.6 constant_dynamic-update-slice_fusion.8
  68.2 1.0 reshape.78
  69.2 0.0 collective-permute-done
  69.2 1.2 %collective-permute-start.5 = (bf16[8,2560]{1,0:T(8,128)(2,1)S(1)}, bf16[8,2560]{1,0:T(8,128)(2,1)S(1)}, u32[]{:S(2)}, u32[]{:S(2)}) collective-permute-start(bf16[8,2560]{1,0:T(8,128)(2,1)S(1)} %bitcast.99), channel_id=1, source_target_pairs={{0,12},{2,14},{4,8},{6,10},{8,4},{10,6},{12,0},{14,2},{1,13},{3,15... | collective-permute-start | bytes 122888 | tf_op jit(solution)/shard_map/ppermute | solution.py:10
  70.4 0.8 constant_dynamic-update-slice_fusion.6
  71.2 0.0 collective-permute-done.1
  71.2 2.4 %collective-permute-start.6 = (bf16[8,2560]{1,0:T(8,128)(2,1)S(1)}, bf16[8,2560]{1,0:T(8,128)(2,1)S(1)}, u32[]{:S(2)}, u32[]{:S(2)}) collective-permute-start(bf16[8,2560]{1,0:T(8,128)(2,1)S(1)} %bitcast.100), channel_id=1, source_target_pairs={{0,14},{2,12},{4,10},{6,8},{8,6},{10,4},{12,2},{14,0},{1,15},{3,13... | collective-permute-start | bytes 122888 | tf_op jit(solution)/shard_map/ppermute | solution.py:10
  73.6 0.8 constant_dynamic-update-slice_fusion.5
  74.3 0.0 collective-permute-done.2
  74.4 0.8 constant_dynamic-update-slice_fusion.4
  75.2 0.0 collective-permute-done.5
  75.2 2.8 %collective-permute-done.6 = bf16[8,2560]{1,0:T(8,128)(2,1)S(1)} collective-permute-done((bf16[8,2560]{1,0:T(8,128)(2,1)S(1)}, bf16[8,2560]{1,0:T(8,128)(2,1)S(1)}, u32[]{:S(2)}, u32[]{:S(2)}) %collective-permute-start.6) | collective-permute-done | bytes 40992 | tf_op jit(solution)/shard_map/ppermute | solution.py:10
  78.0 6.5 %fusion.7 = f32[192,1024]{1,0:T(8,128)S(1)} fusion(bf16[192,2560]{1,0:T(8,128)(2,1)S(1)} %reshape.79, f32[2560,1024]{1,0:T(8,128)} %reshape.82, bf16[64,2560]{1,0:T(8,128)(2,1)S(1)} %constant_dynamic-update-slice_fusion, bf16[64,1024]{1,0:T(8,128)(2,1)S(1)} %reshape.78), kind=kOutput, calls=%fused_computation.15 | convolution fusion | flops 1347420160 | bytes 12713984 | tf_op jit(solution)/shard_map/dot_general | solution.py:69
  84.6 0.7 reshape.80
  85.2 0.0 copy-start.6
  85.3 0.3 constant_dynamic-slice_fusion.1
  85.6 0.1 copy.50
  85.7 0.1 collective-permute-start.14
  85.7 0.9 copy-done.2
  86.6 3.2 %fusion = f32[48,2,4,8,128]{4,3,2,1,0:T(8,128)S(1)} fusion(bf16[48,128,1,2,128]{4,3,2,1,0:T(2,128)(2,1)} %get-tuple-element.9, f32[48,2,128,4,8]{2,4,3,1,0:T(8,128)S(1)} %copy-done.2, f32[48,4,2,8]{3,1,2,0:T(4,128)S(1)} %get-tuple-element.12, pred[48,128]{1,0:T(8,128)(4,1)S(1)} %copy-done.6), kind=kOutput, calls=%fused_computation.2 | convolution fusion | flops 101842944 | bytes 6309888 | tf_op jit(solution)/shard_map/rtgqj,rjgd->rtgqd/dot_general | solution.py:27
  89.9 0.0 collective-permute-done.14
  89.9 0.1 fusion.21
  90.0 0.8 copy.23
  90.9 3.6 %fusion.28 = (f32[48,4,2,8]{3,1,2,0:T(4,128)S(1)}, f32[48,4,2,8,4]{3,4,1,2,0:T(4,128)S(1)}) fusion(bf16[48,4,2,2,128]{4,1,3,0,2:T(4,128)(2,1)S(1)} %fusion.21, pred[4,4]{1,0:T(4,128)(4,1)S(1)} %copy-done.7, bf16[48,4,16,128]{3,2,1,0:T(8,128)(2,1)S(1)} %copy-done), kind=kOutput, calls=%fused_computation.63 | convolution fusion | flops 3179520 | bytes 946688 | tf_op jit(solution)/shard_map/rtgqd,rjgd->rtgqj/dot_general | solution.py:38
  94.4 0.1 max.14
  94.5 0.8 fusion.18
  95.3 0.1 multiply_add_fusion
  95.3 1.5 %fusion.4 = bf16[48,4,2,8,128]{4,3,1,2,0:T(8,128)(2,1)S(1)} fusion(f32[48,2,4,8,128]{4,3,2,1,0:T(8,128)S(1)} %fusion, f32[48,4,2,8]{3,1,2,0:T(4,128)S(1)} %bitcast.92, f32[48,4,2,8]{3,1,2,0:T(4,128)S(1)} %bitcast.93, f32[48,4,2,8,4]{3,4,1,2,0:T(4,128)S(1)} %get-tuple-element.15, f32[48,4,2,8]{3,1,2,0:T(4,128)S(1)} %max.14, pred[4,4]{1,0:T(4,128)(4,1)S(1)} %copy-done.7, ...), kind=kOutput, calls=%fused_computation.8 | convolution fusion | flops 4755456 | bytes 3834368 | tf_op jit(solution)/shard_map/rtgqj,rjgd->rtgqd/dot_general | solution.py:47
  96.9 1.0 %copy.49 = bf16[48,4,2,8,128]{4,3,2,1,0:T(8,128)(2,1)} copy(bf16[48,4,2,8,128]{4,3,1,2,0:T(8,128)(2,1)S(1)} %fusion.4) | data formatting | bytes 1572864 | tf_op jit(solution)/shard_map/convert_element_type | solution.py:50
  (19 shorter events, 0.0 us)
Async XLA Ops:
  0.6 20.0 %copy-start = (bf16[48,4,16,128]{3,2,1,0:T(8,128)(2,1)S(1)}, bf16[48,4,16,128]{3,2,1,0:T(8,128)(2,1)}, u32[]{:S(2)}) copy-start(bf16[48,4,16,128]{3,2,1,0:T(8,128)(2,1)} %param.11) | copy-start | bytes 2359300
  0.6 68.6 %collective-permute-start = (bf16[8,2560]{1,0:T(8,128)(2,1)}, bf16[8,2560]{1,0:T(8,128)(2,1)}, u32[]{:S(2)}, u32[]{:S(2)}) collective-permute-start(bf16[8,2560]{1,0:T(8,128)(2,1)} %bitcast.94), channel_id=1, source_target_pairs={{0,2},{2,0},{4,6},{6,4},{8,10},{10,8},{12,14},{14,12},{1,3},{3,1},... | collective-permute-start | bytes 122888 | tf_op jit(solution)/shard_map/ppermute | solution.py:10
  3.7 67.5 %collective-permute-start.1 = (bf16[8,2560]{1,0:T(8,128)(2,1)}, bf16[8,2560]{1,0:T(8,128)(2,1)}, u32[]{:S(2)}, u32[]{:S(2)}) collective-permute-start(bf16[8,2560]{1,0:T(8,128)(2,1)} %bitcast.95), channel_id=1, source_target_pairs={{0,4},{2,6},{4,0},{6,2},{8,12},{10,14},{12,8},{14,10},{1,5},{3,7},... | collective-permute-start | bytes 122888 | tf_op jit(solution)/shard_map/ppermute | solution.py:10
  5.3 69.1 %collective-permute-start.2 = (bf16[8,2560]{1,0:T(8,128)(2,1)}, bf16[8,2560]{1,0:T(8,128)(2,1)}, u32[]{:S(2)}, u32[]{:S(2)}) collective-permute-start(bf16[8,2560]{1,0:T(8,128)(2,1)} %bitcast.96), channel_id=1, source_target_pairs={{0,6},{2,4},{4,2},{6,0},{8,14},{10,12},{12,10},{14,8},{1,7},{3,5},... | collective-permute-start | bytes 122888 | tf_op jit(solution)/shard_map/ppermute | solution.py:10
  5.3 69.9 %collective-permute-start.3 = (bf16[8,2560]{1,0:T(8,128)(2,1)}, bf16[8,2560]{1,0:T(8,128)(2,1)S(1)}, u32[]{:S(2)}, u32[]{:S(2)}) collective-permute-start(bf16[8,2560]{1,0:T(8,128)(2,1)} %bitcast.97), channel_id=1, source_target_pairs={{0,8},{2,10},{4,12},{6,14},{8,0},{10,2},{12,4},{14,6},{1,9},{3,11}... | collective-permute-start | bytes 122888 | tf_op jit(solution)/shard_map/ppermute | solution.py:10
  8.2 27.1 %collective-permute-start.7 = (bf16[8,2,4,128]{3,2,1,0:T(4,128)(2,1)}, bf16[8,2,4,128]{3,2,1,0:T(4,128)(2,1)}, u32[]{:S(2)}, u32[]{:S(2)}) collective-permute-start(bf16[8,2,4,128]{3,2,1,0:T(4,128)(2,1)} %param.10), channel_id=1, source_target_pairs={{0,2},{2,0},{4,6},{6,4},{8,10},{10,8},{12,14},{14,12},{1,3},{3,1},... | collective-permute-start | bytes 49160 | tf_op jit(solution)/shard_map/ppermute | solution.py:10
  12.6 10.0 %copy-start.5 = (pred[48,128]{1,0:T(8,128)(4,1)}, pred[48,128]{1,0:T(8,128)(4,1)S(1)}, u32[]{:S(2)}) copy-start(pred[48,128]{1,0:T(8,128)(4,1)S(1)} %iota_compare_fusion) | copy-start | bytes 18436
  22.6 1.2 %copy-start.1 = (f32[48,2,128,4,8]{2,4,3,1,0:T(8,128)}, f32[48,2,128,4,8]{2,4,3,1,0:T(8,128)S(1)}, u32[]{:S(2)}) copy-start(f32[48,2,128,4,8]{2,4,3,1,0:T(8,128)S(1)} %get-tuple-element.13) | copy-start | bytes 4718596
  25.3 9.8 %copy-start.3 = (bf16[48,4,2560]{2,1,0:T(4,128)(2,1)S(1)}, bf16[48,4,2560]{2,1,0:T(4,128)(2,1)}, u32[]{:S(2)}) copy-start(bf16[48,4,2560]{2,1,0:T(4,128)(2,1)} %param.7) | copy-start | bytes 2949124
  35.1 32.5 %copy-start.4 = (bf16[2560,8]{0,1:T(8,128)(2,1)S(1)}, bf16[2560,8]{0,1:T(8,128)(2,1)}, u32[]{:S(2)}) copy-start(bf16[2560,8]{0,1:T(8,128)(2,1)} %param.9) | copy-start | bytes 122884
  35.4 4.0 %collective-permute-start.8 = (bf16[8,2,4,128]{3,2,1,0:T(4,128)(2,1)}, bf16[8,2,4,128]{3,2,1,0:T(4,128)(2,1)S(1)}, u32[]{:S(2)}, u32[]{:S(2)}) collective-permute-start(bf16[8,2,4,128]{3,2,1,0:T(4,128)(2,1)} %param.10), channel_id=1, source_target_pairs={{0,4},{2,6},{4,0},{6,2},{8,12},{10,14},{12,8},{14,10},{1,5},{3,7},... | collective-permute-start | bytes 49160 | tf_op jit(solution)/shard_map/ppermute | solution.py:10
  39.4 5.0 %collective-permute-start.9 = (bf16[8,2,4,128]{3,2,1,0:T(4,128)(2,1)}, bf16[8,2,4,128]{3,2,1,0:T(4,128)(2,1)S(1)}, u32[]{:S(2)}, u32[]{:S(2)}) collective-permute-start(bf16[8,2,4,128]{3,2,1,0:T(4,128)(2,1)} %param.10), channel_id=1, source_target_pairs={{0,6},{2,4},{4,2},{6,0},{8,14},{10,12},{12,10},{14,8},{1,7},{3,5},... | collective-permute-start | bytes 49160 | tf_op jit(solution)/shard_map/ppermute | solution.py:10
  44.4 5.0 %collective-permute-start.10 = (bf16[8,2,4,128]{3,2,1,0:T(4,128)(2,1)}, bf16[8,2,4,128]{3,2,1,0:T(4,128)(2,1)S(1)}, u32[]{:S(2)}, u32[]{:S(2)}) collective-permute-start(bf16[8,2,4,128]{3,2,1,0:T(4,128)(2,1)} %param.10), channel_id=1, source_target_pairs={{0,8},{2,10},{4,12},{6,14},{8,0},{10,2},{12,4},{14,6},{1,9},{3,11}... | collective-permute-start | bytes 49160 | tf_op jit(solution)/shard_map/ppermute | solution.py:10
  49.4 5.7 %collective-permute-start.11 = (bf16[8,2,4,128]{3,2,1,0:T(4,128)(2,1)}, bf16[8,2,4,128]{3,2,1,0:T(4,128)(2,1)S(1)}, u32[]{:S(2)}, u32[]{:S(2)}) collective-permute-start(bf16[8,2,4,128]{3,2,1,0:T(4,128)(2,1)} %param.10), channel_id=1, source_target_pairs={{0,10},{2,8},{4,14},{6,12},{8,2},{10,0},{12,6},{14,4},{1,11},{3,9}... | collective-permute-start | bytes 49160 | tf_op jit(solution)/shard_map/ppermute | solution.py:10
  55.1 5.7 %collective-permute-start.12 = (bf16[8,2,4,128]{3,2,1,0:T(4,128)(2,1)}, bf16[8,2,4,128]{3,2,1,0:T(4,128)(2,1)S(1)}, u32[]{:S(2)}, u32[]{:S(2)}) collective-permute-start(bf16[8,2,4,128]{3,2,1,0:T(4,128)(2,1)} %param.10), channel_id=1, source_target_pairs={{0,12},{2,14},{4,8},{6,10},{8,4},{10,6},{12,0},{14,2},{1,13},{3,15... | collective-permute-start | bytes 49160 | tf_op jit(solution)/shard_map/ppermute | solution.py:10
  60.9 6.8 %collective-permute-start.13 = (bf16[8,2,4,128]{3,2,1,0:T(4,128)(2,1)}, bf16[8,2,4,128]{3,2,1,0:T(4,128)(2,1)S(1)}, u32[]{:S(2)}, u32[]{:S(2)}) collective-permute-start(bf16[8,2,4,128]{3,2,1,0:T(4,128)(2,1)} %param.10), channel_id=1, source_target_pairs={{0,14},{2,12},{4,10},{6,8},{8,6},{10,4},{12,2},{14,0},{1,15},{3,13... | collective-permute-start | bytes 49160 | tf_op jit(solution)/shard_map/ppermute | solution.py:10
  67.6 7.5 %collective-permute-start.4 = (bf16[8,2560]{1,0:T(8,128)(2,1)S(1)}, bf16[8,2560]{1,0:T(8,128)(2,1)S(1)}, u32[]{:S(2)}, u32[]{:S(2)}) collective-permute-start(bf16[8,2560]{1,0:T(8,128)(2,1)S(1)} %bitcast.98), channel_id=1, source_target_pairs={{0,10},{2,8},{4,14},{6,12},{8,2},{10,0},{12,6},{14,4},{1,11},{3,9}... | collective-permute-start | bytes 122888 | tf_op jit(solution)/shard_map/ppermute | solution.py:10
  69.2 5.9 %collective-permute-start.5 = (bf16[8,2560]{1,0:T(8,128)(2,1)S(1)}, bf16[8,2560]{1,0:T(8,128)(2,1)S(1)}, u32[]{:S(2)}, u32[]{:S(2)}) collective-permute-start(bf16[8,2560]{1,0:T(8,128)(2,1)S(1)} %bitcast.99), channel_id=1, source_target_pairs={{0,12},{2,14},{4,8},{6,10},{8,4},{10,6},{12,0},{14,2},{1,13},{3,15... | collective-permute-start | bytes 122888 | tf_op jit(solution)/shard_map/ppermute | solution.py:10
  71.2 6.8 %collective-permute-start.6 = (bf16[8,2560]{1,0:T(8,128)(2,1)S(1)}, bf16[8,2560]{1,0:T(8,128)(2,1)S(1)}, u32[]{:S(2)}, u32[]{:S(2)}) collective-permute-start(bf16[8,2560]{1,0:T(8,128)(2,1)S(1)} %bitcast.100), channel_id=1, source_target_pairs={{0,14},{2,12},{4,10},{6,8},{8,6},{10,4},{12,2},{14,0},{1,15},{3,13... | collective-permute-start | bytes 122888 | tf_op jit(solution)/shard_map/ppermute | solution.py:10
  85.2 1.4 %copy-start.2 = (f32[48,2,128,4,8]{2,4,3,1,0:T(8,128)S(1)}, f32[48,2,128,4,8]{2,4,3,1,0:T(8,128)}, u32[]{:S(2)}) copy-start(f32[48,2,128,4,8]{2,4,3,1,0:T(8,128)} %copy-done.1) | copy-start | bytes 4718596
  85.2 1.4 %copy-start.6 = (pred[48,128]{1,0:T(8,128)(4,1)S(1)}, pred[48,128]{1,0:T(8,128)(4,1)}, u32[]{:S(2)}) copy-start(pred[48,128]{1,0:T(8,128)(4,1)} %copy-done.5) | copy-start | bytes 18436
  85.7 4.2 %collective-permute-start.14 = (f32[48,4,2,2,128]{4,1,3,0,2:T(4,128)S(1)}, f32[48,4,2,2,128]{4,1,3,0,2:T(4,128)S(1)}, u32[]{:S(2)}, u32[]{:S(2)}) collective-permute-start(f32[48,4,2,2,128]{4,1,3,0,2:T(4,128)S(1)} %bitcast.91), channel_id=1, source_target_pairs={{0,1},{1,0},{2,3},{3,2},{4,5},{5,4},{6,7},{7,6},{8,9},{9,8},{10,11... | collective-permute-start | bytes 1179656 | tf_op jit(solution)/shard_map/ppermute | solution.py:75
  86.6 4.2 %copy-start.7 = (pred[4,4]{1,0:T(4,128)(4,1)S(1)}, pred[4,4]{1,0:T(4,128)(4,1)}, u32[]{:S(2)}) copy-start(pred[4,4]{1,0:T(4,128)(4,1)} %iota_compare_fusion.1) | copy-start | bytes 52

commit v2 on v1

--- a/solution.py
+++ b/solution.py
@@ -4,11 +4,9 @@
 from jax.sharding import PartitionSpec as P
 
 
-def gather_blocks(x, count):
-    blocks = [x]
-    for k in range(1, count):
-        blocks.append(lax.ppermute(x, "dp", [(i, i ^ k) for i in range(count)]))
-    return blocks
+def gather_rows(x, count):
+    copies = jnp.broadcast_to(x[None], (count,) + x.shape)
+    return lax.all_to_all(copies, "dp", 0, 0, tiled=True).reshape((count * x.shape[0],) + x.shape[1:])
 
 
 def attend_cached(queries, cache, lengths):
@@ -55,15 +53,12 @@
     columns = 2 * kvh_all * size
     own = cache.shape[3]
     rows, steps = hidden.shape[:2]
-    if dp & (dp - 1) == 0 and dp <= 8:
-        down = jnp.concatenate(gather_blocks(factor_a.T, dp), axis=0)
-        up = jnp.concatenate(gather_blocks(factor_b, dp), axis=0)
-    else:
-        down = lax.all_gather(factor_a.T, "dp", axis=0, tiled=True)
-        up = lax.all_gather(factor_b, "dp", axis=0, tiled=True)
+    payload = jnp.concatenate([factor_a.T, factor_b.reshape(factor_b.shape[0], columns)], axis=1)
+    gathered = gather_rows(payload, dp)
+    down, up = gathered[:, :width], gathered[:, width:]
     top, total, summed = attend_cached(queries, cache, lengths)
     low_rank = lax.dot_general(
-        down, up.reshape(up.shape[0], columns), (((0,), (0,)), ((), ())), preferred_element_type=jnp.float32
+        down, up, (((0,), (0,)), ((), ())), preferred_element_type=jnp.float32
     )
     merged = (base_weight.reshape(width, columns).astype(jnp.float32) + low_rank).astype(jnp.bfloat16)
     part = jnp.dot(hidden.reshape(rows * steps, width), merged, preferred_element_type=jnp.float32)

time: 98.8 us -> 57 us (0.58)
  waiting for transfers between devices: 24.8 us -> 0.01 us
  starting transfers between devices: 18.6 us -> 7.35 us
  local copies, waits for them, and re-layouts: 33.5 us -> 26.7 us
  matrix products: 16.7 us -> 18.5 us
    ppermute x14 -> x0, waiting for transfers between devices: 24.8 us -> none  [gather_blocks(): blocks.append(lax.ppermute(x, 'dp', [(i, i ^ k) for i in range(count)]))]
    ppermute x14 -> x0, starting transfers between devices: 18.6 us -> none  [gather_blocks(): blocks.append(lax.ppermute(x, 'dp', [(i, i ^ k) for i in range(count)]))]
    unnamed x31 -> x9, local copies, waits for them, and re-layouts: 11.7 us -> 2.89 us
    all_to_all x0 -> x1, starting transfers between devices: none -> 7.28 us  [gather_rows(): lax.all_to_all(copies, 'dp', 0, 0, tiled=True)]
    dot_general x1, matrix products: 1.88 us -> 3.77 us  [attend_cached(): jnp.einsum('rtgqd,rjgd->rtgqj', grouped, cache[:, :, 0], preferred_elemen...]
    reshape x1, local copies, waits for them, and re-layouts: 0.22 us -> 1.68 us  [shards(): hidden.reshape(rows * steps, width)]
  transfers between devices with their start and end apart: 15 -> 2, of which waited for: 7 -> 0; matrix products, arithmetic and copies ran while one was open for 37% -> 50% of each run, Pallas kernels for 0% -> 0%
where the time goes in v2:
time: 57 us; the launch traced here: 56.2 us
  local copies, waits for them, and re-layouts  26.7 us (47%)
  matrix products  18.5 us (32%)
  starting transfers between devices  7.35 us (13%)
  other arithmetic  2.99 us (5%)
  between operations  0.77 us (1%)
    convert_element_type x1, local copies, waits for them, and re-layouts, shards(): base_weight.reshape(width, columns).astype(jnp.float32) + low_rank  9.76 us
    slice x1, local copies, waits for them, and re-layouts, attend_cached(): cache[:, :, 0]  8.64 us
    all_to_all x1, starting transfers between devices, gather_rows(): lax.all_to_all(copies, 'dp', 0, 0, tiled=True)  7.28 us
    dot_general x1, matrix products, shards(): jnp.dot(hidden.reshape(rows * steps, width), merged, preferred_element_ty...  6.55 us
    dot_general x1, matrix products, attend_cached(): jnp.einsum('rtgqd,rjgd->rtgqj', grouped, cache[:, :, 0], preferred_elemen...  3.77 us
    dot_general x1, matrix products, attend_new(): jnp.einsum('rtgqd,rjgd->rtgqj', grouped, fresh[:, :, 0], preferred_elemen...  3.58 us
    dot_general x1, matrix products, attend_cached(): jnp.einsum('rtgqj,rjgd->rtgqd', expo.astype(jnp.bfloat16), cache[:, :, 1]...  3.04 us
    unnamed x9, local copies, waits for them, and re-layouts  2.89 us
  transfers between devices with their start and end apart: 2, of which 0 were waited for; matrix products, arithmetic and copies ran while one was open for 50% of the time, Pallas kernels for 0%

profile of v2, /device:TPU:0, one launch (start us, length us, event | category | flops | bytes accessed | tf_op | source)
XLA Modules:
  0.0 56.2 jit_solution(9853412150159757812)
XLA Ops:
  0.6 0.0 copy-start
  0.6 0.8 %reshape.82 = bf16[8,1024]{1,0:T(8,128)(2,1)S(1)} reshape(bf16[8,2,4,128]{3,2,1,0:T(4,128)(2,1)} %param.10) | data formatting | bytes 32768 | tf_op jit(solution)/shard_map/reshape | solution.py:56
  1.4 0.8 %pad_maximum_fusion = bf16[8,3584]{1,0:T(8,128)(2,1)S(1)} fusion(bf16[8,1024]{1,0:T(8,128)(2,1)S(1)} %reshape.82, bf16[8,2560]{1,0:T(8,128)(2,1)} %bitcast.93), kind=kLoop, calls=%fused_computation.42 | loop fusion | flops 114688 | bytes 114688 | tf_op jit(solution)/shard_map/concatenate | solution.py:56
  2.2 0.8 %broadcast_in_dim.56 = bf16[8,8,3584]{2,1,0:T(8,128)(2,1)} broadcast(bf16[8,3584]{1,0:T(8,128)(2,1)S(1)} %pad_maximum_fusion), dimensions={1,2} | broadcast | bytes 516096 | tf_op jit(solution)/shard_map/broadcast_in_dim | solution.py:8
  3.0 7.3 %all-to-all-start = ((bf16[8,8,3584]{2,1,0:T(8,128)(2,1)}), bf16[8,8,3584]{2,1,0:T(8,128)(2,1)S(1)}, u32[]{:S(2)}, u32[]{:S(2)}) async-start(bf16[8,8,3584]{2,1,0:T(8,128)(2,1)} %broadcast_in_dim.56), calls=%async_computation | async-start | bytes 917504 | tf_op jit(solution)/shard_map/all_to_all | solution.py:9
  10.3 0.0 copy-start.3
  10.3 8.6 %fusion.31 = (bf16[48,128,1,2,128]{4,3,2,1,0:T(2,128)(2,1)}, bf16[48,128,1,2,128]{4,3,2,1,0:T(2,128)(2,1)}) fusion(bf16[48,128,2,2,128]{4,3,2,1,0:T(2,128)(2,1)} %param.12), kind=kLoop, calls=%fused_computation.49 | loop fusion | bytes 12582912 | tf_op jit(solution)/shard_map/slice | solution.py:17
  19.0 0.0 copy-done.3
  19.0 0.1 iota_compare_fusion
  19.0 1.7 %reshape.84 = bf16[192,2560]{1,0:T(8,128)(2,1)S(1)} reshape(bf16[48,4,2560]{2,1,0:T(4,128)(2,1)} %param.7) | data formatting | bytes 1966080 | tf_op jit(solution)/shard_map/reshape | solution.py:64
  20.7 9.8 %reshape.87 = f32[2560,1024]{1,0:T(8,128)} reshape(bf16[2560,2,4,128]{3,2,1,0:T(4,128)(2,1)} %param.8) | data formatting | bytes 15728640 | tf_op jit(solution)/shard_map/convert_element_type | solution.py:63
  30.5 0.0 copy-done
  30.5 3.8 %bitcast_reduce_fusion = (f32[48,4,2,8]{3,1,2,0:T(4,128)S(1)}, f32[48,2,128,4,8]{2,4,3,1,0:T(8,128)S(1)}) fusion(bf16[48,128,1,2,128]{4,3,2,1,0:T(2,128)(2,1)} %get-tuple-element.8, pred[48,128]{1,0:T(8,128)(4,1)S(1)} %iota_compare_fusion, bf16[48,4,16,128]{3,2,1,0:T(8,128)(2,1)S(1)} %copy-done), kind=kOutput, calls=%fused_computation.11 | convolution fusion | flops 101839872 | bytes 5523456 | tf_op jit(solution)/shard_map/rtgqd,rjgd->rtgqj/dot_general | solution.py:17
  34.3 0.0 copy-start.1
  34.3 1.1 %copy-done.1 = f32[48,2,128,4,8]{2,4,3,1,0:T(8,128)} copy-done((f32[48,2,128,4,8]{2,4,3,1,0:T(8,128)}, f32[48,2,128,4,8]{2,4,3,1,0:T(8,128)S(1)}, u32[]{:S(2)}) %copy-start.1) | copy-done | bytes 1572888
  35.4 1.1 %fusion.10 = f32[48,4,2,8]{3,1,2,0:T(4,128)S(1)} fusion(f32[48,2,128,4,8]{2,4,3,1,0:T(8,128)S(1)} %get-tuple-element.13, f32[48,4,2,8]{3,1,2,0:T(4,128)S(1)} %get-tuple-element.12, pred[48,128]{1,0:T(8,128)(4,1)S(1)} %iota_compare_fusion), kind=kLoop, calls=%fused_computation.19 | loop fusion | flops 1176576 | bytes 1603584 | tf_op jit(solution)/shard_map/reduce_sum | solution.py:24
  36.5 0.0 all-to-all-done
  36.5 6.5 %fusion.7 = f32[192,1024]{1,0:T(8,128)S(1)} fusion(bf16[192,2560]{1,0:T(8,128)(2,1)S(1)} %reshape.84, f32[2560,1024]{1,0:T(8,128)} %reshape.87, bf16[64,3584]{1,0:T(8,128)(2,1)S(1)} %bitcast.84), kind=kOutput, calls=%fused_computation.15 | convolution fusion | flops 1347420160 | bytes 12713984 | tf_op jit(solution)/shard_map/dot_general | solution.py:64
  43.1 0.7 %reshape.85 = f32[48,4,2,2,2,128]{5,4,3,2,1,0:T(2,128)S(1)} reshape(f32[192,1024]{1,0:T(8,128)S(1)} %fusion.7) | data formatting | bytes 1572864 | tf_op jit(solution)/shard_map/reshape | solution.py:65
  43.7 0.0 copy-start.2
  43.8 0.3 constant_dynamic-slice_fusion.1
  44.1 0.1 copy.50
  44.2 0.1 collective-permute-start
  44.2 0.9 %copy-done.2 = f32[48,2,128,4,8]{2,4,3,1,0:T(8,128)S(1)} copy-done((f32[48,2,128,4,8]{2,4,3,1,0:T(8,128)S(1)}, f32[48,2,128,4,8]{2,4,3,1,0:T(8,128)}, u32[]{:S(2)}) %copy-start.2) | copy-done | bytes 1572888
  45.2 3.0 %fusion = f32[48,2,4,8,128]{4,3,2,1,0:T(8,128)S(1)} fusion(bf16[48,128,1,2,128]{4,3,2,1,0:T(2,128)(2,1)} %get-tuple-element.9, f32[48,2,128,4,8]{2,4,3,1,0:T(8,128)S(1)} %copy-done.2, f32[48,4,2,8]{3,1,2,0:T(4,128)S(1)} %get-tuple-element.12, pred[48,128]{1,0:T(8,128)(4,1)S(1)} %iota_compare_fusion), kind=kOutput, calls=%fused_computation.2 | convolution fusion | flops 101842944 | bytes 6309888 | tf_op jit(solution)/shard_map/rtgqj,rjgd->rtgqd/dot_general | solution.py:25
  48.2 0.0 collective-permute-done
  48.2 0.2 fusion.21
  48.4 0.8 %copy.23 = bf16[48,4,2,2,128]{4,3,2,1,0:T(2,128)(2,1)} copy(bf16[48,4,2,2,128]{4,1,3,0,2:T(4,128)(2,1)S(1)} %fusion.21) | data formatting | bytes 393216
  49.2 3.6 %fusion.32 = (f32[48,4,2,8]{3,1,2,0:T(4,128)S(1)}, f32[48,4,2,8,4]{3,4,1,2,0:T(4,128)S(1)}) fusion(bf16[48,4,2,2,128]{4,1,3,0,2:T(4,128)(2,1)S(1)} %fusion.21, pred[4,4]{1,0:T(4,128)(4,1)S(1)} %iota_compare_fusion.1, bf16[48,4,16,128]{3,2,1,0:T(8,128)(2,1)S(1)} %copy-done), kind=kOutput, calls=%fused_computation.50 | convolution fusion | flops 3179520 | bytes 946688 | tf_op jit(solution)/shard_map/rtgqd,rjgd->rtgqj/dot_general | solution.py:36
  52.8 0.1 max.14
  52.8 0.8 %fusion.18 = f32[48,4,2,8]{3,1,2,0:T(4,128)S(1)} fusion(f32[48,4,2,8,4]{3,4,1,2,0:T(4,128)S(1)} %get-tuple-element.15, f32[48,4,2,8]{3,1,2,0:T(4,128)S(1)} %max.14, pred[4,4]{1,0:T(4,128)(4,1)S(1)} %iota_compare_fusion.1), kind=kLoop, calls=%fused_computation.28 | loop fusion | flops 33792 | bytes 73744 | tf_op jit(solution)/shard_map/reduce_sum | solution.py:44
  53.6 0.1 multiply_add_fusion
  53.7 1.5 %fusion.4 = bf16[48,4,2,8,128]{4,3,1,2,0:T(8,128)(2,1)S(1)} fusion(f32[48,2,4,8,128]{4,3,2,1,0:T(8,128)S(1)} %fusion, f32[48,4,2,8]{3,1,2,0:T(4,128)S(1)} %bitcast.91, f32[48,4,2,8]{3,1,2,0:T(4,128)S(1)} %bitcast.92, f32[48,4,2,8,4]{3,4,1,2,0:T(4,128)S(1)} %get-tuple-element.15, f32[48,4,2,8]{3,1,2,0:T(4,128)S(1)} %max.14, ...), kind=kOutput, calls=%fused_computation.8 | convolution fusion | flops 4755456 | bytes 3834368 | tf_op jit(solution)/shard_map/rtgqj,rjgd->rtgqd/dot_general | solution.py:45
  55.2 1.0 %copy.49 = bf16[48,4,2,8,128]{4,3,2,1,0:T(8,128)(2,1)} copy(bf16[48,4,2,8,128]{4,3,1,2,0:T(8,128)(2,1)S(1)} %fusion.4) | data formatting | bytes 1572864 | tf_op jit(solution)/shard_map/convert_element_type | solution.py:48
  (1 shorter events, 0.0 us)
Async XLA Ops:
  0.6 29.9 %copy-start = (bf16[48,4,16,128]{3,2,1,0:T(8,128)(2,1)S(1)}, bf16[48,4,16,128]{3,2,1,0:T(8,128)(2,1)}, u32[]{:S(2)}) copy-start(bf16[48,4,16,128]{3,2,1,0:T(8,128)(2,1)} %param.11) | copy-start | bytes 2359300
  3.0 33.5 %all-to-all-start = ((bf16[8,8,3584]{2,1,0:T(8,128)(2,1)}), bf16[8,8,3584]{2,1,0:T(8,128)(2,1)S(1)}, u32[]{:S(2)}, u32[]{:S(2)}) async-start(bf16[8,8,3584]{2,1,0:T(8,128)(2,1)} %broadcast_in_dim.56), calls=%async_computation | async-start | bytes 917504 | tf_op jit(solution)/shard_map/all_to_all | solution.py:9
  10.3 8.6 %copy-start.3 = (s32[48]{0:T(128)S(1)}, s32[48]{0:T(128)}, u32[]{:S(2)}) copy-start(s32[48]{0:T(128)} %param.13) | copy-start | bytes 580
  34.3 1.1 %copy-start.1 = (f32[48,2,128,4,8]{2,4,3,1,0:T(8,128)}, f32[48,2,128,4,8]{2,4,3,1,0:T(8,128)S(1)}, u32[]{:S(2)}) copy-start(f32[48,2,128,4,8]{2,4,3,1,0:T(8,128)S(1)} %get-tuple-element.13) | copy-start | bytes 4718596
  43.7 1.4 %copy-start.2 = (f32[48,2,128,4,8]{2,4,3,1,0:T(8,128)S(1)}, f32[48,2,128,4,8]{2,4,3,1,0:T(8,128)}, u32[]{:S(2)}) copy-start(f32[48,2,128,4,8]{2,4,3,1,0:T(8,128)} %copy-done.1) | copy-start | bytes 4718596
  44.2 4.0 %collective-permute-start = (f32[48,4,2,2,128]{4,1,3,0,2:T(4,128)S(1)}, f32[48,4,2,2,128]{4,1,3,0,2:T(4,128)S(1)}, u32[]{:S(2)}, u32[]{:S(2)}) collective-permute-start(f32[48,4,2,2,128]{4,1,3,0,2:T(4,128)S(1)} %bitcast.90), channel_id=1, source_target_pairs={{0,1},{1,0},{2,3},{3,2},{4,5},{5,4},{6,7},{7,6},{8,9},{9,8},{10,11... | collective-permute-start | bytes 1179656 | tf_op jit(solution)/shard_map/ppermute | solution.py:70

commit v3 on v2

v3 whole, which is shorter than its diff:
```python
import functools

import jax
import jax.numpy as jnp
from jax import lax
from jax.experimental import pallas as pl
from jax.experimental.pallas import tpu as pltpu
from jax.sharding import PartitionSpec as P

LOW = -1e30
NT = (((1,), (1,)), ((), ()))
VMEM = pl.BlockSpec(memory_space=pltpu.VMEM)


def params(mib):
    return pltpu.CompilerParams(vmem_limit_bytes=mib * 1024 * 1024)


def cost(flops, moved, exps=0):
    return pl.CostEstimate(flops=flops, bytes_accessed=moved, transcendentals=exps)


def payload_kernel(down_ref, up_ref, out_ref, wide):
    ranks, width = down_ref.shape
    groups = up_ref.shape[1] * up_ref.shape[2]
    size = up_ref.shape[3]
    wide[...] = up_ref.reshape(ranks * groups, size)[...].astype(jnp.float32)
    down = down_ref[...]
    ups = [wide[pl.ds(n, ranks, stride=groups), :].astype(jnp.bfloat16) for n in range(groups)]
    for i in range(out_ref.shape[0]):
        out_ref[i, :, :width] = down
        for n in range(groups):
            out_ref[i, :, width + n * size : width + (n + 1) * size] = ups[n]


def make_payload(down, up, count):
    ranks, width = down.shape
    columns = up.shape[1] * up.shape[2] * up.shape[3]
    return pl.pallas_call(
        payload_kernel,
        out_shape=jax.ShapeDtypeStruct((count, ranks, width + columns), jnp.bfloat16),
        in_specs=[VMEM, VMEM],
        out_specs=VMEM,
        scratch_shapes=[pltpu.VMEM((ranks * columns // up.shape[3], up.shape[3]), jnp.float32)],
        compiler_params=params(8),
        name="payload",
    )(down, up)


def arrange_kernel(own, base_ref, out_ref, wide):
    width, two, kvh, size = base_ref.shape
    groups = two * kvh
    wide[...] = base_ref.reshape(width * groups, size)[...].astype(jnp.float32)
    for n in range(groups):
        part, at = n // own, n % own
        out_ref[part, :, at * size : (at + 1) * size] = wide[pl.ds(n, width, stride=groups), :].astype(jnp.bfloat16)


def arrange_base(base, own, step=512):
    width, two, kvh, size = base.shape
    groups = two * kvh
    return pl.pallas_call(
        functools.partial(arrange_kernel, own),
        grid=(width // step,),
        out_shape=jax.ShapeDtypeStruct((groups // own, width, own * size), jnp.bfloat16),
        in_specs=[pl.BlockSpec((step, two, kvh, size), lambda i: (i, 0, 0, 0))],
        out_specs=pl.BlockSpec((groups // own, step, own * size), lambda i: (0, i, 0)),
        scratch_shapes=[pltpu.VMEM((step * groups, size), jnp.float32)],
        compiler_params=params(24),
        cost_estimate=cost(0, 4 * base.size),
        name="arrange_base",
    )(base)


def cached_kernel(heads, scale, lengths_ref, q_ref, k_ref, v_ref, sum_ref, total_ref, top_ref):
    rows, queries, size = q_ref.shape
    slots, own = k_ref.shape[1], k_ref.shape[2]
    keys = slots * own
    at = pl.program_id(0) * rows
    column = lax.broadcasted_iota(jnp.int32, (queries, keys), 1)
    head = lax.broadcasted_iota(jnp.int32, (queries, keys), 0) % heads
    column = jnp.where(column % own == head // (heads // own), column, own * slots)
    ones = jnp.ones((keys, size), jnp.bfloat16)
    k_all = k_ref.reshape(rows, keys, size)
    v_all = v_ref.reshape(rows, keys, size)
    for r in range(rows):
        scores = lax.dot_general(q_ref[r], k_all[r], NT, preferred_element_type=jnp.float32)
        scores = jnp.where(column < own * lengths_ref[at + r], scores, LOW)
        top = jnp.max(scores, axis=-1, keepdims=True)
        weights = jnp.exp((scores - top) * scale).astype(jnp.bfloat16)
        both = jnp.dot(
            weights, jnp.concatenate([v_all[r], ones], axis=1), preferred_element_type=jnp.float32
        )
        sum_ref[r] = both[:, :size]
        total_ref[r] = both[:, size:]
        top_ref[r] = jnp.broadcast_to(top, (queries, size))


def attend_cached(queries, cache, lengths, step=8):
    rows, steps, heads, size = queries.shape
    slots, own = cache.shape[1], cache.shape[3]
    many = steps * heads
    state = jax.ShapeDtypeStruct((rows, many, size), jnp.float32)
    block = pl.BlockSpec((step, many, size), lambda i, *_: (i, 0, 0))

    def half(c):
        return pl.BlockSpec((step, slots, None, own, size), lambda i, *_: (i, 0, c, 0, 0))

    return pl.pallas_call(
        functools.partial(cached_kernel, heads, size ** (-0.5)),
        out_shape=(state, state, state),
        grid_spec=pltpu.PrefetchScalarGridSpec(
            num_scalar_prefetch=1,
            grid=(rows // step,),
            in_specs=[block, half(0), half(1)],
            out_specs=(block, block, block),
        ),
        compiler_params=params(24),
        cost_estimate=cost(
            8 * rows * many * slots * size, 2 * (cache.size + queries.size) + 12 * rows * many * size, rows * many * slots
        ),
        name="attend_cached",
    )(lengths, queries.reshape(rows, many, size), cache, cache)


def project_kernel(down_at, which_ref, hidden_ref, gathered_ref, base_ref, out_ref, merged):
    width, columns = merged.shape
    part = which_ref[0]
    parts = base_ref.shape[0] // 2
    half = columns // 2
    up = jnp.concatenate(
        [
            gathered_ref[:, pl.ds(pl.multiple_of(down_at + (c * parts + part) * half, 128), half)]
            for c in range(2)
        ],
        axis=1,
    )
    step = 512
    for f in range(0, width, step):
        down = gathered_ref[:, f : f + step].T
        low_rank = jnp.dot(down, up, preferred_element_type=jnp.float32)
        for c in range(2):
            base = base_ref[c * parts + part, f : f + step, :].astype(jnp.float32)
            merged[f : f + step, c * half : (c + 1) * half] = (base + low_rank[:, c * half : (c + 1) * half]).astype(
                jnp.bfloat16
            )
    out_ref[...] = jnp.dot(hidden_ref[...], merged[...], preferred_element_type=jnp.float32)


def project(which, hidden, gathered, base):
    tokens, width = hidden.shape
    columns = 2 * base.shape[2]
    return pl.pallas_call(
        functools.partial(project_kernel, width),
        out_shape=jax.ShapeDtypeStruct((tokens, columns), jnp.float32),
        in_specs=[pl.BlockSpec(memory_space=pltpu.SMEM), VMEM, VMEM, VMEM],
        out_specs=VMEM,
        scratch_shapes=[pltpu.VMEM((width, columns), jnp.bfloat16)],
        compiler_params=params(24),
        cost_estimate=cost(
            2 * width * columns * (tokens + gathered.shape[0]), 2 * width * columns + 2 * width * tokens
        ),
        name="project",
    )(which, hidden, gathered, base)


def finish_kernel(steps, heads, scale, group, terms, *refs):
    parts, refs = refs[:terms], refs[terms:]
    q_ref, sum_ref, total_ref, top_ref, fresh_ref, context_ref, wide, bias = refs
    rows, queries, size = q_ref.shape
    own = fresh_ref.shape[3]
    fresh = parts[0][...]
    for part in parts[1:]:
        fresh = fresh + part[...]
    for n in range(2 * own):
        wide[pl.ds(n, rows * steps, stride=2 * own), :] = fresh[:, n * size : (n + 1) * size]
    fresh_ref.reshape(rows * steps * 2 * own, size)[...] = wide[...].astype(jnp.bfloat16)
    fresh = fresh.astype(jnp.bfloat16)
    many, keys = group * queries, own * group * steps
    query = lax.broadcasted_iota(jnp.int32, (many, keys), 0)
    key = lax.broadcasted_iota(jnp.int32, (many, keys), 1)
    same_head = (query % heads) // (heads // own) == key // (group * steps)
    same_row = query // queries == (key // steps) % group
    seen = (query % queries) // heads >= key % steps
    bias[...] = jnp.where(same_head & same_row & seen, 0.0, LOW)
    ones = jnp.ones((keys, size), jnp.bfloat16)
    for at in range(0, rows, group):
        tokens = slice(at * steps, (at + group) * steps)
        keys_new, values_new = [
            jnp.concatenate(
                [fresh[tokens, (c * own + g) * size : (c * own + g + 1) * size] for g in range(own)], axis=0
            )
            for c in range(2)
        ]
        values_new = jnp.concatenate([values_new, ones], axis=1)
        mine = slice(at, at + group)
        scores = lax.dot_general(
            q_ref[mine].reshape(many, size), keys_new, NT, preferred_element_type=jnp.float32
        )
        scores = scores + bias[...]
        top_old = top_ref[mine].reshape(many, size)
        top = jnp.maximum(top_old, jnp.max(scores, axis=-1, keepdims=True))
        weights = jnp.exp((scores - top) * scale).astype(jnp.bfloat16)
        back = jnp.exp((top_old - top) * scale)
        both = jnp.dot(weights, values_new, preferred_element_type=jnp.float32)
        total = back * total_ref[mine].reshape(many, size) + both[:, size:]
        summed = back * sum_ref[mine].reshape(many, size) + both[:, :size]
        context_ref[mine] = (summed / total).astype(jnp.bfloat16).reshape(group, queries, size)


def finish(parts, queries, state, own):
    rows, steps, heads, size = queries.shape
    group = size // (own * steps)
    many = steps * heads
    fresh, context = pl.pallas_call(
        functools.partial(finish_kernel, steps, heads, size ** (-0.5), group, len(parts)),
        out_shape=(
            jax.ShapeDtypeStruct((rows, steps, 2, own, size), jnp.bfloat16),
            jax.ShapeDtypeStruct((rows, many, size), jnp.bfloat16),
        ),
        in_specs=[VMEM] * (len(parts) + 1 + len(state)),
        out_specs=(VMEM, VMEM),
        scratch_shapes=[
            pltpu.VMEM((rows * steps * 2 * own, size), jnp.float32),
            pltpu.VMEM((group * many, own * group * steps), jnp.float32),
        ],
        compiler_params=params(24),
        cost_estimate=cost(rows * many * size * size * 6, 12 * rows * many * size, rows * many * size * 2),
        name="finish",
    )(*parts, queries.reshape(rows, many, size), *state)
    return fresh, context.reshape(rows, steps, heads, size)


def shards(dp, tp, hidden, base_weight, factor_a, factor_b, queries, cache, lengths):
    rows, steps, width = hidden.shape
    own = cache.shape[3]
    payload = make_payload(factor_a.T, factor_b, dp)
    gathered = lax.all_to_all(payload, "dp", 0, 0, tiled=True)
    gathered = gathered.reshape(-1, gathered.shape[-1])
    base = arrange_base(base_weight, own)
    state = attend_cached(queries, cache, lengths)
    tokens = hidden.reshape(rows * steps, width)
    me = lax.axis_index("tp")
    received = []
    for k in range(1, tp):
        other = project(jnp.full((1,), me ^ k, jnp.int32), tokens, gathered, base)
        received.append(lax.ppermute(other, "tp", [(i, i ^ k) for i in range(tp)]))
    mine = project(jnp.full((1,), me, jnp.int32), tokens, gathered, base)
    return finish([mine] + received, queries, state, own)


def solution(mesh):
    return jax.shard_map(
        functools.partial(shards, mesh.shape["dp"], mesh.shape["tp"]),
        mesh=mesh,
        in_specs=(
            P(("parts", "dp"), None, "tp"),
            P("tp", None, None, None),
            P(("parts", "tp"), "dp"),
            P(("parts", "dp"), None, None, None),
            P(("parts", "dp"), None, "tp", None),
            P(("parts", "dp"), None, None, "tp", None),
            P(("parts", "dp")),
        ),
        out_specs=(
            P(("parts", "dp"), None, None, "tp", None),
            P(("parts", "dp"), None, "tp", None),
        ),
        check_vma=False,
    )
```

time: 57 us -> 44.1 us (0.77)
  Pallas kernels: 0 us -> 21.1 us
  matrix products: 18.5 us -> 0 us
  local copies, waits for them, and re-layouts: 26.7 us -> 13.2 us
  other arithmetic: 2.99 us -> 0.01 us
  waiting for transfers between devices: 0.01 us -> 1.2 us
    pallas_call x0 -> x6, Pallas kernels: none -> 21.1 us  [the longest x1 9.59 us: attend_cached(): pl.pallas_call(functools.partial(cached_kernel, heads, size ** (-0.5)), o...]
    dot_general x5 -> x0, matrix products: 18.5 us -> none  [the longest x1 6.55 us: shards(): jnp.dot(hidden.reshape(rows * steps, width), merged, preferred_element_ty...]
    convert_element_type x2 -> x0, local copies, waits for them, and re-layouts: 10.8 us -> none  [the longest x1 9.76 us: shards(): base_weight.reshape(width, columns).astype(jnp.float32) + low_rank]
    unnamed x9 -> x20, local copies, waits for them, and re-layouts: 2.89 us -> 11.5 us
    slice x1 -> x0, local copies, waits for them, and re-layouts: 8.64 us -> none  [attend_cached(): cache[:, :, 0]]
    reduce_sum x2 -> x0, other arithmetic: 1.87 us -> none  [the longest x1 1.08 us: attend_cached(): total = jnp.sum(expo, axis=-1, keepdims=True)]
    reshape x3 -> x1, local copies, waits for them, and re-layouts: 3.15 us -> 1.68 us  [shards(): tokens = hidden.reshape(rows * steps, width)]
    all_to_all x1, waiting for transfers between devices: 0.01 us -> 1.2 us  [shards(): gathered = lax.all_to_all(payload, 'dp', 0, 0, tiled=True)]
  transfers between devices with their start and end apart: 2 -> 2, of which waited for: 0 -> 1; matrix products, arithmetic and copies ran while one was open for 50% -> 4% of each run, Pallas kernels for 0% -> 38%
where the time goes in v3:
time: 44.1 us; the launch traced here: 43.6 us
  Pallas kernels  21.1 us (48%)
  local copies, waits for them, and re-layouts  13.2 us (30%)
  starting transfers between devices  7.35 us (17%)
  waiting for transfers between devices  1.2 us (3%)
  between operations  0.76 us (2%)
    unnamed x20, local copies, waits for them, and re-layouts  11.5 us
    pallas_call x1, Pallas kernels, attend_cached(): pl.pallas_call(functools.partial(cached_kernel, heads, size ** (-0.5)), o...  9.59 us
    all_to_all x1, starting transfers between devices, shards(): gathered = lax.all_to_all(payload, 'dp', 0, 0, tiled=True)  7.28 us
    pallas_call x1, Pallas kernels, arrange_base(): pl.pallas_call(functools.partial(arrange_kernel, own), grid=(width // ste...  5.39 us
    pallas_call x2, Pallas kernels, project(): pl.pallas_call(functools.partial(project_kernel, width), out_shape=jax.Sh...  2.78 us
    pallas_call x1, Pallas kernels, finish(): pl.pallas_call(functools.partial(finish_kernel, steps, heads, size ** (-0...  2.52 us
    reshape x1, local copies, waits for them, and re-layouts, shards(): tokens = hidden.reshape(rows * steps, width)  1.68 us
    all_to_all x1, waiting for transfers between devices, shards(): gathered = lax.all_to_all(payload, 'dp', 0, 0, tiled=True)  1.2 us
  transfers between devices with their start and end apart: 2, of which 1 were waited for; matrix products, arithmetic and copies ran while one was open for 4% of the time, Pallas kernels for 38%

profile of v3, /device:TPU:0, one launch (start us, length us, event | category | flops | bytes accessed | tf_op | source)
XLA Modules:
  0.0 43.6 jit_solution(17775136948532204393)
XLA Ops:
  0.6 0.0 copy-start.5
  0.6 0.8 %copy-done.5 = bf16[2560,8]{0,1:T(8,128)(2,1)S(1)} copy-done((bf16[2560,8]{0,1:T(8,128)(2,1)S(1)}, bf16[2560,8]{0,1:T(8,128)(2,1)}, u32[]{:S(2)}) %copy-start.5) | copy-done | bytes 40984
  1.4 0.0 copy-start.6
  1.4 0.7 %copy-done.6 = bf16[8,2,4,128]{3,2,1,0:T(4,128)(2,1)S(1)} copy-done((bf16[8,2,4,128]{3,2,1,0:T(4,128)(2,1)S(1)}, bf16[8,2,4,128]{3,2,1,0:T(4,128)(2,1)}, u32[]{:S(2)}) %copy-start.6) | copy-done | bytes 16408
  2.1 0.8 %payload.1 = bf16[8,8,3584]{2,1,0:T(8,128)(2,1)} custom-call(bf16[8,2560]{1,0:T(8,128)(2,1)S(1)} %bitcast.12, bf16[8,2,4,128]{3,2,1,0:T(4,128)(2,1)S(1)} %copy-done.6), custom_call_target="tpu_custom_call" | custom-call | tf_op jit(solution)/shard_map/payload/pallas_call | solution.py:39
  2.9 7.3 %all-to-all-start = ((bf16[8,8,3584]{2,1,0:T(8,128)(2,1)}), bf16[8,8,3584]{2,1,0:T(8,128)(2,1)S(1)}, u32[]{:S(2)}, u32[]{:S(2)}) async-start(bf16[8,8,3584]{2,1,0:T(8,128)(2,1)} %payload.1), calls=%async_computation | async-start | bytes 917504 | tf_op jit(solution)/shard_map/all_to_all | solution.py:238
  10.2 1.7 %reshape.17.hidden_ref = bf16[192,2560]{1,0:T(8,128)(2,1)S(1)} reshape(bf16[48,4,2560]{2,1,0:T(4,128)(2,1)} %param.7) | data formatting | bytes 1966080 | tf_op jit(solution)/shard_map/reshape | solution.py:242
  11.9 0.0 copy-start.3
  11.9 2.5 %copy-done.3 = bf16[2560,2,4,128]{3,2,1,0:T(4,128)(2,1)S(1)} copy-done((bf16[2560,2,4,128]{3,2,1,0:T(4,128)(2,1)S(1)}, bf16[2560,2,4,128]{3,2,1,0:T(4,128)(2,1)}, u32[]{:S(2)}) %copy-start.3) | copy-done | bytes 5242904
  14.4 0.0 copy-start.4
  14.4 5.4 %arrange_base.1.base_ref = bf16[4,2560,256]{2,1,0:T(8,128)(2,1)S(1)} custom-call(bf16[2560,2,4,128]{3,2,1,0:T(4,128)(2,1)S(1)} %copy-done.3), custom_call_target="tpu_custom_call" | custom-call | bytes 10485760 | tf_op jit(solution)/shard_map/arrange_base/pallas_call | solution.py:62
  19.8 0.0 copy-start
  19.8 2.3 %copy-done = bf16[4,2560,256]{2,1,0:T(8,128)(2,1)} copy-done((bf16[4,2560,256]{2,1,0:T(8,128)(2,1)}, bf16[4,2560,256]{2,1,0:T(8,128)(2,1)S(1)}, u32[]{:S(2)}) %copy-start) | copy-done | bytes 5242904
  22.1 0.0 copy-start.7
  22.1 1.2 %all-to-all-done = bf16[8,8,3584]{2,1,0:T(8,128)(2,1)S(1)} async-done(((bf16[8,8,3584]{2,1,0:T(8,128)(2,1)}), bf16[8,8,3584]{2,1,0:T(8,128)(2,1)S(1)}, u32[]{:S(2)}, u32[]{:S(2)}) %all-to-all-start) | async-done | bytes 458784 | tf_op jit(solution)/shard_map/all_to_all | solution.py:238
  23.3 0.0 copy-start.1
  23.3 2.5 %copy-done.1 = bf16[4,2560,256]{2,1,0:T(8,128)(2,1)S(1)} copy-done((bf16[4,2560,256]{2,1,0:T(8,128)(2,1)S(1)}, bf16[4,2560,256]{2,1,0:T(8,128)(2,1)}, u32[]{:S(2)}) %copy-start.1) | copy-done | bytes 5242904
  25.8 0.0 slice-start
  25.8 1.4 %project.3 = f32[192,512]{1,0:T(8,128)S(1)} custom-call(s32[1]{0:T(128)} %bitcast.3.which_ref, bf16[192,2560]{1,0:T(8,128)(2,1)S(1)} %reshape.17.hidden_ref, bf16[64,3584]{1,0:T(8,128)(2,1)S(1)} %bitcast.8, bf16[4,2560,256]{2,1,0:T(8,128)(2,1)S(1)} %copy-done.1), custom_call_target="tpu_custom_call" | custom-call | flops 671088640 | bytes 3604480 | tf_op jit(solution)/shard_map/project/pallas_call | solution.py:153
  27.2 0.1 collective-permute-start
  27.3 0.0 copy-done.4
  27.3 0.0 copy-done.7
  27.3 0.0 copy-start.2
  27.3 2.8 %copy-done.2 = bf16[48,128,2,2,128]{4,3,2,1,0:T(2,128)(2,1)S(1)} copy-done((bf16[48,128,2,2,128]{4,3,2,1,0:T(2,128)(2,1)S(1)}, bf16[48,128,2,2,128]{4,3,2,1,0:T(2,128)(2,1)}, u32[]{:S(2)}) %copy-start.2) | copy-done | bytes 6291480
  30.1 0.0 slice-start.1
  30.1 9.6 %attend_cached.1 = (f32[48,64,128]{2,1,0:T(8,128)S(1)}, f32[48,64,128]{2,1,0:T(8,128)S(1)}, f32[48,64,128]{2,1,0:T(8,128)S(1)}) custom-call(s32[48]{0:T(128)S(1)} %copy-done.7, bf16[48,64,128]{2,1,0:T(8,128)(2,1)S(1)} %bitcast.10, bf16[48,128,2,2,128]{4,3,2,1,0:T(2,128)(2,1)S(1)} %copy-done.2, bf16[48,128,2,2,128]{4,3,2,1,0:T(2,128)(2,1)S(1)} %copy-done.2), custom_call_target="tpu_custom_call" | custom-call | flops 402653184 | bytes 11796480 | tf_op jit(solution)/shard_map/attend_cached/pallas_call | solution.py:109
  39.7 0.0 slice-done
  39.7 0.0 slice-done.1
  39.7 1.4 %project.2.refs_0_ = f32[192,512]{1,0:T(8,128)S(1)} custom-call(s32[1]{0:T(128)} %bitcast.which_ref, bf16[192,2560]{1,0:T(8,128)(2,1)S(1)} %reshape.17.hidden_ref, bf16[64,3584]{1,0:T(8,128)(2,1)S(1)} %bitcast.9, bf16[4,2560,256]{2,1,0:T(8,128)(2,1)S(1)} %bitcast.7), custom_call_target="tpu_custom_call" | custom-call | flops 671088640 | bytes 3604480 | tf_op jit(solution)/shard_map/project/pallas_call | solution.py:153
  41.1 0.0 collective-permute-done.refs_1_
  41.1 2.5 %finish.1 = (bf16[48,4,2,2,128]{4,3,2,1,0:T(2,128)(2,1)}, bf16[48,64,128]{2,1,0:T(8,128)(2,1)}) custom-call(f32[192,512]{1,0:T(8,128)S(1)} %project.2.refs_0_, f32[192,512]{1,0:T(8,128)S(1)} %collective-permute-done.refs_1_, bf16[48,64,128]{2,1,0:T(8,128)(2,1)S(1)} %bitcast.11, f32[48,64,128]{2,1,0:T(8,128)S(1)} %get-tuple-element.7.refs_3_, ...), custom_call_target="tpu_custom_call" | custom-call | flops 301989888 | bytes 4718592 | tf_op jit(solution)/shard_map/finish/pallas_call | solution.py:215
  (1 shorter events, 0.0 us)
Async XLA Ops:
  0.6 0.8 %copy-start.5 = (bf16[2560,8]{0,1:T(8,128)(2,1)S(1)}, bf16[2560,8]{0,1:T(8,128)(2,1)}, u32[]{:S(2)}) copy-start(bf16[2560,8]{0,1:T(8,128)(2,1)} %param.9) | copy-start | bytes 122884
  1.4 0.7 %copy-start.6 = (bf16[8,2,4,128]{3,2,1,0:T(4,128)(2,1)S(1)}, bf16[8,2,4,128]{3,2,1,0:T(4,128)(2,1)}, u32[]{:S(2)}) copy-start(bf16[8,2,4,128]{3,2,1,0:T(4,128)(2,1)} %up_ref.1) | copy-start | bytes 49156
  2.9 20.4 %all-to-all-start = ((bf16[8,8,3584]{2,1,0:T(8,128)(2,1)}), bf16[8,8,3584]{2,1,0:T(8,128)(2,1)S(1)}, u32[]{:S(2)}, u32[]{:S(2)}) async-start(bf16[8,8,3584]{2,1,0:T(8,128)(2,1)} %payload.1), calls=%async_computation | async-start | bytes 917504 | tf_op jit(solution)/shard_map/all_to_all | solution.py:238
  11.9 2.5 %copy-start.3 = (bf16[2560,2,4,128]{3,2,1,0:T(4,128)(2,1)S(1)}, bf16[2560,2,4,128]{3,2,1,0:T(4,128)(2,1)}, u32[]{:S(2)}) copy-start(bf16[2560,2,4,128]{3,2,1,0:T(4,128)(2,1)} %base_ref.1) | copy-start | bytes 15728644
  14.4 12.9 %copy-start.4 = (bf16[48,4,16,128]{3,2,1,0:T(8,128)(2,1)S(1)}, bf16[48,4,16,128]{3,2,1,0:T(8,128)(2,1)}, u32[]{:S(2)}) copy-start(bf16[48,4,16,128]{3,2,1,0:T(8,128)(2,1)} %param.11) | copy-start | bytes 2359300
  19.8 2.3 %copy-start = (bf16[4,2560,256]{2,1,0:T(8,128)(2,1)}, bf16[4,2560,256]{2,1,0:T(8,128)(2,1)S(1)}, u32[]{:S(2)}) copy-start(bf16[4,2560,256]{2,1,0:T(8,128)(2,1)S(1)} %arrange_base.1.base_ref) | copy-start | bytes 15728644
  22.1 5.2 %copy-start.7 = (s32[48]{0:T(128)S(1)}, s32[48]{0:T(128)}, u32[]{:S(2)}) copy-start(s32[48]{0:T(128)} %lengths_ref.1) | copy-start | bytes 580
  23.3 2.5 %copy-start.1 = (bf16[4,2560,256]{2,1,0:T(8,128)(2,1)S(1)}, bf16[4,2560,256]{2,1,0:T(8,128)(2,1)}, u32[]{:S(2)}) copy-start(bf16[4,2560,256]{2,1,0:T(8,128)(2,1)} %copy-done) | copy-start | bytes 15728644
  25.8 13.9 %slice-start = ((s8[5242880]{0:T(1024)(128)(4,1)}), s8[4194304]{0:T(1024)(128)(4,1)S(1)}, s32[]{:S(2)}) async-start(s8[5242880]{0:T(1024)(128)(4,1)} %bitcast.6), calls=%async_computation.1 | async-start | bytes 8388608
  27.2 13.9 %collective-permute-start = (f32[192,512]{1,0:T(8,128)S(1)}, f32[192,512]{1,0:T(8,128)S(1)}, u32[]{:S(2)}, u32[]{:S(2)}) collective-permute-start(f32[192,512]{1,0:T(8,128)S(1)} %project.3), channel_id=1, source_target_pairs={{0,1},{1,0},{2,3},{3,2},{4,5},{5,4},{6,7},{7,6},{8,9},{9,8},{10,11... | collective-permute-start | bytes 1179656 | tf_op jit(solution)/shard_map/ppermute | solution.py:247
  27.3 2.8 %copy-start.2 = (bf16[48,128,2,2,128]{4,3,2,1,0:T(2,128)(2,1)S(1)}, bf16[48,128,2,2,128]{4,3,2,1,0:T(2,128)(2,1)}, u32[]{:S(2)}) copy-start(bf16[48,128,2,2,128]{4,3,2,1,0:T(2,128)(2,1)} %v_ref.1) | copy-start | bytes 18874372
  30.1 9.6 %slice-start.1 = ((s8[5242880]{0:T(1024)(128)(4,1)}), s8[1048576]{0:T(1024)(128)(4,1)S(1)}, s32[]{:S(2)}) async-start(s8[5242880]{0:T(1024)(128)(4,1)} %bitcast.6), calls=%async_computation.2 | async-start | bytes 2097152

commit v4 on v3

--- a/solution.py
+++ b/solution.py
@@ -20,54 +20,78 @@
     return pl.CostEstimate(flops=flops, bytes_accessed=moved, transcendentals=exps)
 
 
-def payload_kernel(down_ref, up_ref, out_ref, wide):
-    ranks, width = down_ref.shape
-    groups = up_ref.shape[1] * up_ref.shape[2]
-    size = up_ref.shape[3]
-    wide[...] = up_ref.reshape(ranks * groups, size)[...].astype(jnp.float32)
-    down = down_ref[...]
-    ups = [wide[pl.ds(n, ranks, stride=groups), :].astype(jnp.bfloat16) for n in range(groups)]
-    for i in range(out_ref.shape[0]):
-        out_ref[i, :, :width] = down
-        for n in range(groups):
-            out_ref[i, :, width + n * size : width + (n + 1) * size] = ups[n]
+def payload_kernel(down_hbm, up_hbm, out_hbm, held, ups, wide, sems):
+    ranks, width = down_hbm.shape
+    groups, size = ups.shape[1] * ups.shape[2], ups.shape[3]
+    get_down = pltpu.make_async_copy(down_hbm, held.at[:, pl.ds(0, width)], sems.at[0])
+    get_up = pltpu.make_async_copy(up_hbm, ups, sems.at[1])
+    get_up.start()
+    get_down.start()
+    get_up.wait()
+    wide[...] = ups.reshape(ranks * groups, size)[...].astype(jnp.float32)
+    for n in range(groups):
+        held[:, width + n * size : width + (n + 1) * size] = wide[pl.ds(n, ranks, stride=groups), :].astype(
+            jnp.bfloat16
+        )
+    get_down.wait()
+    puts = [pltpu.make_async_copy(held, out_hbm.at[i], sems.at[2 + i]) for i in range(out_hbm.shape[0])]
+    for put in puts:
+        put.start()
+    for put in puts:
+        put.wait()
 
 
 def make_payload(down, up, count):
     ranks, width = down.shape
-    columns = up.shape[1] * up.shape[2] * up.shape[3]
+    groups, size = up.shape[1] * up.shape[2], up.shape[3]
+    held = (ranks, width + groups * size)
     return pl.pallas_call(
         payload_kernel,
-        out_shape=jax.ShapeDtypeStruct((count, ranks, width + columns), jnp.bfloat16),
-        in_specs=[VMEM, VMEM],
-        out_specs=VMEM,
-        scratch_shapes=[pltpu.VMEM((ranks * columns // up.shape[3], up.shape[3]), jnp.float32)],
+        out_shape=jax.ShapeDtypeStruct((count,) + held, jnp.bfloat16),
+        in_specs=[pl.BlockSpec(memory_space=pltpu.HBM)] * 2,
+        out_specs=pl.BlockSpec(memory_space=pltpu.HBM),
+        scratch_shapes=[
+            pltpu.VMEM(held, jnp.bfloat16),
+            pltpu.VMEM(up.shape, jnp.bfloat16),
+            pltpu.VMEM((ranks * groups, size), jnp.float32),
+            pltpu.SemaphoreType.DMA((2 + count,)),
+        ],
         compiler_params=params(8),
         name="payload",
     )(down, up)
 
 
-def arrange_kernel(own, base_ref, out_ref, wide):
+def arrange_kernel(own, tile, base_ref, out_ref):
     width, two, kvh, size = base_ref.shape
     groups = two * kvh
-    wide[...] = base_ref.reshape(width * groups, size)[...].astype(jnp.float32)
-    for n in range(groups):
-        part, at = n // own, n % own
-        out_ref[part, :, at * size : (at + 1) * size] = wide[pl.ds(n, width, stride=groups), :].astype(jnp.bfloat16)
+    some = tile // groups
+    row = lax.broadcasted_iota(jnp.int32, (tile, tile), 0)
+    column = lax.broadcasted_iota(jnp.int32, (tile, tile), 1)
+    order = (column == (row % some) * groups + row // some).astype(jnp.float32).astype(jnp.bfloat16)
+    flat = base_ref.reshape(width * groups, size)
+    for f in range(0, width, 2 * some):
+        at = f * groups
+        pair = jnp.concatenate([flat[at : at + tile, :], flat[at + tile : at + 2 * tile, :]], axis=1)
+        moved = jnp.dot(order, pair, preferred_element_type=jnp.float32).astype(jnp.bfloat16)
+        for n in range(groups):
+            lanes = slice((n % own) * size, (n % own + 1) * size)
+            for h in range(2):
+                out_ref[n // own, f + h * some : f + (h + 1) * some, lanes] = moved[
+                    n * some : (n + 1) * some, h * size : (h + 1) * size
+                ]
 
 
 def arrange_base(base, own, step=512):
     width, two, kvh, size = base.shape
     groups = two * kvh
     return pl.pallas_call(
-        functools.partial(arrange_kernel, own),
+        functools.partial(arrange_kernel, own, 256),
         grid=(width // step,),
         out_shape=jax.ShapeDtypeStruct((groups // own, width, own * size), jnp.bfloat16),
         in_specs=[pl.BlockSpec((step, two, kvh, size), lambda i: (i, 0, 0, 0))],
         out_specs=pl.BlockSpec((groups // own, step, own * size), lambda i: (0, i, 0)),
-        scratch_shapes=[pltpu.VMEM((step * groups, size), jnp.float32)],
-        compiler_params=params(24),
-        cost_estimate=cost(0, 4 * base.size),
+        compiler_params=params(48),
+        cost_estimate=cost(512 * base.size, 4 * base.size),
         name="arrange_base",
     )(base)
 
@@ -83,17 +107,18 @@
     ones = jnp.ones((keys, size), jnp.bfloat16)
     k_all = k_ref.reshape(rows, keys, size)
     v_all = v_ref.reshape(rows, keys, size)
-    for r in range(rows):
-        scores = lax.dot_general(q_ref[r], k_all[r], NT, preferred_element_type=jnp.float32)
-        scores = jnp.where(column < own * lengths_ref[at + r], scores, LOW)
-        top = jnp.max(scores, axis=-1, keepdims=True)
-        weights = jnp.exp((scores - top) * scale).astype(jnp.bfloat16)
-        both = jnp.dot(
-            weights, jnp.concatenate([v_all[r], ones], axis=1), preferred_element_type=jnp.float32
-        )
-        sum_ref[r] = both[:, :size]
-        total_ref[r] = both[:, size:]
-        top_ref[r] = jnp.broadcast_to(top, (queries, size))
+    some = 4
+    for first in range(0, rows, some):
+        group = range(first, first + some)
+        scores = [lax.dot_general(q_ref[r], k_all[r], NT, preferred_element_type=jnp.float32) for r in group]
+        scores = [jnp.where(column < own * lengths_ref[at + r], s, LOW) for r, s in zip(group, scores)]
+        tops = [jnp.max(s, axis=-1, keepdims=True) for s in scores]
+        weights = [jnp.exp((s - t) * scale).astype(jnp.bfloat16) for s, t in zip(scores, tops)]
+        for r, w, top in zip(group, weights, tops):
+            both = jnp.dot(w, jnp.concatenate([v_all[r], ones], axis=1), preferred_element_type=jnp.float32)
+            sum_ref[r] = both[:, :size]
+            total_ref[r] = both[:, size:]
+            top_ref[r] = jnp.broadcast_to(top, (queries, size))
 
 
 def attend_cached(queries, cache, lengths, step=8):
@@ -115,7 +140,7 @@
             in_specs=[block, half(0), half(1)],
             out_specs=(block, block, block),
         ),
-        compiler_params=params(24),
+        compiler_params=params(48),
         cost_estimate=cost(
             8 * rows * many * slots * size, 2 * (cache.size + queries.size) + 12 * rows * many * size, rows * many * slots
         ),
@@ -237,8 +262,9 @@
     payload = make_payload(factor_a.T, factor_b, dp)
     gathered = lax.all_to_all(payload, "dp", 0, 0, tiled=True)
     gathered = gathered.reshape(-1, gathered.shape[-1])
+    state = attend_cached(queries, cache, lengths)
+    base_weight, state = lax.optimization_barrier((base_weight, state))
     base = arrange_base(base_weight, own)
-    state = attend_cached(queries, cache, lengths)
     tokens = hidden.reshape(rows * steps, width)
     me = lax.axis_index("tp")
     received = []

time: 44.1 us -> 40.8 us (0.925)
  Pallas kernels: 21.1 us -> 19.3 us
  waiting for transfers between devices: 1.2 us -> 0.33 us
  local copies, waits for them, and re-layouts: 13.2 us -> 12.4 us
    pallas_call x1, Pallas kernels: 9.59 us -> 7.79 us  [attend_cached(): pl.pallas_call(functools.partial(cached_kernel, heads, size ** (-0.5)), o...]
    all_to_all x1, waiting for transfers between devices: 1.2 us -> 0.01 us  [shards(): gathered = lax.all_to_all(payload, 'dp', 0, 0, tiled=True)]
    unnamed x20 -> x22, local copies, waits for them, and re-layouts: 11.5 us -> 10.7 us
  transfers between devices with their start and end apart: 2 -> 2, of which waited for: 1 -> 1; matrix products, arithmetic and copies ran while one was open for 4% -> 4% of each run, Pallas kernels for 38% -> 36%
where the time goes in v4:
time: 40.8 us; the launch traced here: 40.2 us
  Pallas kernels  19.3 us (47%)
  local copies, waits for them, and re-layouts  12.4 us (30%)
  starting transfers between devices  7.36 us (18%)
  between operations  0.75 us (2%)
    unnamed x22, local copies, waits for them, and re-layouts  10.7 us
    pallas_call x1, Pallas kernels, attend_cached(): pl.pallas_call(functools.partial(cached_kernel, heads, size ** (-0.5)), o...  7.79 us
    all_to_all x1, starting transfers between devices, shards(): gathered = lax.all_to_all(payload, 'dp', 0, 0, tiled=True)  7.29 us
    pallas_call x1, Pallas kernels, arrange_base(): pl.pallas_call(functools.partial(arrange_kernel, own, 256), grid=(width /...  5.36 us
    pallas_call x2, Pallas kernels, project(): pl.pallas_call(functools.partial(project_kernel, width), out_shape=jax.Sh...  2.75 us
    pallas_call x1, Pallas kernels, finish(): pl.pallas_call(functools.partial(finish_kernel, steps, heads, size ** (-0...  2.51 us
    reshape x1, local copies, waits for them, and re-layouts, shards(): tokens = hidden.reshape(rows * steps, width)  1.68 us
    pallas_call x1, Pallas kernels, make_payload(): pl.pallas_call(payload_kernel, out_shape=jax.ShapeDtypeStruct((count,) +...  0.9 us
  transfers between devices with their start and end apart: 2, of which 1 were waited for; matrix products, arithmetic and copies ran while one was open for 4% of the time, Pallas kernels for 36%

profile of v4, /device:TPU:0, one launch (start us, length us, event | category | flops | bytes accessed | tf_op | source)
XLA Modules:
  0.0 40.2 jit_solution(9326142408872372844)
XLA Ops:
  0.6 0.0 copy-start.8
  0.6 0.8 %copy-done.8 = bf16[2560,8]{0,1:T(8,128)(2,1)S(1)} copy-done((bf16[2560,8]{0,1:T(8,128)(2,1)S(1)}, bf16[2560,8]{0,1:T(8,128)(2,1)}, u32[]{:S(2)}) %copy-start.8) | copy-done | bytes 40984
  1.4 0.0 copy-start.9
  1.4 0.7 %copy-done.9 = bf16[8,2,4,128]{3,2,1,0:T(4,128)(2,1)S(1)} copy-done((bf16[8,2,4,128]{3,2,1,0:T(4,128)(2,1)S(1)}, bf16[8,2,4,128]{3,2,1,0:T(4,128)(2,1)}, u32[]{:S(2)}) %copy-start.9) | copy-done | bytes 16408
  2.1 0.9 %payload.1 = bf16[8,8,3584]{2,1,0:T(8,128)(2,1)} custom-call(bf16[8,2560]{1,0:T(8,128)(2,1)S(1)} %bitcast.10, bf16[8,2,4,128]{3,2,1,0:T(4,128)(2,1)S(1)} %copy-done.9), custom_call_target="tpu_custom_call" | custom-call | tf_op jit(solution)/shard_map/payload/pallas_call | solution.py:48
  3.0 7.3 %all-to-all-start = ((bf16[8,8,3584]{2,1,0:T(8,128)(2,1)}), bf16[8,8,3584]{2,1,0:T(8,128)(2,1)S(1)}, u32[]{:S(2)}, u32[]{:S(2)}) async-start(bf16[8,8,3584]{2,1,0:T(8,128)(2,1)} %payload.1), calls=%async_computation | async-start | bytes 917504 | tf_op jit(solution)/shard_map/all_to_all | solution.py:263
  10.3 1.7 %reshape.17.hidden_ref = bf16[192,2560]{1,0:T(8,128)(2,1)S(1)} reshape(bf16[48,4,2560]{2,1,0:T(4,128)(2,1)} %param.7) | data formatting | bytes 1966080 | tf_op jit(solution)/shard_map/reshape | solution.py:268
  12.0 0.0 copy-start.2
  12.0 1.1 %copy-done.2 = bf16[48,4,16,128]{3,2,1,0:T(8,128)(2,1)S(1)} copy-done((bf16[48,4,16,128]{3,2,1,0:T(8,128)(2,1)S(1)}, bf16[48,4,16,128]{3,2,1,0:T(8,128)(2,1)}, u32[]{:S(2)}) %copy-start.2) | copy-done | bytes 786456
  13.2 0.0 copy-start.10
  13.2 0.7 %copy-done.10 = s32[48]{0:T(128)S(1)} copy-done((s32[48]{0:T(128)S(1)}, s32[48]{0:T(128)}, u32[]{:S(2)}) %copy-start.10) | copy-done | bytes 216
  13.8 7.8 %attend_cached.1 = (f32[48,64,128]{2,1,0:T(8,128)S(1)}, f32[48,64,128]{2,1,0:T(8,128)S(1)}, f32[48,64,128]{2,1,0:T(8,128)S(1)}) custom-call(s32[48]{0:T(128)S(1)} %copy-done.10, bf16[48,64,128]{2,1,0:T(8,128)(2,1)S(1)} %bitcast.8, bf16[48,128,2,2,128]{4,3,2,1,0:T(2,128)(2,1)} %v_ref.1, bf16[48,128,2,2,128]{4,3,2,1,0:T(2,128)(2,1)} %v_ref.1), custom_call_target="tpu_custom_call" | custom-call | flops 402653184 | bytes 11796480 | tf_op jit(solution)/shard_map/attend_cached/pallas_call | solution.py:134
  21.6 0.0 copy-start.4
  21.6 1.2 %copy-done.4 = f32[48,64,128]{2,1,0:T(8,128)} copy-done((f32[48,64,128]{2,1,0:T(8,128)}, f32[48,64,128]{2,1,0:T(8,128)S(1)}, u32[]{:S(2)}) %copy-start.4) | copy-done | bytes 1572888
  22.8 0.0 copy-start.6
  22.8 1.2 %copy-done.6 = f32[48,64,128]{2,1,0:T(8,128)} copy-done((f32[48,64,128]{2,1,0:T(8,128)}, f32[48,64,128]{2,1,0:T(8,128)S(1)}, u32[]{:S(2)}) %copy-start.6) | copy-done | bytes 1572888
  24.0 5.4 %arrange_base.1.base_ref = bf16[4,2560,256]{2,1,0:T(8,128)(2,1)S(1)} custom-call(bf16[2560,2,4,128]{3,2,1,0:T(4,128)(2,1)} %base_ref), custom_call_target="tpu_custom_call" | custom-call | flops 1342177280 | bytes 10485760 | tf_op jit(solution)/shard_map/arrange_base/pallas_call | solution.py:87
  29.3 0.0 copy-start
  29.3 2.3 %copy-done = bf16[4,2560,256]{2,1,0:T(8,128)(2,1)} copy-done((bf16[4,2560,256]{2,1,0:T(8,128)(2,1)}, bf16[4,2560,256]{2,1,0:T(8,128)(2,1)S(1)}, u32[]{:S(2)}) %copy-start) | copy-done | bytes 5242904
  31.6 0.0 all-to-all-done
  31.6 0.0 copy-start.1
  31.6 2.5 %copy-done.1 = bf16[4,2560,256]{2,1,0:T(8,128)(2,1)S(1)} copy-done((bf16[4,2560,256]{2,1,0:T(8,128)(2,1)S(1)}, bf16[4,2560,256]{2,1,0:T(8,128)(2,1)}, u32[]{:S(2)}) %copy-start.1) | copy-done | bytes 5242904
  34.1 1.4 %project.3 = f32[192,512]{1,0:T(8,128)S(1)} custom-call(s32[1]{0:T(128)} %bitcast.4.which_ref, bf16[192,2560]{1,0:T(8,128)(2,1)S(1)} %reshape.17.hidden_ref, bf16[64,3584]{1,0:T(8,128)(2,1)S(1)} %bitcast.6, bf16[4,2560,256]{2,1,0:T(8,128)(2,1)S(1)} %copy-done.1), custom_call_target="tpu_custom_call" | custom-call | flops 671088640 | bytes 3604480 | tf_op jit(solution)/shard_map/project/pallas_call | solution.py:178
  35.5 0.0 copy-start.3
  35.5 0.0 copy-start.5
  35.5 0.0 copy-start.7
  35.5 0.1 collective-permute-start
  35.6 1.4 %project.2.refs_0_ = f32[192,512]{1,0:T(8,128)S(1)} custom-call(s32[1]{0:T(128)} %bitcast.which_ref, bf16[192,2560]{1,0:T(8,128)(2,1)S(1)} %reshape.17.hidden_ref, bf16[64,3584]{1,0:T(8,128)(2,1)S(1)} %bitcast.7, bf16[4,2560,256]{2,1,0:T(8,128)(2,1)S(1)} %copy-done.1), custom_call_target="tpu_custom_call" | custom-call | flops 671088640 | bytes 3604480 | tf_op jit(solution)/shard_map/project/pallas_call | solution.py:178
  37.0 0.3 collective-permute-done.refs_1_
  37.3 0.0 copy-done.3
  37.3 0.0 copy-done.5
  37.3 0.3 copy-done.7
  37.7 2.5 %finish.1 = (bf16[48,4,2,2,128]{4,3,2,1,0:T(2,128)(2,1)}, bf16[48,64,128]{2,1,0:T(8,128)(2,1)}) custom-call(f32[192,512]{1,0:T(8,128)S(1)} %project.2.refs_0_, f32[192,512]{1,0:T(8,128)S(1)} %collective-permute-done.refs_1_, bf16[48,64,128]{2,1,0:T(8,128)(2,1)S(1)} %bitcast.9, f32[48,64,128]{2,1,0:T(8,128)S(1)} %get-tuple-element.15.refs_3_, ...), custom_call_target="tpu_custom_call" | custom-call | flops 301989888 | bytes 4718592 | tf_op jit(solution)/shard_map/finish/pallas_call | solution.py:240
Async XLA Ops:
  0.6 0.8 %copy-start.8 = (bf16[2560,8]{0,1:T(8,128)(2,1)S(1)}, bf16[2560,8]{0,1:T(8,128)(2,1)}, u32[]{:S(2)}) copy-start(bf16[2560,8]{0,1:T(8,128)(2,1)} %param.9) | copy-start | bytes 122884
  1.4 0.7 %copy-start.9 = (bf16[8,2,4,128]{3,2,1,0:T(4,128)(2,1)S(1)}, bf16[8,2,4,128]{3,2,1,0:T(4,128)(2,1)}, u32[]{:S(2)}) copy-start(bf16[8,2,4,128]{3,2,1,0:T(4,128)(2,1)} %up_hbm.1) | copy-start | bytes 49156
  3.0 28.6 %all-to-all-start = ((bf16[8,8,3584]{2,1,0:T(8,128)(2,1)}), bf16[8,8,3584]{2,1,0:T(8,128)(2,1)S(1)}, u32[]{:S(2)}, u32[]{:S(2)}) async-start(bf16[8,8,3584]{2,1,0:T(8,128)(2,1)} %payload.1), calls=%async_computation | async-start | bytes 917504 | tf_op jit(solution)/shard_map/all_to_all | solution.py:263
  12.0 1.1 %copy-start.2 = (bf16[48,4,16,128]{3,2,1,0:T(8,128)(2,1)S(1)}, bf16[48,4,16,128]{3,2,1,0:T(8,128)(2,1)}, u32[]{:S(2)}) copy-start(bf16[48,4,16,128]{3,2,1,0:T(8,128)(2,1)} %param.11) | copy-start | bytes 2359300
  13.2 0.7 %copy-start.10 = (s32[48]{0:T(128)S(1)}, s32[48]{0:T(128)}, u32[]{:S(2)}) copy-start(s32[48]{0:T(128)} %lengths_ref.1) | copy-start | bytes 580
  21.6 1.2 %copy-start.4 = (f32[48,64,128]{2,1,0:T(8,128)}, f32[48,64,128]{2,1,0:T(8,128)S(1)}, u32[]{:S(2)}) copy-start(f32[48,64,128]{2,1,0:T(8,128)S(1)} %get-tuple-element.16.refs_4_) | copy-start | bytes 4718596
  22.8 1.2 %copy-start.6 = (f32[48,64,128]{2,1,0:T(8,128)}, f32[48,64,128]{2,1,0:T(8,128)S(1)}, u32[]{:S(2)}) copy-start(f32[48,64,128]{2,1,0:T(8,128)S(1)} %get-tuple-element.17.refs_5_) | copy-start | bytes 4718596
  29.3 2.3 %copy-start = (bf16[4,2560,256]{2,1,0:T(8,128)(2,1)}, bf16[4,2560,256]{2,1,0:T(8,128)(2,1)S(1)}, u32[]{:S(2)}) copy-start(bf16[4,2560,256]{2,1,0:T(8,128)(2,1)S(1)} %arrange_base.1.base_ref) | copy-start | bytes 15728644
  31.6 2.5 %copy-start.1 = (bf16[4,2560,256]{2,1,0:T(8,128)(2,1)S(1)}, bf16[4,2560,256]{2,1,0:T(8,128)(2,1)}, u32[]{:S(2)}) copy-start(bf16[4,2560,256]{2,1,0:T(8,128)(2,1)} %copy-done) | copy-start | bytes 15728644
  35.5 1.8 %copy-start.3 = (bf16[48,4,16,128]{3,2,1,0:T(8,128)(2,1)S(1)}, bf16[48,4,16,128]{3,2,1,0:T(8,128)(2,1)}, u32[]{:S(2)}) copy-start(bf16[48,4,16,128]{3,2,1,0:T(8,128)(2,1)} %param.11) | copy-start | bytes 2359300
  35.5 1.8 %copy-start.5 = (f32[48,64,128]{2,1,0:T(8,128)S(1)}, f32[48,64,128]{2,1,0:T(8,128)}, u32[]{:S(2)}) copy-start(f32[48,64,128]{2,1,0:T(8,128)} %copy-done.4) | copy-start | bytes 4718596
  35.5 2.1 %copy-start.7 = (f32[48,64,128]{2,1,0:T(8,128)S(1)}, f32[48,64,128]{2,1,0:T(8,128)}, u32[]{:S(2)}) copy-start(f32[48,64,128]{2,1,0:T(8,128)} %copy-done.6) | copy-start | bytes 4718596
  35.5 1.8 %collective-permute-start = (f32[192,512]{1,0:T(8,128)S(1)}, f32[192,512]{1,0:T(8,128)S(1)}, u32[]{:S(2)}, u32[]{:S(2)}) collective-permute-start(f32[192,512]{1,0:T(8,128)S(1)} %project.3), channel_id=1, source_target_pairs={{0,1},{1,0},{2,3},{3,2},{4,5},{5,4},{6,7},{7,6},{8,9},{9,8},{10,11... | collective-permute-start | bytes 1179656 | tf_op jit(solution)/shard_map/ppermute | solution.py:273

commit v5 on v4

--- a/solution.py
+++ b/solution.py
@@ -56,96 +56,125 @@
             pltpu.VMEM((ranks * groups, size), jnp.float32),
             pltpu.SemaphoreType.DMA((2 + count,)),
         ],
-        compiler_params=params(8),
+        compiler_params=params(60),
         name="payload",
     )(down, up)
 
 
-def arrange_kernel(own, tile, base_ref, out_ref):
-    width, two, kvh, size = base_ref.shape
+def local_kernel(chunks, heads, scale, *refs):
+    lengths_ref, hidden_hbm, base_hbm, queries_hbm, cache_hbm = refs[:5]
+    tokens_ref, base_ref, sum_ref, total_ref, top_ref = refs[5:10]
+    hidden, base, q_all, k_all, v_all, sems = refs[10:]
+    rows, queries, size = q_all.shape
+    slots, own = k_all.shape[1:3]
+    keys = slots * own
+    width, two, kvh, _ = base.shape
     groups = two * kvh
+    some_rows, some_width = rows // chunks, width // chunks
+
+    def copies(i):
+        mine = pl.ds(i * some_rows, some_rows)
+        features = pl.ds(i * some_width, some_width)
+        pairs = (
+            (queries_hbm.at[mine], q_all.at[mine]),
+            (cache_hbm.at[mine, :, 0], k_all.at[mine]),
+            (cache_hbm.at[mine, :, 1], v_all.at[mine]),
+            (base_hbm.at[features], base.at[features]),
+        )
+        return [pltpu.make_async_copy(a, b, sems.at[i, n]) for n, (a, b) in enumerate(pairs)]
+
+    get_hidden = pltpu.make_async_copy(hidden_hbm, hidden, sems.at[chunks, 0])
+    for i in range(chunks):
+        for copy in copies(i):
+            copy.start()
+    get_hidden.start()
+
+    column = lax.broadcasted_iota(jnp.int32, (queries, keys), 1)
+    head = lax.broadcasted_iota(jnp.int32, (queries, keys), 0) % heads
+    column = jnp.where(column % own == head // (heads // own), column, own * slots)
+    ones = jnp.ones((keys, size), jnp.bfloat16)
+    tile = 256
     some = tile // groups
     row = lax.broadcasted_iota(jnp.int32, (tile, tile), 0)
-    column = lax.broadcasted_iota(jnp.int32, (tile, tile), 1)
-    order = (column == (row % some) * groups + row // some).astype(jnp.float32).astype(jnp.bfloat16)
-    flat = base_ref.reshape(width * groups, size)
-    for f in range(0, width, 2 * some):
-        at = f * groups
-        pair = jnp.concatenate([flat[at : at + tile, :], flat[at + tile : at + 2 * tile, :]], axis=1)
+    place = lax.broadcasted_iota(jnp.int32, (tile, tile), 1)
+    order = (place == (row % some) * groups + row // some).astype(jnp.float32).astype(jnp.bfloat16)
+    flat_base = base.reshape(width * groups, size)
+    flat_k = k_all.reshape(rows, keys, size)
+    flat_v = v_all.reshape(rows, keys, size)
+
+    def attend(at, count):
+        group = [at + r for r in range(count)]
+        scores = [lax.dot_general(q_all[r], flat_k[r], NT, preferred_element_type=jnp.float32) for r in group]
+        scores = [jnp.where(column < own * lengths_ref[r], s, LOW) for r, s in zip(group, scores)]
+        tops = [jnp.max(s, axis=-1, keepdims=True) for s in scores]
+        weights = [jnp.exp((s - t) * scale).astype(jnp.bfloat16) for s, t in zip(scores, tops)]
+        for r, w, top in zip(group, weights, tops):
+            both = jnp.dot(w, jnp.concatenate([flat_v[r], ones], axis=1), preferred_element_type=jnp.float32)
+            sum_ref[r] = both[:, :size]
+            total_ref[r] = both[:, size:]
+            top_ref[r] = jnp.broadcast_to(top, (queries, size))
+
+    def arrange(f):
+        at = pl.multiple_of(f * groups, tile)
+        pair = jnp.concatenate([flat_base[pl.ds(at + h * tile, tile), :] for h in range(2)], axis=1)
         moved = jnp.dot(order, pair, preferred_element_type=jnp.float32).astype(jnp.bfloat16)
         for n in range(groups):
             lanes = slice((n % own) * size, (n % own + 1) * size)
             for h in range(2):
-                out_ref[n // own, f + h * some : f + (h + 1) * some, lanes] = moved[
+                base_ref[n // own, pl.ds(pl.multiple_of(f + h * some, some), some), lanes] = moved[
                     n * some : (n + 1) * some, h * size : (h + 1) * size
                 ]
 
-
-def arrange_base(base, own, step=512):
-    width, two, kvh, size = base.shape
-    groups = two * kvh
-    return pl.pallas_call(
-        functools.partial(arrange_kernel, own, 256),
-        grid=(width // step,),
-        out_shape=jax.ShapeDtypeStruct((groups // own, width, own * size), jnp.bfloat16),
-        in_specs=[pl.BlockSpec((step, two, kvh, size), lambda i: (i, 0, 0, 0))],
-        out_specs=pl.BlockSpec((groups // own, step, own * size), lambda i: (0, i, 0)),
-        compiler_params=params(48),
-        cost_estimate=cost(512 * base.size, 4 * base.size),
-        name="arrange_base",
-    )(base)
-
-
-def cached_kernel(heads, scale, lengths_ref, q_ref, k_ref, v_ref, sum_ref, total_ref, top_ref):
-    rows, queries, size = q_ref.shape
-    slots, own = k_ref.shape[1], k_ref.shape[2]
-    keys = slots * own
-    at = pl.program_id(0) * rows
-    column = lax.broadcasted_iota(jnp.int32, (queries, keys), 1)
-    head = lax.broadcasted_iota(jnp.int32, (queries, keys), 0) % heads
-    column = jnp.where(column % own == head // (heads // own), column, own * slots)
-    ones = jnp.ones((keys, size), jnp.bfloat16)
-    k_all = k_ref.reshape(rows, keys, size)
-    v_all = v_ref.reshape(rows, keys, size)
-    some = 4
-    for first in range(0, rows, some):
-        group = range(first, first + some)
-        scores = [lax.dot_general(q_ref[r], k_all[r], NT, preferred_element_type=jnp.float32) for r in group]
-        scores = [jnp.where(column < own * lengths_ref[at + r], s, LOW) for r, s in zip(group, scores)]
-        tops = [jnp.max(s, axis=-1, keepdims=True) for s in scores]
-        weights = [jnp.exp((s - t) * scale).astype(jnp.bfloat16) for s, t in zip(scores, tops)]
-        for r, w, top in zip(group, weights, tops):
-            both = jnp.dot(w, jnp.concatenate([v_all[r], ones], axis=1), preferred_element_type=jnp.float32)
-            sum_ref[r] = both[:, :size]
-            total_ref[r] = both[:, size:]
-            top_ref[r] = jnp.broadcast_to(top, (queries, size))
-
-
-def attend_cached(queries, cache, lengths, step=8):
+    @pl.loop(0, chunks)
+    def _(i):
+        for copy in copies(i):
+            copy.wait()
+        for r in range(0, some_rows, 3):
+            attend(i * some_rows + r, 3)
+        for f in range(0, some_width, 2 * some):
+            arrange(i * some_width + f)
+
+    get_hidden.wait()
+    tokens_ref[...] = hidden.reshape(tokens_ref.shape)[...]
+
+
+def local(hidden, base, queries, cache, lengths):
     rows, steps, heads, size = queries.shape
     slots, own = cache.shape[1], cache.shape[3]
+    width, two, kvh, _ = base.shape
     many = steps * heads
+    chunks = 8
     state = jax.ShapeDtypeStruct((rows, many, size), jnp.float32)
-    block = pl.BlockSpec((step, many, size), lambda i, *_: (i, 0, 0))
-
-    def half(c):
-        return pl.BlockSpec((step, slots, None, own, size), lambda i, *_: (i, 0, c, 0, 0))
-
-    return pl.pallas_call(
-        functools.partial(cached_kernel, heads, size ** (-0.5)),
-        out_shape=(state, state, state),
-        grid_spec=pltpu.PrefetchScalarGridSpec(
-            num_scalar_prefetch=1,
-            grid=(rows // step,),
-            in_specs=[block, half(0), half(1)],
-            out_specs=(block, block, block),
-        ),
-        compiler_params=params(48),
+    half = (rows, slots, own, size)
+    outs = (
+        jax.ShapeDtypeStruct((rows * steps, width), jnp.bfloat16),
+        jax.ShapeDtypeStruct((two * kvh // own, width, own * size), jnp.bfloat16),
+        state,
+        state,
+        state,
+    )
+    tokens, base, *state = pl.pallas_call(
+        functools.partial(local_kernel, chunks, heads, size ** (-0.5)),
+        out_shape=outs,
+        in_specs=[pl.BlockSpec(memory_space=pltpu.SMEM)] + [pl.BlockSpec(memory_space=pltpu.HBM)] * 4,
+        out_specs=(VMEM,) * len(outs),
+        scratch_shapes=[
+            pltpu.VMEM(hidden.shape, jnp.bfloat16),
+            pltpu.VMEM(base.shape, jnp.bfloat16),
+            pltpu.VMEM((rows, many, size), jnp.bfloat16),
+            pltpu.VMEM(half, jnp.bfloat16),
+            pltpu.VMEM(half, jnp.bfloat16),
+            pltpu.SemaphoreType.DMA((chunks + 1, 4)),
+        ],
+        compiler_params=params(44),
         cost_estimate=cost(
-            8 * rows * many * slots * size, 2 * (cache.size + queries.size) + 12 * rows * many * size, rows * many * slots
-        ),
-        name="attend_cached",
-    )(lengths, queries.reshape(rows, many, size), cache, cache)
+            8 * rows * many * slots * size + 512 * base.size,
+            2 * (cache.size + queries.size + base.size + hidden.size),
+            rows * many * slots,
+        ),
+        name="local",
+    )(lengths, hidden, base, queries.reshape(rows, many, size), cache)
+    return tokens, base, state
 
 
 def project_kernel(down_at, which_ref, hidden_ref, gathered_ref, base_ref, out_ref, merged):
@@ -257,15 +286,12 @@
 
 
 def shards(dp, tp, hidden, base_weight, factor_a, factor_b, queries, cache, lengths):
-    rows, steps, width = hidden.shape
     own = cache.shape[3]
     payload = make_payload(factor_a.T, factor_b, dp)
     gathered = lax.all_to_all(payload, "dp", 0, 0, tiled=True)
     gathered = gathered.reshape(-1, gathered.shape[-1])
-    state = attend_cached(queries, cache, lengths)
-    base_weight, state = lax.optimization_barrier((base_weight, state))
-    base = arrange_base(base_weight, own)
-    tokens = hidden.reshape(rows * steps, width)
+    tokens, base, state = local(hidden, base_weight, queries, cache, lengths)
+    gathered, base = lax.optimization_barrier((gathered, base))
     me = lax.axis_index("tp")
     received = []
     for k in range(1, tp):

time: 40.8 us -> 36.2 us (0.89)
  local copies, waits for them, and re-layouts: 12.4 us -> 8.16 us
    unnamed x22 -> x18, local copies, waits for them, and re-layouts: 10.7 us -> 8.16 us
    reshape x1 -> x0, local copies, waits for them, and re-layouts: 1.68 us -> none  [shards(): tokens = hidden.reshape(rows * steps, width)]
    pallas_call x1, Pallas kernels: 0.9 us -> 1.63 us  [make_payload(): pl.pallas_call(payload_kernel, out_shape=jax.ShapeDtypeStruct((count,) +...]
    pallas_call x2 -> x1, Pallas kernels: 13.1 us -> 12.5 us  [local(): pl.pallas_call(functools.partial(local_kernel, chunks, heads, size ** (-0...]
  transfers between devices with their start and end apart: 2 -> 2, of which waited for: 1 -> 1; matrix products, arithmetic and copies ran while one was open for 4% -> 0% of each run, Pallas kernels for 36% -> 39%
where the time goes in v5:
time: 36.2 us; the launch traced here: 35.8 us
  Pallas kernels  19.2 us (53%)
  local copies, waits for them, and re-layouts  8.16 us (23%)
  starting transfers between devices  7.36 us (20%)
  between operations  0.71 us (2%)
    pallas_call x1, Pallas kernels, local(): pl.pallas_call(functools.partial(local_kernel, chunks, heads, size ** (-0...  12.5 us
    unnamed x18, local copies, waits for them, and re-layouts  8.16 us
    all_to_all x1, starting transfers between devices, shards(): gathered = lax.all_to_all(payload, 'dp', 0, 0, tiled=True)  7.29 us
    pallas_call x2, Pallas kernels, project(): pl.pallas_call(functools.partial(project_kernel, width), out_shape=jax.Sh...  2.75 us
    pallas_call x1, Pallas kernels, finish(): pl.pallas_call(functools.partial(finish_kernel, steps, heads, size ** (-0...  2.38 us
    pallas_call x1, Pallas kernels, make_payload(): pl.pallas_call(payload_kernel, out_shape=jax.ShapeDtypeStruct((count,) +...  1.63 us
  transfers between devices with their start and end apart: 2, of which 1 were waited for; matrix products, arithmetic and copies ran while one was open for 0% of the time, Pallas kernels for 39%

profile of v5, /device:TPU:0, one launch (start us, length us, event | category | flops | bytes accessed | tf_op | source)
XLA Modules:
  0.0 35.8 jit_solution(945685762546840578)
XLA Ops:
  0.6 1.6 %payload.1 = bf16[8,8,3584]{2,1,0:T(8,128)(2,1)} custom-call(bf16[8,2560]{1,0:T(8,128)(2,1)} %bitcast.10, bf16[8,2,4,128]{3,2,1,0:T(4,128)(2,1)} %up_hbm.1), custom_call_target="tpu_custom_call" | custom-call | tf_op jit(solution)/shard_map/payload/pallas_call | solution.py:48
  2.3 7.3 %all-to-all-start = ((bf16[8,8,3584]{2,1,0:T(8,128)(2,1)}), bf16[8,8,3584]{2,1,0:T(8,128)(2,1)S(1)}, u32[]{:S(2)}, u32[]{:S(2)}) async-start(bf16[8,8,3584]{2,1,0:T(8,128)(2,1)} %payload.1), calls=%async_computation | async-start | bytes 917504 | tf_op jit(solution)/shard_map/all_to_all | solution.py:291
  9.6 0.0 copy-start.1
  9.6 1.1 %copy-done.1 = bf16[48,4,16,128]{3,2,1,0:T(8,128)(2,1)S(1)} copy-done((bf16[48,4,16,128]{3,2,1,0:T(8,128)(2,1)S(1)}, bf16[48,4,16,128]{3,2,1,0:T(8,128)(2,1)}, u32[]{:S(2)}) %copy-start.1) | copy-done | bytes 786456
  10.7 0.0 copy-start.7
  10.7 1.2 %copy-done.7 = bf16[48,4,2560]{2,1,0:T(4,128)(2,1)S(1)} copy-done((bf16[48,4,2560]{2,1,0:T(4,128)(2,1)S(1)}, bf16[48,4,2560]{2,1,0:T(4,128)(2,1)}, u32[]{:S(2)}) %copy-start.7) | copy-done | bytes 983064
  11.9 0.0 copy-start.8
  11.9 0.7 %copy-done.8 = s32[48]{0:T(128)S(1)} copy-done((s32[48]{0:T(128)S(1)}, s32[48]{0:T(128)}, u32[]{:S(2)}) %copy-start.8) | copy-done | bytes 216
  12.6 12.5 %local.1 = (bf16[192,2560]{1,0:T(8,128)(2,1)S(1)}, bf16[4,2560,256]{2,1,0:T(8,128)(2,1)}, f32[48,64,128]{2,1,0:T(8,128)S(1)}, f32[48,64,128]{2,1,0:T(8,128)S(1)}, f32[48,64,128]{2,1,0:T(8,128)S(1)}) custom-call(s32[48]{0:T(128)S(1)} %copy-done.8, bf16[48,4,2560]{2,1,0:T(4,128)(2,1)S(1)} %copy-done.7, bf16[2560,2,4,128]{3,2,1,0:T(4,128)(2,1)} %refs_2_.1, ...), custom_call_target="tpu_custom_call" | custom-call | flops 1744830464 | bytes 13303808 | tf_op jit(solution)/shard_map/local/pallas_call | solution.py:156
  25.0 0.0 copy-start.3
  25.0 1.2 %copy-done.3 = f32[48,64,128]{2,1,0:T(8,128)} copy-done((f32[48,64,128]{2,1,0:T(8,128)}, f32[48,64,128]{2,1,0:T(8,128)S(1)}, u32[]{:S(2)}) %copy-start.3) | copy-done | bytes 1572888
  26.2 0.0 copy-start.5
  26.2 1.2 %copy-done.5 = f32[48,64,128]{2,1,0:T(8,128)} copy-done((f32[48,64,128]{2,1,0:T(8,128)}, f32[48,64,128]{2,1,0:T(8,128)S(1)}, u32[]{:S(2)}) %copy-start.5) | copy-done | bytes 1572888
  27.4 0.0 all-to-all-done
  27.4 0.0 copy-start
  27.4 2.5 %copy-done = bf16[4,2560,256]{2,1,0:T(8,128)(2,1)S(1)} copy-done((bf16[4,2560,256]{2,1,0:T(8,128)(2,1)S(1)}, bf16[4,2560,256]{2,1,0:T(8,128)(2,1)}, u32[]{:S(2)}) %copy-start) | copy-done | bytes 5242904
  29.9 1.4 %project.3 = f32[192,512]{1,0:T(8,128)S(1)} custom-call(s32[1]{0:T(128)} %bitcast.4.which_ref, bf16[192,2560]{1,0:T(8,128)(2,1)S(1)} %get-tuple-element.11.hidden_ref, bf16[64,3584]{1,0:T(8,128)(2,1)S(1)} %bitcast.6, bf16[4,2560,256]{2,1,0:T(8,128)(2,1)S(1)} %copy-done), custom_call_target="tpu_custom_call" | custom-call | flops 671088640 | bytes 3604480 | tf_op jit(solution)/shard_map/project/pallas_call | solution.py:207
  31.3 0.0 copy-start.2
  31.3 0.0 copy-start.4
  31.3 0.0 copy-start.6
  31.3 0.1 collective-permute-start
  31.4 1.4 %project.2.refs_0_ = f32[192,512]{1,0:T(8,128)S(1)} custom-call(s32[1]{0:T(128)} %bitcast.which_ref, bf16[192,2560]{1,0:T(8,128)(2,1)S(1)} %get-tuple-element.11.hidden_ref, bf16[64,3584]{1,0:T(8,128)(2,1)S(1)} %bitcast.7, bf16[4,2560,256]{2,1,0:T(8,128)(2,1)S(1)} %copy-done), custom_call_target="tpu_custom_call" | custom-call | flops 671088640 | bytes 3604480 | tf_op jit(solution)/shard_map/project/pallas_call | solution.py:207
  32.8 0.3 collective-permute-done.refs_1_
  33.1 0.0 copy-done.2
  33.1 0.0 copy-done.4
  33.1 0.3 copy-done.6
  33.4 2.4 %finish.1 = (bf16[48,4,2,2,128]{4,3,2,1,0:T(2,128)(2,1)}, bf16[48,64,128]{2,1,0:T(8,128)(2,1)}) custom-call(f32[192,512]{1,0:T(8,128)S(1)} %project.2.refs_0_, f32[192,512]{1,0:T(8,128)S(1)} %collective-permute-done.refs_1_, bf16[48,64,128]{2,1,0:T(8,128)(2,1)S(1)} %bitcast.9, f32[48,64,128]{2,1,0:T(8,128)S(1)} %get-tuple-element.15.refs_3_, ...), custom_call_target="tpu_custom_call" | custom-call | flops 301989888 | bytes 4718592 | tf_op jit(solution)/shard_map/finish/pallas_call | solution.py:269
Async XLA Ops:
  2.3 25.1 %all-to-all-start = ((bf16[8,8,3584]{2,1,0:T(8,128)(2,1)}), bf16[8,8,3584]{2,1,0:T(8,128)(2,1)S(1)}, u32[]{:S(2)}, u32[]{:S(2)}) async-start(bf16[8,8,3584]{2,1,0:T(8,128)(2,1)} %payload.1), calls=%async_computation | async-start | bytes 917504 | tf_op jit(solution)/shard_map/all_to_all | solution.py:291
  9.6 1.1 %copy-start.1 = (bf16[48,4,16,128]{3,2,1,0:T(8,128)(2,1)S(1)}, bf16[48,4,16,128]{3,2,1,0:T(8,128)(2,1)}, u32[]{:S(2)}) copy-start(bf16[48,4,16,128]{3,2,1,0:T(8,128)(2,1)} %param.11) | copy-start | bytes 2359300
  10.7 1.2 %copy-start.7 = (bf16[48,4,2560]{2,1,0:T(4,128)(2,1)S(1)}, bf16[48,4,2560]{2,1,0:T(4,128)(2,1)}, u32[]{:S(2)}) copy-start(bf16[48,4,2560]{2,1,0:T(4,128)(2,1)} %refs_1_.1) | copy-start | bytes 2949124
  11.9 0.7 %copy-start.8 = (s32[48]{0:T(128)S(1)}, s32[48]{0:T(128)}, u32[]{:S(2)}) copy-start(s32[48]{0:T(128)} %refs_0_.1) | copy-start | bytes 580
  25.0 1.2 %copy-start.3 = (f32[48,64,128]{2,1,0:T(8,128)}, f32[48,64,128]{2,1,0:T(8,128)S(1)}, u32[]{:S(2)}) copy-start(f32[48,64,128]{2,1,0:T(8,128)S(1)} %get-tuple-element.16.refs_4_) | copy-start | bytes 4718596
  26.2 1.2 %copy-start.5 = (f32[48,64,128]{2,1,0:T(8,128)}, f32[48,64,128]{2,1,0:T(8,128)S(1)}, u32[]{:S(2)}) copy-start(f32[48,64,128]{2,1,0:T(8,128)S(1)} %get-tuple-element.17.refs_5_) | copy-start | bytes 4718596
  27.4 2.5 %copy-start = (bf16[4,2560,256]{2,1,0:T(8,128)(2,1)S(1)}, bf16[4,2560,256]{2,1,0:T(8,128)(2,1)}, u32[]{:S(2)}) copy-start(bf16[4,2560,256]{2,1,0:T(8,128)(2,1)} %get-tuple-element.14.base_ref) | copy-start | bytes 15728644
  31.3 1.8 %copy-start.2 = (bf16[48,4,16,128]{3,2,1,0:T(8,128)(2,1)S(1)}, bf16[48,4,16,128]{3,2,1,0:T(8,128)(2,1)}, u32[]{:S(2)}) copy-start(bf16[48,4,16,128]{3,2,1,0:T(8,128)(2,1)} %param.11) | copy-start | bytes 2359300
  31.3 1.8 %copy-start.4 = (f32[48,64,128]{2,1,0:T(8,128)S(1)}, f32[48,64,128]{2,1,0:T(8,128)}, u32[]{:S(2)}) copy-start(f32[48,64,128]{2,1,0:T(8,128)} %copy-done.3) | copy-start | bytes 4718596
  31.3 2.1 %copy-start.6 = (f32[48,64,128]{2,1,0:T(8,128)S(1)}, f32[48,64,128]{2,1,0:T(8,128)}, u32[]{:S(2)}) copy-start(f32[48,64,128]{2,1,0:T(8,128)} %copy-done.5) | copy-start | bytes 4718596
  31.3 1.8 %collective-permute-start = (f32[192,512]{1,0:T(8,128)S(1)}, f32[192,512]{1,0:T(8,128)S(1)}, u32[]{:S(2)}, u32[]{:S(2)}) collective-permute-start(f32[192,512]{1,0:T(8,128)S(1)} %project.3), channel_id=1, source_target_pairs={{0,1},{1,0},{2,3},{3,2},{4,5},{5,4},{6,7},{7,6},{8,9},{9,8},{10,11... | collective-permute-start | bytes 1179656 | tf_op jit(solution)/shard_map/ppermute | solution.py:299

commit v6 on v5

--- a/solution.py
+++ b/solution.py
@@ -14,6 +14,10 @@
 
 def params(mib):
     return pltpu.CompilerParams(vmem_limit_bytes=mib * 1024 * 1024)
+
+
+def in_hbm(x):
+    return pltpu.with_memory_space_constraint(x, pltpu.HBM)
 
 
 def cost(flops, moved, exps=0):
@@ -58,13 +62,13 @@
         ],
         compiler_params=params(60),
         name="payload",
-    )(down, up)
+    )(in_hbm(down), in_hbm(up))
 
 
 def local_kernel(chunks, heads, scale, *refs):
-    lengths_ref, hidden_hbm, base_hbm, queries_hbm, cache_hbm = refs[:5]
-    tokens_ref, base_ref, sum_ref, total_ref, top_ref = refs[5:10]
-    hidden, base, q_all, k_all, v_all, sems = refs[10:]
+    lengths_hbm, hidden_hbm, base_hbm, queries_hbm, cache_hbm = refs[:5]
+    tokens_ref, base_ref, q_all, sum_ref, total_ref, top_ref = refs[5:11]
+    lengths_ref, hidden, base, k_all, v_all, sems = refs[11:]
     rows, queries, size = q_all.shape
     slots, own = k_all.shape[1:3]
     keys = slots * own
@@ -84,6 +88,8 @@
         return [pltpu.make_async_copy(a, b, sems.at[i, n]) for n, (a, b) in enumerate(pairs)]
 
     get_hidden = pltpu.make_async_copy(hidden_hbm, hidden, sems.at[chunks, 0])
+    get_lengths = pltpu.make_async_copy(lengths_hbm, lengths_ref, sems.at[chunks, 1])
+    get_lengths.start()
     for i in range(chunks):
         for copy in copies(i):
             copy.start()
@@ -125,6 +131,8 @@
                     n * some : (n + 1) * some, h * size : (h + 1) * size
                 ]
 
+    get_lengths.wait()
+
     @pl.loop(0, chunks)
     def _(i):
         for copy in copies(i):
@@ -144,37 +152,38 @@
     width, two, kvh, _ = base.shape
     many = steps * heads
     chunks = 8
-    state = jax.ShapeDtypeStruct((rows, many, size), jnp.float32)
+    state = pltpu.VMEM((rows, many, size), jnp.float32)
     half = (rows, slots, own, size)
     outs = (
-        jax.ShapeDtypeStruct((rows * steps, width), jnp.bfloat16),
-        jax.ShapeDtypeStruct((two * kvh // own, width, own * size), jnp.bfloat16),
+        pltpu.VMEM((rows * steps, width), jnp.bfloat16),
+        pltpu.VMEM((two * kvh // own, width, own * size), jnp.bfloat16),
+        pltpu.VMEM((rows, many, size), jnp.bfloat16),
         state,
         state,
         state,
     )
-    tokens, base, *state = pl.pallas_call(
+    tokens, base, queries, *state = pl.pallas_call(
         functools.partial(local_kernel, chunks, heads, size ** (-0.5)),
         out_shape=outs,
-        in_specs=[pl.BlockSpec(memory_space=pltpu.SMEM)] + [pl.BlockSpec(memory_space=pltpu.HBM)] * 4,
+        in_specs=[pl.BlockSpec(memory_space=pltpu.HBM)] * 5,
         out_specs=(VMEM,) * len(outs),
         scratch_shapes=[
+            pltpu.SMEM(lengths.shape, jnp.int32),
             pltpu.VMEM(hidden.shape, jnp.bfloat16),
             pltpu.VMEM(base.shape, jnp.bfloat16),
-            pltpu.VMEM((rows, many, size), jnp.bfloat16),
             pltpu.VMEM(half, jnp.bfloat16),
             pltpu.VMEM(half, jnp.bfloat16),
             pltpu.SemaphoreType.DMA((chunks + 1, 4)),
         ],
-        compiler_params=params(44),
+        compiler_params=params(28),
         cost_estimate=cost(
             8 * rows * many * slots * size + 512 * base.size,
             2 * (cache.size + queries.size + base.size + hidden.size),
             rows * many * slots,
         ),
         name="local",
-    )(lengths, hidden, base, queries.reshape(rows, many, size), cache)
-    return tokens, base, state
+    )(*map(in_hbm, (lengths, hidden, base, queries.reshape(rows, many, size), cache)))
+    return tokens, base, queries, state
 
 
 def project_kernel(down_at, which_ref, hidden_ref, gathered_ref, base_ref, out_ref, merged):
@@ -262,10 +271,10 @@
         context_ref[mine] = (summed / total).astype(jnp.bfloat16).reshape(group, queries, size)
 
 
-def finish(parts, queries, state, own):
-    rows, steps, heads, size = queries.shape
+def finish(parts, queries, state, steps, own):
+    rows, many, size = queries.shape
+    heads = many // steps
     group = size // (own * steps)
-    many = steps * heads
     fresh, context = pl.pallas_call(
         functools.partial(finish_kernel, steps, heads, size ** (-0.5), group, len(parts)),
         out_shape=(
@@ -281,16 +290,16 @@
         compiler_params=params(24),
         cost_estimate=cost(rows * many * size * size * 6, 12 * rows * many * size, rows * many * size * 2),
         name="finish",
-    )(*parts, queries.reshape(rows, many, size), *state)
+    )(*parts, queries, *state)
     return fresh, context.reshape(rows, steps, heads, size)
 
 
 def shards(dp, tp, hidden, base_weight, factor_a, factor_b, queries, cache, lengths):
-    own = cache.shape[3]
+    steps, own = queries.shape[1], cache.shape[3]
     payload = make_payload(factor_a.T, factor_b, dp)
     gathered = lax.all_to_all(payload, "dp", 0, 0, tiled=True)
     gathered = gathered.reshape(-1, gathered.shape[-1])
-    tokens, base, state = local(hidden, base_weight, queries, cache, lengths)
+    tokens, base, queries, state = local(hidden, base_weight, queries, cache, lengths)
     gathered, base = lax.optimization_barrier((gathered, base))
     me = lax.axis_index("tp")
     received = []
@@ -298,7 +307,7 @@
         other = project(jnp.full((1,), me ^ k, jnp.int32), tokens, gathered, base)
         received.append(lax.ppermute(other, "tp", [(i, i ^ k) for i in range(tp)]))
     mine = project(jnp.full((1,), me, jnp.int32), tokens, gathered, base)
-    return finish([mine] + received, queries, state, own)
+    return finish([mine] + received, queries, state, steps, own)
 
 
 def solution(mesh):

time: 36.2 us -> 33.5 us (0.925)
  Pallas kernels: 19.2 us -> 16.5 us
    pallas_call x1, Pallas kernels: 12.5 us -> 9.64 us  [local(): pl.pallas_call(functools.partial(local_kernel, chunks, heads, size ** (-0...]
    unnamed x18 -> x16, local copies, waits for them, and re-layouts: 8.16 us -> 8.31 us
  transfers between devices with their start and end apart: 2 -> 2, of which waited for: 1 -> 1; matrix products, arithmetic and copies ran while one was open for 0% -> 0% of each run, Pallas kernels for 39% -> 33%
where the time goes in v6:
time: 33.5 us; the launch traced here: 33.2 us
  Pallas kernels  16.5 us (49%)
  local copies, waits for them, and re-layouts  8.31 us (25%)
  starting transfers between devices  7.36 us (22%)
  between operations  0.71 us (2%)
    pallas_call x1, Pallas kernels, local(): pl.pallas_call(functools.partial(local_kernel, chunks, heads, size ** (-0...  9.64 us
    unnamed x16, local copies, waits for them, and re-layouts  8.31 us
    all_to_all x1, starting transfers between devices, shards(): gathered = lax.all_to_all(payload, 'dp', 0, 0, tiled=True)  7.29 us
    pallas_call x2, Pallas kernels, project(): pl.pallas_call(functools.partial(project_kernel, width), out_shape=jax.Sh...  2.76 us
    pallas_call x1, Pallas kernels, finish(): pl.pallas_call(functools.partial(finish_kernel, steps, heads, size ** (-0...  2.38 us
    pallas_call x1, Pallas kernels, make_payload(): pl.pallas_call(payload_kernel, out_shape=jax.ShapeDtypeStruct((count,) +...  1.67 us
  transfers between devices with their start and end apart: 2, of which 1 were waited for; matrix products, arithmetic and copies ran while one was open for 0% of the time, Pallas kernels for 33%

profile of v6, /device:TPU:0, one launch (start us, length us, event | category | flops | bytes accessed | tf_op | source)
XLA Modules:
  0.0 33.2 jit_solution(3639571200531454930)
XLA Ops:
  0.6 1.7 %payload.1 = bf16[8,8,3584]{2,1,0:T(8,128)(2,1)} custom-call(bf16[8,2560]{1,0:T(8,128)(2,1)} %bitcast.9, bf16[8,2,4,128]{3,2,1,0:T(4,128)(2,1)} %up_hbm.1), custom_call_target="tpu_custom_call" | custom-call | tf_op jit(solution)/shard_map/payload/pallas_call | solution.py:52
  2.3 7.3 %all-to-all-start = ((bf16[8,8,3584]{2,1,0:T(8,128)(2,1)}), bf16[8,8,3584]{2,1,0:T(8,128)(2,1)S(1)}, u32[]{:S(2)}, u32[]{:S(2)}) async-start(bf16[8,8,3584]{2,1,0:T(8,128)(2,1)} %payload.1), calls=%async_computation | async-start | bytes 917504 | tf_op jit(solution)/shard_map/all_to_all | solution.py:300
  9.6 9.6 %local.1 = (bf16[192,2560]{1,0:T(8,128)(2,1)S(1)}, bf16[4,2560,256]{2,1,0:T(8,128)(2,1)S(1)}, bf16[48,64,128]{2,1,0:T(8,128)(2,1)S(1)}, f32[48,64,128]{2,1,0:T(8...) custom-call(s32[48]{0:T(128)} %refs_0_.1, bf16[48,4,2560]{2,1,0:T(4,128)(2,1)} %refs_1_.1, ...), custom_call_target="tpu_custom_call" | custom-call | flops 1744830464 | bytes 13303808 | tf_op jit(solution)/shard_map/local/pallas_call | solution.py:165
  19.2 0.0 copy-start
  19.3 2.3 %copy-done = bf16[4,2560,256]{2,1,0:T(8,128)(2,1)} copy-done((bf16[4,2560,256]{2,1,0:T(8,128)(2,1)}, bf16[4,2560,256]{2,1,0:T(8,128)(2,1)S(1)}, u32[]{:S(2)}) %copy-start) | copy-done | bytes 5242904
  21.6 0.0 copy-start.2
  21.6 1.2 %copy-done.2 = f32[48,64,128]{2,1,0:T(8,128)} copy-done((f32[48,64,128]{2,1,0:T(8,128)}, f32[48,64,128]{2,1,0:T(8,128)S(1)}, u32[]{:S(2)}) %copy-start.2) | copy-done | bytes 1572888
  22.8 0.0 copy-start.4
  22.8 1.2 %copy-done.4 = f32[48,64,128]{2,1,0:T(8,128)} copy-done((f32[48,64,128]{2,1,0:T(8,128)}, f32[48,64,128]{2,1,0:T(8,128)S(1)}, u32[]{:S(2)}) %copy-start.4) | copy-done | bytes 1572888
  23.9 0.0 copy-start.6
  23.9 0.9 %copy-done.6 = bf16[48,64,128]{2,1,0:T(8,128)(2,1)} copy-done((bf16[48,64,128]{2,1,0:T(8,128)(2,1)}, bf16[48,64,128]{2,1,0:T(8,128)(2,1)S(1)}, u32[]{:S(2)}) %copy-start.6) | copy-done | bytes 786456
  24.8 0.0 all-to-all-done
  24.8 0.0 copy-start.1
  24.8 2.5 %copy-done.1 = bf16[4,2560,256]{2,1,0:T(8,128)(2,1)S(1)} copy-done((bf16[4,2560,256]{2,1,0:T(8,128)(2,1)S(1)}, bf16[4,2560,256]{2,1,0:T(8,128)(2,1)}, u32[]{:S(2)}) %copy-start.1) | copy-done | bytes 5242904
  27.3 1.4 %project.3 = f32[192,512]{1,0:T(8,128)S(1)} custom-call(s32[1]{0:T(128)} %bitcast.4.which_ref, bf16[192,2560]{1,0:T(8,128)(2,1)S(1)} %get-tuple-element.12.hidden_ref, bf16[64,3584]{1,0:T(8,128)(2,1)S(1)} %bitcast.6, bf16[4,2560,256]{2,1,0:T(8,128)(2,1)S(1)} %copy-done.1), custom_call_target="tpu_custom_call" | custom-call | flops 671088640 | bytes 3604480 | tf_op jit(solution)/shard_map/project/pallas_call | solution.py:216
  28.7 0.0 copy-start.3
  28.7 0.0 copy-start.5
  28.7 0.0 copy-start.7
  28.7 0.1 collective-permute-start
  28.8 1.4 %project.2.refs_0_ = f32[192,512]{1,0:T(8,128)S(1)} custom-call(s32[1]{0:T(128)} %bitcast.which_ref, bf16[192,2560]{1,0:T(8,128)(2,1)S(1)} %get-tuple-element.12.hidden_ref, bf16[64,3584]{1,0:T(8,128)(2,1)S(1)} %bitcast.7, bf16[4,2560,256]{2,1,0:T(8,128)(2,1)S(1)} %copy-done.1), custom_call_target="tpu_custom_call" | custom-call | flops 671088640 | bytes 3604480 | tf_op jit(solution)/shard_map/project/pallas_call | solution.py:216
  30.2 0.3 collective-permute-done.refs_1_
  30.5 0.0 copy-done.3
  30.5 0.1 copy-done.5
  30.6 0.2 copy-done.7
  30.8 2.4 %finish.1 = (bf16[48,4,2,2,128]{4,3,2,1,0:T(2,128)(2,1)}, bf16[48,64,128]{2,1,0:T(8,128)(2,1)}) custom-call(f32[192,512]{1,0:T(8,128)S(1)} %project.2.refs_0_, f32[192,512]{1,0:T(8,128)S(1)} %collective-permute-done.refs_1_, bf16[48,64,128]{2,1,0:T(8,128)(2,1)S(1)} %copy-done.7, f32[48,64,128]{2,1,0:T(8,128)S(1)} %get-tuple-element.17.refs_3_, ...), custom_call_target="tpu_custom_call" | custom-call | flops 301989888 | bytes 4718592 | tf_op jit(solution)/shard_map/finish/pallas_call | solution.py:278
Async XLA Ops:
  2.3 22.5 %all-to-all-start = ((bf16[8,8,3584]{2,1,0:T(8,128)(2,1)}), bf16[8,8,3584]{2,1,0:T(8,128)(2,1)S(1)}, u32[]{:S(2)}, u32[]{:S(2)}) async-start(bf16[8,8,3584]{2,1,0:T(8,128)(2,1)} %payload.1), calls=%async_computation | async-start | bytes 917504 | tf_op jit(solution)/shard_map/all_to_all | solution.py:300
  19.2 2.3 %copy-start = (bf16[4,2560,256]{2,1,0:T(8,128)(2,1)}, bf16[4,2560,256]{2,1,0:T(8,128)(2,1)S(1)}, u32[]{:S(2)}) copy-start(bf16[4,2560,256]{2,1,0:T(8,128)(2,1)S(1)} %get-tuple-element.15.base_ref) | copy-start | bytes 15728644
  21.6 1.2 %copy-start.2 = (f32[48,64,128]{2,1,0:T(8,128)}, f32[48,64,128]{2,1,0:T(8,128)S(1)}, u32[]{:S(2)}) copy-start(f32[48,64,128]{2,1,0:T(8,128)S(1)} %get-tuple-element.18.refs_4_) | copy-start | bytes 4718596
  22.8 1.2 %copy-start.4 = (f32[48,64,128]{2,1,0:T(8,128)}, f32[48,64,128]{2,1,0:T(8,128)S(1)}, u32[]{:S(2)}) copy-start(f32[48,64,128]{2,1,0:T(8,128)S(1)} %get-tuple-element.19.refs_5_) | copy-start | bytes 4718596
  23.9 0.9 %copy-start.6 = (bf16[48,64,128]{2,1,0:T(8,128)(2,1)}, bf16[48,64,128]{2,1,0:T(8,128)(2,1)S(1)}, u32[]{:S(2)}) copy-start(bf16[48,64,128]{2,1,0:T(8,128)(2,1)S(1)} %get-tuple-element.16.refs_2_) | copy-start | bytes 2359300
  24.8 2.5 %copy-start.1 = (bf16[4,2560,256]{2,1,0:T(8,128)(2,1)S(1)}, bf16[4,2560,256]{2,1,0:T(8,128)(2,1)}, u32[]{:S(2)}) copy-start(bf16[4,2560,256]{2,1,0:T(8,128)(2,1)} %copy-done) | copy-start | bytes 15728644
  28.7 1.8 %copy-start.3 = (f32[48,64,128]{2,1,0:T(8,128)S(1)}, f32[48,64,128]{2,1,0:T(8,128)}, u32[]{:S(2)}) copy-start(f32[48,64,128]{2,1,0:T(8,128)} %copy-done.2) | copy-start | bytes 4718596
  28.7 1.9 %copy-start.5 = (f32[48,64,128]{2,1,0:T(8,128)S(1)}, f32[48,64,128]{2,1,0:T(8,128)}, u32[]{:S(2)}) copy-start(f32[48,64,128]{2,1,0:T(8,128)} %copy-done.4) | copy-start | bytes 4718596
  28.7 2.1 %copy-start.7 = (bf16[48,64,128]{2,1,0:T(8,128)(2,1)S(1)}, bf16[48,64,128]{2,1,0:T(8,128)(2,1)}, u32[]{:S(2)}) copy-start(bf16[48,64,128]{2,1,0:T(8,128)(2,1)} %copy-done.6) | copy-start | bytes 2359300
  28.7 1.8 %collective-permute-start = (f32[192,512]{1,0:T(8,128)S(1)}, f32[192,512]{1,0:T(8,128)S(1)}, u32[]{:S(2)}, u32[]{:S(2)}) collective-permute-start(f32[192,512]{1,0:T(8,128)S(1)} %project.3), channel_id=1, source_target_pairs={{0,1},{1,0},{2,3},{3,2},{4,5},{5,4},{6,7},{7,6},{8,9},{9,8},{10,11... | collective-permute-start | bytes 1179656 | tf_op jit(solution)/shard_map/ppermute | solution.py:308

commit v7 on v6

--- a/solution.py
+++ b/solution.py
@@ -65,46 +65,41 @@
     )(in_hbm(down), in_hbm(up))
 
 
-def local_kernel(chunks, heads, scale, *refs):
-    lengths_hbm, hidden_hbm, base_hbm, queries_hbm, cache_hbm = refs[:5]
-    tokens_ref, base_ref, q_all, sum_ref, total_ref, top_ref = refs[5:11]
-    lengths_ref, hidden, base, k_all, v_all, sems = refs[11:]
+def cached_kernel(chunks, heads, scale, *refs):
+    lengths_hbm, queries_hbm, cache_hbm = refs[:3]
+    outs_hbm = refs[3:6]
+    lengths_ref, q_all, k_all, v_all, sum_ref, total_ref, top_ref, sems, out_sems, length_sem = refs[6:]
     rows, queries, size = q_all.shape
     slots, own = k_all.shape[1:3]
     keys = slots * own
-    width, two, kvh, _ = base.shape
-    groups = two * kvh
-    some_rows, some_width = rows // chunks, width // chunks
+    some = rows // chunks
 
     def copies(i):
-        mine = pl.ds(i * some_rows, some_rows)
-        features = pl.ds(i * some_width, some_width)
+        mine = pl.ds(i * some, some)
         pairs = (
             (queries_hbm.at[mine], q_all.at[mine]),
             (cache_hbm.at[mine, :, 0], k_all.at[mine]),
             (cache_hbm.at[mine, :, 1], v_all.at[mine]),
-            (base_hbm.at[features], base.at[features]),
         )
         return [pltpu.make_async_copy(a, b, sems.at[i, n]) for n, (a, b) in enumerate(pairs)]
 
-    get_hidden = pltpu.make_async_copy(hidden_hbm, hidden, sems.at[chunks, 0])
-    get_lengths = pltpu.make_async_copy(lengths_hbm, lengths_ref, sems.at[chunks, 1])
+    def puts(i):
+        mine = pl.ds(i * some, some)
+        return [
+            pltpu.make_async_copy(a.at[mine], b.at[mine], out_sems.at[i, n])
+            for n, (a, b) in enumerate(zip((sum_ref, total_ref, top_ref), outs_hbm))
+        ]
+
+    get_lengths = pltpu.make_async_copy(lengths_hbm, lengths_ref, length_sem)
     get_lengths.start()
     for i in range(chunks):
         for copy in copies(i):
             copy.start()
-    get_hidden.start()
 
     column = lax.broadcasted_iota(jnp.int32, (queries, keys), 1)
     head = lax.broadcasted_iota(jnp.int32, (queries, keys), 0) % heads
     column = jnp.where(column % own == head // (heads // own), column, own * slots)
     ones = jnp.ones((keys, size), jnp.bfloat16)
-    tile = 256
-    some = tile // groups
-    row = lax.broadcasted_iota(jnp.int32, (tile, tile), 0)
-    place = lax.broadcasted_iota(jnp.int32, (tile, tile), 1)
-    order = (place == (row % some) * groups + row // some).astype(jnp.float32).astype(jnp.bfloat16)
-    flat_base = base.reshape(width * groups, size)
     flat_k = k_all.reshape(rows, keys, size)
     flat_v = v_all.reshape(rows, keys, size)
 
@@ -120,6 +115,75 @@
             total_ref[r] = both[:, size:]
             top_ref[r] = jnp.broadcast_to(top, (queries, size))
 
+    get_lengths.wait()
+
+    @pl.loop(0, chunks)
+    def _(i):
+        for copy in copies(i):
+            copy.wait()
+        for r in range(0, some, 3):
+            attend(i * some + r, 3)
+        for put in puts(i):
+            put.start()
+
+    for i in range(chunks):
+        for put in puts(i):
+            put.wait()
+
+
+def attend_cached(queries, cache, lengths):
+    rows, steps, heads, size = queries.shape
+    slots, own = cache.shape[1], cache.shape[3]
+    many = steps * heads
+    chunks = 8
+    state = (rows, many, size)
+    half = (rows, slots, own, size)
+    return pl.pallas_call(
+        functools.partial(cached_kernel, chunks, heads, size ** (-0.5)),
+        out_shape=(pltpu.HBM(state, jnp.float32),) * 3,
+        in_specs=[pl.BlockSpec(memory_space=pltpu.HBM)] * 3,
+        out_specs=(pl.BlockSpec(memory_space=pltpu.HBM),) * 3,
+        scratch_shapes=[
+            pltpu.SMEM(lengths.shape, jnp.int32),
+            pltpu.VMEM((rows, many, size), jnp.bfloat16),
+            pltpu.VMEM(half, jnp.bfloat16),
+            pltpu.VMEM(half, jnp.bfloat16),
+            pltpu.VMEM(state, jnp.float32),
+            pltpu.VMEM(state, jnp.float32),
+            pltpu.VMEM(state, jnp.float32),
+            pltpu.SemaphoreType.DMA((chunks, 3)),
+            pltpu.SemaphoreType.DMA((chunks, 3)),
+            pltpu.SemaphoreType.DMA,
+        ],
+        compiler_params=params(28),
+        cost_estimate=cost(
+            8 * rows * many * slots * size, 2 * (cache.size + queries.size) + 12 * rows * many * size, rows * many * slots
+        ),
+        name="attend_cached",
+    )(*map(in_hbm, (lengths, queries.reshape(rows, many, size), cache)))
+
+
+def arrange_kernel(chunks, own, hidden_hbm, base_hbm, tokens_ref, base_ref, hidden, base, sems):
+    width, two, kvh, size = base.shape
+    groups = two * kvh
+    some_width = width // chunks
+
+    def copy(i):
+        features = pl.ds(i * some_width, some_width)
+        return pltpu.make_async_copy(base_hbm.at[features], base.at[features], sems.at[i])
+
+    get_hidden = pltpu.make_async_copy(hidden_hbm, hidden, sems.at[chunks])
+    for i in range(chunks):
+        copy(i).start()
+    get_hidden.start()
+
+    tile = 256
+    some = tile // groups
+    row = lax.broadcasted_iota(jnp.int32, (tile, tile), 0)
+    place = lax.broadcasted_iota(jnp.int32, (tile, tile), 1)
+    order = (place == (row % some) * groups + row // some).astype(jnp.float32).astype(jnp.bfloat16)
+    flat_base = base.reshape(width * groups, size)
+
     def arrange(f):
         at = pl.multiple_of(f * groups, tile)
         pair = jnp.concatenate([flat_base[pl.ds(at + h * tile, tile), :] for h in range(2)], axis=1)
@@ -131,14 +195,9 @@
                     n * some : (n + 1) * some, h * size : (h + 1) * size
                 ]
 
-    get_lengths.wait()
-
     @pl.loop(0, chunks)
     def _(i):
-        for copy in copies(i):
-            copy.wait()
-        for r in range(0, some_rows, 3):
-            attend(i * some_rows + r, 3)
+        copy(i).wait()
         for f in range(0, some_width, 2 * some):
             arrange(i * some_width + f)
 
@@ -146,61 +205,47 @@
     tokens_ref[...] = hidden.reshape(tokens_ref.shape)[...]
 
 
-def local(hidden, base, queries, cache, lengths):
-    rows, steps, heads, size = queries.shape
-    slots, own = cache.shape[1], cache.shape[3]
-    width, two, kvh, _ = base.shape
-    many = steps * heads
+def arrange(hidden, base, own):
+    rows, steps, _ = hidden.shape
+    width, two, kvh, size = base.shape
     chunks = 8
-    state = pltpu.VMEM((rows, many, size), jnp.float32)
-    half = (rows, slots, own, size)
-    outs = (
-        pltpu.VMEM((rows * steps, width), jnp.bfloat16),
-        pltpu.VMEM((two * kvh // own, width, own * size), jnp.bfloat16),
-        pltpu.VMEM((rows, many, size), jnp.bfloat16),
-        state,
-        state,
-        state,
-    )
-    tokens, base, queries, *state = pl.pallas_call(
-        functools.partial(local_kernel, chunks, heads, size ** (-0.5)),
-        out_shape=outs,
-        in_specs=[pl.BlockSpec(memory_space=pltpu.HBM)] * 5,
-        out_specs=(VMEM,) * len(outs),
+    return pl.pallas_call(
+        functools.partial(arrange_kernel, chunks, own),
+        out_shape=(
+            pltpu.VMEM((rows * steps, width), jnp.bfloat16),
+            pltpu.VMEM((two * kvh // own, width, own * size), jnp.bfloat16),
+        ),
+        in_specs=[pl.BlockSpec(memory_space=pltpu.HBM)] * 2,
+        out_specs=(VMEM, VMEM),
         scratch_shapes=[
-            pltpu.SMEM(lengths.shape, jnp.int32),
             pltpu.VMEM(hidden.shape, jnp.bfloat16),
             pltpu.VMEM(base.shape, jnp.bfloat16),
-            pltpu.VMEM(half, jnp.bfloat16),
-            pltpu.VMEM(half, jnp.bfloat16),
-            pltpu.SemaphoreType.DMA((chunks + 1, 4)),
-        ],
-        compiler_params=params(28),
-        cost_estimate=cost(
-            8 * rows * many * slots * size + 512 * base.size,
-            2 * (cache.size + queries.size + base.size + hidden.size),
-            rows * many * slots,
-        ),
-        name="local",
-    )(*map(in_hbm, (lengths, hidden, base, queries.reshape(rows, many, size), cache)))
-    return tokens, base, queries, state
-
-
-def project_kernel(down_at, which_ref, hidden_ref, gathered_ref, base_ref, out_ref, merged):
+            pltpu.SemaphoreType.DMA((chunks + 1,)),
+        ],
+        compiler_params=params(20),
+        cost_estimate=cost(512 * base.size, 4 * (base.size + hidden.size)),
+        name="arrange",
+    )(in_hbm(hidden), in_hbm(base))
+
+
+def project_kernel(which_ref, hidden_ref, base_ref, *refs):
+    gathered, (out_ref, merged) = refs[:-2], refs[-2:]
     width, columns = merged.shape
     part = which_ref[0]
     parts = base_ref.shape[0] // 2
     half = columns // 2
     up = jnp.concatenate(
         [
-            gathered_ref[:, pl.ds(pl.multiple_of(down_at + (c * parts + part) * half, 128), half)]
+            jnp.concatenate(
+                [ref[:, pl.ds(pl.multiple_of(width + (c * parts + part) * half, 128), half)] for ref in gathered], axis=0
+            )
             for c in range(2)
         ],
         axis=1,
     )
     step = 512
     for f in range(0, width, step):
-        down = gathered_ref[:, f : f + step].T
+        down = jnp.concatenate([ref[:, f : f + step] for ref in gathered], axis=0).T
         low_rank = jnp.dot(down, up, preferred_element_type=jnp.float32)
         for c in range(2):
             base = base_ref[c * parts + part, f : f + step, :].astype(jnp.float32)
@@ -210,21 +255,20 @@
     out_ref[...] = jnp.dot(hidden_ref[...], merged[...], preferred_element_type=jnp.float32)
 
 
-def project(which, hidden, gathered, base):
+def project(which, hidden, base, gathered):
     tokens, width = hidden.shape
     columns = 2 * base.shape[2]
+    ranks = sum(g.shape[0] for g in gathered)
     return pl.pallas_call(
-        functools.partial(project_kernel, width),
-        out_shape=jax.ShapeDtypeStruct((tokens, columns), jnp.float32),
-        in_specs=[pl.BlockSpec(memory_space=pltpu.SMEM), VMEM, VMEM, VMEM],
+        project_kernel,
+        out_shape=pltpu.VMEM((tokens, columns), jnp.float32),
+        in_specs=[pl.BlockSpec(memory_space=pltpu.SMEM)] + [VMEM] * (2 + len(gathered)),
         out_specs=VMEM,
         scratch_shapes=[pltpu.VMEM((width, columns), jnp.bfloat16)],
         compiler_params=params(24),
-        cost_estimate=cost(
-            2 * width * columns * (tokens + gathered.shape[0]), 2 * width * columns + 2 * width * tokens
-        ),
+        cost_estimate=cost(2 * width * columns * (tokens + ranks), 2 * width * columns + 2 * width * tokens),
         name="project",
-    )(which, hidden, gathered, base)
+    )(which, hidden, base, *gathered)
 
 
 def finish_kernel(steps, heads, scale, group, terms, *refs):
@@ -294,20 +338,31 @@
     return fresh, context.reshape(rows, steps, heads, size)
 
 
+def gather(payload, dp):
+    ranks, columns = payload.shape[1:]
+    if dp % 2:
+        return [lax.all_to_all(payload, "dp", 0, 0, tiled=True).reshape(dp * ranks, columns)], lambda x: []
+    groups = [[i for i in range(dp) if i % 2 == n] for n in range(2)]
+    mine = lax.all_to_all(payload, "dp", 0, 0, axis_index_groups=groups, tiled=True)
+    return [mine.reshape(dp // 2 * ranks, columns)], lambda x: [lax.ppermute(x, "dp", [(i, i ^ 1) for i in range(dp)])]
+
+
 def shards(dp, tp, hidden, base_weight, factor_a, factor_b, queries, cache, lengths):
-    steps, own = queries.shape[1], cache.shape[3]
-    payload = make_payload(factor_a.T, factor_b, dp)
-    gathered = lax.all_to_all(payload, "dp", 0, 0, tiled=True)
-    gathered = gathered.reshape(-1, gathered.shape[-1])
-    tokens, base, queries, state = local(hidden, base_weight, queries, cache, lengths)
-    gathered, base = lax.optimization_barrier((gathered, base))
+    rows, steps, heads, size = queries.shape
+    own = cache.shape[3]
+    payload = make_payload(factor_a.T, factor_b, dp // 2 if dp % 2 == 0 else dp)
+    gathered, rest = gather(payload, dp)
+    state = attend_cached(queries, cache, lengths)
+    gathered, state, hidden, base_weight = lax.optimization_barrier((gathered, state, hidden, base_weight))
+    gathered = gathered + rest(gathered[0])
+    tokens, base = arrange(hidden, base_weight, own)
     me = lax.axis_index("tp")
     received = []
     for k in range(1, tp):
-        other = project(jnp.full((1,), me ^ k, jnp.int32), tokens, gathered, base)
+        other = project(jnp.full((1,), me ^ k, jnp.int32), tokens, base, gathered)
         received.append(lax.ppermute(other, "tp", [(i, i ^ k) for i in range(tp)]))
-    mine = project(jnp.full((1,), me, jnp.int32), tokens, gathered, base)
-    return finish([mine] + received, queries, state, steps, own)
+    mine = project(jnp.full((1,), me, jnp.int32), tokens, base, gathered)
+    return finish([mine] + received, queries.reshape(rows, steps * heads, size), state, steps, own)
 
 
 def solution(mesh):

time: 33.5 us -> 30.9 us (0.922)
  local copies, waits for them, and re-layouts: 8.31 us -> 0.79 us
  Pallas kernels: 16.5 us -> 19.6 us
  waiting for transfers between devices: 0.33 us -> 1.5 us
  starting transfers between devices: 7.36 us -> 7.99 us
    unnamed x16 -> x8, local copies, waits for them, and re-layouts: 8.31 us -> 0.79 us
    pallas_call x3 -> x4, Pallas kernels: 12.4 us -> 15.7 us  [the longest x1 8.56 us: attend_cached(): pl.pallas_call(functools.partial(cached_kernel, chunks, heads, size ** (-...]
    ppermute x0 -> x1, starting transfers between devices: none -> 1.59 us  [gather(): lax.ppermute(x, 'dp', [(i, i ^ 1) for i in range(dp)])]
    ppermute x0 -> x1, waiting for transfers between devices: none -> 1.17 us  [gather(): lax.ppermute(x, 'dp', [(i, i ^ 1) for i in range(dp)])]
    all_to_all x1, starting transfers between devices: 7.29 us -> 6.33 us  [gather(): lax.all_to_all(payload, 'dp', 0, 0, axis_index_groups=groups, tiled=True)]
  transfers between devices with their start and end apart: 2 -> 3, of which waited for: 1 -> 2; matrix products, arithmetic and copies ran while one was open for 0% -> 0% of each run, Pallas kernels for 33% -> 47%
where the time goes in v7:
time: 30.9 us; the launch traced here: 30.6 us
  Pallas kernels  19.6 us (63%)
  starting transfers between devices  7.99 us (26%)
  waiting for transfers between devices  1.5 us (5%)
  local copies, waits for them, and re-layouts  0.79 us (3%)
  between operations  0.72 us (2%)
    pallas_call x1, Pallas kernels, attend_cached(): pl.pallas_call(functools.partial(cached_kernel, chunks, heads, size ** (-...  8.56 us
    all_to_all x1, starting transfers between devices, gather(): lax.all_to_all(payload, 'dp', 0, 0, axis_index_groups=groups, tiled=True)  6.33 us
    pallas_call x1, Pallas kernels, arrange(): pl.pallas_call(functools.partial(arrange_kernel, chunks, own), out_shape=...  4.37 us
    pallas_call x2, Pallas kernels, project(): pl.pallas_call(project_kernel, out_shape=pltpu.VMEM((tokens, columns), jn...  2.76 us
    pallas_call x1, Pallas kernels, finish(): pl.pallas_call(functools.partial(finish_kernel, steps, heads, size ** (-0...  2.39 us
    ppermute x1, starting transfers between devices, gather(): lax.ppermute(x, 'dp', [(i, i ^ 1) for i in range(dp)])  1.59 us
    pallas_call x1, Pallas kernels, make_payload(): pl.pallas_call(payload_kernel, out_shape=jax.ShapeDtypeStruct((count,) +...  1.52 us
    ppermute x1, waiting for transfers between devices, gather(): lax.ppermute(x, 'dp', [(i, i ^ 1) for i in range(dp)])  1.17 us
  transfers between devices with their start and end apart: 3, of which 2 were waited for; matrix products, arithmetic and copies ran while one was open for 0% of the time, Pallas kernels for 47%

profile of v7, /device:TPU:0, one launch (start us, length us, event | category | flops | bytes accessed | tf_op | source)
XLA Modules:
  0.0 30.6 jit_solution(12497980470314896073)
XLA Ops:
  0.6 1.5 %payload.1 = bf16[4,8,3584]{2,1,0:T(8,128)(2,1)} custom-call(bf16[8,2560]{1,0:T(8,128)(2,1)} %bitcast.11, bf16[8,2,4,128]{3,2,1,0:T(4,128)(2,1)} %up_hbm.1), custom_call_target="tpu_custom_call" | custom-call | tf_op jit(solution)/shard_map/payload/pallas_call | solution.py:52
  2.2 6.3 %all-to-all-start = ((bf16[4,8,3584]{2,1,0:T(8,128)(2,1)}), bf16[4,8,3584]{2,1,0:T(8,128)(2,1)S(1)}, u32[]{:S(2)}, u32[]{:S(2)}) async-start(bf16[4,8,3584]{2,1,0:T(8,128)(2,1)} %payload.1), calls=%async_computation | async-start | bytes 458752 | tf_op jit(solution)/shard_map/all_to_all | solution.py:346
  8.5 8.6 %attend_cached.1 = (f32[48,64,128]{2,1,0:T(8,128)}, f32[48,64,128]{2,1,0:T(8,128)}, f32[48,64,128]{2,1,0:T(8,128)}) custom-call(s32[48]{0:T(128)} %refs_0_.1, bf16[48,64,128]{2,1,0:T(8,128)(2,1)} %bitcast.6, bf16[48,128,2,2,128]{4,3,2,1,0:T(2,128)(2,1)} %refs_2_.1), custom_call_target="tpu_custom_call" | custom-call | flops 402653184 | bytes 11796480 | tf_op jit(solution)/shard_map/attend_cached/pallas_call | solution.py:141
  17.1 0.0 all-to-all-done
  17.1 1.6 %collective-permute-start = (bf16[32,3584]{1,0:T(8,128)(2,1)S(1)}, bf16[32,3584]{1,0:T(8,128)(2,1)S(1)}, u32[]{:S(2)}, u32[]{:S(2)}) collective-permute-start(bf16[32,3584]{1,0:T(8,128)(2,1)S(1)} %bitcast.8), channel_id=1, source_target_pairs={{0,2},{2,0},{4,6},{6,4},{8,10},{10,8},{12,14},{14,12},{1,3},{3,1},... | collective-permute-start | bytes 688136 | tf_op jit(solution)/shard_map/ppermute | solution.py:347
  18.7 4.4 %arrange.1 = (bf16[192,2560]{1,0:T(8,128)(2,1)S(1)}, bf16[4,2560,256]{2,1,0:T(8,128)(2,1)S(1)}) custom-call(bf16[48,4,2560]{2,1,0:T(4,128)(2,1)} %hidden_hbm, bf16[2560,2,4,128]{3,2,1,0:T(4,128)(2,1)} %base_hbm), custom_call_target="tpu_custom_call" | custom-call | flops 1342177280 | bytes 12451840 | tf_op jit(solution)/shard_map/arrange/pallas_call | solution.py:212
  23.0 1.2 %collective-permute-done.refs_1_ = bf16[32,3584]{1,0:T(8,128)(2,1)S(1)} collective-permute-done((bf16[32,3584]{1,0:T(8,128)(2,1)S(1)}, bf16[32,3584]{1,0:T(8,128)(2,1)S(1)}, u32[]{:S(2)}, u32[]{:S(2)}) %collective-permute-start) | collective-permute-done | bytes 229408 | tf_op jit(solution)/shard_map/ppermute | solution.py:347
  24.2 1.4 %project.3 = f32[192,512]{1,0:T(8,128)S(1)} custom-call(s32[1]{0:T(128)} %bitcast.4.which_ref, bf16[192,2560]{1,0:T(8,128)(2,1)S(1)} %get-tuple-element.20.hidden_ref, bf16[4,2560,256]{2,1,0:T(8,128)(2,1)S(1)} %get-tuple-element.21.base_ref, bf16[32,3584]{1,0:T(8,128)(2,1)S(1)} %bitcast.9, bf16[32,3584]{1,0:T(8,128)(2,1)S(1)} %collective-permute-done.refs_1_), custom_call_target="tpu_custom_call" | custom-call | flops 671088640 | bytes 3604480 | tf_op jit(solution)/shard_map/project/pallas_call | solution.py:262
  25.6 0.0 copy-start
  25.6 0.0 copy-start.1
  25.6 0.0 copy-start.2
  25.6 0.0 copy-start.3
  25.6 0.1 collective-permute-start.1
  25.7 1.4 %project.2.refs_0_ = f32[192,512]{1,0:T(8,128)S(1)} custom-call(s32[1]{0:T(128)} %bitcast.which_ref, bf16[192,2560]{1,0:T(8,128)(2,1)S(1)} %get-tuple-element.20.hidden_ref, bf16[4,2560,256]{2,1,0:T(8,128)(2,1)S(1)} %get-tuple-element.21.base_ref, bf16[32,3584]{1,0:T(8,128)(2,1)S(1)} %bitcast.10, bf16[32,3584]{1,0:T(8,128)(2,1)S(1)} %collective-permute-done.refs_1_), custom_call_target="tpu_custom_call" | custom-call | flops 671088640 | bytes 3604480 | tf_op jit(solution)/shard_map/project/pallas_call | solution.py:262
  27.1 0.3 %collective-permute-done.1.refs_1_ = f32[192,512]{1,0:T(8,128)S(1)} collective-permute-done((f32[192,512]{1,0:T(8,128)S(1)}, f32[192,512]{1,0:T(8,128)S(1)}, u32[]{:S(2)}, u32[]{:S(2)}) %collective-permute-start.1) | collective-permute-done | bytes 393248 | tf_op jit(solution)/shard_map/ppermute | solution.py:363
  27.4 0.0 copy-done
  27.4 0.0 copy-done.1
  27.4 0.3 copy-done.2
  27.7 0.5 %copy-done.3 = f32[48,64,128]{2,1,0:T(8,128)S(1)} copy-done((f32[48,64,128]{2,1,0:T(8,128)S(1)}, f32[48,64,128]{2,1,0:T(8,128)}, u32[]{:S(2)}) %copy-start.3) | copy-done | bytes 1572888
  28.2 2.4 %finish.1 = (bf16[48,4,2,2,128]{4,3,2,1,0:T(2,128)(2,1)}, bf16[48,64,128]{2,1,0:T(8,128)(2,1)}) custom-call(f32[192,512]{1,0:T(8,128)S(1)} %project.2.refs_0_, f32[192,512]{1,0:T(8,128)S(1)} %collective-permute-done.1.refs_1_, bf16[48,64,128]{2,1,0:T(8,128)(2,1)S(1)} %bitcast.7, f32[48,64,128]{2,1,0:T(8,128)S(1)} %copy-done.1, f32[48,64,128]{2,1,0:T(8,128)S(1)} %copy-done.2, ...), custom_call_target="tpu_custom_call" | custom-call | flops 301989888 | bytes 4718592 | tf_op jit(solution)/shard_map/finish/pallas_call | solution.py:322
Async XLA Ops:
  2.2 14.9 %all-to-all-start = ((bf16[4,8,3584]{2,1,0:T(8,128)(2,1)}), bf16[4,8,3584]{2,1,0:T(8,128)(2,1)S(1)}, u32[]{:S(2)}, u32[]{:S(2)}) async-start(bf16[4,8,3584]{2,1,0:T(8,128)(2,1)} %payload.1), calls=%async_computation | async-start | bytes 458752 | tf_op jit(solution)/shard_map/all_to_all | solution.py:346
  17.1 7.1 %collective-permute-start = (bf16[32,3584]{1,0:T(8,128)(2,1)S(1)}, bf16[32,3584]{1,0:T(8,128)(2,1)S(1)}, u32[]{:S(2)}, u32[]{:S(2)}) collective-permute-start(bf16[32,3584]{1,0:T(8,128)(2,1)S(1)} %bitcast.8), channel_id=1, source_target_pairs={{0,2},{2,0},{4,6},{6,4},{8,10},{10,8},{12,14},{14,12},{1,3},{3,1},... | collective-permute-start | bytes 688136 | tf_op jit(solution)/shard_map/ppermute | solution.py:347
  25.6 1.8 %copy-start = (bf16[48,4,16,128]{3,2,1,0:T(8,128)(2,1)S(1)}, bf16[48,4,16,128]{3,2,1,0:T(8,128)(2,1)}, u32[]{:S(2)}) copy-start(bf16[48,4,16,128]{3,2,1,0:T(8,128)(2,1)} %param.11) | copy-start | bytes 2359300
  25.6 1.8 %copy-start.1 = (f32[48,64,128]{2,1,0:T(8,128)S(1)}, f32[48,64,128]{2,1,0:T(8,128)}, u32[]{:S(2)}) copy-start(f32[48,64,128]{2,1,0:T(8,128)} %get-tuple-element.23.refs_3_) | copy-start | bytes 4718596
  25.6 2.1 %copy-start.2 = (f32[48,64,128]{2,1,0:T(8,128)S(1)}, f32[48,64,128]{2,1,0:T(8,128)}, u32[]{:S(2)}) copy-start(f32[48,64,128]{2,1,0:T(8,128)} %get-tuple-element.24.refs_4_) | copy-start | bytes 4718596
  25.6 2.6 %copy-start.3 = (f32[48,64,128]{2,1,0:T(8,128)S(1)}, f32[48,64,128]{2,1,0:T(8,128)}, u32[]{:S(2)}) copy-start(f32[48,64,128]{2,1,0:T(8,128)} %get-tuple-element.25.refs_5_) | copy-start | bytes 4718596
  25.6 1.8 %collective-permute-start.1 = (f32[192,512]{1,0:T(8,128)S(1)}, f32[192,512]{1,0:T(8,128)S(1)}, u32[]{:S(2)}, u32[]{:S(2)}) collective-permute-start(f32[192,512]{1,0:T(8,128)S(1)} %project.3), channel_id=1, source_target_pairs={{0,1},{1,0},{2,3},{3,2},{4,5},{5,4},{6,7},{7,6},{8,9},{9,8},{10,11... | collective-permute-start | bytes 1179656 | tf_op jit(solution)/shard_map/ppermute | solution.py:363

commit v8 on v7

--- a/solution.py
+++ b/solution.py
@@ -66,9 +66,10 @@
 
 
 def cached_kernel(chunks, heads, scale, *refs):
-    lengths_hbm, queries_hbm, cache_hbm = refs[:3]
-    outs_hbm = refs[3:6]
-    lengths_ref, q_all, k_all, v_all, sum_ref, total_ref, top_ref, sems, out_sems, length_sem = refs[6:]
+    lengths_hbm, queries_hbm, cache_hbm, out_hbm, log_hbm = refs[:5]
+    lengths_ref, q_all, k_all, v_all, out_ref, log_ref = refs[5:11]
+    scores_refs, weights_refs, total_refs = refs[11:13], refs[13:15], refs[15:17]
+    sems, out_sems, length_sem = refs[17:]
     rows, queries, size = q_all.shape
     slots, own = k_all.shape[1:3]
     keys = slots * own
@@ -85,10 +86,8 @@
 
     def puts(i):
         mine = pl.ds(i * some, some)
-        return [
-            pltpu.make_async_copy(a.at[mine], b.at[mine], out_sems.at[i, n])
-            for n, (a, b) in enumerate(zip((sum_ref, total_ref, top_ref), outs_hbm))
-        ]
+        pairs = ((out_ref.at[mine], out_hbm.at[mine]), (log_ref.at[mine], log_hbm.at[mine]))
+        return [pltpu.make_async_copy(a, b, out_sems.at[i, n]) for n, (a, b) in enumerate(pairs)]
 
     get_lengths = pltpu.make_async_copy(lengths_hbm, lengths_ref, length_sem)
     get_lengths.start()
@@ -99,33 +98,70 @@
     column = lax.broadcasted_iota(jnp.int32, (queries, keys), 1)
     head = lax.broadcasted_iota(jnp.int32, (queries, keys), 0) % heads
     column = jnp.where(column % own == head // (heads // own), column, own * slots)
-    ones = jnp.ones((keys, size), jnp.bfloat16)
+    nothing = jnp.zeros((queries, size), jnp.bfloat16)
     flat_k = k_all.reshape(rows, keys, size)
     flat_v = v_all.reshape(rows, keys, size)
 
-    def attend(at, count):
-        group = [at + r for r in range(count)]
-        scores = [lax.dot_general(q_all[r], flat_k[r], NT, preferred_element_type=jnp.float32) for r in group]
-        scores = [jnp.where(column < own * lengths_ref[r], s, LOW) for r, s in zip(group, scores)]
-        tops = [jnp.max(s, axis=-1, keepdims=True) for s in scores]
-        weights = [jnp.exp((s - t) * scale).astype(jnp.bfloat16) for s, t in zip(scores, tops)]
-        for r, w, top in zip(group, weights, tops):
-            both = jnp.dot(w, jnp.concatenate([flat_v[r], ones], axis=1), preferred_element_type=jnp.float32)
-            sum_ref[r] = both[:, :size]
-            total_ref[r] = both[:, size:]
-            top_ref[r] = jnp.broadcast_to(top, (queries, size))
-
-    get_lengths.wait()
-
-    @pl.loop(0, chunks)
-    def _(i):
+    def await_chunk(i):
         for copy in copies(i):
             copy.wait()
-        for r in range(0, some, 3):
-            attend(i * some + r, 3)
+
+    def score(i, slot):
+        for p in range(some // 2):
+            r = i * some + 2 * p
+            both = jnp.concatenate(
+                [
+                    jnp.concatenate([q_all[r], nothing], axis=1),
+                    jnp.concatenate([nothing, q_all[r + 1]], axis=1),
+                ],
+                axis=0,
+            )
+            both_k = jnp.concatenate([flat_k[r], flat_k[r + 1]], axis=1)
+            scores_refs[slot][p] = lax.dot_general(both, both_k, NT, preferred_element_type=jnp.float32)
+
+    def soften(i, slot):
+        for p in range(some // 2):
+            for h in range(2):
+                r = i * some + 2 * p + h
+                mine = slice(h * queries, (h + 1) * queries)
+                scores = jnp.where(column < own * lengths_ref[r], scores_refs[slot][p, mine], LOW)
+                top = jnp.max(scores, axis=-1, keepdims=True)
+                expo = jnp.exp((scores - top) * scale)
+                total = jnp.sum(expo, axis=-1, keepdims=True)
+                weights_refs[slot][p, mine] = expo.astype(jnp.bfloat16)
+                total_refs[slot][p, mine] = jnp.broadcast_to(1.0 / total, (queries, size))
+                log_ref[r] = jnp.broadcast_to(top * scale + jnp.log(total), (queries, size))
+
+    def collect(i, slot):
+        for p in range(some // 2):
+            r = i * some + 2 * p
+            both_v = jnp.concatenate([flat_v[r], flat_v[r + 1]], axis=1)
+            both = jnp.dot(weights_refs[slot][p], both_v, preferred_element_type=jnp.float32)
+            for h in range(2):
+                mine = slice(h * queries, (h + 1) * queries)
+                out_ref[r + h] = both[mine, h * size : (h + 1) * size] * total_refs[slot][p, mine]
         for put in puts(i):
             put.start()
 
+    get_lengths.wait()
+    await_chunk(0)
+    score(0, 0)
+    await_chunk(1)
+    score(1, 1)
+    soften(0, 0)
+
+    @pl.loop(1, chunks // 2)
+    def _(t):
+        for slot in range(2):
+            i = 2 * t + slot
+            await_chunk(i)
+            score(i, slot)
+            soften(i - 1, 1 - slot)
+            collect(i - 2, slot)
+
+    soften(chunks - 1, 1)
+    collect(chunks - 2, 0)
+    collect(chunks - 1, 1)
     for i in range(chunks):
         for put in puts(i):
             put.wait()
@@ -136,13 +172,14 @@
     slots, own = cache.shape[1], cache.shape[3]
     many = steps * heads
     chunks = 8
+    pairs = rows // chunks // 2
     state = (rows, many, size)
     half = (rows, slots, own, size)
     return pl.pallas_call(
         functools.partial(cached_kernel, chunks, heads, size ** (-0.5)),
-        out_shape=(pltpu.HBM(state, jnp.float32),) * 3,
+        out_shape=(pltpu.HBM(state, jnp.float32),) * 2,
         in_specs=[pl.BlockSpec(memory_space=pltpu.HBM)] * 3,
-        out_specs=(pl.BlockSpec(memory_space=pltpu.HBM),) * 3,
+        out_specs=(pl.BlockSpec(memory_space=pltpu.HBM),) * 2,
         scratch_shapes=[
             pltpu.SMEM(lengths.shape, jnp.int32),
             pltpu.VMEM((rows, many, size), jnp.bfloat16),
@@ -150,14 +187,19 @@
             pltpu.VMEM(half, jnp.bfloat16),
             pltpu.VMEM(state, jnp.float32),
             pltpu.VMEM(state, jnp.float32),
-            pltpu.VMEM(state, jnp.float32),
+            pltpu.VMEM((pairs, 2 * many, slots * own), jnp.float32),
+            pltpu.VMEM((pairs, 2 * many, slots * own), jnp.float32),
+            pltpu.VMEM((pairs, 2 * many, slots * own), jnp.bfloat16),
+            pltpu.VMEM((pairs, 2 * many, slots * own), jnp.bfloat16),
+            pltpu.VMEM((pairs, 2 * many, size), jnp.float32),
+            pltpu.VMEM((pairs, 2 * many, size), jnp.float32),
             pltpu.SemaphoreType.DMA((chunks, 3)),
-            pltpu.SemaphoreType.DMA((chunks, 3)),
+            pltpu.SemaphoreType.DMA((chunks, 2)),
             pltpu.SemaphoreType.DMA,
         ],
         compiler_params=params(28),
         cost_estimate=cost(
-            8 * rows * many * slots * size, 2 * (cache.size + queries.size) + 12 * rows * many * size, rows * many * slots
+            8 * rows * many * slots * size, 2 * (cache.size + queries.size) + 8 * rows * many * size, rows * many * slots
         ),
         name="attend_cached",
     )(*map(in_hbm, (lengths, queries.reshape(rows, many, size), cache)))
@@ -173,9 +215,9 @@
         return pltpu.make_async_copy(base_hbm.at[features], base.at[features], sems.at[i])
 
     get_hidden = pltpu.make_async_copy(hidden_hbm, hidden, sems.at[chunks])
+    get_hidden.start()
     for i in range(chunks):
         copy(i).start()
-    get_hidden.start()
 
     tile = 256
     some = tile // groups
@@ -195,14 +237,14 @@
                     n * some : (n + 1) * some, h * size : (h + 1) * size
                 ]
 
+    get_hidden.wait()
+    tokens_ref[...] = hidden.reshape(tokens_ref.shape)[...]
+
     @pl.loop(0, chunks)
     def _(i):
         copy(i).wait()
         for f in range(0, some_width, 2 * some):
             arrange(i * some_width + f)
-
-    get_hidden.wait()
-    tokens_ref[...] = hidden.reshape(tokens_ref.shape)[...]
 
 
 def arrange(hidden, base, own):
@@ -228,10 +270,10 @@
     )(in_hbm(hidden), in_hbm(base))
 
 
-def project_kernel(which_ref, hidden_ref, base_ref, *refs):
+def project_kernel(k, hidden_ref, base_ref, *refs):
     gathered, (out_ref, merged) = refs[:-2], refs[-2:]
     width, columns = merged.shape
-    part = which_ref[0]
+    part = lax.axis_index("tp") ^ k
     parts = base_ref.shape[0] // 2
     half = columns // 2
     up = jnp.concatenate(
@@ -255,25 +297,25 @@
     out_ref[...] = jnp.dot(hidden_ref[...], merged[...], preferred_element_type=jnp.float32)
 
 
-def project(which, hidden, base, gathered):
+def project(k, hidden, base, gathered):
     tokens, width = hidden.shape
     columns = 2 * base.shape[2]
     ranks = sum(g.shape[0] for g in gathered)
     return pl.pallas_call(
-        project_kernel,
+        functools.partial(project_kernel, k),
         out_shape=pltpu.VMEM((tokens, columns), jnp.float32),
-        in_specs=[pl.BlockSpec(memory_space=pltpu.SMEM)] + [VMEM] * (2 + len(gathered)),
+        in_specs=[VMEM] * (2 + len(gathered)),
         out_specs=VMEM,
         scratch_shapes=[pltpu.VMEM((width, columns), jnp.bfloat16)],
         compiler_params=params(24),
         cost_estimate=cost(2 * width * columns * (tokens + ranks), 2 * width * columns + 2 * width * tokens),
         name="project",
-    )(which, hidden, base, *gathered)
+    )(hidden, base, *gathered)
 
 
 def finish_kernel(steps, heads, scale, group, terms, *refs):
     parts, refs = refs[:terms], refs[terms:]
-    q_ref, sum_ref, total_ref, top_ref, fresh_ref, context_ref, wide, bias = refs
+    q_ref, old_ref, log_ref, fresh_ref, context_ref, wide, bias = refs
     rows, queries, size = q_ref.shape
     own = fresh_ref.shape[3]
     fresh = parts[0][...]
@@ -304,14 +346,14 @@
         scores = lax.dot_general(
             q_ref[mine].reshape(many, size), keys_new, NT, preferred_element_type=jnp.float32
         )
-        scores = scores + bias[...]
-        top_old = top_ref[mine].reshape(many, size)
-        top = jnp.maximum(top_old, jnp.max(scores, axis=-1, keepdims=True))
-        weights = jnp.exp((scores - top) * scale).astype(jnp.bfloat16)
-        back = jnp.exp((top_old - top) * scale)
+        scores = scores * scale + bias[...]
+        log_old = log_ref[mine].reshape(many, size)
+        top = jnp.maximum(log_old, jnp.max(scores, axis=-1, keepdims=True))
+        weights = jnp.exp(scores - top).astype(jnp.bfloat16)
+        back = jnp.exp(log_old - top)
         both = jnp.dot(weights, values_new, preferred_element_type=jnp.float32)
-        total = back * total_ref[mine].reshape(many, size) + both[:, size:]
-        summed = back * sum_ref[mine].reshape(many, size) + both[:, :size]
+        total = back + both[:, size:]
+        summed = back * old_ref[mine].reshape(many, size) + both[:, :size]
         context_ref[mine] = (summed / total).astype(jnp.bfloat16).reshape(group, queries, size)
 
 
@@ -356,12 +398,11 @@
     gathered, state, hidden, base_weight = lax.optimization_barrier((gathered, state, hidden, base_weight))
     gathered = gathered + rest(gathered[0])
     tokens, base = arrange(hidden, base_weight, own)
-    me = lax.axis_index("tp")
     received = []
     for k in range(1, tp):
-        other = project(jnp.full((1,), me ^ k, jnp.int32), tokens, base, gathered)
+        other = project(k, tokens, base, gathered)
         received.append(lax.ppermute(other, "tp", [(i, i ^ k) for i in range(tp)]))
-    mine = project(jnp.full((1,), me, jnp.int32), tokens, base, gathered)
+    mine = project(0, tokens, base, gathered)
     return finish([mine] + received, queries.reshape(rows, steps * heads, size), state, steps, own)
 
 

time: 30.9 us -> 29.2 us (0.945)
  Pallas kernels: 19.6 us -> 18.6 us
  local copies, waits for them, and re-layouts: 0.79 us -> 0.32 us
    pallas_call x1, Pallas kernels: 8.56 us -> 7.45 us  [attend_cached(): pl.pallas_call(functools.partial(cached_kernel, chunks, heads, size ** (-...]
    ppermute x1, waiting for transfers between devices: 1.17 us -> 0.3 us  [gather(): lax.ppermute(x, 'dp', [(i, i ^ 1) for i in range(dp)])]
    all_to_all x1, waiting for transfers between devices: 0.01 us -> 0.76 us  [gather(): lax.all_to_all(payload, 'dp', 0, 0, axis_index_groups=groups, tiled=True)]
    unnamed x8 -> x6, local copies, waits for them, and re-layouts: 0.79 us -> 0.32 us
  transfers between devices with their start and end apart: 3 -> 3, of which waited for: 2 -> 3; matrix products, arithmetic and copies ran while one was open for 0% -> 0% of each run, Pallas kernels for 47% -> 46%
where the time goes in v8:
time: 29.2 us; the launch traced here: 28.9 us
  Pallas kernels  18.6 us (64%)
  starting transfers between devices  7.92 us (27%)
  waiting for transfers between devices  1.39 us (5%)
  between operations  0.71 us (2%)
  local copies, waits for them, and re-layouts  0.32 us (1%)
    pallas_call x1, Pallas kernels, attend_cached(): pl.pallas_call(functools.partial(cached_kernel, chunks, heads, size ** (-...  7.45 us
    all_to_all x1, starting transfers between devices, gather(): lax.all_to_all(payload, 'dp', 0, 0, axis_index_groups=groups, tiled=True)  6.33 us
    pallas_call x1, Pallas kernels, arrange(): pl.pallas_call(functools.partial(arrange_kernel, chunks, own), out_shape=...  4.55 us
    pallas_call x2, Pallas kernels, project(): pl.pallas_call(functools.partial(project_kernel, k), out_shape=pltpu.VMEM...  2.75 us
    pallas_call x1, Pallas kernels, finish(): pl.pallas_call(functools.partial(finish_kernel, steps, heads, size ** (-0...  2.28 us
    pallas_call x1, Pallas kernels, make_payload(): pl.pallas_call(payload_kernel, out_shape=jax.ShapeDtypeStruct((count,) +...  1.52 us
    ppermute x1, starting transfers between devices, gather(): lax.ppermute(x, 'dp', [(i, i ^ 1) for i in range(dp)])  1.52 us
    all_to_all x1, waiting for transfers between devices, gather(): lax.all_to_all(payload, 'dp', 0, 0, axis_index_groups=groups, tiled=True)  0.76 us
  transfers between devices with their start and end apart: 3, of which 3 were waited for; matrix products, arithmetic and copies ran while one was open for 0% of the time, Pallas kernels for 46%

profile of v8, /device:TPU:0, one launch (start us, length us, event | category | flops | bytes accessed | tf_op | source)
XLA Modules:
  0.0 28.9 jit_solution(8639127794053540419)
XLA Ops:
  0.6 1.5 %payload.1 = bf16[4,8,3584]{2,1,0:T(8,128)(2,1)} custom-call(bf16[8,2560]{1,0:T(8,128)(2,1)} %bitcast.9, bf16[8,2,4,128]{3,2,1,0:T(4,128)(2,1)} %up_hbm.1), custom_call_target="tpu_custom_call" | custom-call | tf_op jit(solution)/shard_map/payload/pallas_call | solution.py:52
  2.2 6.3 %all-to-all-start = ((bf16[4,8,3584]{2,1,0:T(8,128)(2,1)}), bf16[4,8,3584]{2,1,0:T(8,128)(2,1)S(1)}, u32[]{:S(2)}, u32[]{:S(2)}) async-start(bf16[4,8,3584]{2,1,0:T(8,128)(2,1)} %payload.1), calls=%async_computation | async-start | bytes 458752 | tf_op jit(solution)/shard_map/all_to_all | solution.py:388
  8.5 7.4 %attend_cached.1 = (f32[48,64,128]{2,1,0:T(8,128)}, f32[48,64,128]{2,1,0:T(8,128)}) custom-call(s32[48]{0:T(128)} %refs_0_.1, bf16[48,64,128]{2,1,0:T(8,128)(2,1)} %bitcast.4, bf16[48,128,2,2,128]{4,3,2,1,0:T(2,128)(2,1)} %refs_2_.1), custom_call_target="tpu_custom_call" | custom-call | flops 402653184 | bytes 10223616 | tf_op jit(solution)/shard_map/attend_cached/pallas_call | solution.py:178
  15.9 0.8 %all-to-all-done = bf16[4,8,3584]{2,1,0:T(8,128)(2,1)S(1)} async-done(((bf16[4,8,3584]{2,1,0:T(8,128)(2,1)}), bf16[4,8,3584]{2,1,0:T(8,128)(2,1)S(1)}, u32[]{:S(2)}, u32[]{:S(2)}) %all-to-all-start) | async-done | bytes 229408 | tf_op jit(solution)/shard_map/all_to_all | solution.py:388
  16.7 1.5 %collective-permute-start = (bf16[32,3584]{1,0:T(8,128)(2,1)S(1)}, bf16[32,3584]{1,0:T(8,128)(2,1)S(1)}, u32[]{:S(2)}, u32[]{:S(2)}) collective-permute-start(bf16[32,3584]{1,0:T(8,128)(2,1)S(1)} %bitcast.6), channel_id=1, source_target_pairs={{0,2},{2,0},{4,6},{6,4},{8,10},{10,8},{12,14},{14,12},{1,3},{3,1},... | collective-permute-start | bytes 688136 | tf_op jit(solution)/shard_map/ppermute | solution.py:389
  18.2 4.5 %arrange.1 = (bf16[192,2560]{1,0:T(8,128)(2,1)S(1)}, bf16[4,2560,256]{2,1,0:T(8,128)(2,1)S(1)}) custom-call(bf16[48,4,2560]{2,1,0:T(4,128)(2,1)} %hidden_hbm, bf16[2560,2,4,128]{3,2,1,0:T(4,128)(2,1)} %base_hbm), custom_call_target="tpu_custom_call" | custom-call | flops 1342177280 | bytes 12451840 | tf_op jit(solution)/shard_map/arrange/pallas_call | solution.py:254
  22.8 0.3 %collective-permute-done.refs_1_ = bf16[32,3584]{1,0:T(8,128)(2,1)S(1)} collective-permute-done((bf16[32,3584]{1,0:T(8,128)(2,1)S(1)}, bf16[32,3584]{1,0:T(8,128)(2,1)S(1)}, u32[]{:S(2)}, u32[]{:S(2)}) %collective-permute-start) | collective-permute-done | bytes 229408 | tf_op jit(solution)/shard_map/ppermute | solution.py:389
  23.1 1.4 %project.3 = f32[192,512]{1,0:T(8,128)S(1)} custom-call(bf16[192,2560]{1,0:T(8,128)(2,1)S(1)} %get-tuple-element.17.hidden_ref, bf16[4,2560,256]{2,1,0:T(8,128)(2,1)S(1)} %get-tuple-element.18.base_ref, bf16[32,3584]{1,0:T(8,128)(2,1)S(1)} %bitcast.7, bf16[32,3584]{1,0:T(8,128)(2,1)S(1)} %collective-permute-done.refs_1_), custom_call_target="tpu_custom_call" | custom-call | flops 671088640 | bytes 3604480 | tf_op jit(solution)/shard_map/project/pallas_call | solution.py:304
  24.5 0.0 copy-start
  24.5 0.0 copy-start.1
  24.5 0.0 copy-start.2
  24.5 0.1 collective-permute-start.1
  24.6 1.4 %project.2.refs_0_ = f32[192,512]{1,0:T(8,128)S(1)} custom-call(bf16[192,2560]{1,0:T(8,128)(2,1)S(1)} %get-tuple-element.17.hidden_ref, bf16[4,2560,256]{2,1,0:T(8,128)(2,1)S(1)} %get-tuple-element.18.base_ref, bf16[32,3584]{1,0:T(8,128)(2,1)S(1)} %bitcast.8, bf16[32,3584]{1,0:T(8,128)(2,1)S(1)} %collective-permute-done.refs_1_), custom_call_target="tpu_custom_call" | custom-call | flops 671088640 | bytes 3604480 | tf_op jit(solution)/shard_map/project/pallas_call | solution.py:304
  26.0 0.3 %collective-permute-done.1.refs_1_ = f32[192,512]{1,0:T(8,128)S(1)} collective-permute-done((f32[192,512]{1,0:T(8,128)S(1)}, f32[192,512]{1,0:T(8,128)S(1)}, u32[]{:S(2)}, u32[]{:S(2)}) %collective-permute-start.1) | collective-permute-done | bytes 393248 | tf_op jit(solution)/shard_map/ppermute | solution.py:404
  26.3 0.0 copy-done
  26.3 0.0 copy-done.1
  26.3 0.3 %copy-done.2 = f32[48,64,128]{2,1,0:T(8,128)S(1)} copy-done((f32[48,64,128]{2,1,0:T(8,128)S(1)}, f32[48,64,128]{2,1,0:T(8,128)}, u32[]{:S(2)}) %copy-start.2) | copy-done | bytes 1572888
  26.6 2.3 %finish.1 = (bf16[48,4,2,2,128]{4,3,2,1,0:T(2,128)(2,1)}, bf16[48,64,128]{2,1,0:T(8,128)(2,1)}) custom-call(f32[192,512]{1,0:T(8,128)S(1)} %project.2.refs_0_, f32[192,512]{1,0:T(8,128)S(1)} %collective-permute-done.1.refs_1_, bf16[48,64,128]{2,1,0:T(8,128)(2,1)S(1)} %bitcast.5, f32[48,64,128]{2,1,0:T(8,128)S(1)} %copy-done.1, f32[48,64,128]{2,1,0:T(8,128)S(1)} %copy-done.2), custom_call_target="tpu_custom_call" | custom-call | flops 301989888 | bytes 4718592 | tf_op jit(solution)/shard_map/finish/pallas_call | solution.py:364
Async XLA Ops:
  2.2 14.5 %all-to-all-start = ((bf16[4,8,3584]{2,1,0:T(8,128)(2,1)}), bf16[4,8,3584]{2,1,0:T(8,128)(2,1)S(1)}, u32[]{:S(2)}, u32[]{:S(2)}) async-start(bf16[4,8,3584]{2,1,0:T(8,128)(2,1)} %payload.1), calls=%async_computation | async-start | bytes 458752 | tf_op jit(solution)/shard_map/all_to_all | solution.py:388
  16.7 6.4 %collective-permute-start = (bf16[32,3584]{1,0:T(8,128)(2,1)S(1)}, bf16[32,3584]{1,0:T(8,128)(2,1)S(1)}, u32[]{:S(2)}, u32[]{:S(2)}) collective-permute-start(bf16[32,3584]{1,0:T(8,128)(2,1)S(1)} %bitcast.6), channel_id=1, source_target_pairs={{0,2},{2,0},{4,6},{6,4},{8,10},{10,8},{12,14},{14,12},{1,3},{3,1},... | collective-permute-start | bytes 688136 | tf_op jit(solution)/shard_map/ppermute | solution.py:389
  24.5 1.8 %copy-start = (bf16[48,4,16,128]{3,2,1,0:T(8,128)(2,1)S(1)}, bf16[48,4,16,128]{3,2,1,0:T(8,128)(2,1)}, u32[]{:S(2)}) copy-start(bf16[48,4,16,128]{3,2,1,0:T(8,128)(2,1)} %param.11) | copy-start | bytes 2359300
  24.5 1.8 %copy-start.1 = (f32[48,64,128]{2,1,0:T(8,128)S(1)}, f32[48,64,128]{2,1,0:T(8,128)}, u32[]{:S(2)}) copy-start(f32[48,64,128]{2,1,0:T(8,128)} %get-tuple-element.20.refs_3_) | copy-start | bytes 4718596
  24.5 2.1 %copy-start.2 = (f32[48,64,128]{2,1,0:T(8,128)S(1)}, f32[48,64,128]{2,1,0:T(8,128)}, u32[]{:S(2)}) copy-start(f32[48,64,128]{2,1,0:T(8,128)} %get-tuple-element.21.refs_4_) | copy-start | bytes 4718596
  24.5 1.8 %collective-permute-start.1 = (f32[192,512]{1,0:T(8,128)S(1)}, f32[192,512]{1,0:T(8,128)S(1)}, u32[]{:S(2)}, u32[]{:S(2)}) collective-permute-start(f32[192,512]{1,0:T(8,128)S(1)} %project.3), channel_id=1, source_target_pairs={{0,1},{1,0},{2,3},{3,2},{4,5},{5,4},{6,7},{7,6},{8,9},{9,8},{10,11... | collective-permute-start | bytes 1179656 | tf_op jit(solution)/shard_map/ppermute | solution.py:404

commit v9 on v8

--- a/solution.py
+++ b/solution.py
@@ -24,52 +24,45 @@
     return pl.CostEstimate(flops=flops, bytes_accessed=moved, transcendentals=exps)
 
 
-def payload_kernel(down_hbm, up_hbm, out_hbm, held, ups, wide, sems):
+def payload_kernel(down_hbm, up_hbm, out_ref, ups, wide, sems):
     ranks, width = down_hbm.shape
     groups, size = ups.shape[1] * ups.shape[2], ups.shape[3]
-    get_down = pltpu.make_async_copy(down_hbm, held.at[:, pl.ds(0, width)], sems.at[0])
+    get_down = pltpu.make_async_copy(down_hbm, out_ref.at[:, pl.ds(0, width)], sems.at[0])
     get_up = pltpu.make_async_copy(up_hbm, ups, sems.at[1])
     get_up.start()
     get_down.start()
     get_up.wait()
     wide[...] = ups.reshape(ranks * groups, size)[...].astype(jnp.float32)
     for n in range(groups):
-        held[:, width + n * size : width + (n + 1) * size] = wide[pl.ds(n, ranks, stride=groups), :].astype(
+        out_ref[:, width + n * size : width + (n + 1) * size] = wide[pl.ds(n, ranks, stride=groups), :].astype(
             jnp.bfloat16
         )
     get_down.wait()
-    puts = [pltpu.make_async_copy(held, out_hbm.at[i], sems.at[2 + i]) for i in range(out_hbm.shape[0])]
-    for put in puts:
-        put.start()
-    for put in puts:
-        put.wait()
-
-
-def make_payload(down, up, count):
+
+
+def make_payload(down, up):
     ranks, width = down.shape
     groups, size = up.shape[1] * up.shape[2], up.shape[3]
-    held = (ranks, width + groups * size)
     return pl.pallas_call(
         payload_kernel,
-        out_shape=jax.ShapeDtypeStruct((count,) + held, jnp.bfloat16),
+        out_shape=pltpu.VMEM((ranks, width + groups * size), jnp.bfloat16),
         in_specs=[pl.BlockSpec(memory_space=pltpu.HBM)] * 2,
-        out_specs=pl.BlockSpec(memory_space=pltpu.HBM),
+        out_specs=VMEM,
         scratch_shapes=[
-            pltpu.VMEM(held, jnp.bfloat16),
             pltpu.VMEM(up.shape, jnp.bfloat16),
             pltpu.VMEM((ranks * groups, size), jnp.float32),
-            pltpu.SemaphoreType.DMA((2 + count,)),
+            pltpu.SemaphoreType.DMA((2,)),
         ],
-        compiler_params=params(60),
+        compiler_params=params(8),
         name="payload",
     )(in_hbm(down), in_hbm(up))
 
 
 def cached_kernel(chunks, heads, scale, *refs):
-    lengths_hbm, queries_hbm, cache_hbm, out_hbm, log_hbm = refs[:5]
-    lengths_ref, q_all, k_all, v_all, out_ref, log_ref = refs[5:11]
-    scores_refs, weights_refs, total_refs = refs[11:13], refs[13:15], refs[15:17]
-    sems, out_sems, length_sem = refs[17:]
+    lengths_hbm, queries_hbm, cache_hbm, q_all, out_ref, log_ref = refs[:6]
+    lengths_ref, k_all, v_all = refs[6:9]
+    scores_refs, weights_refs, total_refs = refs[9:11], refs[11:13], refs[13:15]
+    sems, length_sem = refs[15:]
     rows, queries, size = q_all.shape
     slots, own = k_all.shape[1:3]
     keys = slots * own
@@ -83,11 +76,6 @@
             (cache_hbm.at[mine, :, 1], v_all.at[mine]),
         )
         return [pltpu.make_async_copy(a, b, sems.at[i, n]) for n, (a, b) in enumerate(pairs)]
-
-    def puts(i):
-        mine = pl.ds(i * some, some)
-        pairs = ((out_ref.at[mine], out_hbm.at[mine]), (log_ref.at[mine], log_hbm.at[mine]))
-        return [pltpu.make_async_copy(a, b, out_sems.at[i, n]) for n, (a, b) in enumerate(pairs)]
 
     get_lengths = pltpu.make_async_copy(lengths_hbm, lengths_ref, length_sem)
     get_lengths.start()
@@ -140,8 +128,6 @@
             for h in range(2):
                 mine = slice(h * queries, (h + 1) * queries)
                 out_ref[r + h] = both[mine, h * size : (h + 1) * size] * total_refs[slot][p, mine]
-        for put in puts(i):
-            put.start()
 
     get_lengths.wait()
     await_chunk(0)
@@ -162,9 +148,6 @@
     soften(chunks - 1, 1)
     collect(chunks - 2, 0)
     collect(chunks - 1, 1)
-    for i in range(chunks):
-        for put in puts(i):
-            put.wait()
 
 
 def attend_cached(queries, cache, lengths):
@@ -177,16 +160,17 @@
     half = (rows, slots, own, size)
     return pl.pallas_call(
         functools.partial(cached_kernel, chunks, heads, size ** (-0.5)),
-        out_shape=(pltpu.HBM(state, jnp.float32),) * 2,
+        out_shape=(
+            pltpu.VMEM(state, jnp.bfloat16),
+            pltpu.VMEM(state, jnp.float32),
+            pltpu.VMEM(state, jnp.float32),
+        ),
         in_specs=[pl.BlockSpec(memory_space=pltpu.HBM)] * 3,
-        out_specs=(pl.BlockSpec(memory_space=pltpu.HBM),) * 2,
+        out_specs=(VMEM,) * 3,
         scratch_shapes=[
             pltpu.SMEM(lengths.shape, jnp.int32),
-            pltpu.VMEM((rows, many, size), jnp.bfloat16),
             pltpu.VMEM(half, jnp.bfloat16),
             pltpu.VMEM(half, jnp.bfloat16),
-            pltpu.VMEM(state, jnp.float32),
-            pltpu.VMEM(state, jnp.float32),
             pltpu.VMEM((pairs, 2 * many, slots * own), jnp.float32),
             pltpu.VMEM((pairs, 2 * many, slots * own), jnp.float32),
             pltpu.VMEM((pairs, 2 * many, slots * own), jnp.bfloat16),
@@ -194,7 +178,6 @@
             pltpu.VMEM((pairs, 2 * many, size), jnp.float32),
             pltpu.VMEM((pairs, 2 * many, size), jnp.float32),
             pltpu.SemaphoreType.DMA((chunks, 3)),
-            pltpu.SemaphoreType.DMA((chunks, 2)),
             pltpu.SemaphoreType.DMA,
         ],
         compiler_params=params(28),
@@ -380,30 +363,56 @@
     return fresh, context.reshape(rows, steps, heads, size)
 
 
-def gather(payload, dp):
-    ranks, columns = payload.shape[1:]
-    if dp % 2:
-        return [lax.all_to_all(payload, "dp", 0, 0, tiled=True).reshape(dp * ranks, columns)], lambda x: []
+def join_kernel(*refs):
+    blocks, out_ref = refs[:-1], refs[-1]
+    at = 0
+    for block in blocks:
+        out_ref[at : at + block.shape[0], :] = block[...]
+        at += block.shape[0]
+
+
+def join(blocks):
+    rows = sum(b.shape[0] for b in blocks)
+    return pl.pallas_call(
+        join_kernel,
+        out_shape=pltpu.VMEM((rows, blocks[0].shape[1]), jnp.bfloat16),
+        in_specs=[VMEM] * len(blocks),
+        out_specs=VMEM,
+        compiler_params=params(8),
+        name="join",
+    )(*blocks)
+
+
+def gather_second(factor_a, factor_b, dp):
+    count = dp // 2
+    ranks = factor_b.shape[0]
+    if ranks % 8 == 0 and count in (1, 2, 4):
+        payload = make_payload(factor_a.T, factor_b)
+        return [payload] + [lax.ppermute(payload, "dp", [(i, i ^ (2 * k)) for i in range(dp)]) for k in range(1, count)]
+    payload = jnp.concatenate([factor_a.T, factor_b.reshape(ranks, -1)], axis=1)
     groups = [[i for i in range(dp) if i % 2 == n] for n in range(2)]
-    mine = lax.all_to_all(payload, "dp", 0, 0, axis_index_groups=groups, tiled=True)
-    return [mine.reshape(dp // 2 * ranks, columns)], lambda x: [lax.ppermute(x, "dp", [(i, i ^ 1) for i in range(dp)])]
+    copies = jnp.broadcast_to(payload[None], (count,) + payload.shape)
+    blocks = lax.all_to_all(copies, "dp", 0, 0, axis_index_groups=groups, tiled=True)
+    return [blocks.reshape(count * ranks, payload.shape[1])]
 
 
 def shards(dp, tp, hidden, base_weight, factor_a, factor_b, queries, cache, lengths):
-    rows, steps, heads, size = queries.shape
-    own = cache.shape[3]
-    payload = make_payload(factor_a.T, factor_b, dp // 2 if dp % 2 == 0 else dp)
-    gathered, rest = gather(payload, dp)
-    state = attend_cached(queries, cache, lengths)
-    gathered, state, hidden, base_weight = lax.optimization_barrier((gathered, state, hidden, base_weight))
-    gathered = gathered + rest(gathered[0])
+    steps, own = queries.shape[1], cache.shape[3]
+    assert dp % 2 == 0
+    blocks = gather_second(factor_a, factor_b, dp)
+    queries, *state = attend_cached(queries, cache, lengths)
+    blocks, state, queries, hidden, base_weight = lax.optimization_barrier(
+        (blocks, state, queries, hidden, base_weight)
+    )
+    gathered = join(blocks) if len(blocks) > 1 else blocks[0]
+    gathered = [gathered, lax.ppermute(gathered, "dp", [(i, i ^ 1) for i in range(dp)])]
     tokens, base = arrange(hidden, base_weight, own)
     received = []
     for k in range(1, tp):
         other = project(k, tokens, base, gathered)
         received.append(lax.ppermute(other, "tp", [(i, i ^ k) for i in range(tp)]))
     mine = project(0, tokens, base, gathered)
-    return finish([mine] + received, queries.reshape(rows, steps * heads, size), state, steps, own)
+    return finish([mine] + received, queries, state, steps, own)
 
 
 def solution(mesh):

time: 29.2 us -> 26.4 us (0.904)
  Pallas kernels: 18.6 us -> 17 us
  waiting for transfers between devices: 1.39 us -> 0.88 us
  starting transfers between devices: 7.92 us -> 7.56 us
  local copies, waits for them, and re-layouts: 0.32 us -> 0 us
    all_to_all x1 -> x0, starting transfers between devices: 6.33 us -> none  [gather(): lax.all_to_all(payload, 'dp', 0, 0, axis_index_groups=groups, tiled=True)]
    ppermute x1 -> x4, starting transfers between devices: 1.52 us -> 7.49 us  [the longest x3 5.76 us: gather_second(): lax.ppermute(payload, 'dp', [(i, i ^ 2 * k) for i in range(dp)])]
    pallas_call x1, Pallas kernels: 7.45 us -> 6.54 us  [attend_cached(): pl.pallas_call(functools.partial(cached_kernel, chunks, heads, size ** (-...]
    all_to_all x1 -> x0, waiting for transfers between devices: 0.76 us -> none  [gather(): lax.all_to_all(payload, 'dp', 0, 0, axis_index_groups=groups, tiled=True)]
    pallas_call x1 -> x2, Pallas kernels: 1.52 us -> 0.83 us  [the longest x1 0.81 us: make_payload(): pl.pallas_call(payload_kernel, out_shape=pltpu.VMEM((ranks, width + group...]
    unnamed x6 -> x0, local copies, waits for them, and re-layouts: 0.32 us -> none
  transfers between devices with their start and end apart: 3 -> 5, of which waited for: 3 -> 2; matrix products, arithmetic and copies ran while one was open for 0% -> 0% of each run, Pallas kernels for 46% -> 48%
where the time goes in v9:
time: 26.4 us; the launch traced here: 26.1 us
  Pallas kernels  17 us (64%)
  starting transfers between devices  7.56 us (29%)
  waiting for transfers between devices  0.88 us (3%)
  between operations  0.71 us (3%)
    pallas_call x1, Pallas kernels, attend_cached(): pl.pallas_call(functools.partial(cached_kernel, chunks, heads, size ** (-...  6.54 us
    ppermute x3, starting transfers between devices, gather_second(): lax.ppermute(payload, 'dp', [(i, i ^ 2 * k) for i in range(dp)])  5.76 us
    pallas_call x1, Pallas kernels, arrange(): pl.pallas_call(functools.partial(arrange_kernel, chunks, own), out_shape=...  4.56 us
    pallas_call x2, Pallas kernels, project(): pl.pallas_call(functools.partial(project_kernel, k), out_shape=pltpu.VMEM...  2.75 us
    pallas_call x1, Pallas kernels, finish(): pl.pallas_call(functools.partial(finish_kernel, steps, heads, size ** (-0...  2.28 us
    ppermute x1, starting transfers between devices, shards(): lax.ppermute(gathered, 'dp', [(i, i ^ 1) for i in range(dp)])  1.73 us
    pallas_call x1, Pallas kernels, make_payload(): pl.pallas_call(payload_kernel, out_shape=pltpu.VMEM((ranks, width + group...  0.81 us
    ppermute x1, waiting for transfers between devices, shards(): lax.ppermute(gathered, 'dp', [(i, i ^ 1) for i in range(dp)])  0.55 us
  transfers between devices with their start and end apart: 5, of which 2 were waited for; matrix products, arithmetic and copies ran while one was open for 0% of the time, Pallas kernels for 48%

profile of v9, /device:TPU:0, one launch (start us, length us, event | category | flops | bytes accessed | tf_op | source)
XLA Modules:
  0.0 26.1 jit_solution(89243509261131358)
XLA Ops:
  0.6 0.8 %payload.1.refs_0_ = bf16[8,3584]{1,0:T(8,128)(2,1)S(1)} custom-call(bf16[8,2560]{1,0:T(8,128)(2,1)} %bitcast.4, bf16[8,2,4,128]{3,2,1,0:T(4,128)(2,1)} %up_hbm.1), custom_call_target="tpu_custom_call" | custom-call | tf_op jit(solution)/shard_map/payload/pallas_call | solution.py:46
  1.5 5.1 %collective-permute-start.2 = (bf16[8,3584]{1,0:T(8,128)(2,1)S(1)}, bf16[8,3584]{1,0:T(8,128)(2,1)S(1)}, u32[]{:S(2)}, u32[]{:S(2)}) collective-permute-start(bf16[8,3584]{1,0:T(8,128)(2,1)S(1)} %payload.1.refs_0_), channel_id=1, source_target_pairs={{0,12},{2,14},{4,8},{6,10},{8,4},{10,6},{12,0},{14,2},{1,13},{3,15... | collective-permute-start | bytes 172040 | tf_op jit(solution)/shard_map/ppermute | solution.py:391
  6.6 0.0 collective-permute-start.1
  6.6 0.6 %collective-permute-start = (bf16[8,3584]{1,0:T(8,128)(2,1)S(1)}, bf16[8,3584]{1,0:T(8,128)(2,1)S(1)}, u32[]{:S(2)}, u32[]{:S(2)}) collective-permute-start(bf16[8,3584]{1,0:T(8,128)(2,1)S(1)} %payload.1.refs_0_), channel_id=1, source_target_pairs={{0,4},{2,6},{4,0},{6,2},{8,12},{10,14},{12,8},{14,10},{1,5},{3,7},... | collective-permute-start | bytes 172040 | tf_op jit(solution)/shard_map/ppermute | solution.py:391
  7.2 6.5 %attend_cached.1 = (bf16[48,64,128]{2,1,0:T(8,128)(2,1)S(1)}, f32[48,64,128]{2,1,0:T(8,128)S(1)}, f32[48,64,128]{2,1,0:T(8,128)S(1)}) custom-call(s32[48]{0:T(128)} %refs_0_.1, bf16[48,64,128]{2,1,0:T(8,128)(2,1)} %bitcast.3, bf16[48,128,2,2,128]{4,3,2,1,0:T(2,128)(2,1)} %refs_2_.1), custom_call_target="tpu_custom_call" | custom-call | flops 402653184 | bytes 10223616 | tf_op jit(solution)/shard_map/attend_cached/pallas_call | solution.py:161
  13.8 0.0 collective-permute-done.2.refs_3_
  13.8 0.0 collective-permute-done.1.refs_2_
  13.8 0.0 collective-permute-done.refs_1_
  13.8 1.7 %collective-permute-start.3 = (bf16[32,3584]{1,0:T(8,128)(2,1)S(1)}, bf16[32,3584]{1,0:T(8,128)(2,1)S(1)}, u32[]{:S(2)}, u32[]{:S(2)}) collective-permute-start(bf16[32,3584]{1,0:T(8,128)(2,1)S(1)} %join.1.refs_0_), channel_id=1, source_target_pairs={{0,2},{2,0},{4,6},{6,4},{8,10},{10,8},{12,14},{14,12},{1,3},{3,1},... | collective-permute-start | bytes 688136 | tf_op jit(solution)/shard_map/ppermute | solution.py:408
  15.5 4.6 %arrange.1 = (bf16[192,2560]{1,0:T(8,128)(2,1)S(1)}, bf16[4,2560,256]{2,1,0:T(8,128)(2,1)S(1)}) custom-call(bf16[48,4,2560]{2,1,0:T(4,128)(2,1)} %hidden_hbm, bf16[2560,2,4,128]{3,2,1,0:T(4,128)(2,1)} %base_hbm), custom_call_target="tpu_custom_call" | custom-call | flops 1342177280 | bytes 12451840 | tf_op jit(solution)/shard_map/arrange/pallas_call | solution.py:237
  20.1 0.6 %collective-permute-done.3.refs_1_ = bf16[32,3584]{1,0:T(8,128)(2,1)S(1)} collective-permute-done((bf16[32,3584]{1,0:T(8,128)(2,1)S(1)}, bf16[32,3584]{1,0:T(8,128)(2,1)S(1)}, u32[]{:S(2)}, u32[]{:S(2)}) %collective-permute-start.3) | collective-permute-done | bytes 229408 | tf_op jit(solution)/shard_map/ppermute | solution.py:408
  20.7 1.4 %project.3 = f32[192,512]{1,0:T(8,128)S(1)} custom-call(bf16[192,2560]{1,0:T(8,128)(2,1)S(1)} %get-tuple-element.23.hidden_ref, bf16[4,2560,256]{2,1,0:T(8,128)(2,1)S(1)} %get-tuple-element.24.base_ref, bf16[32,3584]{1,0:T(8,128)(2,1)S(1)} %join.1.refs_0_, bf16[32,3584]{1,0:T(8,128)(2,1)S(1)} %collective-permute-done.3.refs_1_), custom_call_target="tpu_custom_call" | custom-call | flops 671088640 | bytes 3604480 | tf_op jit(solution)/shard_map/project/pallas_call | solution.py:287
  22.0 0.1 collective-permute-start.4
  22.1 1.4 %project.2.refs_0_ = f32[192,512]{1,0:T(8,128)S(1)} custom-call(bf16[192,2560]{1,0:T(8,128)(2,1)S(1)} %get-tuple-element.23.hidden_ref, bf16[4,2560,256]{2,1,0:T(8,128)(2,1)S(1)} %get-tuple-element.24.base_ref, bf16[32,3584]{1,0:T(8,128)(2,1)S(1)} %join.1.refs_0_, bf16[32,3584]{1,0:T(8,128)(2,1)S(1)} %collective-permute-done.3.refs_1_), custom_call_target="tpu_custom_call" | custom-call | flops 671088640 | bytes 3604480 | tf_op jit(solution)/shard_map/project/pallas_call | solution.py:287
  23.5 0.3 %collective-permute-done.4.refs_1_ = f32[192,512]{1,0:T(8,128)S(1)} collective-permute-done((f32[192,512]{1,0:T(8,128)S(1)}, f32[192,512]{1,0:T(8,128)S(1)}, u32[]{:S(2)}, u32[]{:S(2)}) %collective-permute-start.4) | collective-permute-done | bytes 393248 | tf_op jit(solution)/shard_map/ppermute | solution.py:413
  23.8 2.3 %finish.1 = (bf16[48,4,2,2,128]{4,3,2,1,0:T(2,128)(2,1)}, bf16[48,64,128]{2,1,0:T(8,128)(2,1)}) custom-call(f32[192,512]{1,0:T(8,128)S(1)} %project.2.refs_0_, f32[192,512]{1,0:T(8,128)S(1)} %collective-permute-done.4.refs_1_, bf16[48,64,128]{2,1,0:T(8,128)(2,1)S(1)} %get-tuple-element.29.refs_2_, f32[48,64,128]{2,1,0:T(8,128)S(1)} %get-tuple-element.30.refs_3_, ...), custom_call_target="tpu_custom_call" | custom-call | flops 301989888 | bytes 4718592 | tf_op jit(solution)/shard_map/finish/pallas_call | solution.py:347
  (1 shorter events, 0.0 us)
Async XLA Ops:
  1.5 12.3 %collective-permute-start.2 = (bf16[8,3584]{1,0:T(8,128)(2,1)S(1)}, bf16[8,3584]{1,0:T(8,128)(2,1)S(1)}, u32[]{:S(2)}, u32[]{:S(2)}) collective-permute-start(bf16[8,3584]{1,0:T(8,128)(2,1)S(1)} %payload.1.refs_0_), channel_id=1, source_target_pairs={{0,12},{2,14},{4,8},{6,10},{8,4},{10,6},{12,0},{14,2},{1,13},{3,15... | collective-permute-start | bytes 172040 | tf_op jit(solution)/shard_map/ppermute | solution.py:391
  6.6 7.2 %collective-permute-start.1 = (bf16[8,3584]{1,0:T(8,128)(2,1)S(1)}, bf16[8,3584]{1,0:T(8,128)(2,1)S(1)}, u32[]{:S(2)}, u32[]{:S(2)}) collective-permute-start(bf16[8,3584]{1,0:T(8,128)(2,1)S(1)} %payload.1.refs_0_), channel_id=1, source_target_pairs={{0,8},{2,10},{4,12},{6,14},{8,0},{10,2},{12,4},{14,6},{1,9},{3,11}... | collective-permute-start | bytes 172040 | tf_op jit(solution)/shard_map/ppermute | solution.py:391
  6.6 7.2 %collective-permute-start = (bf16[8,3584]{1,0:T(8,128)(2,1)S(1)}, bf16[8,3584]{1,0:T(8,128)(2,1)S(1)}, u32[]{:S(2)}, u32[]{:S(2)}) collective-permute-start(bf16[8,3584]{1,0:T(8,128)(2,1)S(1)} %payload.1.refs_0_), channel_id=1, source_target_pairs={{0,4},{2,6},{4,0},{6,2},{8,12},{10,14},{12,8},{14,10},{1,5},{3,7},... | collective-permute-start | bytes 172040 | tf_op jit(solution)/shard_map/ppermute | solution.py:391
  13.8 6.8 %collective-permute-start.3 = (bf16[32,3584]{1,0:T(8,128)(2,1)S(1)}, bf16[32,3584]{1,0:T(8,128)(2,1)S(1)}, u32[]{:S(2)}, u32[]{:S(2)}) collective-permute-start(bf16[32,3584]{1,0:T(8,128)(2,1)S(1)} %join.1.refs_0_), channel_id=1, source_target_pairs={{0,2},{2,0},{4,6},{6,4},{8,10},{10,8},{12,14},{14,12},{1,3},{3,1},... | collective-permute-start | bytes 688136 | tf_op jit(solution)/shard_map/ppermute | solution.py:408
  22.0 1.8 %collective-permute-start.4 = (f32[192,512]{1,0:T(8,128)S(1)}, f32[192,512]{1,0:T(8,128)S(1)}, u32[]{:S(2)}, u32[]{:S(2)}) collective-permute-start(f32[192,512]{1,0:T(8,128)S(1)} %project.3), channel_id=1, source_target_pairs={{0,1},{1,0},{2,3},{3,2},{4,5},{5,4},{6,7},{7,6},{8,9},{9,8},{10,11... | collective-permute-start | bytes 1179656 | tf_op jit(solution)/shard_map/ppermute | solution.py:413

commit v10 on v9

--- a/solution.py
+++ b/solution.py
@@ -60,20 +60,19 @@
 
 def cached_kernel(chunks, heads, scale, *refs):
     lengths_hbm, queries_hbm, cache_hbm, q_all, out_ref, log_ref = refs[:6]
-    lengths_ref, k_all, v_all = refs[6:9]
-    scores_refs, weights_refs, total_refs = refs[9:11], refs[11:13], refs[13:15]
-    sems, length_sem = refs[15:]
+    lengths_ref, cached = refs[6:8]
+    scores_refs, weights_refs, total_refs = refs[8:10], refs[10:12], refs[12:14]
+    sems, length_sem = refs[14:]
     rows, queries, size = q_all.shape
-    slots, own = k_all.shape[1:3]
-    keys = slots * own
+    slots, own = cached.shape[1], cached.shape[3]
+    lines = slots * 2 * own
     some = rows // chunks
 
     def copies(i):
         mine = pl.ds(i * some, some)
         pairs = (
             (queries_hbm.at[mine], q_all.at[mine]),
-            (cache_hbm.at[mine, :, 0], k_all.at[mine]),
-            (cache_hbm.at[mine, :, 1], v_all.at[mine]),
+            (cache_hbm.at[mine], cached.at[pl.ds(1 + i * some, some)]),
         )
         return [pltpu.make_async_copy(a, b, sems.at[i, n]) for n, (a, b) in enumerate(pairs)]
 
@@ -83,12 +82,18 @@
         for copy in copies(i):
             copy.start()
 
-    column = lax.broadcasted_iota(jnp.int32, (queries, keys), 1)
-    head = lax.broadcasted_iota(jnp.int32, (queries, keys), 0) % heads
-    column = jnp.where(column % own == head // (heads // own), column, own * slots)
+    each = (own, heads // own, lines)
+    line = lax.broadcasted_iota(jnp.int32, each, 2)
+    fits = ((line // own) % 2 == 1) & (line % own == lax.broadcasted_iota(jnp.int32, each, 0))
+    line = jnp.where(fits, line, lines)
     nothing = jnp.zeros((queries, size), jnp.bfloat16)
-    flat_k = k_all.reshape(rows, keys, size)
-    flat_v = v_all.reshape(rows, keys, size)
+    flat = cached.reshape((rows + 1) * lines, size)
+
+    def keys(r):
+        return flat[pl.ds(pl.multiple_of((r + 1) * lines - own, own), lines), :]
+
+    def values(r):
+        return flat[pl.ds(pl.multiple_of((r + 1) * lines, own), lines), :]
 
     def await_chunk(i):
         for copy in copies(i):
@@ -104,7 +109,7 @@
                 ],
                 axis=0,
             )
-            both_k = jnp.concatenate([flat_k[r], flat_k[r + 1]], axis=1)
+            both_k = jnp.concatenate([keys(r), keys(r + 1)], axis=1)
             scores_refs[slot][p] = lax.dot_general(both, both_k, NT, preferred_element_type=jnp.float32)
 
     def soften(i, slot):
@@ -112,7 +117,9 @@
             for h in range(2):
                 r = i * some + 2 * p + h
                 mine = slice(h * queries, (h + 1) * queries)
-                scores = jnp.where(column < own * lengths_ref[r], scores_refs[slot][p, mine], LOW)
+                live = line < 2 * own * lengths_ref[r]
+                scores = scores_refs[slot][p, mine].reshape((queries // heads,) + each)
+                scores = jnp.where(live[None], scores, LOW).reshape(queries, lines)
                 top = jnp.max(scores, axis=-1, keepdims=True)
                 expo = jnp.exp((scores - top) * scale)
                 total = jnp.sum(expo, axis=-1, keepdims=True)
@@ -123,7 +130,7 @@
     def collect(i, slot):
         for p in range(some // 2):
             r = i * some + 2 * p
-            both_v = jnp.concatenate([flat_v[r], flat_v[r + 1]], axis=1)
+            both_v = jnp.concatenate([values(r), values(r + 1)], axis=1)
             both = jnp.dot(weights_refs[slot][p], both_v, preferred_element_type=jnp.float32)
             for h in range(2):
                 mine = slice(h * queries, (h + 1) * queries)
@@ -156,8 +163,8 @@
     many = steps * heads
     chunks = 8
     pairs = rows // chunks // 2
+    lines = slots * 2 * own
     state = (rows, many, size)
-    half = (rows, slots, own, size)
     return pl.pallas_call(
         functools.partial(cached_kernel, chunks, heads, size ** (-0.5)),
         out_shape=(
@@ -169,20 +176,19 @@
         out_specs=(VMEM,) * 3,
         scratch_shapes=[
             pltpu.SMEM(lengths.shape, jnp.int32),
-            pltpu.VMEM(half, jnp.bfloat16),
-            pltpu.VMEM(half, jnp.bfloat16),
-            pltpu.VMEM((pairs, 2 * many, slots * own), jnp.float32),
-            pltpu.VMEM((pairs, 2 * many, slots * own), jnp.float32),
-            pltpu.VMEM((pairs, 2 * many, slots * own), jnp.bfloat16),
-            pltpu.VMEM((pairs, 2 * many, slots * own), jnp.bfloat16),
+            pltpu.VMEM((rows + 1,) + cache.shape[1:], jnp.bfloat16),
+            pltpu.VMEM((pairs, 2 * many, lines), jnp.float32),
+            pltpu.VMEM((pairs, 2 * many, lines), jnp.float32),
+            pltpu.VMEM((pairs, 2 * many, lines), jnp.bfloat16),
+            pltpu.VMEM((pairs, 2 * many, lines), jnp.bfloat16),
             pltpu.VMEM((pairs, 2 * many, size), jnp.float32),
             pltpu.VMEM((pairs, 2 * many, size), jnp.float32),
-            pltpu.SemaphoreType.DMA((chunks, 3)),
+            pltpu.SemaphoreType.DMA((chunks, 2)),
             pltpu.SemaphoreType.DMA,
         ],
         compiler_params=params(28),
         cost_estimate=cost(
-            8 * rows * many * slots * size, 2 * (cache.size + queries.size) + 8 * rows * many * size, rows * many * slots
+            16 * rows * many * slots * size, 2 * (cache.size + queries.size) + 8 * rows * many * size, rows * many * lines
         ),
         name="attend_cached",
     )(*map(in_hbm, (lengths, queries.reshape(rows, many, size), cache)))
@@ -198,9 +204,9 @@
         return pltpu.make_async_copy(base_hbm.at[features], base.at[features], sems.at[i])
 
     get_hidden = pltpu.make_async_copy(hidden_hbm, hidden, sems.at[chunks])
-    get_hidden.start()
     for i in range(chunks):
         copy(i).start()
+    get_hidden.start()
 
     tile = 256
     some = tile // groups
@@ -220,20 +226,20 @@
                     n * some : (n + 1) * some, h * size : (h + 1) * size
                 ]
 
-    get_hidden.wait()
-    tokens_ref[...] = hidden.reshape(tokens_ref.shape)[...]
-
     @pl.loop(0, chunks)
     def _(i):
         copy(i).wait()
         for f in range(0, some_width, 2 * some):
             arrange(i * some_width + f)
 
+    get_hidden.wait()
+    tokens_ref[...] = hidden.reshape(tokens_ref.shape)[...]
+
 
 def arrange(hidden, base, own):
     rows, steps, _ = hidden.shape
     width, two, kvh, size = base.shape
-    chunks = 8
+    chunks = 4
     return pl.pallas_call(
         functools.partial(arrange_kernel, chunks, own),
         out_shape=(

time: 26.4 us -> 30 us (1.14)
  Pallas kernels: 17 us -> 19.8 us
  waiting for transfers between devices: 0.88 us -> 1.69 us
    pallas_call x1, Pallas kernels: 6.54 us -> 10.2 us  [attend_cached(): pl.pallas_call(functools.partial(cached_kernel, chunks, heads, size ** (-...]
    ppermute x1, waiting for transfers between devices: 0.55 us -> 1.35 us  [shards(): lax.ppermute(gathered, 'dp', [(i, i ^ 1) for i in range(dp)])]
    pallas_call x1, Pallas kernels: 4.56 us -> 3.76 us  [arrange(): pl.pallas_call(functools.partial(arrange_kernel, chunks, own), out_shape=...]
  transfers between devices with their start and end apart: 5 -> 5, of which waited for: 2 -> 2; matrix products, arithmetic and copies ran while one was open for 0% -> 0% of each run, Pallas kernels for 48% -> 51%
where the time goes in v10:
time: 30 us; the launch traced here: 29.8 us
  Pallas kernels  19.8 us (66%)
  starting transfers between devices  7.55 us (25%)
  waiting for transfers between devices  1.69 us (6%)
  between operations  0.71 us (2%)
    pallas_call x1, Pallas kernels, attend_cached(): pl.pallas_call(functools.partial(cached_kernel, chunks, heads, size ** (-...  10.2 us
    ppermute x3, starting transfers between devices, gather_second(): lax.ppermute(payload, 'dp', [(i, i ^ 2 * k) for i in range(dp)])  5.76 us
    pallas_call x1, Pallas kernels, arrange(): pl.pallas_call(functools.partial(arrange_kernel, chunks, own), out_shape=...  3.76 us
    pallas_call x2, Pallas kernels, project(): pl.pallas_call(functools.partial(project_kernel, k), out_shape=pltpu.VMEM...  2.75 us
    pallas_call x1, Pallas kernels, finish(): pl.pallas_call(functools.partial(finish_kernel, steps, heads, size ** (-0...  2.29 us
    ppermute x1, starting transfers between devices, shards(): lax.ppermute(gathered, 'dp', [(i, i ^ 1) for i in range(dp)])  1.73 us
    ppermute x1, waiting for transfers between devices, shards(): lax.ppermute(gathered, 'dp', [(i, i ^ 1) for i in range(dp)])  1.35 us
    pallas_call x1, Pallas kernels, make_payload(): pl.pallas_call(payload_kernel, out_shape=pltpu.VMEM((ranks, width + group...  0.81 us
  transfers between devices with their start and end apart: 5, of which 2 were waited for; matrix products, arithmetic and copies ran while one was open for 0% of the time, Pallas kernels for 51%

profile of v10, /device:TPU:0, one launch (start us, length us, event | category | flops | bytes accessed | tf_op | source)
XLA Modules:
  0.0 29.8 jit_solution(2574747226104033975)
XLA Ops:
  0.6 0.8 %payload.1.refs_0_ = bf16[8,3584]{1,0:T(8,128)(2,1)S(1)} custom-call(bf16[8,2560]{1,0:T(8,128)(2,1)} %bitcast.4, bf16[8,2,4,128]{3,2,1,0:T(4,128)(2,1)} %up_hbm.1), custom_call_target="tpu_custom_call" | custom-call | tf_op jit(solution)/shard_map/payload/pallas_call | solution.py:46
  1.5 5.1 %collective-permute-start.2 = (bf16[8,3584]{1,0:T(8,128)(2,1)S(1)}, bf16[8,3584]{1,0:T(8,128)(2,1)S(1)}, u32[]{:S(2)}, u32[]{:S(2)}) collective-permute-start(bf16[8,3584]{1,0:T(8,128)(2,1)S(1)} %payload.1.refs_0_), channel_id=1, source_target_pairs={{0,12},{2,14},{4,8},{6,10},{8,4},{10,6},{12,0},{14,2},{1,13},{3,15... | collective-permute-start | bytes 172040 | tf_op jit(solution)/shard_map/ppermute | solution.py:397
  6.6 0.0 collective-permute-start.1
  6.6 0.6 %collective-permute-start = (bf16[8,3584]{1,0:T(8,128)(2,1)S(1)}, bf16[8,3584]{1,0:T(8,128)(2,1)S(1)}, u32[]{:S(2)}, u32[]{:S(2)}) collective-permute-start(bf16[8,3584]{1,0:T(8,128)(2,1)S(1)} %payload.1.refs_0_), channel_id=1, source_target_pairs={{0,4},{2,6},{4,0},{6,2},{8,12},{10,14},{12,8},{14,10},{1,5},{3,7},... | collective-permute-start | bytes 172040 | tf_op jit(solution)/shard_map/ppermute | solution.py:397
  7.2 10.2 %attend_cached.1 = (bf16[48,64,128]{2,1,0:T(8,128)(2,1)S(1)}, f32[48,64,128]{2,1,0:T(8,128)S(1)}, f32[48,64,128]{2,1,0:T(8,128)S(1)}) custom-call(s32[48]{0:T(128)} %refs_0_.1, bf16[48,64,128]{2,1,0:T(8,128)(2,1)} %bitcast.3, bf16[48,128,2,2,128]{4,3,2,1,0:T(2,128)(2,1)} %refs_2_.1), custom_call_target="tpu_custom_call" | custom-call | flops 805306368 | bytes 10223616 | tf_op jit(solution)/shard_map/attend_cached/pallas_call | solution.py:168
  17.4 0.0 collective-permute-done.2.refs_3_
  17.4 0.0 collective-permute-done.1.refs_2_
  17.4 0.0 collective-permute-done.refs_1_
  17.5 1.7 %collective-permute-start.3 = (bf16[32,3584]{1,0:T(8,128)(2,1)S(1)}, bf16[32,3584]{1,0:T(8,128)(2,1)S(1)}, u32[]{:S(2)}, u32[]{:S(2)}) collective-permute-start(bf16[32,3584]{1,0:T(8,128)(2,1)S(1)} %join.1.refs_0_), channel_id=1, source_target_pairs={{0,2},{2,0},{4,6},{6,4},{8,10},{10,8},{12,14},{14,12},{1,3},{3,1},... | collective-permute-start | bytes 688136 | tf_op jit(solution)/shard_map/ppermute | solution.py:414
  19.2 3.8 %arrange.1 = (bf16[192,2560]{1,0:T(8,128)(2,1)S(1)}, bf16[4,2560,256]{2,1,0:T(8,128)(2,1)S(1)}) custom-call(bf16[48,4,2560]{2,1,0:T(4,128)(2,1)} %hidden_hbm, bf16[2560,2,4,128]{3,2,1,0:T(4,128)(2,1)} %base_hbm), custom_call_target="tpu_custom_call" | custom-call | flops 1342177280 | bytes 12451840 | tf_op jit(solution)/shard_map/arrange/pallas_call | solution.py:243
  23.0 1.4 %collective-permute-done.3.refs_1_ = bf16[32,3584]{1,0:T(8,128)(2,1)S(1)} collective-permute-done((bf16[32,3584]{1,0:T(8,128)(2,1)S(1)}, bf16[32,3584]{1,0:T(8,128)(2,1)S(1)}, u32[]{:S(2)}, u32[]{:S(2)}) %collective-permute-start.3) | collective-permute-done | bytes 229408 | tf_op jit(solution)/shard_map/ppermute | solution.py:414
  24.3 1.4 %project.3 = f32[192,512]{1,0:T(8,128)S(1)} custom-call(bf16[192,2560]{1,0:T(8,128)(2,1)S(1)} %get-tuple-element.23.hidden_ref, bf16[4,2560,256]{2,1,0:T(8,128)(2,1)S(1)} %get-tuple-element.24.base_ref, bf16[32,3584]{1,0:T(8,128)(2,1)S(1)} %join.1.refs_0_, bf16[32,3584]{1,0:T(8,128)(2,1)S(1)} %collective-permute-done.3.refs_1_), custom_call_target="tpu_custom_call" | custom-call | flops 671088640 | bytes 3604480 | tf_op jit(solution)/shard_map/project/pallas_call | solution.py:293
  25.7 0.1 collective-permute-start.4
  25.8 1.4 %project.2.refs_0_ = f32[192,512]{1,0:T(8,128)S(1)} custom-call(bf16[192,2560]{1,0:T(8,128)(2,1)S(1)} %get-tuple-element.23.hidden_ref, bf16[4,2560,256]{2,1,0:T(8,128)(2,1)S(1)} %get-tuple-element.24.base_ref, bf16[32,3584]{1,0:T(8,128)(2,1)S(1)} %join.1.refs_0_, bf16[32,3584]{1,0:T(8,128)(2,1)S(1)} %collective-permute-done.3.refs_1_), custom_call_target="tpu_custom_call" | custom-call | flops 671088640 | bytes 3604480 | tf_op jit(solution)/shard_map/project/pallas_call | solution.py:293
  27.2 0.3 %collective-permute-done.4.refs_1_ = f32[192,512]{1,0:T(8,128)S(1)} collective-permute-done((f32[192,512]{1,0:T(8,128)S(1)}, f32[192,512]{1,0:T(8,128)S(1)}, u32[]{:S(2)}, u32[]{:S(2)}) %collective-permute-start.4) | collective-permute-done | bytes 393248 | tf_op jit(solution)/shard_map/ppermute | solution.py:419
  27.5 2.3 %finish.1 = (bf16[48,4,2,2,128]{4,3,2,1,0:T(2,128)(2,1)}, bf16[48,64,128]{2,1,0:T(8,128)(2,1)}) custom-call(f32[192,512]{1,0:T(8,128)S(1)} %project.2.refs_0_, f32[192,512]{1,0:T(8,128)S(1)} %collective-permute-done.4.refs_1_, bf16[48,64,128]{2,1,0:T(8,128)(2,1)S(1)} %get-tuple-element.29.refs_2_, f32[48,64,128]{2,1,0:T(8,128)S(1)} %get-tuple-element.30.refs_3_, ...), custom_call_target="tpu_custom_call" | custom-call | flops 301989888 | bytes 4718592 | tf_op jit(solution)/shard_map/finish/pallas_call | solution.py:353
  (1 shorter events, 0.0 us)
Async XLA Ops:
  1.5 16.0 %collective-permute-start.2 = (bf16[8,3584]{1,0:T(8,128)(2,1)S(1)}, bf16[8,3584]{1,0:T(8,128)(2,1)S(1)}, u32[]{:S(2)}, u32[]{:S(2)}) collective-permute-start(bf16[8,3584]{1,0:T(8,128)(2,1)S(1)} %payload.1.refs_0_), channel_id=1, source_target_pairs={{0,12},{2,14},{4,8},{6,10},{8,4},{10,6},{12,0},{14,2},{1,13},{3,15... | collective-permute-start | bytes 172040 | tf_op jit(solution)/shard_map/ppermute | solution.py:397
  6.6 10.9 %collective-permute-start.1 = (bf16[8,3584]{1,0:T(8,128)(2,1)S(1)}, bf16[8,3584]{1,0:T(8,128)(2,1)S(1)}, u32[]{:S(2)}, u32[]{:S(2)}) collective-permute-start(bf16[8,3584]{1,0:T(8,128)(2,1)S(1)} %payload.1.refs_0_), channel_id=1, source_target_pairs={{0,8},{2,10},{4,12},{6,14},{8,0},{10,2},{12,4},{14,6},{1,9},{3,11}... | collective-permute-start | bytes 172040 | tf_op jit(solution)/shard_map/ppermute | solution.py:397
  6.6 10.9 %collective-permute-start = (bf16[8,3584]{1,0:T(8,128)(2,1)S(1)}, bf16[8,3584]{1,0:T(8,128)(2,1)S(1)}, u32[]{:S(2)}, u32[]{:S(2)}) collective-permute-start(bf16[8,3584]{1,0:T(8,128)(2,1)S(1)} %payload.1.refs_0_), channel_id=1, source_target_pairs={{0,4},{2,6},{4,0},{6,2},{8,12},{10,14},{12,8},{14,10},{1,5},{3,7},... | collective-permute-start | bytes 172040 | tf_op jit(solution)/shard_map/ppermute | solution.py:397
  17.5 6.8 %collective-permute-start.3 = (bf16[32,3584]{1,0:T(8,128)(2,1)S(1)}, bf16[32,3584]{1,0:T(8,128)(2,1)S(1)}, u32[]{:S(2)}, u32[]{:S(2)}) collective-permute-start(bf16[32,3584]{1,0:T(8,128)(2,1)S(1)} %join.1.refs_0_), channel_id=1, source_target_pairs={{0,2},{2,0},{4,6},{6,4},{8,10},{10,8},{12,14},{14,12},{1,3},{3,1},... | collective-permute-start | bytes 688136 | tf_op jit(solution)/shard_map/ppermute | solution.py:414
  25.7 1.8 %collective-permute-start.4 = (f32[192,512]{1,0:T(8,128)S(1)}, f32[192,512]{1,0:T(8,128)S(1)}, u32[]{:S(2)}, u32[]{:S(2)}) collective-permute-start(f32[192,512]{1,0:T(8,128)S(1)} %project.3), channel_id=1, source_target_pairs={{0,1},{1,0},{2,3},{3,2},{4,5},{5,4},{6,7},{7,6},{8,9},{9,8},{10,11... | collective-permute-start | bytes 1179656 | tf_op jit(solution)/shard_map/ppermute | solution.py:419

commit v11 on v9

--- a/solution.py
+++ b/solution.py
@@ -9,6 +9,7 @@
 
 LOW = -1e30
 NT = (((1,), (1,)), ((), ()))
+TN = (((0,), (0,)), ((), ()))
 VMEM = pl.BlockSpec(memory_space=pltpu.VMEM)
 
 
@@ -59,10 +60,10 @@
 
 
 def cached_kernel(chunks, heads, scale, *refs):
-    lengths_hbm, queries_hbm, cache_hbm, q_all, out_ref, log_ref = refs[:6]
-    lengths_ref, k_all, v_all = refs[6:9]
-    scores_refs, weights_refs, total_refs = refs[9:11], refs[11:13], refs[13:15]
-    sems, length_sem = refs[15:]
+    lengths_hbm, queries_hbm, cache_hbm, q_all, sum_ref, top_ref, total_ref = refs[:7]
+    lengths_ref, k_all, v_all = refs[7:10]
+    scores_refs, weights_refs = refs[10:12], refs[12:14]
+    sems, length_sem = refs[14:]
     rows, queries, size = q_all.shape
     slots, own = k_all.shape[1:3]
     keys = slots * own
@@ -83,9 +84,10 @@
         for copy in copies(i):
             copy.start()
 
-    column = lax.broadcasted_iota(jnp.int32, (queries, keys), 1)
-    head = lax.broadcasted_iota(jnp.int32, (queries, keys), 0) % heads
-    column = jnp.where(column % own == head // (heads // own), column, own * slots)
+    line = lax.broadcasted_iota(jnp.int32, (keys, 2 * queries), 0)
+    query = lax.broadcasted_iota(jnp.int32, (keys, 2 * queries), 1)
+    line = jnp.where(line % own == (query % heads) // (heads // own), line, keys)
+    first = lax.broadcasted_iota(jnp.int32, (1, 2 * queries), 1) < queries
     nothing = jnp.zeros((queries, size), jnp.bfloat16)
     flat_k = k_all.reshape(rows, keys, size)
     flat_v = v_all.reshape(rows, keys, size)
@@ -97,7 +99,7 @@
     def score(i, slot):
         for p in range(some // 2):
             r = i * some + 2 * p
-            both = jnp.concatenate(
+            both_q = jnp.concatenate(
                 [
                     jnp.concatenate([q_all[r], nothing], axis=1),
                     jnp.concatenate([nothing, q_all[r + 1]], axis=1),
@@ -105,29 +107,27 @@
                 axis=0,
             )
             both_k = jnp.concatenate([flat_k[r], flat_k[r + 1]], axis=1)
-            scores_refs[slot][p] = lax.dot_general(both, both_k, NT, preferred_element_type=jnp.float32)
+            scores_refs[slot][p] = lax.dot_general(both_k, both_q, NT, preferred_element_type=jnp.float32)
 
     def soften(i, slot):
         for p in range(some // 2):
-            for h in range(2):
-                r = i * some + 2 * p + h
-                mine = slice(h * queries, (h + 1) * queries)
-                scores = jnp.where(column < own * lengths_ref[r], scores_refs[slot][p, mine], LOW)
-                top = jnp.max(scores, axis=-1, keepdims=True)
-                expo = jnp.exp((scores - top) * scale)
-                total = jnp.sum(expo, axis=-1, keepdims=True)
-                weights_refs[slot][p, mine] = expo.astype(jnp.bfloat16)
-                total_refs[slot][p, mine] = jnp.broadcast_to(1.0 / total, (queries, size))
-                log_ref[r] = jnp.broadcast_to(top * scale + jnp.log(total), (queries, size))
+            r = i * some + 2 * p
+            limit = jnp.where(first, own * lengths_ref[r], own * lengths_ref[r + 1])
+            scores = jnp.where(line < limit, scores_refs[slot][p], LOW)
+            top = jnp.max(scores, axis=0, keepdims=True)
+            expo = jnp.exp((scores - top) * scale)
+            weights_refs[slot][p] = expo.astype(jnp.bfloat16)
+            pair = pl.ds(i * (some // 2) + p, 1)
+            top_ref[pair, :] = top
+            total_ref[pair, :] = jnp.sum(expo, axis=0, keepdims=True)
 
     def collect(i, slot):
         for p in range(some // 2):
             r = i * some + 2 * p
             both_v = jnp.concatenate([flat_v[r], flat_v[r + 1]], axis=1)
-            both = jnp.dot(weights_refs[slot][p], both_v, preferred_element_type=jnp.float32)
+            both = lax.dot_general(weights_refs[slot][p], both_v, TN, preferred_element_type=jnp.float32)
             for h in range(2):
-                mine = slice(h * queries, (h + 1) * queries)
-                out_ref[r + h] = both[mine, h * size : (h + 1) * size] * total_refs[slot][p, mine]
+                sum_ref[r + h] = both[h * queries : (h + 1) * queries, h * size : (h + 1) * size]
 
     get_lengths.wait()
     await_chunk(0)
@@ -156,6 +156,7 @@
     many = steps * heads
     chunks = 8
     pairs = rows // chunks // 2
+    keys = slots * own
     state = (rows, many, size)
     half = (rows, slots, own, size)
     return pl.pallas_call(
@@ -163,26 +164,25 @@
         out_shape=(
             pltpu.VMEM(state, jnp.bfloat16),
             pltpu.VMEM(state, jnp.float32),
-            pltpu.VMEM(state, jnp.float32),
+            pltpu.VMEM((rows // 2, 2 * many), jnp.float32),
+            pltpu.VMEM((rows // 2, 2 * many), jnp.float32),
         ),
         in_specs=[pl.BlockSpec(memory_space=pltpu.HBM)] * 3,
-        out_specs=(VMEM,) * 3,
+        out_specs=(VMEM,) * 4,
         scratch_shapes=[
             pltpu.SMEM(lengths.shape, jnp.int32),
             pltpu.VMEM(half, jnp.bfloat16),
             pltpu.VMEM(half, jnp.bfloat16),
-            pltpu.VMEM((pairs, 2 * many, slots * own), jnp.float32),
-            pltpu.VMEM((pairs, 2 * many, slots * own), jnp.float32),
-            pltpu.VMEM((pairs, 2 * many, slots * own), jnp.bfloat16),
-            pltpu.VMEM((pairs, 2 * many, slots * own), jnp.bfloat16),
-            pltpu.VMEM((pairs, 2 * many, size), jnp.float32),
-            pltpu.VMEM((pairs, 2 * many, size), jnp.float32),
+            pltpu.VMEM((pairs, keys, 2 * many), jnp.float32),
+            pltpu.VMEM((pairs, keys, 2 * many), jnp.float32),
+            pltpu.VMEM((pairs, keys, 2 * many), jnp.bfloat16),
+            pltpu.VMEM((pairs, keys, 2 * many), jnp.bfloat16),
             pltpu.SemaphoreType.DMA((chunks, 3)),
             pltpu.SemaphoreType.DMA,
         ],
         compiler_params=params(28),
         cost_estimate=cost(
-            8 * rows * many * slots * size, 2 * (cache.size + queries.size) + 8 * rows * many * size, rows * many * slots
+            8 * rows * many * slots * size, 2 * (cache.size + queries.size) + 4 * rows * many * size, rows * many * keys
         ),
         name="attend_cached",
     )(*map(in_hbm, (lengths, queries.reshape(rows, many, size), cache)))
@@ -198,9 +198,9 @@
         return pltpu.make_async_copy(base_hbm.at[features], base.at[features], sems.at[i])
 
     get_hidden = pltpu.make_async_copy(hidden_hbm, hidden, sems.at[chunks])
-    get_hidden.start()
     for i in range(chunks):
         copy(i).start()
+    get_hidden.start()
 
     tile = 256
     some = tile // groups
@@ -220,20 +220,20 @@
                     n * some : (n + 1) * some, h * size : (h + 1) * size
                 ]
 
-    get_hidden.wait()
-    tokens_ref[...] = hidden.reshape(tokens_ref.shape)[...]
-
     @pl.loop(0, chunks)
     def _(i):
         copy(i).wait()
         for f in range(0, some_width, 2 * some):
             arrange(i * some_width + f)
 
+    get_hidden.wait()
+    tokens_ref[...] = hidden.reshape(tokens_ref.shape)[...]
+
 
 def arrange(hidden, base, own):
     rows, steps, _ = hidden.shape
     width, two, kvh, size = base.shape
-    chunks = 8
+    chunks = 4
     return pl.pallas_call(
         functools.partial(arrange_kernel, chunks, own),
         out_shape=(
@@ -298,7 +298,7 @@
 
 def finish_kernel(steps, heads, scale, group, terms, *refs):
     parts, refs = refs[:terms], refs[terms:]
-    q_ref, old_ref, log_ref, fresh_ref, context_ref, wide, bias = refs
+    q_ref, old_ref, top_ref, total_ref, fresh_hbm, context_hbm, wide, fresh_ref, context_ref, sems = refs
     rows, queries, size = q_ref.shape
     own = fresh_ref.shape[3]
     fresh = parts[0][...]
@@ -307,57 +307,77 @@
     for n in range(2 * own):
         wide[pl.ds(n, rows * steps, stride=2 * own), :] = fresh[:, n * size : (n + 1) * size]
     fresh_ref.reshape(rows * steps * 2 * own, size)[...] = wide[...].astype(jnp.bfloat16)
-    fresh = fresh.astype(jnp.bfloat16)
-    many, keys = group * queries, own * group * steps
-    query = lax.broadcasted_iota(jnp.int32, (many, keys), 0)
-    key = lax.broadcasted_iota(jnp.int32, (many, keys), 1)
-    same_head = (query % heads) // (heads // own) == key // (group * steps)
-    same_row = query // queries == (key // steps) % group
-    seen = (query % queries) // heads >= key % steps
-    bias[...] = jnp.where(same_head & same_row & seen, 0.0, LOW)
-    ones = jnp.ones((keys, size), jnp.bfloat16)
-    for at in range(0, rows, group):
-        tokens = slice(at * steps, (at + group) * steps)
-        keys_new, values_new = [
-            jnp.concatenate(
-                [fresh[tokens, (c * own + g) * size : (c * own + g + 1) * size] for g in range(own)], axis=0
+    puts = [pltpu.make_async_copy(fresh_ref, fresh_hbm, sems.at[0])]
+    puts[0].start()
+    keys, many = 2 * own * steps, 2 * queries
+    key = lax.broadcasted_iota(jnp.int32, (keys, many), 0)
+    query = lax.broadcasted_iota(jnp.int32, (keys, many), 1)
+    same_head = (query % heads) // (heads // own) == key // (2 * steps)
+    same_row = query // queries == (key // steps) % 2
+    live = same_head & same_row & ((query % queries) // heads >= key % steps)
+    nothing = jnp.zeros((keys, size), jnp.bfloat16)
+
+    def new_lines(c, pair):
+        tokens = slice(pair * 2 * steps, (pair + 1) * 2 * steps)
+        lines = [fresh[tokens, (c * own + g) * size : (c * own + g + 1) * size] for g in range(own)]
+        return jnp.concatenate(lines, axis=0).astype(jnp.bfloat16)
+
+    for at in range(0, rows // 2, group):
+        pairs = range(at, at + group)
+        scores = [
+            lax.dot_general(
+                new_lines(0, p), q_ref[2 * p : 2 * p + 2].reshape(many, size), NT, preferred_element_type=jnp.float32
             )
-            for c in range(2)
+            for p in pairs
         ]
-        values_new = jnp.concatenate([values_new, ones], axis=1)
-        mine = slice(at, at + group)
-        scores = lax.dot_general(
-            q_ref[mine].reshape(many, size), keys_new, NT, preferred_element_type=jnp.float32
+        scores = jnp.stack([jnp.where(live, s, LOW) for s in scores])
+        old_top = top_ref[at : at + group, :]
+        top = jnp.maximum(old_top, jnp.max(scores, axis=1))
+        expo = jnp.exp((scores - top[:, None, :]) * scale)
+        back = jnp.exp((old_top - top) * scale)
+        inverse = 1.0 / (back * total_ref[at : at + group, :] + jnp.sum(expo, axis=1))
+        weights = (expo * inverse[:, None, :]).astype(jnp.bfloat16).reshape(group * keys, many)
+        back = (back * inverse).T
+        values = jnp.concatenate(
+            [
+                jnp.concatenate([new_lines(1, p) if n == p else nothing for n in pairs], axis=1)
+                for p in pairs
+            ],
+            axis=0,
         )
-        scores = scores * scale + bias[...]
-        log_old = log_ref[mine].reshape(many, size)
-        top = jnp.maximum(log_old, jnp.max(scores, axis=-1, keepdims=True))
-        weights = jnp.exp(scores - top).astype(jnp.bfloat16)
-        back = jnp.exp(log_old - top)
-        both = jnp.dot(weights, values_new, preferred_element_type=jnp.float32)
-        total = back + both[:, size:]
-        summed = back * old_ref[mine].reshape(many, size) + both[:, :size]
-        context_ref[mine] = (summed / total).astype(jnp.bfloat16).reshape(group, queries, size)
+        new = lax.dot_general(weights, values, TN, preferred_element_type=jnp.float32)
+        for n, p in enumerate(pairs):
+            old = old_ref[2 * p : 2 * p + 2].reshape(many, size)
+            both = new[:, n * size : (n + 1) * size] + back[:, n : n + 1] * old
+            context_ref[2 * p : 2 * p + 2] = both.astype(jnp.bfloat16).reshape(2, queries, size)
+        mine = pl.ds(2 * at, 2 * group)
+        puts.append(pltpu.make_async_copy(context_ref.at[mine], context_hbm.at[mine], sems.at[1 + at // group]))
+        puts[-1].start()
+    for put in puts:
+        put.wait()
 
 
 def finish(parts, queries, state, steps, own):
     rows, many, size = queries.shape
     heads = many // steps
-    group = size // (own * steps)
+    group = size // (2 * own * steps)
+    fresh = (rows, steps, 2, own, size)
     fresh, context = pl.pallas_call(
         functools.partial(finish_kernel, steps, heads, size ** (-0.5), group, len(parts)),
         out_shape=(
-            jax.ShapeDtypeStruct((rows, steps, 2, own, size), jnp.bfloat16),
+            jax.ShapeDtypeStruct(fresh, jnp.bfloat16),
             jax.ShapeDtypeStruct((rows, many, size), jnp.bfloat16),
         ),
         in_specs=[VMEM] * (len(parts) + 1 + len(state)),
-        out_specs=(VMEM, VMEM),
+        out_specs=(pl.BlockSpec(memory_space=pltpu.HBM),) * 2,
         scratch_shapes=[
             pltpu.VMEM((rows * steps * 2 * own, size), jnp.float32),
-            pltpu.VMEM((group * many, own * group * steps), jnp.float32),
+            pltpu.VMEM(fresh, jnp.bfloat16),
+            pltpu.VMEM((rows, many, size), jnp.bfloat16),
+            pltpu.SemaphoreType.DMA((1 + rows // 2 // group,)),
         ],
         compiler_params=params(24),
-        cost_estimate=cost(rows * many * size * size * 6, 12 * rows * many * size, rows * many * size * 2),
+        cost_estimate=cost(rows * many * size * size * 6, 8 * rows * many * size, rows * many * size * 2),
         name="finish",
     )(*parts, queries, *state)
     return fresh, context.reshape(rows, steps, heads, size)

time: 26.4 us -> 26.5 us (level)
  waiting for transfers between devices: 0.88 us -> 1.69 us
  Pallas kernels: 17 us -> 16.3 us
    ppermute x1, waiting for transfers between devices: 0.55 us -> 1.35 us  [shards(): lax.ppermute(gathered, 'dp', [(i, i ^ 1) for i in range(dp)])]
    pallas_call x1, Pallas kernels: 4.56 us -> 3.76 us  [arrange(): pl.pallas_call(functools.partial(arrange_kernel, chunks, own), out_shape=...]
  transfers between devices with their start and end apart: 5 -> 5, of which waited for: 2 -> 2; matrix products, arithmetic and copies ran while one was open for 0% -> 0% of each run, Pallas kernels for 48% -> 45%
where the time goes in v11:
time: 26.5 us; the launch traced here: 26.2 us
  Pallas kernels  16.3 us (62%)
  starting transfers between devices  7.55 us (28%)
  waiting for transfers between devices  1.69 us (6%)
  between operations  0.71 us (3%)
    pallas_call x1, Pallas kernels, attend_cached(): pl.pallas_call(functools.partial(cached_kernel, chunks, heads, size ** (-...  6.56 us
    ppermute x3, starting transfers between devices, gather_second(): lax.ppermute(payload, 'dp', [(i, i ^ 2 * k) for i in range(dp)])  5.76 us
    pallas_call x1, Pallas kernels, arrange(): pl.pallas_call(functools.partial(arrange_kernel, chunks, own), out_shape=...  3.76 us
    pallas_call x2, Pallas kernels, project(): pl.pallas_call(functools.partial(project_kernel, k), out_shape=pltpu.VMEM...  2.75 us
    pallas_call x1, Pallas kernels, finish(): pl.pallas_call(functools.partial(finish_kernel, steps, heads, size ** (-0...  2.35 us
    ppermute x1, starting transfers between devices, shards(): lax.ppermute(gathered, 'dp', [(i, i ^ 1) for i in range(dp)])  1.73 us
    ppermute x1, waiting for transfers between devices, shards(): lax.ppermute(gathered, 'dp', [(i, i ^ 1) for i in range(dp)])  1.35 us
    pallas_call x1, Pallas kernels, make_payload(): pl.pallas_call(payload_kernel, out_shape=pltpu.VMEM((ranks, width + group...  0.81 us
  transfers between devices with their start and end apart: 5, of which 2 were waited for; matrix products, arithmetic and copies ran while one was open for 0% of the time, Pallas kernels for 45%

profile of v11, /device:TPU:0, one launch (start us, length us, event | category | flops | bytes accessed | tf_op | source)
XLA Modules:
  0.0 26.2 jit_solution(8213187709254215945)
XLA Ops:
  0.6 0.8 %payload.1.refs_0_ = bf16[8,3584]{1,0:T(8,128)(2,1)S(1)} custom-call(bf16[8,2560]{1,0:T(8,128)(2,1)} %bitcast.4, bf16[8,2,4,128]{3,2,1,0:T(4,128)(2,1)} %up_hbm.1), custom_call_target="tpu_custom_call" | custom-call | tf_op jit(solution)/shard_map/payload/pallas_call | solution.py:47
  1.5 5.1 %collective-permute-start.2 = (bf16[8,3584]{1,0:T(8,128)(2,1)S(1)}, bf16[8,3584]{1,0:T(8,128)(2,1)S(1)}, u32[]{:S(2)}, u32[]{:S(2)}) collective-permute-start(bf16[8,3584]{1,0:T(8,128)(2,1)S(1)} %payload.1.refs_0_), channel_id=1, source_target_pairs={{0,12},{2,14},{4,8},{6,10},{8,4},{10,6},{12,0},{14,2},{1,13},{3,15... | collective-permute-start | bytes 172040 | tf_op jit(solution)/shard_map/ppermute | solution.py:411
  6.6 0.0 collective-permute-start.1
  6.6 0.6 %collective-permute-start = (bf16[8,3584]{1,0:T(8,128)(2,1)S(1)}, bf16[8,3584]{1,0:T(8,128)(2,1)S(1)}, u32[]{:S(2)}, u32[]{:S(2)}) collective-permute-start(bf16[8,3584]{1,0:T(8,128)(2,1)S(1)} %payload.1.refs_0_), channel_id=1, source_target_pairs={{0,4},{2,6},{4,0},{6,2},{8,12},{10,14},{12,8},{14,10},{1,5},{3,7},... | collective-permute-start | bytes 172040 | tf_op jit(solution)/shard_map/ppermute | solution.py:411
  7.2 6.6 %attend_cached.1 = (bf16[48,64,128]{2,1,0:T(8,128)(2,1)S(1)}, f32[48,64,128]{2,1,0:T(8,128)S(1)}, f32[24,128]{1,0:T(8,128)S(1)}, f32[24,128]{1,0:T(8,128)S(1)}) custom-call(s32[48]{0:T(128)} %refs_0_.1, bf16[48,64,128]{2,1,0:T(8,128)(2,1)} %bitcast.3, bf16[48,128,2,2,128]{4,3,2,1,0:T(2,128)(2,1)} %refs_2_.1), custom_call_target="tpu_custom_call" | custom-call | flops 402653184 | bytes 8650752 | tf_op jit(solution)/shard_map/attend_cached/pallas_call | solution.py:162
  13.8 0.0 collective-permute-done.2.refs_3_
  13.8 0.0 collective-permute-done.1.refs_2_
  13.8 0.0 collective-permute-done.refs_1_
  13.8 1.7 %collective-permute-start.3 = (bf16[32,3584]{1,0:T(8,128)(2,1)S(1)}, bf16[32,3584]{1,0:T(8,128)(2,1)S(1)}, u32[]{:S(2)}, u32[]{:S(2)}) collective-permute-start(bf16[32,3584]{1,0:T(8,128)(2,1)S(1)} %join.1.refs_0_), channel_id=1, source_target_pairs={{0,2},{2,0},{4,6},{6,4},{8,10},{10,8},{12,14},{14,12},{1,3},{3,1},... | collective-permute-start | bytes 688136 | tf_op jit(solution)/shard_map/ppermute | solution.py:428
  15.6 3.8 %arrange.1 = (bf16[192,2560]{1,0:T(8,128)(2,1)S(1)}, bf16[4,2560,256]{2,1,0:T(8,128)(2,1)S(1)}) custom-call(bf16[48,4,2560]{2,1,0:T(4,128)(2,1)} %hidden_hbm, bf16[2560,2,4,128]{3,2,1,0:T(4,128)(2,1)} %base_hbm), custom_call_target="tpu_custom_call" | custom-call | flops 1342177280 | bytes 12451840 | tf_op jit(solution)/shard_map/arrange/pallas_call | solution.py:237
  19.3 1.4 %collective-permute-done.3.refs_1_ = bf16[32,3584]{1,0:T(8,128)(2,1)S(1)} collective-permute-done((bf16[32,3584]{1,0:T(8,128)(2,1)S(1)}, bf16[32,3584]{1,0:T(8,128)(2,1)S(1)}, u32[]{:S(2)}, u32[]{:S(2)}) %collective-permute-start.3) | collective-permute-done | bytes 229408 | tf_op jit(solution)/shard_map/ppermute | solution.py:428
  20.7 1.4 %project.3 = f32[192,512]{1,0:T(8,128)S(1)} custom-call(bf16[192,2560]{1,0:T(8,128)(2,1)S(1)} %get-tuple-element.26.hidden_ref, bf16[4,2560,256]{2,1,0:T(8,128)(2,1)S(1)} %get-tuple-element.27.base_ref, bf16[32,3584]{1,0:T(8,128)(2,1)S(1)} %join.1.refs_0_, bf16[32,3584]{1,0:T(8,128)(2,1)S(1)} %collective-permute-done.3.refs_1_), custom_call_target="tpu_custom_call" | custom-call | flops 671088640 | bytes 3604480 | tf_op jit(solution)/shard_map/project/pallas_call | solution.py:287
  22.1 0.1 collective-permute-start.4
  22.1 1.4 %project.2.refs_0_ = f32[192,512]{1,0:T(8,128)S(1)} custom-call(bf16[192,2560]{1,0:T(8,128)(2,1)S(1)} %get-tuple-element.26.hidden_ref, bf16[4,2560,256]{2,1,0:T(8,128)(2,1)S(1)} %get-tuple-element.27.base_ref, bf16[32,3584]{1,0:T(8,128)(2,1)S(1)} %join.1.refs_0_, bf16[32,3584]{1,0:T(8,128)(2,1)S(1)} %collective-permute-done.3.refs_1_), custom_call_target="tpu_custom_call" | custom-call | flops 671088640 | bytes 3604480 | tf_op jit(solution)/shard_map/project/pallas_call | solution.py:287
  23.5 0.3 %collective-permute-done.4.refs_1_ = f32[192,512]{1,0:T(8,128)S(1)} collective-permute-done((f32[192,512]{1,0:T(8,128)S(1)}, f32[192,512]{1,0:T(8,128)S(1)}, u32[]{:S(2)}, u32[]{:S(2)}) %collective-permute-start.4) | collective-permute-done | bytes 393248 | tf_op jit(solution)/shard_map/ppermute | solution.py:433
  23.8 2.4 %finish.1 = (bf16[48,4,2,2,128]{4,3,2,1,0:T(2,128)(2,1)}, bf16[48,64,128]{2,1,0:T(8,128)(2,1)}) custom-call(f32[192,512]{1,0:T(8,128)S(1)} %project.2.refs_0_, f32[192,512]{1,0:T(8,128)S(1)} %collective-permute-done.4.refs_1_, bf16[48,64,128]{2,1,0:T(8,128)(2,1)S(1)} %get-tuple-element.32.refs_2_, f32[48,64,128]{2,1,0:T(8,128)S(1)} %get-tuple-element.33.refs_3_, ...), custom_call_target="tpu_custom_call" | custom-call | flops 301989888 | bytes 3145728 | tf_op jit(solution)/shard_map/finish/pallas_call | solution.py:365
  (1 shorter events, 0.0 us)
Async XLA Ops:
  1.5 12.3 %collective-permute-start.2 = (bf16[8,3584]{1,0:T(8,128)(2,1)S(1)}, bf16[8,3584]{1,0:T(8,128)(2,1)S(1)}, u32[]{:S(2)}, u32[]{:S(2)}) collective-permute-start(bf16[8,3584]{1,0:T(8,128)(2,1)S(1)} %payload.1.refs_0_), channel_id=1, source_target_pairs={{0,12},{2,14},{4,8},{6,10},{8,4},{10,6},{12,0},{14,2},{1,13},{3,15... | collective-permute-start | bytes 172040 | tf_op jit(solution)/shard_map/ppermute | solution.py:411
  6.6 7.2 %collective-permute-start.1 = (bf16[8,3584]{1,0:T(8,128)(2,1)S(1)}, bf16[8,3584]{1,0:T(8,128)(2,1)S(1)}, u32[]{:S(2)}, u32[]{:S(2)}) collective-permute-start(bf16[8,3584]{1,0:T(8,128)(2,1)S(1)} %payload.1.refs_0_), channel_id=1, source_target_pairs={{0,8},{2,10},{4,12},{6,14},{8,0},{10,2},{12,4},{14,6},{1,9},{3,11}... | collective-permute-start | bytes 172040 | tf_op jit(solution)/shard_map/ppermute | solution.py:411
  6.6 7.2 %collective-permute-start = (bf16[8,3584]{1,0:T(8,128)(2,1)S(1)}, bf16[8,3584]{1,0:T(8,128)(2,1)S(1)}, u32[]{:S(2)}, u32[]{:S(2)}) collective-permute-start(bf16[8,3584]{1,0:T(8,128)(2,1)S(1)} %payload.1.refs_0_), channel_id=1, source_target_pairs={{0,4},{2,6},{4,0},{6,2},{8,12},{10,14},{12,8},{14,10},{1,5},{3,7},... | collective-permute-start | bytes 172040 | tf_op jit(solution)/shard_map/ppermute | solution.py:411
  13.8 6.8 %collective-permute-start.3 = (bf16[32,3584]{1,0:T(8,128)(2,1)S(1)}, bf16[32,3584]{1,0:T(8,128)(2,1)S(1)}, u32[]{:S(2)}, u32[]{:S(2)}) collective-permute-start(bf16[32,3584]{1,0:T(8,128)(2,1)S(1)} %join.1.refs_0_), channel_id=1, source_target_pairs={{0,2},{2,0},{4,6},{6,4},{8,10},{10,8},{12,14},{14,12},{1,3},{3,1},... | collective-permute-start | bytes 688136 | tf_op jit(solution)/shard_map/ppermute | solution.py:428
  22.1 1.8 %collective-permute-start.4 = (f32[192,512]{1,0:T(8,128)S(1)}, f32[192,512]{1,0:T(8,128)S(1)}, u32[]{:S(2)}, u32[]{:S(2)}) collective-permute-start(f32[192,512]{1,0:T(8,128)S(1)} %project.3), channel_id=1, source_target_pairs={{0,1},{1,0},{2,3},{3,2},{4,5},{5,4},{6,7},{7,6},{8,9},{9,8},{10,11... | collective-permute-start | bytes 1179656 | tf_op jit(solution)/shard_map/ppermute | solution.py:433

commit v12 on v11

--- a/solution.py
+++ b/solution.py
@@ -61,9 +61,9 @@
 
 def cached_kernel(chunks, heads, scale, *refs):
     lengths_hbm, queries_hbm, cache_hbm, q_all, sum_ref, top_ref, total_ref = refs[:7]
-    lengths_ref, k_all, v_all = refs[7:10]
-    scores_refs, weights_refs = refs[10:12], refs[12:14]
-    sems, length_sem = refs[14:]
+    lengths_ref, raw, k_all, v_all = refs[7:11]
+    scores_refs, weights_refs = refs[11:13], refs[13:15]
+    sems, length_sem = refs[15:]
     rows, queries, size = q_all.shape
     slots, own = k_all.shape[1:3]
     keys = slots * own
@@ -71,12 +71,13 @@
 
     def copies(i):
         mine = pl.ds(i * some, some)
-        pairs = (
-            (queries_hbm.at[mine], q_all.at[mine]),
-            (cache_hbm.at[mine, :, 0], k_all.at[mine]),
-            (cache_hbm.at[mine, :, 1], v_all.at[mine]),
-        )
+        pairs = ((cache_hbm.at[mine], raw.at[mine]), (queries_hbm.at[mine], q_all.at[mine]))
         return [pltpu.make_async_copy(a, b, sems.at[i, n]) for n, (a, b) in enumerate(pairs)]
+
+    def splits(i):
+        mine = pl.ds(i * some, some)
+        pairs = ((raw.at[mine, :, 0], k_all.at[mine]), (raw.at[mine, :, 1], v_all.at[mine]))
+        return [pltpu.make_async_copy(a, b, sems.at[i, 2 + n]) for n, (a, b) in enumerate(pairs)]
 
     get_lengths = pltpu.make_async_copy(lengths_hbm, lengths_ref, length_sem)
     get_lengths.start()
@@ -92,9 +93,15 @@
     flat_k = k_all.reshape(rows, keys, size)
     flat_v = v_all.reshape(rows, keys, size)
 
-    def await_chunk(i):
+    def part_chunk(i):
         for copy in copies(i):
             copy.wait()
+        for split in splits(i):
+            split.start()
+
+    def await_chunk(i):
+        for split in splits(i):
+            split.wait()
 
     def score(i, slot):
         for p in range(some // 2):
@@ -130,8 +137,11 @@
                 sum_ref[r + h] = both[h * queries : (h + 1) * queries, h * size : (h + 1) * size]
 
     get_lengths.wait()
+    part_chunk(0)
+    part_chunk(1)
     await_chunk(0)
     score(0, 0)
+    part_chunk(2)
     await_chunk(1)
     score(1, 1)
     soften(0, 0)
@@ -140,6 +150,11 @@
     def _(t):
         for slot in range(2):
             i = 2 * t + slot
+
+            @pl.when(i + 1 < chunks)
+            def _():
+                part_chunk(i + 1)
+
             await_chunk(i)
             score(i, slot)
             soften(i - 1, 1 - slot)
@@ -171,13 +186,14 @@
         out_specs=(VMEM,) * 4,
         scratch_shapes=[
             pltpu.SMEM(lengths.shape, jnp.int32),
+            pltpu.VMEM(cache.shape, jnp.bfloat16),
             pltpu.VMEM(half, jnp.bfloat16),
             pltpu.VMEM(half, jnp.bfloat16),
             pltpu.VMEM((pairs, keys, 2 * many), jnp.float32),
             pltpu.VMEM((pairs, keys, 2 * many), jnp.float32),
             pltpu.VMEM((pairs, keys, 2 * many), jnp.bfloat16),
             pltpu.VMEM((pairs, keys, 2 * many), jnp.bfloat16),
-            pltpu.SemaphoreType.DMA((chunks, 3)),
+            pltpu.SemaphoreType.DMA((chunks, 4)),
             pltpu.SemaphoreType.DMA,
         ],
         compiler_params=params(28),
@@ -383,56 +399,60 @@
     return fresh, context.reshape(rows, steps, heads, size)
 
 
-def join_kernel(*refs):
-    blocks, out_ref = refs[:-1], refs[-1]
-    at = 0
-    for block in blocks:
-        out_ref[at : at + block.shape[0], :] = block[...]
-        at += block.shape[0]
-
-
-def join(blocks):
-    rows = sum(b.shape[0] for b in blocks)
+def join_kernel(counts, *refs):
+    blocks, outs = refs[: sum(counts)], refs[sum(counts) :]
+    first = 0
+    for count, out_ref in zip(counts, outs):
+        at = 0
+        for block in blocks[first : first + count]:
+            out_ref[at : at + block.shape[0], :] = block[...]
+            at += block.shape[0]
+        first += count
+
+
+def join(*lists):
+    blocks = [block for blocks in lists for block in blocks]
+    rows = [sum(b.shape[0] for b in blocks) for blocks in lists]
     return pl.pallas_call(
-        join_kernel,
-        out_shape=pltpu.VMEM((rows, blocks[0].shape[1]), jnp.bfloat16),
+        functools.partial(join_kernel, [len(blocks) for blocks in lists]),
+        out_shape=[pltpu.VMEM((n, blocks[0].shape[1]), jnp.bfloat16) for n in rows],
         in_specs=[VMEM] * len(blocks),
-        out_specs=VMEM,
+        out_specs=[VMEM] * len(lists),
         compiler_params=params(8),
         name="join",
     )(*blocks)
 
 
-def gather_second(factor_a, factor_b, dp):
-    count = dp // 2
-    ranks = factor_b.shape[0]
-    if ranks % 8 == 0 and count in (1, 2, 4):
-        payload = make_payload(factor_a.T, factor_b)
-        return [payload] + [lax.ppermute(payload, "dp", [(i, i ^ (2 * k)) for i in range(dp)]) for k in range(1, count)]
-    payload = jnp.concatenate([factor_a.T, factor_b.reshape(ranks, -1)], axis=1)
-    groups = [[i for i in range(dp) if i % 2 == n] for n in range(2)]
-    copies = jnp.broadcast_to(payload[None], (count,) + payload.shape)
-    blocks = lax.all_to_all(copies, "dp", 0, 0, axis_index_groups=groups, tiled=True)
-    return [blocks.reshape(count * ranks, payload.shape[1])]
-
-
 def shards(dp, tp, hidden, base_weight, factor_a, factor_b, queries, cache, lengths):
     steps, own = queries.shape[1], cache.shape[3]
-    assert dp % 2 == 0
-    blocks = gather_second(factor_a, factor_b, dp)
-    queries, *state = attend_cached(queries, cache, lengths)
-    blocks, state, queries, hidden, base_weight = lax.optimization_barrier(
-        (blocks, state, queries, hidden, base_weight)
-    )
-    gathered = join(blocks) if len(blocks) > 1 else blocks[0]
-    gathered = [gathered, lax.ppermute(gathered, "dp", [(i, i ^ 1) for i in range(dp)])]
+    ranks = factor_b.shape[0]
+
+    def swap(x, k):
+        return lax.ppermute(x, "dp", [(i, i ^ k) for i in range(dp)])
+
+    def local(operands):
+        done, *state = attend_cached(queries, cache, lengths)
+        return lax.optimization_barrier((operands, done, state, hidden, base_weight))
+
+    if dp == 8 and ranks % 8 == 0:
+        payload = make_payload(factor_a.T, factor_b)
+        blocks = {k: swap(payload, k) for k in (6, 4, 2, 3, 1)}
+        blocks, rotated, state, hidden, base_weight = local(blocks)
+        rest, gathered = join([blocks[4], blocks[6]], [payload] + [blocks[k] for k in (1, 2, 3, 4, 6)])
+        gathered = [gathered, swap(rest, 1)]
+    else:
+        payload = jnp.concatenate([factor_a.T, factor_b.reshape(ranks, -1)], axis=1)
+        copies = jnp.broadcast_to(payload[None], (dp,) + payload.shape)
+        blocks = lax.all_to_all(copies, "dp", 0, 0, tiled=True)
+        gathered = [blocks.reshape(dp * ranks, payload.shape[1])]
+        gathered, rotated, state, hidden, base_weight = local(gathered)
     tokens, base = arrange(hidden, base_weight, own)
     received = []
     for k in range(1, tp):
         other = project(k, tokens, base, gathered)
         received.append(lax.ppermute(other, "tp", [(i, i ^ k) for i in range(tp)]))
     mine = project(0, tokens, base, gathered)
-    return finish([mine] + received, queries, state, steps, own)
+    return finish([mine] + received, rotated, state, steps, own)
 
 
 def solution(mesh):

time: 26.5 us -> 32.2 us (1.22)
  Pallas kernels: 16.3 us -> 20.6 us
  starting transfers between devices: 7.55 us -> 10.3 us
  waiting for transfers between devices: 1.69 us -> 0.34 us
    pallas_call x1, Pallas kernels: 6.56 us -> 10.9 us  [attend_cached(): pl.pallas_call(functools.partial(cached_kernel, chunks, heads, size ** (-...]
    ppermute x4 -> x6, starting transfers between devices: 7.48 us -> 10.2 us  [swap(): return lax.ppermute(x, 'dp', [(i, i ^ k) for i in range(dp)])]
    ppermute x4 -> x6, waiting for transfers between devices: 1.36 us -> 0.02 us  [swap(): return lax.ppermute(x, 'dp', [(i, i ^ k) for i in range(dp)])]
  transfers between devices with their start and end apart: 5 -> 7, of which waited for: 2 -> 1; matrix products, arithmetic and copies ran while one was open for 0% -> 0% of each run, Pallas kernels for 45% -> 50%
where the time goes in v12:
time: 32.2 us; the launch traced here: 32 us
  Pallas kernels  20.6 us (64%)
  starting transfers between devices  10.3 us (32%)
  between operations  0.74 us (2%)
  waiting for transfers between devices  0.34 us (1%)
    pallas_call x1, Pallas kernels, attend_cached(): pl.pallas_call(functools.partial(cached_kernel, chunks, heads, size ** (-...  10.9 us
    ppermute x6, starting transfers between devices, swap(): return lax.ppermute(x, 'dp', [(i, i ^ k) for i in range(dp)])  10.2 us
    pallas_call x1, Pallas kernels, arrange(): pl.pallas_call(functools.partial(arrange_kernel, chunks, own), out_shape=...  3.76 us
    pallas_call x2, Pallas kernels, project(): pl.pallas_call(functools.partial(project_kernel, k), out_shape=pltpu.VMEM...  2.75 us
    pallas_call x1, Pallas kernels, finish(): pl.pallas_call(functools.partial(finish_kernel, steps, heads, size ** (-0...  2.35 us
    pallas_call x1, Pallas kernels, make_payload(): pl.pallas_call(payload_kernel, out_shape=pltpu.VMEM((ranks, width + group...  0.81 us
  transfers between devices with their start and end apart: 7, of which 1 were waited for; matrix products, arithmetic and copies ran while one was open for 0% of the time, Pallas kernels for 50%

profile of v12, /device:TPU:0, one launch (start us, length us, event | category | flops | bytes accessed | tf_op | source)
XLA Modules:
  0.0 32.0 jit_solution(5852858639680883305)
XLA Ops:
  0.6 0.8 %payload.1.refs_2_ = bf16[8,3584]{1,0:T(8,128)(2,1)S(1)} custom-call(bf16[8,2560]{1,0:T(8,128)(2,1)} %bitcast.4, bf16[8,2,4,128]{3,2,1,0:T(4,128)(2,1)} %up_hbm.1), custom_call_target="tpu_custom_call" | custom-call | tf_op jit(solution)/shard_map/payload/pallas_call | solution.py:47
  1.5 5.1 %collective-permute-start.4 = (bf16[8,3584]{1,0:T(8,128)(2,1)S(1)}, bf16[8,3584]{1,0:T(8,128)(2,1)S(1)}, u32[]{:S(2)}, u32[]{:S(2)}) collective-permute-start(bf16[8,3584]{1,0:T(8,128)(2,1)S(1)} %payload.1.refs_2_), channel_id=1, source_target_pairs={{0,12},{2,14},{4,8},{6,10},{8,4},{10,6},{12,0},{14,2},{1,13},{3,15... | collective-permute-start | bytes 172040 | tf_op jit(solution)/shard_map/ppermute | solution.py:431
  6.6 0.0 collective-permute-start.3
  6.6 1.7 %collective-permute-start.2 = (bf16[8,3584]{1,0:T(8,128)(2,1)S(1)}, bf16[8,3584]{1,0:T(8,128)(2,1)S(1)}, u32[]{:S(2)}, u32[]{:S(2)}) collective-permute-start(bf16[8,3584]{1,0:T(8,128)(2,1)S(1)} %payload.1.refs_2_), channel_id=1, source_target_pairs={{0,6},{2,4},{4,2},{6,0},{8,14},{10,12},{12,10},{14,8},{1,7},{3,5},... | collective-permute-start | bytes 172040 | tf_op jit(solution)/shard_map/ppermute | solution.py:431
  8.3 1.2 %collective-permute-start.1 = (bf16[8,3584]{1,0:T(8,128)(2,1)S(1)}, bf16[8,3584]{1,0:T(8,128)(2,1)S(1)}, u32[]{:S(2)}, u32[]{:S(2)}) collective-permute-start(bf16[8,3584]{1,0:T(8,128)(2,1)S(1)} %payload.1.refs_2_), channel_id=1, source_target_pairs={{0,4},{2,6},{4,0},{6,2},{8,12},{10,14},{12,8},{14,10},{1,5},{3,7},... | collective-permute-start | bytes 172040 | tf_op jit(solution)/shard_map/ppermute | solution.py:431
  9.6 0.5 %collective-permute-start = (bf16[8,3584]{1,0:T(8,128)(2,1)S(1)}, bf16[8,3584]{1,0:T(8,128)(2,1)S(1)}, u32[]{:S(2)}, u32[]{:S(2)}) collective-permute-start(bf16[8,3584]{1,0:T(8,128)(2,1)S(1)} %payload.1.refs_2_), channel_id=1, source_target_pairs={{0,2},{2,0},{4,6},{6,4},{8,10},{10,8},{12,14},{14,12},{1,3},{3,1},... | collective-permute-start | bytes 172040 | tf_op jit(solution)/shard_map/ppermute | solution.py:431
  10.1 10.9 %attend_cached.1 = (bf16[48,64,128]{2,1,0:T(8,128)(2,1)S(1)}, f32[48,64,128]{2,1,0:T(8,128)S(1)}, f32[24,128]{1,0:T(8,128)S(1)}, f32[24,128]{1,0:T(8,128)S(1)}) custom-call(s32[48]{0:T(128)} %refs_0_.1, bf16[48,64,128]{2,1,0:T(8,128)(2,1)} %bitcast.3, bf16[48,128,2,2,128]{4,3,2,1,0:T(2,128)(2,1)} %refs_2_.1), custom_call_target="tpu_custom_call" | custom-call | flops 402653184 | bytes 8650752 | tf_op jit(solution)/shard_map/attend_cached/pallas_call | solution.py:177
  21.0 0.0 collective-permute-done.4.refs_1_.refs_7_
  21.0 0.0 collective-permute-done.3.refs_0_.refs_6_
  21.0 0.0 collective-permute-done.2.refs_5_
  21.0 0.0 collective-permute-done.1.refs_4_
  21.0 0.0 collective-permute-done.refs_3_
  21.1 1.6 %collective-permute-start.5 = (bf16[16,3584]{1,0:T(8,128)(2,1)S(1)}, bf16[16,3584]{1,0:T(8,128)(2,1)S(1)}, u32[]{:S(2)}, u32[]{:S(2)}) collective-permute-start(bf16[16,3584]{1,0:T(8,128)(2,1)S(1)} %get-tuple-element.37), channel_id=1, source_target_pairs={{0,2},{2,0},{4,6},{6,4},{8,10},{10,8},{12,14},{14,12},{1,3},{3,1},... | collective-permute-start | bytes 344072 | tf_op jit(solution)/shard_map/ppermute | solution.py:431
  22.7 3.8 %arrange.1 = (bf16[192,2560]{1,0:T(8,128)(2,1)S(1)}, bf16[4,2560,256]{2,1,0:T(8,128)(2,1)S(1)}) custom-call(bf16[48,4,2560]{2,1,0:T(4,128)(2,1)} %hidden_hbm, bf16[2560,2,4,128]{3,2,1,0:T(4,128)(2,1)} %base_hbm), custom_call_target="tpu_custom_call" | custom-call | flops 1342177280 | bytes 12451840 | tf_op jit(solution)/shard_map/arrange/pallas_call | solution.py:253
  26.4 0.0 collective-permute-done.5.refs_1_
  26.5 1.4 %project.3 = f32[192,512]{1,0:T(8,128)S(1)} custom-call(bf16[192,2560]{1,0:T(8,128)(2,1)S(1)} %get-tuple-element.29.hidden_ref, bf16[4,2560,256]{2,1,0:T(8,128)(2,1)S(1)} %get-tuple-element.30.base_ref, bf16[48,3584]{1,0:T(8,128)(2,1)S(1)} %get-tuple-element.36.refs_0_, bf16[16,3584]{1,0:T(8,128)(2,1)S(1)} %collective-permute-done.5.refs_1_), custom_call_target="tpu_custom_call" | custom-call | flops 671088640 | bytes 3604480 | tf_op jit(solution)/shard_map/project/pallas_call | solution.py:303
  27.8 0.1 collective-permute-start.6
  27.9 1.4 %project.2.refs_0_ = f32[192,512]{1,0:T(8,128)S(1)} custom-call(bf16[192,2560]{1,0:T(8,128)(2,1)S(1)} %get-tuple-element.29.hidden_ref, bf16[4,2560,256]{2,1,0:T(8,128)(2,1)S(1)} %get-tuple-element.30.base_ref, bf16[48,3584]{1,0:T(8,128)(2,1)S(1)} %get-tuple-element.36.refs_0_, bf16[16,3584]{1,0:T(8,128)(2,1)S(1)} %collective-permute-done.5.refs_1_), custom_call_target="tpu_custom_call" | custom-call | flops 671088640 | bytes 3604480 | tf_op jit(solution)/shard_map/project/pallas_call | solution.py:303
  29.3 0.3 %collective-permute-done.6.refs_1_ = f32[192,512]{1,0:T(8,128)S(1)} collective-permute-done((f32[192,512]{1,0:T(8,128)S(1)}, f32[192,512]{1,0:T(8,128)S(1)}, u32[]{:S(2)}, u32[]{:S(2)}) %collective-permute-start.6) | collective-permute-done | bytes 393248 | tf_op jit(solution)/shard_map/ppermute | solution.py:453
  29.6 2.4 %finish.1 = (bf16[48,4,2,2,128]{4,3,2,1,0:T(2,128)(2,1)}, bf16[48,64,128]{2,1,0:T(8,128)(2,1)}) custom-call(f32[192,512]{1,0:T(8,128)S(1)} %project.2.refs_0_, f32[192,512]{1,0:T(8,128)S(1)} %collective-permute-done.6.refs_1_, bf16[48,64,128]{2,1,0:T(8,128)(2,1)S(1)} %get-tuple-element.38.refs_2_, f32[48,64,128]{2,1,0:T(8,128)S(1)} %get-tuple-element.39.refs_3_, ...), custom_call_target="tpu_custom_call" | custom-call | flops 301989888 | bytes 3145728 | tf_op jit(solution)/shard_map/finish/pallas_call | solution.py:381
  (1 shorter events, 0.0 us)
Async XLA Ops:
  1.5 19.5 %collective-permute-start.4 = (bf16[8,3584]{1,0:T(8,128)(2,1)S(1)}, bf16[8,3584]{1,0:T(8,128)(2,1)S(1)}, u32[]{:S(2)}, u32[]{:S(2)}) collective-permute-start(bf16[8,3584]{1,0:T(8,128)(2,1)S(1)} %payload.1.refs_2_), channel_id=1, source_target_pairs={{0,12},{2,14},{4,8},{6,10},{8,4},{10,6},{12,0},{14,2},{1,13},{3,15... | collective-permute-start | bytes 172040 | tf_op jit(solution)/shard_map/ppermute | solution.py:431
  6.6 14.4 %collective-permute-start.3 = (bf16[8,3584]{1,0:T(8,128)(2,1)S(1)}, bf16[8,3584]{1,0:T(8,128)(2,1)S(1)}, u32[]{:S(2)}, u32[]{:S(2)}) collective-permute-start(bf16[8,3584]{1,0:T(8,128)(2,1)S(1)} %payload.1.refs_2_), channel_id=1, source_target_pairs={{0,8},{2,10},{4,12},{6,14},{8,0},{10,2},{12,4},{14,6},{1,9},{3,11}... | collective-permute-start | bytes 172040 | tf_op jit(solution)/shard_map/ppermute | solution.py:431
  6.6 14.4 %collective-permute-start.2 = (bf16[8,3584]{1,0:T(8,128)(2,1)S(1)}, bf16[8,3584]{1,0:T(8,128)(2,1)S(1)}, u32[]{:S(2)}, u32[]{:S(2)}) collective-permute-start(bf16[8,3584]{1,0:T(8,128)(2,1)S(1)} %payload.1.refs_2_), channel_id=1, source_target_pairs={{0,6},{2,4},{4,2},{6,0},{8,14},{10,12},{12,10},{14,8},{1,7},{3,5},... | collective-permute-start | bytes 172040 | tf_op jit(solution)/shard_map/ppermute | solution.py:431
  8.3 12.7 %collective-permute-start.1 = (bf16[8,3584]{1,0:T(8,128)(2,1)S(1)}, bf16[8,3584]{1,0:T(8,128)(2,1)S(1)}, u32[]{:S(2)}, u32[]{:S(2)}) collective-permute-start(bf16[8,3584]{1,0:T(8,128)(2,1)S(1)} %payload.1.refs_2_), channel_id=1, source_target_pairs={{0,4},{2,6},{4,0},{6,2},{8,12},{10,14},{12,8},{14,10},{1,5},{3,7},... | collective-permute-start | bytes 172040 | tf_op jit(solution)/shard_map/ppermute | solution.py:431
  9.6 11.5 %collective-permute-start = (bf16[8,3584]{1,0:T(8,128)(2,1)S(1)}, bf16[8,3584]{1,0:T(8,128)(2,1)S(1)}, u32[]{:S(2)}, u32[]{:S(2)}) collective-permute-start(bf16[8,3584]{1,0:T(8,128)(2,1)S(1)} %payload.1.refs_2_), channel_id=1, source_target_pairs={{0,2},{2,0},{4,6},{6,4},{8,10},{10,8},{12,14},{14,12},{1,3},{3,1},... | collective-permute-start | bytes 172040 | tf_op jit(solution)/shard_map/ppermute | solution.py:431
  21.1 5.4 %collective-permute-start.5 = (bf16[16,3584]{1,0:T(8,128)(2,1)S(1)}, bf16[16,3584]{1,0:T(8,128)(2,1)S(1)}, u32[]{:S(2)}, u32[]{:S(2)}) collective-permute-start(bf16[16,3584]{1,0:T(8,128)(2,1)S(1)} %get-tuple-element.37), channel_id=1, source_target_pairs={{0,2},{2,0},{4,6},{6,4},{8,10},{10,8},{12,14},{14,12},{1,3},{3,1},... | collective-permute-start | bytes 344072 | tf_op jit(solution)/shard_map/ppermute | solution.py:431
  27.8 1.8 %collective-permute-start.6 = (f32[192,512]{1,0:T(8,128)S(1)}, f32[192,512]{1,0:T(8,128)S(1)}, u32[]{:S(2)}, u32[]{:S(2)}) collective-permute-start(f32[192,512]{1,0:T(8,128)S(1)} %project.3), channel_id=1, source_target_pairs={{0,1},{1,0},{2,3},{3,2},{4,5},{5,4},{6,7},{7,6},{8,9},{9,8},{10,11... | collective-permute-start | bytes 1179656 | tf_op jit(solution)/shard_map/ppermute | solution.py:453

commit v13 on v11

v13 whole, which is shorter than its diff:
```python
import functools

import jax
import jax.numpy as jnp
from jax import lax
from jax.experimental import pallas as pl
from jax.experimental.pallas import tpu as pltpu
from jax.sharding import PartitionSpec as P

LOW = -1e30
NT = (((1,), (1,)), ((), ()))
TN = (((0,), (0,)), ((), ()))
VMEM = pl.BlockSpec(memory_space=pltpu.VMEM)


def params(mib):
    return pltpu.CompilerParams(vmem_limit_bytes=mib * 1024 * 1024)


def in_hbm(x):
    return pltpu.with_memory_space_constraint(x, pltpu.HBM)


def cost(flops, moved, exps=0):
    return pl.CostEstimate(flops=flops, bytes_accessed=moved, transcendentals=exps)


def payload_kernel(down_hbm, up_hbm, out_ref, ups, wide, sems):
    ranks, width = down_hbm.shape
    groups, size = ups.shape[1] * ups.shape[2], ups.shape[3]
    get_down = pltpu.make_async_copy(down_hbm, out_ref.at[:, pl.ds(0, width)], sems.at[0])
    get_up = pltpu.make_async_copy(up_hbm, ups, sems.at[1])
    get_up.start()
    get_down.start()
    get_up.wait()
    wide[...] = ups.reshape(ranks * groups, size)[...].astype(jnp.float32)
    for n in range(groups):
        out_ref[:, width + n * size : width + (n + 1) * size] = wide[pl.ds(n, ranks, stride=groups), :].astype(
            jnp.bfloat16
        )
    get_down.wait()


def make_payload(down, up):
    ranks, width = down.shape
    groups, size = up.shape[1] * up.shape[2], up.shape[3]
    return pl.pallas_call(
        payload_kernel,
        out_shape=pltpu.VMEM((ranks, width + groups * size), jnp.bfloat16),
        in_specs=[pl.BlockSpec(memory_space=pltpu.HBM)] * 2,
        out_specs=VMEM,
        scratch_shapes=[
            pltpu.VMEM(up.shape, jnp.bfloat16),
            pltpu.VMEM((ranks * groups, size), jnp.float32),
            pltpu.SemaphoreType.DMA((2,)),
        ],
        compiler_params=params(8),
        name="payload",
    )(in_hbm(down), in_hbm(up))


class Cached:
    def __init__(self, first, chunk, heads, scale, inputs, outputs, scratch):
        self.first, self.chunk, self.heads, self.scale = first, chunk, heads, scale
        self.lengths_hbm, self.queries_hbm, self.cache_hbm = inputs
        self.q, self.sums, self.tops, self.totals = outputs
        self.lengths, self.k, self.v, *rest = scratch
        self.scores, self.weights = rest[0:2], rest[2:4]
        self.sems, self.length_sem = rest[4:]
        self.rows, self.queries, self.size = self.q.shape
        self.slots, self.own = self.k.shape[1:3]
        self.keys = self.slots * self.own
        own, queries = self.own, self.queries
        line = lax.broadcasted_iota(jnp.int32, (self.keys, 2 * queries), 0)
        query = lax.broadcasted_iota(jnp.int32, (self.keys, 2 * queries), 1)
        self.line = jnp.where(line % own == (query % heads) // (heads // own), line, self.keys)
        self.one = lax.broadcasted_iota(jnp.int32, (1, 2 * queries), 1) < queries
        self.nothing = jnp.zeros((queries, self.size), jnp.bfloat16)

    @staticmethod
    def outputs(rows, many, size):
        return (
            pltpu.VMEM((rows, many, size), jnp.bfloat16),
            pltpu.VMEM((rows, many, size), jnp.float32),
            pltpu.VMEM((rows // 2, 2 * many), jnp.float32),
            pltpu.VMEM((rows // 2, 2 * many), jnp.float32),
        )

    @staticmethod
    def scratch(rows, chunk, many, cache, lengths):
        slots, own, size = cache.shape[1], cache.shape[3], cache.shape[4]
        half = (rows, slots, own, size)
        scores = (chunk // 2, slots * own, 2 * many)
        return [
            pltpu.SMEM(lengths.shape, jnp.int32),
            pltpu.VMEM(half, jnp.bfloat16),
            pltpu.VMEM(half, jnp.bfloat16),
            pltpu.VMEM(scores, jnp.float32),
            pltpu.VMEM(scores, jnp.float32),
            pltpu.VMEM(scores, jnp.bfloat16),
            pltpu.VMEM(scores, jnp.bfloat16),
            pltpu.SemaphoreType.DMA((rows // chunk, 3)),
            pltpu.SemaphoreType.DMA,
        ]

    def copies(self, i):
        mine, theirs = pl.ds(i * self.chunk, self.chunk), pl.ds(self.first + i * self.chunk, self.chunk)
        pairs = (
            (self.queries_hbm.at[theirs], self.q.at[mine]),
            (self.cache_hbm.at[theirs, :, 0], self.k.at[mine]),
            (self.cache_hbm.at[theirs, :, 1], self.v.at[mine]),
        )
        return [pltpu.make_async_copy(a, b, self.sems.at[i, n]) for n, (a, b) in enumerate(pairs)]

    def lengths_copy(self):
        return pltpu.make_async_copy(self.lengths_hbm, self.lengths, self.length_sem)

    def start(self, i):
        for copy in self.copies(i):
            copy.start()

    def arrive(self, i):
        for copy in self.copies(i):
            copy.wait()

    def lines(self, ref, r):
        flat = ref.reshape(self.rows, self.keys, self.size)
        return jnp.concatenate([flat[r], flat[r + 1]], axis=1)

    def score(self, i, slot):
        for p in range(self.chunk // 2):
            r = i * self.chunk + 2 * p
            both_q = jnp.concatenate(
                [
                    jnp.concatenate([self.q[r], self.nothing], axis=1),
                    jnp.concatenate([self.nothing, self.q[r + 1]], axis=1),
                ],
                axis=0,
            )
            self.scores[slot][p] = lax.dot_general(
                self.lines(self.k, r), both_q, NT, preferred_element_type=jnp.float32
            )

    def soften(self, i, slot):
        for p in range(self.chunk // 2):
            r = self.first + i * self.chunk + 2 * p
            limit = jnp.where(self.one, self.own * self.lengths[r], self.own * self.lengths[r + 1])
            scores = jnp.where(self.line < limit, self.scores[slot][p], LOW)
            top = jnp.max(scores, axis=0, keepdims=True)
            expo = jnp.exp((scores - top) * self.scale)
            self.weights[slot][p] = expo.astype(jnp.bfloat16)
            pair = pl.ds(i * (self.chunk // 2) + p, 1)
            self.tops[pair, :] = top
            self.totals[pair, :] = jnp.sum(expo, axis=0, keepdims=True)

    def collect(self, i, slot):
        queries, size = self.queries, self.size
        for p in range(self.chunk // 2):
            r = i * self.chunk + 2 * p
            both = lax.dot_general(
                self.weights[slot][p], self.lines(self.v, r), TN, preferred_element_type=jnp.float32
            )
            for h in range(2):
                self.sums[r + h] = both[h * queries : (h + 1) * queries, h * size : (h + 1) * size]


def cached_kernel(chunk, heads, scale, *refs):
    cached = Cached(0, chunk, heads, scale, refs[:3], refs[3:7], refs[7:])
    chunks = cached.rows // chunk
    cached.lengths_copy().start()
    for i in range(chunks):
        cached.start(i)
    cached.lengths_copy().wait()
    cached.arrive(0)
    cached.score(0, 0)
    cached.arrive(1)
    cached.score(1, 1)
    cached.soften(0, 0)

    @pl.loop(1, chunks // 2)
    def _(t):
        for slot in range(2):
            i = 2 * t + slot
            cached.arrive(i)
            cached.score(i, slot)
            cached.soften(i - 1, 1 - slot)
            cached.collect(i - 2, slot)

    cached.soften(chunks - 1, 1)
    cached.collect(chunks - 2, 0)
    cached.collect(chunks - 1, 1)


def attend_cached(queries, cache, lengths, rows):
    _, steps, heads, size = queries.shape
    slots, own = cache.shape[1], cache.shape[3]
    many = steps * heads
    chunk = 4
    return pl.pallas_call(
        functools.partial(cached_kernel, chunk, heads, size ** (-0.5)),
        out_shape=Cached.outputs(rows, many, size),
        in_specs=[pl.BlockSpec(memory_space=pltpu.HBM)] * 3,
        out_specs=(VMEM,) * 4,
        scratch_shapes=Cached.scratch(rows, chunk, many, cache, lengths),
        compiler_params=params(28),
        cost_estimate=cost(
            8 * rows * many * slots * size, 4 * rows * slots * own * size, rows * many * slots * own
        ),
        name="attend_cached",
    )(*map(in_hbm, (lengths, queries.reshape(-1, many, size), cache)))


def arrange_kernel(first, chunk, chunks, own, heads, scale, *refs):
    hidden_hbm, base_hbm = refs[:2]
    tokens_ref, base_ref = refs[5:7]
    hidden, base, sems = refs[11:14]
    cached = Cached(first, chunk, heads, scale, refs[2:5], refs[7:11], refs[14:])
    width, two, kvh, size = base.shape
    groups = two * kvh
    some_width = width // chunks

    def copy(i):
        features = pl.ds(i * some_width, some_width)
        return pltpu.make_async_copy(base_hbm.at[features], base.at[features], sems.at[i])

    get_hidden = pltpu.make_async_copy(hidden_hbm, hidden, sems.at[chunks])
    cached.lengths_copy().start()
    copy(0).start()
    cached.start(0)
    copy(1).start()
    cached.start(1)
    for i in range(2, chunks):
        copy(i).start()
    get_hidden.start()

    tile = 256
    some = tile // groups
    row = lax.broadcasted_iota(jnp.int32, (tile, tile), 0)
    place = lax.broadcasted_iota(jnp.int32, (tile, tile), 1)
    order = (place == (row % some) * groups + row // some).astype(jnp.float32).astype(jnp.bfloat16)
    flat_base = base.reshape(width * groups, size)

    def arrange(f):
        at = f * groups
        pair = jnp.concatenate([flat_base[at + h * tile : at + (h + 1) * tile, :] for h in range(2)], axis=1)
        moved = jnp.dot(order, pair, preferred_element_type=jnp.float32).astype(jnp.bfloat16)
        for n in range(groups):
            lanes = slice((n % own) * size, (n % own + 1) * size)
            for h in range(2):
                base_ref[n // own, f + h * some : f + (h + 1) * some, lanes] = moved[
                    n * some : (n + 1) * some, h * size : (h + 1) * size
                ]

    cached.lengths_copy().wait()
    for i in range(chunks):
        copy(i).wait()
        if i < 2:
            cached.arrive(i)
            cached.score(i, i)
        if 1 <= i < 3:
            cached.soften(i - 1, i - 1)
        if 2 <= i < 4:
            cached.collect(i - 2, i - 2)
        for f in range(i * some_width, (i + 1) * some_width, 2 * some):
            arrange(f)
    get_hidden.wait()
    tokens_ref[...] = hidden.reshape(tokens_ref.shape)[...]


def arrange(hidden, base, queries, cache, lengths, rows):
    _, steps, heads, size = queries.shape
    slots, own = cache.shape[1], cache.shape[3]
    many = steps * heads
    width, two, kvh, size = base.shape
    chunks = 4
    rest = hidden.shape[0] - rows
    chunk = rest // 2
    outs = (
        pltpu.VMEM((hidden.shape[0] * steps, width), jnp.bfloat16),
        pltpu.VMEM((two * kvh // own, width, own * size), jnp.bfloat16),
    ) + Cached.outputs(rest, many, size)
    tokens, base, *state = pl.pallas_call(
        functools.partial(arrange_kernel, rows, chunk, chunks, own, heads, size ** (-0.5)),
        out_shape=outs,
        in_specs=[pl.BlockSpec(memory_space=pltpu.HBM)] * 5,
        out_specs=(VMEM,) * len(outs),
        scratch_shapes=[
            pltpu.VMEM(hidden.shape, jnp.bfloat16),
            pltpu.VMEM(base.shape, jnp.bfloat16),
            pltpu.SemaphoreType.DMA((chunks + 1,)),
        ]
        + Cached.scratch(rest, chunk, many, cache, lengths),
        compiler_params=params(28),
        cost_estimate=cost(
            512 * base.size + 8 * rest * many * slots * size,
            4 * (base.size + hidden.size + rest * slots * own * size),
            rest * many * slots * own,
        ),
        name="arrange",
    )(*map(in_hbm, (hidden, base, lengths, queries.reshape(-1, many, size), cache)))
    return tokens, base, state


def project_kernel(k, hidden_ref, base_ref, *refs):
    gathered, (out_ref, merged) = refs[:-2], refs[-2:]
    width, columns = merged.shape
    part = lax.axis_index("tp") ^ k
    parts = base_ref.shape[0] // 2
    half = columns // 2
    up = jnp.concatenate(
        [
            jnp.concatenate(
                [ref[:, pl.ds(pl.multiple_of(width + (c * parts + part) * half, 128), half)] for ref in gathered], axis=0
            )
            for c in range(2)
        ],
        axis=1,
    )
    step = 512
    for f in range(0, width, step):
        down = jnp.concatenate([ref[:, f : f + step] for ref in gathered], axis=0).T
        low_rank = jnp.dot(down, up, preferred_element_type=jnp.float32)
        for c in range(2):
            base = base_ref[c * parts + part, f : f + step, :].astype(jnp.float32)
            merged[f : f + step, c * half : (c + 1) * half] = (base + low_rank[:, c * half : (c + 1) * half]).astype(
                jnp.bfloat16
            )
    out_ref[...] = jnp.dot(hidden_ref[...], merged[...], preferred_element_type=jnp.float32)


def project(k, hidden, base, gathered):
    tokens, width = hidden.shape
    columns = 2 * base.shape[2]
    ranks = sum(g.shape[0] for g in gathered)
    return pl.pallas_call(
        functools.partial(project_kernel, k),
        out_shape=pltpu.VMEM((tokens, columns), jnp.float32),
        in_specs=[VMEM] * (2 + len(gathered)),
        out_specs=VMEM,
        scratch_shapes=[pltpu.VMEM((width, columns), jnp.bfloat16)],
        compiler_params=params(24),
        cost_estimate=cost(2 * width * columns * (tokens + ranks), 2 * width * columns + 2 * width * tokens),
        name="project",
    )(hidden, base, *gathered)


def finish_kernel(steps, heads, scale, terms, *refs):
    parts, refs = refs[:terms], refs[terms:]
    states, refs = (refs[:4], refs[4:8]), refs[8:]
    fresh_hbm, context_hbm, wide, fresh_ref, context_ref, sems = refs
    rows, queries, size = context_ref.shape
    own = fresh_ref.shape[3]
    fresh = parts[0][...]
    for part in parts[1:]:
        fresh = fresh + part[...]
    keys, many = 2 * own * steps, 2 * queries
    group = size // keys
    key = lax.broadcasted_iota(jnp.int32, (keys, many), 0)
    query = lax.broadcasted_iota(jnp.int32, (keys, many), 1)
    same_head = (query % heads) // (heads // own) == key // (2 * steps)
    same_row = query // queries == (key // steps) % 2
    live = same_head & same_row & ((query % queries) // heads >= key % steps)
    nothing = jnp.zeros((keys, size), jnp.bfloat16)

    def new_lines(c, pair):
        tokens = slice(pair * 2 * steps, (pair + 1) * 2 * steps)
        lines = [fresh[tokens, (c * own + g) * size : (c * own + g + 1) * size] for g in range(own)]
        return jnp.concatenate(lines, axis=0).astype(jnp.bfloat16)

    def old(n, pair):
        count = states[0][0].shape[0] // 2
        return (states[0][n], pair) if pair < count else (states[1][n], pair - count)

    def rows_of(n, pair):
        ref, at = old(n, pair)
        return ref[2 * at : 2 * at + 2].reshape(many, size)

    scores = [
        lax.dot_general(new_lines(0, p), rows_of(0, p), NT, preferred_element_type=jnp.float32)
        for p in range(rows // 2)
    ]
    scores = jnp.stack([jnp.where(live, s, LOW) for s in scores])
    old_top, old_total = [jnp.concatenate([states[0][n][...], states[1][n][...]], axis=0) for n in (2, 3)]
    top = jnp.maximum(old_top, jnp.max(scores, axis=1))
    expo = jnp.exp((scores - top[:, None, :]) * scale)
    back = jnp.exp((old_top - top) * scale)
    inverse = 1.0 / (back * old_total + jnp.sum(expo, axis=1))
    weights = (expo * inverse[:, None, :]).astype(jnp.bfloat16)
    back = back * inverse

    for n in range(2 * own):
        wide[pl.ds(n, rows * steps, stride=2 * own), :] = fresh[:, n * size : (n + 1) * size]
    fresh_ref.reshape(rows * steps * 2 * own, size)[...] = wide[...].astype(jnp.bfloat16)
    puts = [pltpu.make_async_copy(fresh_ref, fresh_hbm, sems.at[0])]
    puts[0].start()

    for at in range(0, rows // 2, group):
        pairs = range(at, at + group)
        values = jnp.concatenate(
            [
                jnp.concatenate([new_lines(1, p) if n == p else nothing for n in pairs], axis=1)
                for p in pairs
            ],
            axis=0,
        )
        new = lax.dot_general(
            weights[at : at + group].reshape(group * keys, many), values, TN, preferred_element_type=jnp.float32
        )
        factors = back[at : at + group].T
        for n, p in enumerate(pairs):
            both = new[:, n * size : (n + 1) * size] + factors[:, n : n + 1] * rows_of(1, p)
            context_ref[2 * p : 2 * p + 2] = both.astype(jnp.bfloat16).reshape(2, queries, size)
        mine = pl.ds(2 * at, 2 * group)
        puts.append(pltpu.make_async_copy(context_ref.at[mine], context_hbm.at[mine], sems.at[1 + at // group]))
        puts[-1].start()
    for put in puts:
        put.wait()


def finish(parts, states, steps, own):
    _, many, size = states[0][0].shape
    rows = sum(state[0].shape[0] for state in states)
    heads = many // steps
    groups = rows * own * steps // size
    fresh = (rows, steps, 2, own, size)
    fresh, context = pl.pallas_call(
        functools.partial(finish_kernel, steps, heads, size ** (-0.5), len(parts)),
        out_shape=(
            jax.ShapeDtypeStruct(fresh, jnp.bfloat16),
            jax.ShapeDtypeStruct((rows, many, size), jnp.bfloat16),
        ),
        in_specs=[VMEM] * (len(parts) + 8),
        out_specs=(pl.BlockSpec(memory_space=pltpu.HBM),) * 2,
        scratch_shapes=[
            pltpu.VMEM((rows * steps * 2 * own, size), jnp.float32),
            pltpu.VMEM(fresh, jnp.bfloat16),
            pltpu.VMEM((rows, many, size), jnp.bfloat16),
            pltpu.SemaphoreType.DMA((1 + groups,)),
        ],
        compiler_params=params(24),
        cost_estimate=cost(rows * many * size * size * 6, 8 * rows * many * size, rows * many * size * 2),
        name="finish",
    )(*parts, *states[0], *states[1])
    return fresh, context.reshape(rows, steps, heads, size)


def join_kernel(*refs):
    blocks, out_ref = refs[:-1], refs[-1]
    at = 0
    for block in blocks:
        out_ref[at : at + block.shape[0], :] = block[...]
        at += block.shape[0]


def join(blocks):
    rows = sum(b.shape[0] for b in blocks)
    return pl.pallas_call(
        join_kernel,
        out_shape=pltpu.VMEM((rows, blocks[0].shape[1]), jnp.bfloat16),
        in_specs=[VMEM] * len(blocks),
        out_specs=VMEM,
        compiler_params=params(8),
        name="join",
    )(*blocks)


def gather_second(factor_a, factor_b, dp):
    count = dp // 2
    ranks = factor_b.shape[0]
    if ranks % 8 == 0 and count in (1, 2, 4):
        payload = make_payload(factor_a.T, factor_b)
        return [payload] + [lax.ppermute(payload, "dp", [(i, i ^ (2 * k)) for i in range(dp)]) for k in range(1, count)]
    payload = jnp.concatenate([factor_a.T, factor_b.reshape(ranks, -1)], axis=1)
    groups = [[i for i in range(dp) if i % 2 == n] for n in range(2)]
    copies = jnp.broadcast_to(payload[None], (count,) + payload.shape)
    blocks = lax.all_to_all(copies, "dp", 0, 0, axis_index_groups=groups, tiled=True)
    return [blocks.reshape(count * ranks, payload.shape[1])]


def shards(dp, tp, hidden, base_weight, factor_a, factor_b, queries, cache, lengths):
    steps, own = queries.shape[1], cache.shape[3]
    assert dp % 2 == 0
    early = queries.shape[0] * 2 // 3
    blocks = gather_second(factor_a, factor_b, dp)
    state = attend_cached(queries, cache, lengths, early)
    blocks, state, hidden, base_weight = lax.optimization_barrier((blocks, state, hidden, base_weight))
    gathered = join(blocks) if len(blocks) > 1 else blocks[0]
    gathered = [gathered, lax.ppermute(gathered, "dp", [(i, i ^ 1) for i in range(dp)])]
    tokens, base, late = arrange(hidden, base_weight, queries, cache, lengths, early)
    received = []
    for k in range(1, tp):
        other = project(k, tokens, base, gathered)
        received.append(lax.ppermute(other, "tp", [(i, i ^ k) for i in range(tp)]))
    mine = project(0, tokens, base, gathered)
    return finish([mine] + received, [state, late], steps, own)


def solution(mesh):
    return jax.shard_map(
        functools.partial(shards, mesh.shape["dp"], mesh.shape["tp"]),
        mesh=mesh,
        in_specs=(
            P(("parts", "dp"), None, "tp"),
            P("tp", None, None, None),
            P(("parts", "tp"), "dp"),
            P(("parts", "dp"), None, None, None),
            P(("parts", "dp"), None, "tp", None),
            P(("parts", "dp"), None, None, "tp", None),
            P(("parts", "dp")),
        ),
        out_specs=(
            P(("parts", "dp"), None, None, "tp", None),
            P(("parts", "dp"), None, "tp", None),
        ),
        check_vma=False,
    )
```

time: 26.5 us -> 25.9 us (0.977)
  waiting for transfers between devices: 1.69 us -> 0.32 us
  Pallas kernels: 16.3 us -> 17 us
    ppermute x1, waiting for transfers between devices: 1.35 us -> 0.01 us  [shards(): lax.ppermute(gathered, 'dp', [(i, i ^ 1) for i in range(dp)])]
    pallas_call x2, Pallas kernels: 10.3 us -> 11.4 us  [the longest x1 6.18 us: arrange(): pl.pallas_call(functools.partial(arrange_kernel, rows, chunk, chunks, own...]
    pallas_call x1, Pallas kernels: 2.35 us -> 2.05 us  [finish(): pl.pallas_call(functools.partial(finish_kernel, steps, heads, size ** (-0...]
  transfers between devices with their start and end apart: 5 -> 5, of which waited for: 2 -> 1; matrix products, arithmetic and copies ran while one was open for 0% -> 0% of each run, Pallas kernels for 45% -> 50%
where the time goes in v13:
time: 25.9 us; the launch traced here: 25.6 us
  Pallas kernels  17 us (66%)
  starting transfers between devices  7.55 us (29%)
  between operations  0.72 us (3%)
  waiting for transfers between devices  0.32 us (1%)
    pallas_call x1, Pallas kernels, arrange(): pl.pallas_call(functools.partial(arrange_kernel, rows, chunk, chunks, own...  6.18 us
    ppermute x3, starting transfers between devices, gather_second(): lax.ppermute(payload, 'dp', [(i, i ^ 2 * k) for i in range(dp)])  5.76 us
    pallas_call x1, Pallas kernels, attend_cached(): pl.pallas_call(functools.partial(cached_kernel, chunk, heads, size ** (-0...  5.2 us
    pallas_call x2, Pallas kernels, project(): pl.pallas_call(functools.partial(project_kernel, k), out_shape=pltpu.VMEM...  2.79 us
    pallas_call x1, Pallas kernels, finish(): pl.pallas_call(functools.partial(finish_kernel, steps, heads, size ** (-0...  2.05 us
    ppermute x1, starting transfers between devices, shards(): lax.ppermute(gathered, 'dp', [(i, i ^ 1) for i in range(dp)])  1.73 us
    pallas_call x1, Pallas kernels, make_payload(): pl.pallas_call(payload_kernel, out_shape=pltpu.VMEM((ranks, width + group...  0.81 us
  transfers between devices with their start and end apart: 5, of which 1 were waited for; matrix products, arithmetic and copies ran while one was open for 0% of the time, Pallas kernels for 50%

profile of v13, /device:TPU:0, one launch (start us, length us, event | category | flops | bytes accessed | tf_op | source)
XLA Modules:
  0.0 25.6 jit_solution(13498812585657742433)
XLA Ops:
  0.6 0.8 %payload.1.refs_0_ = bf16[8,3584]{1,0:T(8,128)(2,1)S(1)} custom-call(bf16[8,2560]{1,0:T(8,128)(2,1)} %bitcast.5, bf16[8,2,4,128]{3,2,1,0:T(4,128)(2,1)} %up_hbm.1), custom_call_target="tpu_custom_call" | custom-call | tf_op jit(solution)/shard_map/payload/pallas_call | solution.py:47
  1.5 5.1 %collective-permute-start.2 = (bf16[8,3584]{1,0:T(8,128)(2,1)S(1)}, bf16[8,3584]{1,0:T(8,128)(2,1)S(1)}, u32[]{:S(2)}, u32[]{:S(2)}) collective-permute-start(bf16[8,3584]{1,0:T(8,128)(2,1)S(1)} %payload.1.refs_0_), channel_id=1, source_target_pairs={{0,12},{2,14},{4,8},{6,10},{8,4},{10,6},{12,0},{14,2},{1,13},{3,15... | collective-permute-start | bytes 172040 | tf_op jit(solution)/shard_map/ppermute | solution.py:472
  6.6 0.0 collective-permute-start.1
  6.6 0.6 %collective-permute-start = (bf16[8,3584]{1,0:T(8,128)(2,1)S(1)}, bf16[8,3584]{1,0:T(8,128)(2,1)S(1)}, u32[]{:S(2)}, u32[]{:S(2)}) collective-permute-start(bf16[8,3584]{1,0:T(8,128)(2,1)S(1)} %payload.1.refs_0_), channel_id=1, source_target_pairs={{0,4},{2,6},{4,0},{6,2},{8,12},{10,14},{12,8},{14,10},{1,5},{3,7},... | collective-permute-start | bytes 172040 | tf_op jit(solution)/shard_map/ppermute | solution.py:472
  7.2 5.2 %attend_cached.1 = (bf16[32,64,128]{2,1,0:T(8,128)(2,1)S(1)}, f32[32,64,128]{2,1,0:T(8,128)S(1)}, f32[16,128]{1,0:T(8,128)S(1)}, f32[16,128]{1,0:T(8,128)S(1)}) custom-call(s32[48]{0:T(128)} %refs_2_.3, bf16[48,64,128]{2,1,0:T(8,128)(2,1)} %bitcast.3, bf16[48,128,2,2,128]{4,3,2,1,0:T(2,128)(2,1)} %refs_4_.1), custom_call_target="tpu_custom_call" | custom-call | flops 268435456 | bytes 4194304 | tf_op jit(solution)/shard_map/attend_cached/pallas_call | solution.py:199
  12.4 0.0 collective-permute-done.2.refs_3_
  12.4 0.0 collective-permute-done.1.refs_2_
  12.4 0.0 collective-permute-done.refs_1_
  12.5 1.7 %collective-permute-start.3 = (bf16[32,3584]{1,0:T(8,128)(2,1)S(1)}, bf16[32,3584]{1,0:T(8,128)(2,1)S(1)}, u32[]{:S(2)}, u32[]{:S(2)}) collective-permute-start(bf16[32,3584]{1,0:T(8,128)(2,1)S(1)} %join.1.refs_0_), channel_id=1, source_target_pairs={{0,2},{2,0},{4,6},{6,4},{8,10},{10,8},{12,14},{14,12},{1,3},{3,1},... | collective-permute-start | bytes 688136 | tf_op jit(solution)/shard_map/ppermute | solution.py:488
  14.2 6.2 %arrange.1 = (bf16[192,2560]{1,0:T(8,128)(2,1)S(1)}, bf16[4,2560,256]{2,1,0:T(8,128)(2,1)S(1)}, bf16[16,64,128]{2,1,0:T(8,128)(2,1)S(1)}, f32[16,64,128]{2,1,0:T...) custom-call(bf16[48,4,2560]{2,1,0:T(4,128)(2,1)} %refs_0_.2, bf16[2560,2,4,128]{3,2,1,0:T(4,128)(2,1)} %refs_1_, ...), custom_call_target="tpu_custom_call" | custom-call | flops 1476395008 | bytes 14548992 | tf_op jit(solution)/shard_map/arrange/pallas_call | solution.py:282
  20.4 0.0 collective-permute-done.3.refs_1_
  20.4 1.4 %project.3 = f32[192,512]{1,0:T(8,128)S(1)} custom-call(bf16[192,2560]{1,0:T(8,128)(2,1)S(1)} %get-tuple-element.30.hidden_ref, bf16[4,2560,256]{2,1,0:T(8,128)(2,1)S(1)} %get-tuple-element.31.base_ref, bf16[32,3584]{1,0:T(8,128)(2,1)S(1)} %join.1.refs_0_, bf16[32,3584]{1,0:T(8,128)(2,1)S(1)} %collective-permute-done.3.refs_1_), custom_call_target="tpu_custom_call" | custom-call | flops 671088640 | bytes 3604480 | tf_op jit(solution)/shard_map/project/pallas_call | solution.py:335
  21.8 0.1 collective-permute-start.4
  21.9 1.4 %project.2.refs_0_ = f32[192,512]{1,0:T(8,128)S(1)} custom-call(bf16[192,2560]{1,0:T(8,128)(2,1)S(1)} %get-tuple-element.30.hidden_ref, bf16[4,2560,256]{2,1,0:T(8,128)(2,1)S(1)} %get-tuple-element.31.base_ref, bf16[32,3584]{1,0:T(8,128)(2,1)S(1)} %join.1.refs_0_, bf16[32,3584]{1,0:T(8,128)(2,1)S(1)} %collective-permute-done.3.refs_1_), custom_call_target="tpu_custom_call" | custom-call | flops 671088640 | bytes 3604480 | tf_op jit(solution)/shard_map/project/pallas_call | solution.py:335
  23.3 0.3 %collective-permute-done.4.refs_1_ = f32[192,512]{1,0:T(8,128)S(1)} collective-permute-done((f32[192,512]{1,0:T(8,128)S(1)}, f32[192,512]{1,0:T(8,128)S(1)}, u32[]{:S(2)}, u32[]{:S(2)}) %collective-permute-start.4) | collective-permute-done | bytes 393248 | tf_op jit(solution)/shard_map/ppermute | solution.py:493
  23.6 2.0 %finish.1 = (bf16[48,4,2,2,128]{4,3,2,1,0:T(2,128)(2,1)}, bf16[48,64,128]{2,1,0:T(8,128)(2,1)}) custom-call(f32[192,512]{1,0:T(8,128)S(1)} %project.2.refs_0_, f32[192,512]{1,0:T(8,128)S(1)} %collective-permute-done.4.refs_1_, bf16[32,64,128]{2,1,0:T(8,128)(2,1)S(1)} %get-tuple-element.36.refs_2_, f32[32,64,128]{2,1,0:T(8,128)S(1)} %get-tuple-element.37.refs_3_, ...), custom_call_target="tpu_custom_call" | custom-call | flops 301989888 | bytes 3145728 | tf_op jit(solution)/shard_map/finish/pallas_call | solution.py:426
  (1 shorter events, 0.0 us)
Async XLA Ops:
  1.5 11.0 %collective-permute-start.2 = (bf16[8,3584]{1,0:T(8,128)(2,1)S(1)}, bf16[8,3584]{1,0:T(8,128)(2,1)S(1)}, u32[]{:S(2)}, u32[]{:S(2)}) collective-permute-start(bf16[8,3584]{1,0:T(8,128)(2,1)S(1)} %payload.1.refs_0_), channel_id=1, source_target_pairs={{0,12},{2,14},{4,8},{6,10},{8,4},{10,6},{12,0},{14,2},{1,13},{3,15... | collective-permute-start | bytes 172040 | tf_op jit(solution)/shard_map/ppermute | solution.py:472
  6.6 5.9 %collective-permute-start.1 = (bf16[8,3584]{1,0:T(8,128)(2,1)S(1)}, bf16[8,3584]{1,0:T(8,128)(2,1)S(1)}, u32[]{:S(2)}, u32[]{:S(2)}) collective-permute-start(bf16[8,3584]{1,0:T(8,128)(2,1)S(1)} %payload.1.refs_0_), channel_id=1, source_target_pairs={{0,8},{2,10},{4,12},{6,14},{8,0},{10,2},{12,4},{14,6},{1,9},{3,11}... | collective-permute-start | bytes 172040 | tf_op jit(solution)/shard_map/ppermute | solution.py:472
  6.6 5.9 %collective-permute-start = (bf16[8,3584]{1,0:T(8,128)(2,1)S(1)}, bf16[8,3584]{1,0:T(8,128)(2,1)S(1)}, u32[]{:S(2)}, u32[]{:S(2)}) collective-permute-start(bf16[8,3584]{1,0:T(8,128)(2,1)S(1)} %payload.1.refs_0_), channel_id=1, source_target_pairs={{0,4},{2,6},{4,0},{6,2},{8,12},{10,14},{12,8},{14,10},{1,5},{3,7},... | collective-permute-start | bytes 172040 | tf_op jit(solution)/shard_map/ppermute | solution.py:472
  12.5 7.9 %collective-permute-start.3 = (bf16[32,3584]{1,0:T(8,128)(2,1)S(1)}, bf16[32,3584]{1,0:T(8,128)(2,1)S(1)}, u32[]{:S(2)}, u32[]{:S(2)}) collective-permute-start(bf16[32,3584]{1,0:T(8,128)(2,1)S(1)} %join.1.refs_0_), channel_id=1, source_target_pairs={{0,2},{2,0},{4,6},{6,4},{8,10},{10,8},{12,14},{14,12},{1,3},{3,1},... | collective-permute-start | bytes 688136 | tf_op jit(solution)/shard_map/ppermute | solution.py:488
  21.8 1.8 %collective-permute-start.4 = (f32[192,512]{1,0:T(8,128)S(1)}, f32[192,512]{1,0:T(8,128)S(1)}, u32[]{:S(2)}, u32[]{:S(2)}) collective-permute-start(f32[192,512]{1,0:T(8,128)S(1)} %project.3), channel_id=1, source_target_pairs={{0,1},{1,0},{2,3},{3,2},{4,5},{5,4},{6,7},{7,6},{8,9},{9,8},{10,11... | collective-permute-start | bytes 1179656 | tf_op jit(solution)/shard_map/ppermute | solution.py:493

commit v14 on v13

--- a/solution.py
+++ b/solution.py
@@ -165,11 +165,14 @@
 
 
 def cached_kernel(chunk, heads, scale, *refs):
-    cached = Cached(0, chunk, heads, scale, refs[:3], refs[3:7], refs[7:])
+    hidden_hbm, tokens_ref, hidden, hidden_sem = refs[3], refs[8], refs[9], refs[10]
+    cached = Cached(0, chunk, heads, scale, refs[:3], refs[4:8], refs[11:])
     chunks = cached.rows // chunk
+    get_hidden = pltpu.make_async_copy(hidden_hbm, hidden, hidden_sem)
     cached.lengths_copy().start()
     for i in range(chunks):
         cached.start(i)
+    get_hidden.start()
     cached.lengths_copy().wait()
     cached.arrive(0)
     cached.score(0, 0)
@@ -186,52 +189,46 @@
             cached.soften(i - 1, 1 - slot)
             cached.collect(i - 2, slot)
 
+    get_hidden.wait()
     cached.soften(chunks - 1, 1)
     cached.collect(chunks - 2, 0)
+    tokens_ref[...] = hidden.reshape(tokens_ref.shape)[...]
     cached.collect(chunks - 1, 1)
 
 
-def attend_cached(queries, cache, lengths, rows):
-    _, steps, heads, size = queries.shape
+def attend_cached(queries, cache, lengths, hidden):
+    rows, steps, heads, size = queries.shape
     slots, own = cache.shape[1], cache.shape[3]
     many = steps * heads
-    chunk = 4
-    return pl.pallas_call(
+    chunk = 6
+    outs = Cached.outputs(rows, many, size) + (pltpu.VMEM((rows * steps, hidden.shape[2]), jnp.bfloat16),)
+    *state, tokens = pl.pallas_call(
         functools.partial(cached_kernel, chunk, heads, size ** (-0.5)),
-        out_shape=Cached.outputs(rows, many, size),
-        in_specs=[pl.BlockSpec(memory_space=pltpu.HBM)] * 3,
-        out_specs=(VMEM,) * 4,
-        scratch_shapes=Cached.scratch(rows, chunk, many, cache, lengths),
+        out_shape=outs,
+        in_specs=[pl.BlockSpec(memory_space=pltpu.HBM)] * 4,
+        out_specs=(VMEM,) * 5,
+        scratch_shapes=[pltpu.VMEM(hidden.shape, jnp.bfloat16), pltpu.SemaphoreType.DMA]
+        + Cached.scratch(rows, chunk, many, cache, lengths),
         compiler_params=params(28),
         cost_estimate=cost(
             8 * rows * many * slots * size, 4 * rows * slots * own * size, rows * many * slots * own
         ),
         name="attend_cached",
-    )(*map(in_hbm, (lengths, queries.reshape(-1, many, size), cache)))
-
-
-def arrange_kernel(first, chunk, chunks, own, heads, scale, *refs):
-    hidden_hbm, base_hbm = refs[:2]
-    tokens_ref, base_ref = refs[5:7]
-    hidden, base, sems = refs[11:14]
-    cached = Cached(first, chunk, heads, scale, refs[2:5], refs[7:11], refs[14:])
+    )(*map(in_hbm, (lengths, queries.reshape(-1, many, size), cache, hidden)))
+    return state, tokens
+
+
+def arrange_kernel(first, chunks, own, base_hbm, base_ref, base, sems):
     width, two, kvh, size = base.shape
     groups = two * kvh
     some_width = width // chunks
 
     def copy(i):
-        features = pl.ds(i * some_width, some_width)
-        return pltpu.make_async_copy(base_hbm.at[features], base.at[features], sems.at[i])
-
-    get_hidden = pltpu.make_async_copy(hidden_hbm, hidden, sems.at[chunks])
-    cached.lengths_copy().start()
-    copy(0).start()
-    cached.start(0)
-    copy(1).start()
-    cached.start(1)
-    for i in range(2, chunks):
+        theirs, mine = pl.ds(first + i * some_width, some_width), pl.ds(i * some_width, some_width)
+        return pltpu.make_async_copy(base_hbm.at[theirs], base.at[mine], sems.at[i])
+
+    for i in range(chunks):
         copy(i).start()
-    get_hidden.start()
 
     tile = 256
     some = tile // groups
@@ -251,61 +248,36 @@
                     n * some : (n + 1) * some, h * size : (h + 1) * size
                 ]
 
-    cached.lengths_copy().wait()
     for i in range(chunks):
         copy(i).wait()
-        if i < 2:
-            cached.arrive(i)
-            cached.score(i, i)
-        if 1 <= i < 3:
-            cached.soften(i - 1, i - 1)
-        if 2 <= i < 4:
-            cached.collect(i - 2, i - 2)
         for f in range(i * some_width, (i + 1) * some_width, 2 * some):
             arrange(f)
-    get_hidden.wait()
-    tokens_ref[...] = hidden.reshape(tokens_ref.shape)[...]
-
-
-def arrange(hidden, base, queries, cache, lengths, rows):
-    _, steps, heads, size = queries.shape
-    slots, own = cache.shape[1], cache.shape[3]
-    many = steps * heads
+
+
+def arrange(base, own, first, count):
     width, two, kvh, size = base.shape
-    chunks = 4
-    rest = hidden.shape[0] - rows
-    chunk = rest // 2
-    outs = (
-        pltpu.VMEM((hidden.shape[0] * steps, width), jnp.bfloat16),
-        pltpu.VMEM((two * kvh // own, width, own * size), jnp.bfloat16),
-    ) + Cached.outputs(rest, many, size)
-    tokens, base, *state = pl.pallas_call(
-        functools.partial(arrange_kernel, rows, chunk, chunks, own, heads, size ** (-0.5)),
-        out_shape=outs,
-        in_specs=[pl.BlockSpec(memory_space=pltpu.HBM)] * 5,
-        out_specs=(VMEM,) * len(outs),
+    chunks = 2
+    return pl.pallas_call(
+        functools.partial(arrange_kernel, first, chunks, own),
+        out_shape=pltpu.VMEM((two * kvh // own, count, own * size), jnp.bfloat16),
+        in_specs=[pl.BlockSpec(memory_space=pltpu.HBM)],
+        out_specs=VMEM,
         scratch_shapes=[
-            pltpu.VMEM(hidden.shape, jnp.bfloat16),
-            pltpu.VMEM(base.shape, jnp.bfloat16),
-            pltpu.SemaphoreType.DMA((chunks + 1,)),
-        ]
-        + Cached.scratch(rest, chunk, many, cache, lengths),
-        compiler_params=params(28),
-        cost_estimate=cost(
-            512 * base.size + 8 * rest * many * slots * size,
-            4 * (base.size + hidden.size + rest * slots * own * size),
-            rest * many * slots * own,
-        ),
+            pltpu.VMEM((count, two, kvh, size), jnp.bfloat16),
+            pltpu.SemaphoreType.DMA((chunks,)),
+        ],
+        compiler_params=params(20),
+        cost_estimate=cost(512 * two * kvh * size * count, 4 * two * kvh * size * count),
         name="arrange",
-    )(*map(in_hbm, (hidden, base, lengths, queries.reshape(-1, many, size), cache)))
-    return tokens, base, state
-
-
-def project_kernel(k, hidden_ref, base_ref, *refs):
-    gathered, (out_ref, merged) = refs[:-2], refs[-2:]
+    )(in_hbm(base))
+
+
+def project_kernel(k, bases, hidden_ref, *refs):
+    bases, gathered, (out_ref, merged) = refs[:bases], refs[bases:-2], refs[-2:]
     width, columns = merged.shape
+    some_width = bases[0].shape[1]
     part = lax.axis_index("tp") ^ k
-    parts = base_ref.shape[0] // 2
+    parts = bases[0].shape[0] // 2
     half = columns // 2
     up = jnp.concatenate(
         [
@@ -316,37 +288,39 @@
         ],
         axis=1,
     )
-    step = 512
+    step = 256
     for f in range(0, width, step):
         down = jnp.concatenate([ref[:, f : f + step] for ref in gathered], axis=0).T
         low_rank = jnp.dot(down, up, preferred_element_type=jnp.float32)
         for c in range(2):
-            base = base_ref[c * parts + part, f : f + step, :].astype(jnp.float32)
+            base_ref, at = bases[f // some_width], f % some_width
+            base = base_ref[c * parts + part, at : at + step, :].astype(jnp.float32)
             merged[f : f + step, c * half : (c + 1) * half] = (base + low_rank[:, c * half : (c + 1) * half]).astype(
                 jnp.bfloat16
             )
     out_ref[...] = jnp.dot(hidden_ref[...], merged[...], preferred_element_type=jnp.float32)
 
 
-def project(k, hidden, base, gathered):
+def project(k, hidden, bases, gathered):
     tokens, width = hidden.shape
-    columns = 2 * base.shape[2]
+    columns = 2 * bases[0].shape[2]
     ranks = sum(g.shape[0] for g in gathered)
     return pl.pallas_call(
-        functools.partial(project_kernel, k),
+        functools.partial(project_kernel, k, len(bases)),
         out_shape=pltpu.VMEM((tokens, columns), jnp.float32),
-        in_specs=[VMEM] * (2 + len(gathered)),
+        in_specs=[VMEM] * (1 + len(bases) + len(gathered)),
         out_specs=VMEM,
         scratch_shapes=[pltpu.VMEM((width, columns), jnp.bfloat16)],
         compiler_params=params(24),
         cost_estimate=cost(2 * width * columns * (tokens + ranks), 2 * width * columns + 2 * width * tokens),
         name="project",
-    )(hidden, base, *gathered)
+    )(hidden, *bases, *gathered)
 
 
 def finish_kernel(steps, heads, scale, terms, *refs):
     parts, refs = refs[:terms], refs[terms:]
-    states, refs = (refs[:4], refs[4:8]), refs[8:]
+    q_ref, old_ref, top_ref, total_ref = refs[:4]
+    refs = refs[4:]
     fresh_hbm, context_hbm, wide, fresh_ref, context_ref, sems = refs
     rows, queries, size = context_ref.shape
     own = fresh_ref.shape[3]
@@ -367,24 +341,19 @@
         lines = [fresh[tokens, (c * own + g) * size : (c * own + g + 1) * size] for g in range(own)]
         return jnp.concatenate(lines, axis=0).astype(jnp.bfloat16)
 
-    def old(n, pair):
-        count = states[0][0].shape[0] // 2
-        return (states[0][n], pair) if pair < count else (states[1][n], pair - count)
-
-    def rows_of(n, pair):
-        ref, at = old(n, pair)
-        return ref[2 * at : 2 * at + 2].reshape(many, size)
+    def rows_of(ref, pair):
+        return ref[2 * pair : 2 * pair + 2].reshape(many, size)
 
     scores = [
-        lax.dot_general(new_lines(0, p), rows_of(0, p), NT, preferred_element_type=jnp.float32)
+        lax.dot_general(new_lines(0, p), rows_of(q_ref, p), NT, preferred_element_type=jnp.float32)
         for p in range(rows // 2)
     ]
     scores = jnp.stack([jnp.where(live, s, LOW) for s in scores])
-    old_top, old_total = [jnp.concatenate([states[0][n][...], states[1][n][...]], axis=0) for n in (2, 3)]
+    old_top = top_ref[...]
     top = jnp.maximum(old_top, jnp.max(scores, axis=1))
     expo = jnp.exp((scores - top[:, None, :]) * scale)
     back = jnp.exp((old_top - top) * scale)
-    inverse = 1.0 / (back * old_total + jnp.sum(expo, axis=1))
+    inverse = 1.0 / (back * total_ref[...] + jnp.sum(expo, axis=1))
     weights = (expo * inverse[:, None, :]).astype(jnp.bfloat16)
     back = back * inverse
 
@@ -408,7 +377,7 @@
         )
         factors = back[at : at + group].T
         for n, p in enumerate(pairs):
-            both = new[:, n * size : (n + 1) * size] + factors[:, n : n + 1] * rows_of(1, p)
+            both = new[:, n * size : (n + 1) * size] + factors[:, n : n + 1] * rows_of(old_ref, p)
             context_ref[2 * p : 2 * p + 2] = both.astype(jnp.bfloat16).reshape(2, queries, size)
         mine = pl.ds(2 * at, 2 * group)
         puts.append(pltpu.make_async_copy(context_ref.at[mine], context_hbm.at[mine], sems.at[1 + at // group]))
@@ -417,9 +386,8 @@
         put.wait()
 
 
-def finish(parts, states, steps, own):
-    _, many, size = states[0][0].shape
-    rows = sum(state[0].shape[0] for state in states)
+def finish(parts, state, steps, own):
+    rows, many, size = state[0].shape
     heads = many // steps
     groups = rows * own * steps // size
     fresh = (rows, steps, 2, own, size)
@@ -429,7 +397,7 @@
             jax.ShapeDtypeStruct(fresh, jnp.bfloat16),
             jax.ShapeDtypeStruct((rows, many, size), jnp.bfloat16),
         ),
-        in_specs=[VMEM] * (len(parts) + 8),
+        in_specs=[VMEM] * (len(parts) + 4),
         out_specs=(pl.BlockSpec(memory_space=pltpu.HBM),) * 2,
         scratch_shapes=[
             pltpu.VMEM((rows * steps * 2 * own, size), jnp.float32),
@@ -440,7 +408,7 @@
         compiler_params=params(24),
         cost_estimate=cost(rows * many * size * size * 6, 8 * rows * many * size, rows * many * size * 2),
         name="finish",
-    )(*parts, *states[0], *states[1])
+    )(*parts, *state)
     return fresh, context.reshape(rows, steps, heads, size)
 
 
@@ -464,35 +432,38 @@
     )(*blocks)
 
 
-def gather_second(factor_a, factor_b, dp):
-    count = dp // 2
-    ranks = factor_b.shape[0]
-    if ranks % 8 == 0 and count in (1, 2, 4):
-        payload = make_payload(factor_a.T, factor_b)
-        return [payload] + [lax.ppermute(payload, "dp", [(i, i ^ (2 * k)) for i in range(dp)]) for k in range(1, count)]
-    payload = jnp.concatenate([factor_a.T, factor_b.reshape(ranks, -1)], axis=1)
-    groups = [[i for i in range(dp) if i % 2 == n] for n in range(2)]
-    copies = jnp.broadcast_to(payload[None], (count,) + payload.shape)
-    blocks = lax.all_to_all(copies, "dp", 0, 0, axis_index_groups=groups, tiled=True)
-    return [blocks.reshape(count * ranks, payload.shape[1])]
-
-
 def shards(dp, tp, hidden, base_weight, factor_a, factor_b, queries, cache, lengths):
     steps, own = queries.shape[1], cache.shape[3]
-    assert dp % 2 == 0
-    early = queries.shape[0] * 2 // 3
-    blocks = gather_second(factor_a, factor_b, dp)
-    state = attend_cached(queries, cache, lengths, early)
-    blocks, state, hidden, base_weight = lax.optimization_barrier((blocks, state, hidden, base_weight))
-    gathered = join(blocks) if len(blocks) > 1 else blocks[0]
-    gathered = [gathered, lax.ppermute(gathered, "dp", [(i, i ^ 1) for i in range(dp)])]
-    tokens, base, late = arrange(hidden, base_weight, queries, cache, lengths, early)
+    ranks = factor_b.shape[0]
+    half = base_weight.shape[0] // 2
+
+    def swap(x, k):
+        return lax.ppermute(x, "dp", [(i, i ^ k) for i in range(dp)])
+
+    if dp == 8 and ranks % 8 == 0:
+        block = make_payload(factor_a.T, factor_b)
+        other = swap(block, 4)
+        base = arrange(base_weight, own, 0, half)
+        block, other, base, base_weight = lax.optimization_barrier((block, other, base, base_weight))
+        block = join([block, other])
+        other = swap(block, 2)
+        bases = [base, arrange(base_weight, own, half, half)]
+        block, other, bases, cache = lax.optimization_barrier((block, other, bases, cache))
+        block = join([block, other])
+        gathered = [block, swap(block, 1)]
+    else:
+        payload = jnp.concatenate([factor_a.T, factor_b.reshape(ranks, -1)], axis=1)
+        copies = jnp.broadcast_to(payload[None], (dp,) + payload.shape)
+        blocks = lax.all_to_all(copies, "dp", 0, 0, tiled=True)
+        gathered = [blocks.reshape(dp * ranks, payload.shape[1])]
+        bases = [arrange(base_weight, own, n * half, half) for n in range(2)]
+    state, tokens = attend_cached(queries, cache, lengths, hidden)
     received = []
     for k in range(1, tp):
-        other = project(k, tokens, base, gathered)
+        other = project(k, tokens, bases, gathered)
         received.append(lax.ppermute(other, "tp", [(i, i ^ k) for i in range(tp)]))
-    mine = project(0, tokens, base, gathered)
-    return finish([mine] + received, [state, late], steps, own)
+    mine = project(0, tokens, bases, gathered)
+    return finish([mine] + received, state, steps, own)
 
 
 def solution(mesh):

time: 25.9 us -> 27.3 us (1.054)
  waiting for transfers between devices: 0.32 us -> 1.59 us
  Pallas kernels: 17 us -> 17.4 us
    pallas_call x1, Pallas kernels: 5.2 us -> 6.69 us  [attend_cached(): pl.pallas_call(functools.partial(cached_kernel, chunk, heads, size ** (-0...]
    ppermute x4 -> x3, waiting for transfers between devices: 0.01 us -> 1.28 us  [swap(): return lax.ppermute(x, 'dp', [(i, i ^ k) for i in range(dp)])]
    pallas_call x3 -> x4, Pallas kernels: 8.96 us -> 7.75 us  [the longest x2 4.96 us: arrange(): pl.pallas_call(functools.partial(arrange_kernel, first, chunks, own), out...]
    ppermute x4 -> x3, starting transfers between devices: 7.48 us -> 7.28 us  [swap(): return lax.ppermute(x, 'dp', [(i, i ^ k) for i in range(dp)])]
  transfers between devices with their start and end apart: 5 -> 4, of which waited for: 1 -> 3; matrix products, arithmetic and copies ran while one was open for 0% -> 0% of each run, Pallas kernels for 50% -> 48%
where the time goes in v14:
time: 27.3 us; the launch traced here: 27 us
  Pallas kernels  17.4 us (64%)
  starting transfers between devices  7.35 us (27%)
  waiting for transfers between devices  1.59 us (6%)
  between operations  0.7 us (3%)
    ppermute x3, starting transfers between devices, swap(): return lax.ppermute(x, 'dp', [(i, i ^ k) for i in range(dp)])  7.28 us
    pallas_call x1, Pallas kernels, attend_cached(): pl.pallas_call(functools.partial(cached_kernel, chunk, heads, size ** (-0...  6.69 us
    pallas_call x2, Pallas kernels, arrange(): pl.pallas_call(functools.partial(arrange_kernel, first, chunks, own), out...  4.96 us
    pallas_call x2, Pallas kernels, project(): pl.pallas_call(functools.partial(project_kernel, k, len(bases)), out_shap...  2.79 us
    pallas_call x1, Pallas kernels, finish(): pl.pallas_call(functools.partial(finish_kernel, steps, heads, size ** (-0...  2.08 us
    ppermute x3, waiting for transfers between devices, swap(): return lax.ppermute(x, 'dp', [(i, i ^ k) for i in range(dp)])  1.28 us
    pallas_call x1, Pallas kernels, make_payload(): pl.pallas_call(payload_kernel, out_shape=pltpu.VMEM((ranks, width + group...  0.81 us
  transfers between devices with their start and end apart: 4, of which 3 were waited for; matrix products, arithmetic and copies ran while one was open for 0% of the time, Pallas kernels for 48%

profile of v14, /device:TPU:0, one launch (start us, length us, event | category | flops | bytes accessed | tf_op | source)
XLA Modules:
  0.0 27.0 jit_solution(6501521203941549911)
XLA Ops:
  0.6 0.8 %payload.1.refs_0_ = bf16[8,3584]{1,0:T(8,128)(2,1)S(1)} custom-call(bf16[8,2560]{1,0:T(8,128)(2,1)} %bitcast.4, bf16[8,2,4,128]{3,2,1,0:T(4,128)(2,1)} %up_hbm.1), custom_call_target="tpu_custom_call" | custom-call | tf_op jit(solution)/shard_map/payload/pallas_call | solution.py:47
  1.5 4.1 %collective-permute-start = (bf16[8,3584]{1,0:T(8,128)(2,1)S(1)}, bf16[8,3584]{1,0:T(8,128)(2,1)S(1)}, u32[]{:S(2)}, u32[]{:S(2)}) collective-permute-start(bf16[8,3584]{1,0:T(8,128)(2,1)S(1)} %payload.1.refs_0_), channel_id=1, source_target_pairs={{0,8},{2,10},{4,12},{6,14},{8,0},{10,2},{12,4},{14,6},{1,9},{3,11}... | collective-permute-start | bytes 172040 | tf_op jit(solution)/shard_map/ppermute | solution.py:441
  5.6 2.5 %arrange.2.refs_0_ = bf16[4,1280,256]{2,1,0:T(8,128)(2,1)S(1)} custom-call(bf16[2560,2,4,128]{3,2,1,0:T(4,128)(2,1)} %base_hbm.2), custom_call_target="tpu_custom_call" | custom-call | flops 671088640 | bytes 5242880 | tf_op jit(solution)/shard_map/arrange/pallas_call | solution.py:260
  8.0 0.3 %collective-permute-done.refs_1_ = bf16[8,3584]{1,0:T(8,128)(2,1)S(1)} collective-permute-done((bf16[8,3584]{1,0:T(8,128)(2,1)S(1)}, bf16[8,3584]{1,0:T(8,128)(2,1)S(1)}, u32[]{:S(2)}, u32[]{:S(2)}) %collective-permute-start) | collective-permute-done | bytes 57376 | tf_op jit(solution)/shard_map/ppermute | solution.py:441
  8.3 1.4 %collective-permute-start.1 = (bf16[16,3584]{1,0:T(8,128)(2,1)S(1)}, bf16[16,3584]{1,0:T(8,128)(2,1)S(1)}, u32[]{:S(2)}, u32[]{:S(2)}) collective-permute-start(bf16[16,3584]{1,0:T(8,128)(2,1)S(1)} %join.2.refs_0_), channel_id=1, source_target_pairs={{0,4},{2,6},{4,0},{6,2},{8,12},{10,14},{12,8},{14,10},{1,5},{3,7},... | collective-permute-start | bytes 344072 | tf_op jit(solution)/shard_map/ppermute | solution.py:441
  9.7 2.5 %arrange.3.refs_1_ = bf16[4,1280,256]{2,1,0:T(8,128)(2,1)S(1)} custom-call(bf16[2560,2,4,128]{3,2,1,0:T(4,128)(2,1)} %base_hbm.2), custom_call_target="tpu_custom_call" | custom-call | flops 671088640 | bytes 5242880 | tf_op jit(solution)/shard_map/arrange/pallas_call | solution.py:260
  12.2 1.0 %collective-permute-done.1.refs_1_ = bf16[16,3584]{1,0:T(8,128)(2,1)S(1)} collective-permute-done((bf16[16,3584]{1,0:T(8,128)(2,1)S(1)}, bf16[16,3584]{1,0:T(8,128)(2,1)S(1)}, u32[]{:S(2)}, u32[]{:S(2)}) %collective-permute-start.1) | collective-permute-done | bytes 114720 | tf_op jit(solution)/shard_map/ppermute | solution.py:441
  13.2 1.8 %collective-permute-start.2 = (bf16[32,3584]{1,0:T(8,128)(2,1)S(1)}, bf16[32,3584]{1,0:T(8,128)(2,1)S(1)}, u32[]{:S(2)}, u32[]{:S(2)}) collective-permute-start(bf16[32,3584]{1,0:T(8,128)(2,1)S(1)} %join.3.refs_2_), channel_id=1, source_target_pairs={{0,2},{2,0},{4,6},{6,4},{8,10},{10,8},{12,14},{14,12},{1,3},{3,1},... | collective-permute-start | bytes 688136 | tf_op jit(solution)/shard_map/ppermute | solution.py:441
  15.0 6.7 %attend_cached.1 = (bf16[48,64,128]{2,1,0:T(8,128)(2,1)S(1)}, f32[48,64,128]{2,1,0:T(8,128)S(1)}, f32[24,128]{1,0:T(8,128)S(1)}, f32[24,128]{1,0:T(8,128)S(1)}, bf16[192,2560]{1,0:T(8,128)(2,1)S(1)}) custom-call(s32[48]{0:T(128)} %refs_0_.1, bf16[48,64,128]{2,1,0:T(8,128)(2,1)} %bitcast.3, bf16[48,128,2,2,128]{4,3,2,1,0:T(2,128)(2,1)} %refs_2_, ...), custom_call_target="tpu_custom_call" | custom-call | flops 402653184 | bytes 6291456 | tf_op jit(solution)/shard_map/attend_cached/pallas_call | solution.py:205
  21.7 0.0 collective-permute-done.2.refs_3_
  21.7 1.4 %project.3 = f32[192,512]{1,0:T(8,128)S(1)} custom-call(bf16[192,2560]{1,0:T(8,128)(2,1)S(1)} %get-tuple-element.23.hidden_ref, bf16[4,1280,256]{2,1,0:T(8,128)(2,1)S(1)} %arrange.2.refs_0_, bf16[4,1280,256]{2,1,0:T(8,128)(2,1)S(1)} %arrange.3.refs_1_, bf16[32,3584]{1,0:T(8,128)(2,1)S(1)} %join.3.refs_2_, bf16[32,3584]{1,0:T(8,128)(2,1)S(1)} %collective-permute-done.2.refs_3_), custom_call_target="tpu_custom_call" | custom-call | flops 671088640 | bytes 3604480 | tf_op jit(solution)/shard_map/project/pallas_call | solution.py:308
  23.1 0.1 collective-permute-start.3
  23.2 1.4 %project.2.refs_0_ = f32[192,512]{1,0:T(8,128)S(1)} custom-call(bf16[192,2560]{1,0:T(8,128)(2,1)S(1)} %get-tuple-element.23.hidden_ref, bf16[4,1280,256]{2,1,0:T(8,128)(2,1)S(1)} %arrange.2.refs_0_, bf16[4,1280,256]{2,1,0:T(8,128)(2,1)S(1)} %arrange.3.refs_1_, bf16[32,3584]{1,0:T(8,128)(2,1)S(1)} %join.3.refs_2_, ...), custom_call_target="tpu_custom_call" | custom-call | flops 671088640 | bytes 3604480 | tf_op jit(solution)/shard_map/project/pallas_call | solution.py:308
  24.6 0.3 %collective-permute-done.3.refs_1_ = f32[192,512]{1,0:T(8,128)S(1)} collective-permute-done((f32[192,512]{1,0:T(8,128)S(1)}, f32[192,512]{1,0:T(8,128)S(1)}, u32[]{:S(2)}, u32[]{:S(2)}) %collective-permute-start.3) | collective-permute-done | bytes 393248 | tf_op jit(solution)/shard_map/ppermute | solution.py:464
  24.9 2.1 %finish.1 = (bf16[48,4,2,2,128]{4,3,2,1,0:T(2,128)(2,1)}, bf16[48,64,128]{2,1,0:T(8,128)(2,1)}) custom-call(f32[192,512]{1,0:T(8,128)S(1)} %project.2.refs_0_, f32[192,512]{1,0:T(8,128)S(1)} %collective-permute-done.3.refs_1_, bf16[48,64,128]{2,1,0:T(8,128)(2,1)S(1)} %get-tuple-element.28.refs_2_, f32[48,64,128]{2,1,0:T(8,128)S(1)} %get-tuple-element.29.refs_3_, ...), custom_call_target="tpu_custom_call" | custom-call | flops 301989888 | bytes 3145728 | tf_op jit(solution)/shard_map/finish/pallas_call | solution.py:394
  (2 shorter events, 0.0 us)
Async XLA Ops:
  1.5 6.9 %collective-permute-start = (bf16[8,3584]{1,0:T(8,128)(2,1)S(1)}, bf16[8,3584]{1,0:T(8,128)(2,1)S(1)}, u32[]{:S(2)}, u32[]{:S(2)}) collective-permute-start(bf16[8,3584]{1,0:T(8,128)(2,1)S(1)} %payload.1.refs_0_), channel_id=1, source_target_pairs={{0,8},{2,10},{4,12},{6,14},{8,0},{10,2},{12,4},{14,6},{1,9},{3,11}... | collective-permute-start | bytes 172040 | tf_op jit(solution)/shard_map/ppermute | solution.py:441
  8.3 4.9 %collective-permute-start.1 = (bf16[16,3584]{1,0:T(8,128)(2,1)S(1)}, bf16[16,3584]{1,0:T(8,128)(2,1)S(1)}, u32[]{:S(2)}, u32[]{:S(2)}) collective-permute-start(bf16[16,3584]{1,0:T(8,128)(2,1)S(1)} %join.2.refs_0_), channel_id=1, source_target_pairs={{0,4},{2,6},{4,0},{6,2},{8,12},{10,14},{12,8},{14,10},{1,5},{3,7},... | collective-permute-start | bytes 344072 | tf_op jit(solution)/shard_map/ppermute | solution.py:441
  13.2 8.5 %collective-permute-start.2 = (bf16[32,3584]{1,0:T(8,128)(2,1)S(1)}, bf16[32,3584]{1,0:T(8,128)(2,1)S(1)}, u32[]{:S(2)}, u32[]{:S(2)}) collective-permute-start(bf16[32,3584]{1,0:T(8,128)(2,1)S(1)} %join.3.refs_2_), channel_id=1, source_target_pairs={{0,2},{2,0},{4,6},{6,4},{8,10},{10,8},{12,14},{14,12},{1,3},{3,1},... | collective-permute-start | bytes 688136 | tf_op jit(solution)/shard_map/ppermute | solution.py:441
  23.1 1.8 %collective-permute-start.3 = (f32[192,512]{1,0:T(8,128)S(1)}, f32[192,512]{1,0:T(8,128)S(1)}, u32[]{:S(2)}, u32[]{:S(2)}) collective-permute-start(f32[192,512]{1,0:T(8,128)S(1)} %project.3), channel_id=1, source_target_pairs={{0,1},{1,0},{2,3},{3,2},{4,5},{5,4},{6,7},{7,6},{8,9},{9,8},{10,11... | collective-permute-start | bytes 1179656 | tf_op jit(solution)/shard_map/ppermute | solution.py:464

commit v15 on v13

--- a/solution.py
+++ b/solution.py
@@ -116,8 +116,8 @@
         return pltpu.make_async_copy(self.lengths_hbm, self.lengths, self.length_sem)
 
     def start(self, i):
-        for copy in self.copies(i):
-            copy.start()
+        for n, copy in enumerate(self.copies(i)):
+            copy.start(priority=n // 2)
 
     def arrive(self, i):
         for copy in self.copies(i):
@@ -480,7 +480,7 @@
 def shards(dp, tp, hidden, base_weight, factor_a, factor_b, queries, cache, lengths):
     steps, own = queries.shape[1], cache.shape[3]
     assert dp % 2 == 0
-    early = queries.shape[0] * 2 // 3
+    early = queries.shape[0] * 5 // 6
     blocks = gather_second(factor_a, factor_b, dp)
     state = attend_cached(queries, cache, lengths, early)
     blocks, state, hidden, base_weight = lax.optimization_barrier((blocks, state, hidden, base_weight))

time: 25.9 us -> 27.7 us (1.069)
  Pallas kernels: 17 us -> 18.9 us
    pallas_call x1, Pallas kernels: 5.2 us -> 7.08 us  [attend_cached(): pl.pallas_call(functools.partial(cached_kernel, chunk, heads, size ** (-0...]
  transfers between devices with their start and end apart: 5 -> 5, of which waited for: 1 -> 1; matrix products, arithmetic and copies ran while one was open for 0% -> 0% of each run, Pallas kernels for 50% -> 53%
where the time goes in v15:
time: 27.7 us; the launch traced here: 27.5 us
  Pallas kernels  18.9 us (68%)
  starting transfers between devices  7.56 us (27%)
  between operations  0.72 us (3%)
  waiting for transfers between devices  0.32 us (1%)
    pallas_call x1, Pallas kernels, attend_cached(): pl.pallas_call(functools.partial(cached_kernel, chunk, heads, size ** (-0...  7.08 us
    pallas_call x1, Pallas kernels, arrange(): pl.pallas_call(functools.partial(arrange_kernel, rows, chunk, chunks, own...  6.13 us
    ppermute x3, starting transfers between devices, gather_second(): lax.ppermute(payload, 'dp', [(i, i ^ 2 * k) for i in range(dp)])  5.76 us
    pallas_call x2, Pallas kernels, project(): pl.pallas_call(functools.partial(project_kernel, k), out_shape=pltpu.VMEM...  2.79 us
    pallas_call x1, Pallas kernels, finish(): pl.pallas_call(functools.partial(finish_kernel, steps, heads, size ** (-0...  2.05 us
    ppermute x1, starting transfers between devices, shards(): lax.ppermute(gathered, 'dp', [(i, i ^ 1) for i in range(dp)])  1.74 us
    pallas_call x1, Pallas kernels, make_payload(): pl.pallas_call(payload_kernel, out_shape=pltpu.VMEM((ranks, width + group...  0.81 us
  transfers between devices with their start and end apart: 5, of which 1 were waited for; matrix products, arithmetic and copies ran while one was open for 0% of the time, Pallas kernels for 53%

profile of v15, /device:TPU:0, one launch (start us, length us, event | category | flops | bytes accessed | tf_op | source)
XLA Modules:
  0.0 27.5 jit_solution(9151830474729470173)
XLA Ops:
  0.6 0.8 %payload.1.refs_0_ = bf16[8,3584]{1,0:T(8,128)(2,1)S(1)} custom-call(bf16[8,2560]{1,0:T(8,128)(2,1)} %bitcast.5, bf16[8,2,4,128]{3,2,1,0:T(4,128)(2,1)} %up_hbm.1), custom_call_target="tpu_custom_call" | custom-call | tf_op jit(solution)/shard_map/payload/pallas_call | solution.py:47
  1.5 5.1 %collective-permute-start.2 = (bf16[8,3584]{1,0:T(8,128)(2,1)S(1)}, bf16[8,3584]{1,0:T(8,128)(2,1)S(1)}, u32[]{:S(2)}, u32[]{:S(2)}) collective-permute-start(bf16[8,3584]{1,0:T(8,128)(2,1)S(1)} %payload.1.refs_0_), channel_id=1, source_target_pairs={{0,12},{2,14},{4,8},{6,10},{8,4},{10,6},{12,0},{14,2},{1,13},{3,15... | collective-permute-start | bytes 172040 | tf_op jit(solution)/shard_map/ppermute | solution.py:472
  6.6 0.0 collective-permute-start.1
  6.6 0.6 %collective-permute-start = (bf16[8,3584]{1,0:T(8,128)(2,1)S(1)}, bf16[8,3584]{1,0:T(8,128)(2,1)S(1)}, u32[]{:S(2)}, u32[]{:S(2)}) collective-permute-start(bf16[8,3584]{1,0:T(8,128)(2,1)S(1)} %payload.1.refs_0_), channel_id=1, source_target_pairs={{0,4},{2,6},{4,0},{6,2},{8,12},{10,14},{12,8},{14,10},{1,5},{3,7},... | collective-permute-start | bytes 172040 | tf_op jit(solution)/shard_map/ppermute | solution.py:472
  7.2 7.1 %attend_cached.1 = (bf16[40,64,128]{2,1,0:T(8,128)(2,1)S(1)}, f32[40,64,128]{2,1,0:T(8,128)S(1)}, f32[20,128]{1,0:T(8,128)S(1)}, f32[20,128]{1,0:T(8,128)S(1)}) custom-call(s32[48]{0:T(128)} %refs_2_.3, bf16[48,64,128]{2,1,0:T(8,128)(2,1)} %bitcast.3, bf16[48,128,2,2,128]{4,3,2,1,0:T(2,128)(2,1)} %refs_4_.1), custom_call_target="tpu_custom_call" | custom-call | flops 335544320 | bytes 5242880 | tf_op jit(solution)/shard_map/attend_cached/pallas_call | solution.py:199
  14.3 0.0 collective-permute-done.2.refs_3_
  14.3 0.0 collective-permute-done.1.refs_2_
  14.3 0.0 collective-permute-done.refs_1_
  14.4 1.7 %collective-permute-start.3 = (bf16[32,3584]{1,0:T(8,128)(2,1)S(1)}, bf16[32,3584]{1,0:T(8,128)(2,1)S(1)}, u32[]{:S(2)}, u32[]{:S(2)}) collective-permute-start(bf16[32,3584]{1,0:T(8,128)(2,1)S(1)} %join.1.refs_0_), channel_id=1, source_target_pairs={{0,2},{2,0},{4,6},{6,4},{8,10},{10,8},{12,14},{14,12},{1,3},{3,1},... | collective-permute-start | bytes 688136 | tf_op jit(solution)/shard_map/ppermute | solution.py:488
  16.1 6.1 %arrange.1 = (bf16[192,2560]{1,0:T(8,128)(2,1)S(1)}, bf16[4,2560,256]{2,1,0:T(8,128)(2,1)S(1)}, bf16[8,64,128]{2,1,0:T(8,128)(2,1)S(1)}, f32[8,64,128]{2,1,0:T(8...) custom-call(bf16[48,4,2560]{2,1,0:T(4,128)(2,1)} %refs_0_.2, bf16[2560,2,4,128]{3,2,1,0:T(4,128)(2,1)} %refs_1_, ...), custom_call_target="tpu_custom_call" | custom-call | flops 1409286144 | bytes 13500416 | tf_op jit(solution)/shard_map/arrange/pallas_call | solution.py:282
  22.2 0.0 collective-permute-done.3.refs_1_
  22.2 1.4 %project.3 = f32[192,512]{1,0:T(8,128)S(1)} custom-call(bf16[192,2560]{1,0:T(8,128)(2,1)S(1)} %get-tuple-element.30.hidden_ref, bf16[4,2560,256]{2,1,0:T(8,128)(2,1)S(1)} %get-tuple-element.31.base_ref, bf16[32,3584]{1,0:T(8,128)(2,1)S(1)} %join.1.refs_0_, bf16[32,3584]{1,0:T(8,128)(2,1)S(1)} %collective-permute-done.3.refs_1_), custom_call_target="tpu_custom_call" | custom-call | flops 671088640 | bytes 3604480 | tf_op jit(solution)/shard_map/project/pallas_call | solution.py:335
  23.6 0.1 collective-permute-start.4
  23.7 1.4 %project.2.refs_0_ = f32[192,512]{1,0:T(8,128)S(1)} custom-call(bf16[192,2560]{1,0:T(8,128)(2,1)S(1)} %get-tuple-element.30.hidden_ref, bf16[4,2560,256]{2,1,0:T(8,128)(2,1)S(1)} %get-tuple-element.31.base_ref, bf16[32,3584]{1,0:T(8,128)(2,1)S(1)} %join.1.refs_0_, bf16[32,3584]{1,0:T(8,128)(2,1)S(1)} %collective-permute-done.3.refs_1_), custom_call_target="tpu_custom_call" | custom-call | flops 671088640 | bytes 3604480 | tf_op jit(solution)/shard_map/project/pallas_call | solution.py:335
  25.1 0.3 %collective-permute-done.4.refs_1_ = f32[192,512]{1,0:T(8,128)S(1)} collective-permute-done((f32[192,512]{1,0:T(8,128)S(1)}, f32[192,512]{1,0:T(8,128)S(1)}, u32[]{:S(2)}, u32[]{:S(2)}) %collective-permute-start.4) | collective-permute-done | bytes 393248 | tf_op jit(solution)/shard_map/ppermute | solution.py:493
  25.4 2.1 %finish.1 = (bf16[48,4,2,2,128]{4,3,2,1,0:T(2,128)(2,1)}, bf16[48,64,128]{2,1,0:T(8,128)(2,1)}) custom-call(f32[192,512]{1,0:T(8,128)S(1)} %project.2.refs_0_, f32[192,512]{1,0:T(8,128)S(1)} %collective-permute-done.4.refs_1_, bf16[40,64,128]{2,1,0:T(8,128)(2,1)S(1)} %get-tuple-element.36.refs_2_, f32[40,64,128]{2,1,0:T(8,128)S(1)} %get-tuple-element.37.refs_3_, ...), custom_call_target="tpu_custom_call" | custom-call | flops 301989888 | bytes 3145728 | tf_op jit(solution)/shard_map/finish/pallas_call | solution.py:426
  (1 shorter events, 0.0 us)
Async XLA Ops:
  1.5 12.8 %collective-permute-start.2 = (bf16[8,3584]{1,0:T(8,128)(2,1)S(1)}, bf16[8,3584]{1,0:T(8,128)(2,1)S(1)}, u32[]{:S(2)}, u32[]{:S(2)}) collective-permute-start(bf16[8,3584]{1,0:T(8,128)(2,1)S(1)} %payload.1.refs_0_), channel_id=1, source_target_pairs={{0,12},{2,14},{4,8},{6,10},{8,4},{10,6},{12,0},{14,2},{1,13},{3,15... | collective-permute-start | bytes 172040 | tf_op jit(solution)/shard_map/ppermute | solution.py:472
  6.6 7.7 %collective-permute-start.1 = (bf16[8,3584]{1,0:T(8,128)(2,1)S(1)}, bf16[8,3584]{1,0:T(8,128)(2,1)S(1)}, u32[]{:S(2)}, u32[]{:S(2)}) collective-permute-start(bf16[8,3584]{1,0:T(8,128)(2,1)S(1)} %payload.1.refs_0_), channel_id=1, source_target_pairs={{0,8},{2,10},{4,12},{6,14},{8,0},{10,2},{12,4},{14,6},{1,9},{3,11}... | collective-permute-start | bytes 172040 | tf_op jit(solution)/shard_map/ppermute | solution.py:472
  6.6 7.8 %collective-permute-start = (bf16[8,3584]{1,0:T(8,128)(2,1)S(1)}, bf16[8,3584]{1,0:T(8,128)(2,1)S(1)}, u32[]{:S(2)}, u32[]{:S(2)}) collective-permute-start(bf16[8,3584]{1,0:T(8,128)(2,1)S(1)} %payload.1.refs_0_), channel_id=1, source_target_pairs={{0,4},{2,6},{4,0},{6,2},{8,12},{10,14},{12,8},{14,10},{1,5},{3,7},... | collective-permute-start | bytes 172040 | tf_op jit(solution)/shard_map/ppermute | solution.py:472
  14.4 7.9 %collective-permute-start.3 = (bf16[32,3584]{1,0:T(8,128)(2,1)S(1)}, bf16[32,3584]{1,0:T(8,128)(2,1)S(1)}, u32[]{:S(2)}, u32[]{:S(2)}) collective-permute-start(bf16[32,3584]{1,0:T(8,128)(2,1)S(1)} %join.1.refs_0_), channel_id=1, source_target_pairs={{0,2},{2,0},{4,6},{6,4},{8,10},{10,8},{12,14},{14,12},{1,3},{3,1},... | collective-permute-start | bytes 688136 | tf_op jit(solution)/shard_map/ppermute | solution.py:488
  23.6 1.8 %collective-permute-start.4 = (f32[192,512]{1,0:T(8,128)S(1)}, f32[192,512]{1,0:T(8,128)S(1)}, u32[]{:S(2)}, u32[]{:S(2)}) collective-permute-start(f32[192,512]{1,0:T(8,128)S(1)} %project.3), channel_id=1, source_target_pairs={{0,1},{1,0},{2,3},{3,2},{4,5},{5,4},{6,7},{7,6},{8,9},{9,8},{10,11... | collective-permute-start | bytes 1179656 | tf_op jit(solution)/shard_map/ppermute | solution.py:493

commit v16 on v13

--- a/solution.py
+++ b/solution.py
@@ -65,8 +65,7 @@
         self.lengths_hbm, self.queries_hbm, self.cache_hbm = inputs
         self.q, self.sums, self.tops, self.totals = outputs
         self.lengths, self.k, self.v, *rest = scratch
-        self.scores, self.weights = rest[0:2], rest[2:4]
-        self.sems, self.length_sem = rest[4:]
+        self.scores, self.weights, self.sems, self.length_sem = rest
         self.rows, self.queries, self.size = self.q.shape
         self.slots, self.own = self.k.shape[1:3]
         self.keys = self.slots * self.own
@@ -90,14 +89,12 @@
     def scratch(rows, chunk, many, cache, lengths):
         slots, own, size = cache.shape[1], cache.shape[3], cache.shape[4]
         half = (rows, slots, own, size)
-        scores = (chunk // 2, slots * own, 2 * many)
+        scores = (2, chunk // 2, slots * own, 2 * many)
         return [
             pltpu.SMEM(lengths.shape, jnp.int32),
             pltpu.VMEM(half, jnp.bfloat16),
             pltpu.VMEM(half, jnp.bfloat16),
             pltpu.VMEM(scores, jnp.float32),
-            pltpu.VMEM(scores, jnp.float32),
-            pltpu.VMEM(scores, jnp.bfloat16),
             pltpu.VMEM(scores, jnp.bfloat16),
             pltpu.SemaphoreType.DMA((rows // chunk, 3)),
             pltpu.SemaphoreType.DMA,
@@ -137,7 +134,7 @@
                 ],
                 axis=0,
             )
-            self.scores[slot][p] = lax.dot_general(
+            self.scores[slot, p] = lax.dot_general(
                 self.lines(self.k, r), both_q, NT, preferred_element_type=jnp.float32
             )
 
@@ -145,10 +142,10 @@
         for p in range(self.chunk // 2):
             r = self.first + i * self.chunk + 2 * p
             limit = jnp.where(self.one, self.own * self.lengths[r], self.own * self.lengths[r + 1])
-            scores = jnp.where(self.line < limit, self.scores[slot][p], LOW)
+            scores = jnp.where(self.line < limit, self.scores[slot, p], LOW)
             top = jnp.max(scores, axis=0, keepdims=True)
             expo = jnp.exp((scores - top) * self.scale)
-            self.weights[slot][p] = expo.astype(jnp.bfloat16)
+            self.weights[slot, p] = expo.astype(jnp.bfloat16)
             pair = pl.ds(i * (self.chunk // 2) + p, 1)
             self.tops[pair, :] = top
             self.totals[pair, :] = jnp.sum(expo, axis=0, keepdims=True)
@@ -158,7 +155,7 @@
         for p in range(self.chunk // 2):
             r = i * self.chunk + 2 * p
             both = lax.dot_general(
-                self.weights[slot][p], self.lines(self.v, r), TN, preferred_element_type=jnp.float32
+                self.weights[slot, p], self.lines(self.v, r), TN, preferred_element_type=jnp.float32
             )
             for h in range(2):
                 self.sums[r + h] = both[h * queries : (h + 1) * queries, h * size : (h + 1) * size]
@@ -171,31 +168,24 @@
     for i in range(chunks):
         cached.start(i)
     cached.lengths_copy().wait()
-    cached.arrive(0)
-    cached.score(0, 0)
-    cached.arrive(1)
-    cached.score(1, 1)
-    cached.soften(0, 0)
-
-    @pl.loop(1, chunks // 2)
-    def _(t):
-        for slot in range(2):
-            i = 2 * t + slot
+
+    @pl.loop(0, chunks + 2)
+    def _(i):
+        @pl.when(i < chunks)
+        def _():
             cached.arrive(i)
-            cached.score(i, slot)
-            cached.soften(i - 1, 1 - slot)
-            cached.collect(i - 2, slot)
-
-    cached.soften(chunks - 1, 1)
-    cached.collect(chunks - 2, 0)
-    cached.collect(chunks - 1, 1)
-
-
-def attend_cached(queries, cache, lengths, rows):
-    _, steps, heads, size = queries.shape
+
+        slot = i % 2
+        cached.collect(jnp.clip(i - 2, 0, chunks - 1), slot)
+        cached.soften(jnp.clip(i - 1, 0, chunks - 1), 1 - slot)
+        cached.score(jnp.minimum(i, chunks - 1), slot)
+
+
+def attend_cached(queries, cache, lengths):
+    rows, steps, heads, size = queries.shape
     slots, own = cache.shape[1], cache.shape[3]
     many = steps * heads
-    chunk = 4
+    chunk = 6
     return pl.pallas_call(
         functools.partial(cached_kernel, chunk, heads, size ** (-0.5)),
         out_shape=Cached.outputs(rows, many, size),
@@ -210,11 +200,7 @@
     )(*map(in_hbm, (lengths, queries.reshape(-1, many, size), cache)))
 
 
-def arrange_kernel(first, chunk, chunks, own, heads, scale, *refs):
-    hidden_hbm, base_hbm = refs[:2]
-    tokens_ref, base_ref = refs[5:7]
-    hidden, base, sems = refs[11:14]
-    cached = Cached(first, chunk, heads, scale, refs[2:5], refs[7:11], refs[14:])
+def arrange_kernel(chunks, own, hidden_hbm, base_hbm, tokens_ref, base_ref, hidden, base, sems):
     width, two, kvh, size = base.shape
     groups = two * kvh
     some_width = width // chunks
@@ -224,12 +210,7 @@
         return pltpu.make_async_copy(base_hbm.at[features], base.at[features], sems.at[i])
 
     get_hidden = pltpu.make_async_copy(hidden_hbm, hidden, sems.at[chunks])
-    cached.lengths_copy().start()
-    copy(0).start()
-    cached.start(0)
-    copy(1).start()
-    cached.start(1)
-    for i in range(2, chunks):
+    for i in range(chunks):
         copy(i).start()
     get_hidden.start()
 
@@ -241,64 +222,47 @@
     flat_base = base.reshape(width * groups, size)
 
     def arrange(f):
-        at = f * groups
-        pair = jnp.concatenate([flat_base[at + h * tile : at + (h + 1) * tile, :] for h in range(2)], axis=1)
+        at = pl.multiple_of(f * groups, tile)
+        pair = jnp.concatenate([flat_base[pl.ds(at + h * tile, tile), :] for h in range(2)], axis=1)
         moved = jnp.dot(order, pair, preferred_element_type=jnp.float32).astype(jnp.bfloat16)
         for n in range(groups):
             lanes = slice((n % own) * size, (n % own + 1) * size)
             for h in range(2):
-                base_ref[n // own, f + h * some : f + (h + 1) * some, lanes] = moved[
+                base_ref[n // own, pl.ds(pl.multiple_of(f + h * some, some), some), lanes] = moved[
                     n * some : (n + 1) * some, h * size : (h + 1) * size
                 ]
 
-    cached.lengths_copy().wait()
-    for i in range(chunks):
+    @pl.loop(0, chunks)
+    def _(i):
         copy(i).wait()
-        if i < 2:
-            cached.arrive(i)
-            cached.score(i, i)
-        if 1 <= i < 3:
-            cached.soften(i - 1, i - 1)
-        if 2 <= i < 4:
-            cached.collect(i - 2, i - 2)
-        for f in range(i * some_width, (i + 1) * some_width, 2 * some):
-            arrange(f)
+        for f in range(0, some_width, 2 * some):
+            arrange(i * some_width + f)
+
     get_hidden.wait()
     tokens_ref[...] = hidden.reshape(tokens_ref.shape)[...]
 
 
-def arrange(hidden, base, queries, cache, lengths, rows):
-    _, steps, heads, size = queries.shape
-    slots, own = cache.shape[1], cache.shape[3]
-    many = steps * heads
+def arrange(hidden, base, own):
+    rows, steps, _ = hidden.shape
     width, two, kvh, size = base.shape
     chunks = 4
-    rest = hidden.shape[0] - rows
-    chunk = rest // 2
-    outs = (
-        pltpu.VMEM((hidden.shape[0] * steps, width), jnp.bfloat16),
-        pltpu.VMEM((two * kvh // own, width, own * size), jnp.bfloat16),
-    ) + Cached.outputs(rest, many, size)
-    tokens, base, *state = pl.pallas_call(
-        functools.partial(arrange_kernel, rows, chunk, chunks, own, heads, size ** (-0.5)),
-        out_shape=outs,
-        in_specs=[pl.BlockSpec(memory_space=pltpu.HBM)] * 5,
-        out_specs=(VMEM,) * len(outs),
+    return pl.pallas_call(
+        functools.partial(arrange_kernel, chunks, own),
+        out_shape=(
+            pltpu.VMEM((rows * steps, width), jnp.bfloat16),
+            pltpu.VMEM((two * kvh // own, width, own * size), jnp.bfloat16),
+        ),
+        in_specs=[pl.BlockSpec(memory_space=pltpu.HBM)] * 2,
+        out_specs=(VMEM, VMEM),
         scratch_shapes=[
             pltpu.VMEM(hidden.shape, jnp.bfloat16),
             pltpu.VMEM(base.shape, jnp.bfloat16),
             pltpu.SemaphoreType.DMA((chunks + 1,)),
-        ]
-        + Cached.scratch(rest, chunk, many, cache, lengths),
-        compiler_params=params(28),
-        cost_estimate=cost(
-            512 * base.size + 8 * rest * many * slots * size,
-            4 * (base.size + hidden.size + rest * slots * own * size),
-            rest * many * slots * own,
-        ),
+        ],
+        compiler_params=params(20),
+        cost_estimate=cost(512 * base.size, 4 * (base.size + hidden.size)),
         name="arrange",
-    )(*map(in_hbm, (hidden, base, lengths, queries.reshape(-1, many, size), cache)))
-    return tokens, base, state
+    )(in_hbm(hidden), in_hbm(base))
 
 
 def project_kernel(k, hidden_ref, base_ref, *refs):
@@ -346,7 +310,8 @@
 
 def finish_kernel(steps, heads, scale, terms, *refs):
     parts, refs = refs[:terms], refs[terms:]
-    states, refs = (refs[:4], refs[4:8]), refs[8:]
+    q_ref, old_ref, top_ref, total_ref = refs[:4]
+    refs = refs[4:]
     fresh_hbm, context_hbm, wide, fresh_ref, context_ref, sems = refs
     rows, queries, size = context_ref.shape
     own = fresh_ref.shape[3]
@@ -367,24 +332,19 @@
         lines = [fresh[tokens, (c * own + g) * size : (c * own + g + 1) * size] for g in range(own)]
         return jnp.concatenate(lines, axis=0).astype(jnp.bfloat16)
 
-    def old(n, pair):
-        count = states[0][0].shape[0] // 2
-        return (states[0][n], pair) if pair < count else (states[1][n], pair - count)
-
-    def rows_of(n, pair):
-        ref, at = old(n, pair)
-        return ref[2 * at : 2 * at + 2].reshape(many, size)
+    def rows_of(ref, pair):
+        return ref[2 * pair : 2 * pair + 2].reshape(many, size)
 
     scores = [
-        lax.dot_general(new_lines(0, p), rows_of(0, p), NT, preferred_element_type=jnp.float32)
+        lax.dot_general(new_lines(0, p), rows_of(q_ref, p), NT, preferred_element_type=jnp.float32)
         for p in range(rows // 2)
     ]
     scores = jnp.stack([jnp.where(live, s, LOW) for s in scores])
-    old_top, old_total = [jnp.concatenate([states[0][n][...], states[1][n][...]], axis=0) for n in (2, 3)]
+    old_top = top_ref[...]
     top = jnp.maximum(old_top, jnp.max(scores, axis=1))
     expo = jnp.exp((scores - top[:, None, :]) * scale)
     back = jnp.exp((old_top - top) * scale)
-    inverse = 1.0 / (back * old_total + jnp.sum(expo, axis=1))
+    inverse = 1.0 / (back * total_ref[...] + jnp.sum(expo, axis=1))
     weights = (expo * inverse[:, None, :]).astype(jnp.bfloat16)
     back = back * inverse
 
@@ -408,7 +368,7 @@
         )
         factors = back[at : at + group].T
         for n, p in enumerate(pairs):
-            both = new[:, n * size : (n + 1) * size] + factors[:, n : n + 1] * rows_of(1, p)
+            both = new[:, n * size : (n + 1) * size] + factors[:, n : n + 1] * rows_of(old_ref, p)
             context_ref[2 * p : 2 * p + 2] = both.astype(jnp.bfloat16).reshape(2, queries, size)
         mine = pl.ds(2 * at, 2 * group)
         puts.append(pltpu.make_async_copy(context_ref.at[mine], context_hbm.at[mine], sems.at[1 + at // group]))
@@ -417,9 +377,8 @@
         put.wait()
 
 
-def finish(parts, states, steps, own):
-    _, many, size = states[0][0].shape
-    rows = sum(state[0].shape[0] for state in states)
+def finish(parts, state, steps, own):
+    rows, many, size = state[0].shape
     heads = many // steps
     groups = rows * own * steps // size
     fresh = (rows, steps, 2, own, size)
@@ -429,7 +388,7 @@
             jax.ShapeDtypeStruct(fresh, jnp.bfloat16),
             jax.ShapeDtypeStruct((rows, many, size), jnp.bfloat16),
         ),
-        in_specs=[VMEM] * (len(parts) + 8),
+        in_specs=[VMEM] * (len(parts) + 4),
         out_specs=(pl.BlockSpec(memory_space=pltpu.HBM),) * 2,
         scratch_shapes=[
             pltpu.VMEM((rows * steps * 2 * own, size), jnp.float32),
@@ -440,7 +399,7 @@
         compiler_params=params(24),
         cost_estimate=cost(rows * many * size * size * 6, 8 * rows * many * size, rows * many * size * 2),
         name="finish",
-    )(*parts, *states[0], *states[1])
+    )(*parts, *state)
     return fresh, context.reshape(rows, steps, heads, size)
 
 
@@ -480,19 +439,18 @@
 def shards(dp, tp, hidden, base_weight, factor_a, factor_b, queries, cache, lengths):
     steps, own = queries.shape[1], cache.shape[3]
     assert dp % 2 == 0
-    early = queries.shape[0] * 2 // 3
     blocks = gather_second(factor_a, factor_b, dp)
-    state = attend_cached(queries, cache, lengths, early)
+    state = attend_cached(queries, cache, lengths)
     blocks, state, hidden, base_weight = lax.optimization_barrier((blocks, state, hidden, base_weight))
     gathered = join(blocks) if len(blocks) > 1 else blocks[0]
     gathered = [gathered, lax.ppermute(gathered, "dp", [(i, i ^ 1) for i in range(dp)])]
-    tokens, base, late = arrange(hidden, base_weight, queries, cache, lengths, early)
+    tokens, base = arrange(hidden, base_weight, own)
     received = []
     for k in range(1, tp):
         other = project(k, tokens, base, gathered)
         received.append(lax.ppermute(other, "tp", [(i, i ^ k) for i in range(tp)]))
     mine = project(0, tokens, base, gathered)
-    return finish([mine] + received, [state, late], steps, own)
+    return finish([mine] + received, state, steps, own)
 
 
 def solution(mesh):

time: 25.9 us -> 26.5 us (1.023)
  waiting for transfers between devices: 0.32 us -> 1.69 us
  Pallas kernels: 17 us -> 16.3 us
    pallas_call x1, Pallas kernels: 6.18 us -> 3.76 us  [arrange(): pl.pallas_call(functools.partial(arrange_kernel, chunks, own), out_shape=...]
    pallas_call x1, Pallas kernels: 5.2 us -> 6.94 us  [attend_cached(): pl.pallas_call(functools.partial(cached_kernel, chunk, heads, size ** (-0...]
    ppermute x1, waiting for transfers between devices: 0.01 us -> 1.36 us  [shards(): lax.ppermute(gathered, 'dp', [(i, i ^ 1) for i in range(dp)])]
  transfers between devices with their start and end apart: 5 -> 5, of which waited for: 1 -> 2; matrix products, arithmetic and copies ran while one was open for 0% -> 0% of each run, Pallas kernels for 50% -> 46%
where the time goes in v16:
time: 26.5 us; the launch traced here: 26.3 us
  Pallas kernels  16.3 us (62%)
  starting transfers between devices  7.55 us (28%)
  waiting for transfers between devices  1.69 us (6%)
  between operations  0.71 us (3%)
    pallas_call x1, Pallas kernels, attend_cached(): pl.pallas_call(functools.partial(cached_kernel, chunk, heads, size ** (-0...  6.94 us
    ppermute x3, starting transfers between devices, gather_second(): lax.ppermute(payload, 'dp', [(i, i ^ 2 * k) for i in range(dp)])  5.76 us
    pallas_call x1, Pallas kernels, arrange(): pl.pallas_call(functools.partial(arrange_kernel, chunks, own), out_shape=...  3.76 us
    pallas_call x2, Pallas kernels, project(): pl.pallas_call(functools.partial(project_kernel, k), out_shape=pltpu.VMEM...  2.75 us
    pallas_call x1, Pallas kernels, finish(): pl.pallas_call(functools.partial(finish_kernel, steps, heads, size ** (-0...  2.05 us
    ppermute x1, starting transfers between devices, shards(): lax.ppermute(gathered, 'dp', [(i, i ^ 1) for i in range(dp)])  1.73 us
    ppermute x1, waiting for transfers between devices, shards(): lax.ppermute(gathered, 'dp', [(i, i ^ 1) for i in range(dp)])  1.36 us
    pallas_call x1, Pallas kernels, make_payload(): pl.pallas_call(payload_kernel, out_shape=pltpu.VMEM((ranks, width + group...  0.81 us
  transfers between devices with their start and end apart: 5, of which 2 were waited for; matrix products, arithmetic and copies ran while one was open for 0% of the time, Pallas kernels for 46%

profile of v16, /device:TPU:0, one launch (start us, length us, event | category | flops | bytes accessed | tf_op | source)
XLA Modules:
  0.0 26.3 jit_solution(4809829234707454351)
XLA Ops:
  0.6 0.8 %payload.1.refs_0_ = bf16[8,3584]{1,0:T(8,128)(2,1)S(1)} custom-call(bf16[8,2560]{1,0:T(8,128)(2,1)} %bitcast.4, bf16[8,2,4,128]{3,2,1,0:T(4,128)(2,1)} %up_hbm.1), custom_call_target="tpu_custom_call" | custom-call | tf_op jit(solution)/shard_map/payload/pallas_call | solution.py:47
  1.5 5.1 %collective-permute-start.2 = (bf16[8,3584]{1,0:T(8,128)(2,1)S(1)}, bf16[8,3584]{1,0:T(8,128)(2,1)S(1)}, u32[]{:S(2)}, u32[]{:S(2)}) collective-permute-start(bf16[8,3584]{1,0:T(8,128)(2,1)S(1)} %payload.1.refs_0_), channel_id=1, source_target_pairs={{0,12},{2,14},{4,8},{6,10},{8,4},{10,6},{12,0},{14,2},{1,13},{3,15... | collective-permute-start | bytes 172040 | tf_op jit(solution)/shard_map/ppermute | solution.py:431
  6.6 0.0 collective-permute-start.1
  6.6 0.6 %collective-permute-start = (bf16[8,3584]{1,0:T(8,128)(2,1)S(1)}, bf16[8,3584]{1,0:T(8,128)(2,1)S(1)}, u32[]{:S(2)}, u32[]{:S(2)}) collective-permute-start(bf16[8,3584]{1,0:T(8,128)(2,1)S(1)} %payload.1.refs_0_), channel_id=1, source_target_pairs={{0,4},{2,6},{4,0},{6,2},{8,12},{10,14},{12,8},{14,10},{1,5},{3,7},... | collective-permute-start | bytes 172040 | tf_op jit(solution)/shard_map/ppermute | solution.py:431
  7.2 6.9 %attend_cached.1 = (bf16[48,64,128]{2,1,0:T(8,128)(2,1)S(1)}, f32[48,64,128]{2,1,0:T(8,128)S(1)}, f32[24,128]{1,0:T(8,128)S(1)}, f32[24,128]{1,0:T(8,128)S(1)}) custom-call(s32[48]{0:T(128)} %refs_0_.1, bf16[48,64,128]{2,1,0:T(8,128)(2,1)} %bitcast.3, bf16[48,128,2,2,128]{4,3,2,1,0:T(2,128)(2,1)} %refs_2_.1), custom_call_target="tpu_custom_call" | custom-call | flops 402653184 | bytes 6291456 | tf_op jit(solution)/shard_map/attend_cached/pallas_call | solution.py:189
  14.2 0.0 collective-permute-done.2.refs_3_
  14.2 0.0 collective-permute-done.1.refs_2_
  14.2 0.0 collective-permute-done.refs_1_
  14.2 1.7 %collective-permute-start.3 = (bf16[32,3584]{1,0:T(8,128)(2,1)S(1)}, bf16[32,3584]{1,0:T(8,128)(2,1)S(1)}, u32[]{:S(2)}, u32[]{:S(2)}) collective-permute-start(bf16[32,3584]{1,0:T(8,128)(2,1)S(1)} %join.1.refs_0_), channel_id=1, source_target_pairs={{0,2},{2,0},{4,6},{6,4},{8,10},{10,8},{12,14},{14,12},{1,3},{3,1},... | collective-permute-start | bytes 688136 | tf_op jit(solution)/shard_map/ppermute | solution.py:446
  15.9 3.8 %arrange.1 = (bf16[192,2560]{1,0:T(8,128)(2,1)S(1)}, bf16[4,2560,256]{2,1,0:T(8,128)(2,1)S(1)}) custom-call(bf16[48,4,2560]{2,1,0:T(4,128)(2,1)} %hidden_hbm, bf16[2560,2,4,128]{3,2,1,0:T(4,128)(2,1)} %base_hbm), custom_call_target="tpu_custom_call" | custom-call | flops 1342177280 | bytes 12451840 | tf_op jit(solution)/shard_map/arrange/pallas_call | solution.py:249
  19.7 1.4 %collective-permute-done.3.refs_1_ = bf16[32,3584]{1,0:T(8,128)(2,1)S(1)} collective-permute-done((bf16[32,3584]{1,0:T(8,128)(2,1)S(1)}, bf16[32,3584]{1,0:T(8,128)(2,1)S(1)}, u32[]{:S(2)}, u32[]{:S(2)}) %collective-permute-start.3) | collective-permute-done | bytes 229408 | tf_op jit(solution)/shard_map/ppermute | solution.py:446
  21.1 1.4 %project.3 = f32[192,512]{1,0:T(8,128)S(1)} custom-call(bf16[192,2560]{1,0:T(8,128)(2,1)S(1)} %get-tuple-element.26.hidden_ref, bf16[4,2560,256]{2,1,0:T(8,128)(2,1)S(1)} %get-tuple-element.27.base_ref, bf16[32,3584]{1,0:T(8,128)(2,1)S(1)} %join.1.refs_0_, bf16[32,3584]{1,0:T(8,128)(2,1)S(1)} %collective-permute-done.3.refs_1_), custom_call_target="tpu_custom_call" | custom-call | flops 671088640 | bytes 3604480 | tf_op jit(solution)/shard_map/project/pallas_call | solution.py:299
  22.4 0.1 collective-permute-start.4
  22.5 1.4 %project.2.refs_0_ = f32[192,512]{1,0:T(8,128)S(1)} custom-call(bf16[192,2560]{1,0:T(8,128)(2,1)S(1)} %get-tuple-element.26.hidden_ref, bf16[4,2560,256]{2,1,0:T(8,128)(2,1)S(1)} %get-tuple-element.27.base_ref, bf16[32,3584]{1,0:T(8,128)(2,1)S(1)} %join.1.refs_0_, bf16[32,3584]{1,0:T(8,128)(2,1)S(1)} %collective-permute-done.3.refs_1_), custom_call_target="tpu_custom_call" | custom-call | flops 671088640 | bytes 3604480 | tf_op jit(solution)/shard_map/project/pallas_call | solution.py:299
  23.9 0.3 %collective-permute-done.4.refs_1_ = f32[192,512]{1,0:T(8,128)S(1)} collective-permute-done((f32[192,512]{1,0:T(8,128)S(1)}, f32[192,512]{1,0:T(8,128)S(1)}, u32[]{:S(2)}, u32[]{:S(2)}) %collective-permute-start.4) | collective-permute-done | bytes 393248 | tf_op jit(solution)/shard_map/ppermute | solution.py:451
  24.2 2.0 %finish.1 = (bf16[48,4,2,2,128]{4,3,2,1,0:T(2,128)(2,1)}, bf16[48,64,128]{2,1,0:T(8,128)(2,1)}) custom-call(f32[192,512]{1,0:T(8,128)S(1)} %project.2.refs_0_, f32[192,512]{1,0:T(8,128)S(1)} %collective-permute-done.4.refs_1_, bf16[48,64,128]{2,1,0:T(8,128)(2,1)S(1)} %get-tuple-element.32.refs_2_, f32[48,64,128]{2,1,0:T(8,128)S(1)} %get-tuple-element.33.refs_3_, ...), custom_call_target="tpu_custom_call" | custom-call | flops 301989888 | bytes 3145728 | tf_op jit(solution)/shard_map/finish/pallas_call | solution.py:385
  (1 shorter events, 0.0 us)
Async XLA Ops:
  1.5 12.7 %collective-permute-start.2 = (bf16[8,3584]{1,0:T(8,128)(2,1)S(1)}, bf16[8,3584]{1,0:T(8,128)(2,1)S(1)}, u32[]{:S(2)}, u32[]{:S(2)}) collective-permute-start(bf16[8,3584]{1,0:T(8,128)(2,1)S(1)} %payload.1.refs_0_), channel_id=1, source_target_pairs={{0,12},{2,14},{4,8},{6,10},{8,4},{10,6},{12,0},{14,2},{1,13},{3,15... | collective-permute-start | bytes 172040 | tf_op jit(solution)/shard_map/ppermute | solution.py:431
  6.6 7.6 %collective-permute-start.1 = (bf16[8,3584]{1,0:T(8,128)(2,1)S(1)}, bf16[8,3584]{1,0:T(8,128)(2,1)S(1)}, u32[]{:S(2)}, u32[]{:S(2)}) collective-permute-start(bf16[8,3584]{1,0:T(8,128)(2,1)S(1)} %payload.1.refs_0_), channel_id=1, source_target_pairs={{0,8},{2,10},{4,12},{6,14},{8,0},{10,2},{12,4},{14,6},{1,9},{3,11}... | collective-permute-start | bytes 172040 | tf_op jit(solution)/shard_map/ppermute | solution.py:431
  6.6 7.6 %collective-permute-start = (bf16[8,3584]{1,0:T(8,128)(2,1)S(1)}, bf16[8,3584]{1,0:T(8,128)(2,1)S(1)}, u32[]{:S(2)}, u32[]{:S(2)}) collective-permute-start(bf16[8,3584]{1,0:T(8,128)(2,1)S(1)} %payload.1.refs_0_), channel_id=1, source_target_pairs={{0,4},{2,6},{4,0},{6,2},{8,12},{10,14},{12,8},{14,10},{1,5},{3,7},... | collective-permute-start | bytes 172040 | tf_op jit(solution)/shard_map/ppermute | solution.py:431
  14.2 6.9 %collective-permute-start.3 = (bf16[32,3584]{1,0:T(8,128)(2,1)S(1)}, bf16[32,3584]{1,0:T(8,128)(2,1)S(1)}, u32[]{:S(2)}, u32[]{:S(2)}) collective-permute-start(bf16[32,3584]{1,0:T(8,128)(2,1)S(1)} %join.1.refs_0_), channel_id=1, source_target_pairs={{0,2},{2,0},{4,6},{6,4},{8,10},{10,8},{12,14},{14,12},{1,3},{3,1},... | collective-permute-start | bytes 688136 | tf_op jit(solution)/shard_map/ppermute | solution.py:446
  22.4 1.8 %collective-permute-start.4 = (f32[192,512]{1,0:T(8,128)S(1)}, f32[192,512]{1,0:T(8,128)S(1)}, u32[]{:S(2)}, u32[]{:S(2)}) collective-permute-start(f32[192,512]{1,0:T(8,128)S(1)} %project.3), channel_id=1, source_target_pairs={{0,1},{1,0},{2,3},{3,2},{4,5},{5,4},{6,7},{7,6},{8,9},{9,8},{10,11... | collective-permute-start | bytes 1179656 | tf_op jit(solution)/shard_map/ppermute | solution.py:451

commit v17 on v16

--- a/solution.py
+++ b/solution.py
@@ -65,7 +65,8 @@
         self.lengths_hbm, self.queries_hbm, self.cache_hbm = inputs
         self.q, self.sums, self.tops, self.totals = outputs
         self.lengths, self.k, self.v, *rest = scratch
-        self.scores, self.weights, self.sems, self.length_sem = rest
+        self.scores, self.weights = rest[0:2], rest[2:4]
+        self.sems, self.length_sem = rest[4:]
         self.rows, self.queries, self.size = self.q.shape
         self.slots, self.own = self.k.shape[1:3]
         self.keys = self.slots * self.own
@@ -89,12 +90,14 @@
     def scratch(rows, chunk, many, cache, lengths):
         slots, own, size = cache.shape[1], cache.shape[3], cache.shape[4]
         half = (rows, slots, own, size)
-        scores = (2, chunk // 2, slots * own, 2 * many)
+        scores = (chunk // 2, slots * own, 2 * many)
         return [
             pltpu.SMEM(lengths.shape, jnp.int32),
             pltpu.VMEM(half, jnp.bfloat16),
             pltpu.VMEM(half, jnp.bfloat16),
             pltpu.VMEM(scores, jnp.float32),
+            pltpu.VMEM(scores, jnp.float32),
+            pltpu.VMEM(scores, jnp.bfloat16),
             pltpu.VMEM(scores, jnp.bfloat16),
             pltpu.SemaphoreType.DMA((rows // chunk, 3)),
             pltpu.SemaphoreType.DMA,
@@ -134,7 +137,7 @@
                 ],
                 axis=0,
             )
-            self.scores[slot, p] = lax.dot_general(
+            self.scores[slot][p] = lax.dot_general(
                 self.lines(self.k, r), both_q, NT, preferred_element_type=jnp.float32
             )
 
@@ -142,10 +145,10 @@
         for p in range(self.chunk // 2):
             r = self.first + i * self.chunk + 2 * p
             limit = jnp.where(self.one, self.own * self.lengths[r], self.own * self.lengths[r + 1])
-            scores = jnp.where(self.line < limit, self.scores[slot, p], LOW)
+            scores = jnp.where(self.line < limit, self.scores[slot][p], LOW)
             top = jnp.max(scores, axis=0, keepdims=True)
             expo = jnp.exp((scores - top) * self.scale)
-            self.weights[slot, p] = expo.astype(jnp.bfloat16)
+            self.weights[slot][p] = expo.astype(jnp.bfloat16)
             pair = pl.ds(i * (self.chunk // 2) + p, 1)
             self.tops[pair, :] = top
             self.totals[pair, :] = jnp.sum(expo, axis=0, keepdims=True)
@@ -155,7 +158,7 @@
         for p in range(self.chunk // 2):
             r = i * self.chunk + 2 * p
             both = lax.dot_general(
-                self.weights[slot, p], self.lines(self.v, r), TN, preferred_element_type=jnp.float32
+                self.weights[slot][p], self.lines(self.v, r), TN, preferred_element_type=jnp.float32
             )
             for h in range(2):
                 self.sums[r + h] = both[h * queries : (h + 1) * queries, h * size : (h + 1) * size]
@@ -168,17 +171,24 @@
     for i in range(chunks):
         cached.start(i)
     cached.lengths_copy().wait()
-
-    @pl.loop(0, chunks + 2)
-    def _(i):
-        @pl.when(i < chunks)
-        def _():
+    cached.arrive(0)
+    cached.score(0, 0)
+    cached.arrive(1)
+    cached.score(1, 1)
+    cached.soften(0, 0)
+
+    @pl.loop(1, chunks // 2)
+    def _(t):
+        for slot in range(2):
+            i = 2 * t + slot
             cached.arrive(i)
-
-        slot = i % 2
-        cached.collect(jnp.clip(i - 2, 0, chunks - 1), slot)
-        cached.soften(jnp.clip(i - 1, 0, chunks - 1), 1 - slot)
-        cached.score(jnp.minimum(i, chunks - 1), slot)
+            cached.score(i, slot)
+            cached.soften(i - 1, 1 - slot)
+            cached.collect(i - 2, slot)
+
+    cached.soften(chunks - 1, 1)
+    cached.collect(chunks - 2, 0)
+    cached.collect(chunks - 1, 1)
 
 
 def attend_cached(queries, cache, lengths):
@@ -440,11 +450,11 @@
     steps, own = queries.shape[1], cache.shape[3]
     assert dp % 2 == 0
     blocks = gather_second(factor_a, factor_b, dp)
-    state = attend_cached(queries, cache, lengths)
-    blocks, state, hidden, base_weight = lax.optimization_barrier((blocks, state, hidden, base_weight))
+    tokens, base = arrange(hidden, base_weight, own)
+    blocks, tokens, base, cache = lax.optimization_barrier((blocks, tokens, base, cache))
     gathered = join(blocks) if len(blocks) > 1 else blocks[0]
     gathered = [gathered, lax.ppermute(gathered, "dp", [(i, i ^ 1) for i in range(dp)])]
-    tokens, base = arrange(hidden, base_weight, own)
+    state = attend_cached(queries, cache, lengths)
     received = []
     for k in range(1, tp):
         other = project(k, tokens, base, gathered)

time: 26.5 us -> 30.2 us (1.14)
  waiting for transfers between devices: 1.69 us -> 5.76 us
    ppermute x1, waiting for transfers between devices: 1.36 us -> 5.1 us  [shards(): lax.ppermute(gathered, 'dp', [(i, i ^ 1) for i in range(dp)])]
    ppermute x3, waiting for transfers between devices: 0.01 us -> 0.66 us  [gather_second(): lax.ppermute(payload, 'dp', [(i, i ^ 2 * k) for i in range(dp)])]
    pallas_call x1, Pallas kernels: 6.94 us -> 6.56 us  [attend_cached(): pl.pallas_call(functools.partial(cached_kernel, chunk, heads, size ** (-0...]
    ppermute x1, waiting for transfers between devices: 0.32 us -> 0.01 us  [shards(): received.append(lax.ppermute(other, 'tp', [(i, i ^ k) for i in range(tp)]))]
  transfers between devices with their start and end apart: 5 -> 5, of which waited for: 2 -> 2; matrix products, arithmetic and copies ran while one was open for 0% -> 0% of each run, Pallas kernels for 46% -> 39%
where the time goes in v17:
time: 30.2 us; the launch traced here: 29.9 us
  Pallas kernels  16 us (53%)
  starting transfers between devices  7.44 us (25%)
  waiting for transfers between devices  5.76 us (19%)
  between operations  0.7 us (2%)
    pallas_call x1, Pallas kernels, attend_cached(): pl.pallas_call(functools.partial(cached_kernel, chunk, heads, size ** (-0...  6.56 us
    ppermute x3, starting transfers between devices, gather_second(): lax.ppermute(payload, 'dp', [(i, i ^ 2 * k) for i in range(dp)])  5.76 us
    ppermute x1, waiting for transfers between devices, shards(): lax.ppermute(gathered, 'dp', [(i, i ^ 1) for i in range(dp)])  5.1 us
    pallas_call x1, Pallas kernels, arrange(): pl.pallas_call(functools.partial(arrange_kernel, chunks, own), out_shape=...  3.76 us
    pallas_call x2, Pallas kernels, project(): pl.pallas_call(functools.partial(project_kernel, k), out_shape=pltpu.VMEM...  2.76 us
    pallas_call x1, Pallas kernels, finish(): pl.pallas_call(functools.partial(finish_kernel, steps, heads, size ** (-0...  2.06 us
    ppermute x1, starting transfers between devices, shards(): lax.ppermute(gathered, 'dp', [(i, i ^ 1) for i in range(dp)])  1.61 us
    pallas_call x1, Pallas kernels, make_payload(): pl.pallas_call(payload_kernel, out_shape=pltpu.VMEM((ranks, width + group...  0.81 us
  transfers between devices with their start and end apart: 5, of which 2 were waited for; matrix products, arithmetic and copies ran while one was open for 0% of the time, Pallas kernels for 39%

profile of v17, /device:TPU:0, one launch (start us, length us, event | category | flops | bytes accessed | tf_op | source)
XLA Modules:
  0.0 29.9 jit_solution(16347136131770061386)
XLA Ops:
  0.6 0.8 %payload.1.refs_0_ = bf16[8,3584]{1,0:T(8,128)(2,1)S(1)} custom-call(bf16[8,2560]{1,0:T(8,128)(2,1)} %bitcast.4, bf16[8,2,4,128]{3,2,1,0:T(4,128)(2,1)} %up_hbm.1), custom_call_target="tpu_custom_call" | custom-call | tf_op jit(solution)/shard_map/payload/pallas_call | solution.py:47
  1.5 5.1 %collective-permute-start.2 = (bf16[8,3584]{1,0:T(8,128)(2,1)S(1)}, bf16[8,3584]{1,0:T(8,128)(2,1)S(1)}, u32[]{:S(2)}, u32[]{:S(2)}) collective-permute-start(bf16[8,3584]{1,0:T(8,128)(2,1)S(1)} %payload.1.refs_0_), channel_id=1, source_target_pairs={{0,12},{2,14},{4,8},{6,10},{8,4},{10,6},{12,0},{14,2},{1,13},{3,15... | collective-permute-start | bytes 172040 | tf_op jit(solution)/shard_map/ppermute | solution.py:441
  6.6 0.0 collective-permute-start.1
  6.6 0.6 %collective-permute-start = (bf16[8,3584]{1,0:T(8,128)(2,1)S(1)}, bf16[8,3584]{1,0:T(8,128)(2,1)S(1)}, u32[]{:S(2)}, u32[]{:S(2)}) collective-permute-start(bf16[8,3584]{1,0:T(8,128)(2,1)S(1)} %payload.1.refs_0_), channel_id=1, source_target_pairs={{0,4},{2,6},{4,0},{6,2},{8,12},{10,14},{12,8},{14,10},{1,5},{3,7},... | collective-permute-start | bytes 172040 | tf_op jit(solution)/shard_map/ppermute | solution.py:441
  7.2 3.8 %arrange.1 = (bf16[192,2560]{1,0:T(8,128)(2,1)S(1)}, bf16[4,2560,256]{2,1,0:T(8,128)(2,1)S(1)}) custom-call(bf16[48,4,2560]{2,1,0:T(4,128)(2,1)} %hidden_hbm.1, bf16[2560,2,4,128]{3,2,1,0:T(4,128)(2,1)} %base_hbm.1), custom_call_target="tpu_custom_call" | custom-call | flops 1342177280 | bytes 12451840 | tf_op jit(solution)/shard_map/arrange/pallas_call | solution.py:259
  11.0 0.0 collective-permute-done.2.refs_3_
  11.0 0.7 %collective-permute-done.1.refs_2_ = bf16[8,3584]{1,0:T(8,128)(2,1)S(1)} collective-permute-done((bf16[8,3584]{1,0:T(8,128)(2,1)S(1)}, bf16[8,3584]{1,0:T(8,128)(2,1)S(1)}, u32[]{:S(2)}, u32[]{:S(2)}) %collective-permute-start.1) | collective-permute-done | bytes 57376 | tf_op jit(solution)/shard_map/ppermute | solution.py:441
  11.6 0.0 collective-permute-done.refs_1_
  11.7 1.6 %collective-permute-start.3 = (bf16[32,3584]{1,0:T(8,128)(2,1)S(1)}, bf16[32,3584]{1,0:T(8,128)(2,1)S(1)}, u32[]{:S(2)}, u32[]{:S(2)}) collective-permute-start(bf16[32,3584]{1,0:T(8,128)(2,1)S(1)} %join.1.refs_0_), channel_id=1, source_target_pairs={{0,2},{2,0},{4,6},{6,4},{8,10},{10,8},{12,14},{14,12},{1,3},{3,1},... | collective-permute-start | bytes 688136 | tf_op jit(solution)/shard_map/ppermute | solution.py:456
  13.3 5.1 %collective-permute-done.3.refs_1_ = bf16[32,3584]{1,0:T(8,128)(2,1)S(1)} collective-permute-done((bf16[32,3584]{1,0:T(8,128)(2,1)S(1)}, bf16[32,3584]{1,0:T(8,128)(2,1)S(1)}, u32[]{:S(2)}, u32[]{:S(2)}) %collective-permute-start.3) | collective-permute-done | bytes 229408 | tf_op jit(solution)/shard_map/ppermute | solution.py:456
  18.4 1.4 %project.3 = f32[192,512]{1,0:T(8,128)S(1)} custom-call(bf16[192,2560]{1,0:T(8,128)(2,1)S(1)} %get-tuple-element.19.hidden_ref, bf16[4,2560,256]{2,1,0:T(8,128)(2,1)S(1)} %get-tuple-element.20.base_ref, bf16[32,3584]{1,0:T(8,128)(2,1)S(1)} %join.1.refs_0_, bf16[32,3584]{1,0:T(8,128)(2,1)S(1)} %collective-permute-done.3.refs_1_), custom_call_target="tpu_custom_call" | custom-call | flops 671088640 | bytes 3604480 | tf_op jit(solution)/shard_map/project/pallas_call | solution.py:309
  19.8 0.1 collective-permute-start.4
  19.8 6.6 %attend_cached.1 = (bf16[48,64,128]{2,1,0:T(8,128)(2,1)S(1)}, f32[48,64,128]{2,1,0:T(8,128)S(1)}, f32[24,128]{1,0:T(8,128)S(1)}, f32[24,128]{1,0:T(8,128)S(1)}) custom-call(s32[48]{0:T(128)} %refs_0_.1, bf16[48,64,128]{2,1,0:T(8,128)(2,1)} %bitcast.3, bf16[48,128,2,2,128]{4,3,2,1,0:T(2,128)(2,1)} %refs_2_), custom_call_target="tpu_custom_call" | custom-call | flops 402653184 | bytes 6291456 | tf_op jit(solution)/shard_map/attend_cached/pallas_call | solution.py:199
  26.4 1.4 %project.2.refs_0_ = f32[192,512]{1,0:T(8,128)S(1)} custom-call(bf16[192,2560]{1,0:T(8,128)(2,1)S(1)} %get-tuple-element.19.hidden_ref, bf16[4,2560,256]{2,1,0:T(8,128)(2,1)S(1)} %get-tuple-element.20.base_ref, bf16[32,3584]{1,0:T(8,128)(2,1)S(1)} %join.1.refs_0_, bf16[32,3584]{1,0:T(8,128)(2,1)S(1)} %collective-permute-done.3.refs_1_), custom_call_target="tpu_custom_call" | custom-call | flops 671088640 | bytes 3604480 | tf_op jit(solution)/shard_map/project/pallas_call | solution.py:309
  27.8 0.0 collective-permute-done.4.refs_1_
  27.8 2.1 %finish.1 = (bf16[48,4,2,2,128]{4,3,2,1,0:T(2,128)(2,1)}, bf16[48,64,128]{2,1,0:T(8,128)(2,1)}) custom-call(f32[192,512]{1,0:T(8,128)S(1)} %project.2.refs_0_, f32[192,512]{1,0:T(8,128)S(1)} %collective-permute-done.4.refs_1_, bf16[48,64,128]{2,1,0:T(8,128)(2,1)S(1)} %get-tuple-element.26.refs_2_, f32[48,64,128]{2,1,0:T(8,128)S(1)} %get-tuple-element.27.refs_3_, ...), custom_call_target="tpu_custom_call" | custom-call | flops 301989888 | bytes 3145728 | tf_op jit(solution)/shard_map/finish/pallas_call | solution.py:395
  (1 shorter events, 0.0 us)
Async XLA Ops:
  1.5 9.5 %collective-permute-start.2 = (bf16[8,3584]{1,0:T(8,128)(2,1)S(1)}, bf16[8,3584]{1,0:T(8,128)(2,1)S(1)}, u32[]{:S(2)}, u32[]{:S(2)}) collective-permute-start(bf16[8,3584]{1,0:T(8,128)(2,1)S(1)} %payload.1.refs_0_), channel_id=1, source_target_pairs={{0,12},{2,14},{4,8},{6,10},{8,4},{10,6},{12,0},{14,2},{1,13},{3,15... | collective-permute-start | bytes 172040 | tf_op jit(solution)/shard_map/ppermute | solution.py:441
  6.6 5.1 %collective-permute-start.1 = (bf16[8,3584]{1,0:T(8,128)(2,1)S(1)}, bf16[8,3584]{1,0:T(8,128)(2,1)S(1)}, u32[]{:S(2)}, u32[]{:S(2)}) collective-permute-start(bf16[8,3584]{1,0:T(8,128)(2,1)S(1)} %payload.1.refs_0_), channel_id=1, source_target_pairs={{0,8},{2,10},{4,12},{6,14},{8,0},{10,2},{12,4},{14,6},{1,9},{3,11}... | collective-permute-start | bytes 172040 | tf_op jit(solution)/shard_map/ppermute | solution.py:441
  6.6 5.1 %collective-permute-start = (bf16[8,3584]{1,0:T(8,128)(2,1)S(1)}, bf16[8,3584]{1,0:T(8,128)(2,1)S(1)}, u32[]{:S(2)}, u32[]{:S(2)}) collective-permute-start(bf16[8,3584]{1,0:T(8,128)(2,1)S(1)} %payload.1.refs_0_), channel_id=1, source_target_pairs={{0,4},{2,6},{4,0},{6,2},{8,12},{10,14},{12,8},{14,10},{1,5},{3,7},... | collective-permute-start | bytes 172040 | tf_op jit(solution)/shard_map/ppermute | solution.py:441
  11.7 6.7 %collective-permute-start.3 = (bf16[32,3584]{1,0:T(8,128)(2,1)S(1)}, bf16[32,3584]{1,0:T(8,128)(2,1)S(1)}, u32[]{:S(2)}, u32[]{:S(2)}) collective-permute-start(bf16[32,3584]{1,0:T(8,128)(2,1)S(1)} %join.1.refs_0_), channel_id=1, source_target_pairs={{0,2},{2,0},{4,6},{6,4},{8,10},{10,8},{12,14},{14,12},{1,3},{3,1},... | collective-permute-start | bytes 688136 | tf_op jit(solution)/shard_map/ppermute | solution.py:456
  19.8 8.0 %collective-permute-start.4 = (f32[192,512]{1,0:T(8,128)S(1)}, f32[192,512]{1,0:T(8,128)S(1)}, u32[]{:S(2)}, u32[]{:S(2)}) collective-permute-start(f32[192,512]{1,0:T(8,128)S(1)} %project.3), channel_id=1, source_target_pairs={{0,1},{1,0},{2,3},{3,2},{4,5},{5,4},{6,7},{7,6},{8,9},{9,8},{10,11... | collective-permute-start | bytes 1179656 | tf_op jit(solution)/shard_map/ppermute | solution.py:461

commit v18 on v17

--- a/solution.py
+++ b/solution.py
@@ -19,6 +19,10 @@
 
 def in_hbm(x):
     return pltpu.with_memory_space_constraint(x, pltpu.HBM)
+
+
+def in_vmem(x):
+    return pltpu.with_memory_space_constraint(x, pltpu.VMEM)
 
 
 def cost(flops, moved, exps=0):
@@ -59,12 +63,17 @@
     )(in_hbm(down), in_hbm(up))
 
 
+def cache_copies(cache_hbm, k, v, sems, i, chunk):
+    mine = pl.ds(i * chunk, chunk)
+    return [pltpu.make_async_copy(cache_hbm.at[mine, :, n], ref.at[mine], sems.at[i, n]) for n, ref in enumerate((k, v))]
+
+
 class Cached:
-    def __init__(self, first, chunk, heads, scale, inputs, outputs, scratch):
-        self.first, self.chunk, self.heads, self.scale = first, chunk, heads, scale
-        self.lengths_hbm, self.queries_hbm, self.cache_hbm = inputs
-        self.q, self.sums, self.tops, self.totals = outputs
-        self.lengths, self.k, self.v, *rest = scratch
+    def __init__(self, chunk, heads, scale, inputs, outputs, scratch):
+        self.chunk, self.heads, self.scale = chunk, heads, scale
+        self.lengths_hbm, self.cache_hbm, self.q = inputs
+        self.k, self.v, self.sums, self.tops, self.totals = outputs
+        self.lengths, *rest = scratch
         self.scores, self.weights = rest[0:2], rest[2:4]
         self.sems, self.length_sem = rest[4:]
         self.rows, self.queries, self.size = self.q.shape
@@ -77,40 +86,8 @@
         self.one = lax.broadcasted_iota(jnp.int32, (1, 2 * queries), 1) < queries
         self.nothing = jnp.zeros((queries, self.size), jnp.bfloat16)
 
-    @staticmethod
-    def outputs(rows, many, size):
-        return (
-            pltpu.VMEM((rows, many, size), jnp.bfloat16),
-            pltpu.VMEM((rows, many, size), jnp.float32),
-            pltpu.VMEM((rows // 2, 2 * many), jnp.float32),
-            pltpu.VMEM((rows // 2, 2 * many), jnp.float32),
-        )
-
-    @staticmethod
-    def scratch(rows, chunk, many, cache, lengths):
-        slots, own, size = cache.shape[1], cache.shape[3], cache.shape[4]
-        half = (rows, slots, own, size)
-        scores = (chunk // 2, slots * own, 2 * many)
-        return [
-            pltpu.SMEM(lengths.shape, jnp.int32),
-            pltpu.VMEM(half, jnp.bfloat16),
-            pltpu.VMEM(half, jnp.bfloat16),
-            pltpu.VMEM(scores, jnp.float32),
-            pltpu.VMEM(scores, jnp.float32),
-            pltpu.VMEM(scores, jnp.bfloat16),
-            pltpu.VMEM(scores, jnp.bfloat16),
-            pltpu.SemaphoreType.DMA((rows // chunk, 3)),
-            pltpu.SemaphoreType.DMA,
-        ]
-
     def copies(self, i):
-        mine, theirs = pl.ds(i * self.chunk, self.chunk), pl.ds(self.first + i * self.chunk, self.chunk)
-        pairs = (
-            (self.queries_hbm.at[theirs], self.q.at[mine]),
-            (self.cache_hbm.at[theirs, :, 0], self.k.at[mine]),
-            (self.cache_hbm.at[theirs, :, 1], self.v.at[mine]),
-        )
-        return [pltpu.make_async_copy(a, b, self.sems.at[i, n]) for n, (a, b) in enumerate(pairs)]
+        return cache_copies(self.cache_hbm, self.k, self.v, self.sems, i, self.chunk)
 
     def lengths_copy(self):
         return pltpu.make_async_copy(self.lengths_hbm, self.lengths, self.length_sem)
@@ -143,7 +120,7 @@
 
     def soften(self, i, slot):
         for p in range(self.chunk // 2):
-            r = self.first + i * self.chunk + 2 * p
+            r = i * self.chunk + 2 * p
             limit = jnp.where(self.one, self.own * self.lengths[r], self.own * self.lengths[r + 1])
             scores = jnp.where(self.line < limit, self.scores[slot][p], LOW)
             top = jnp.max(scores, axis=0, keepdims=True)
@@ -164,16 +141,14 @@
                 self.sums[r + h] = both[h * queries : (h + 1) * queries, h * size : (h + 1) * size]
 
 
-def cached_kernel(chunk, heads, scale, *refs):
-    cached = Cached(0, chunk, heads, scale, refs[:3], refs[3:7], refs[7:])
+def cached_kernel(chunk, early, heads, scale, *refs):
+    cached = Cached(chunk, heads, scale, refs[:3], refs[5:10], refs[10:])
     chunks = cached.rows // chunk
     cached.lengths_copy().start()
-    for i in range(chunks):
+    for i in range(early, chunks):
         cached.start(i)
     cached.lengths_copy().wait()
-    cached.arrive(0)
     cached.score(0, 0)
-    cached.arrive(1)
     cached.score(1, 1)
     cached.soften(0, 0)
 
@@ -181,7 +156,11 @@
     def _(t):
         for slot in range(2):
             i = 2 * t + slot
-            cached.arrive(i)
+
+            @pl.when(i >= early)
+            def _():
+                cached.arrive(i)
+
             cached.score(i, slot)
             cached.soften(i - 1, 1 - slot)
             cached.collect(i - 2, slot)
@@ -191,38 +170,60 @@
     cached.collect(chunks - 1, 1)
 
 
-def attend_cached(queries, cache, lengths):
-    rows, steps, heads, size = queries.shape
+def attend_cached(queries, cache, lengths, keys, values, steps, chunk, early):
+    rows, many, size = queries.shape
     slots, own = cache.shape[1], cache.shape[3]
-    many = steps * heads
-    chunk = 6
-    return pl.pallas_call(
-        functools.partial(cached_kernel, chunk, heads, size ** (-0.5)),
-        out_shape=Cached.outputs(rows, many, size),
-        in_specs=[pl.BlockSpec(memory_space=pltpu.HBM)] * 3,
-        out_specs=(VMEM,) * 4,
-        scratch_shapes=Cached.scratch(rows, chunk, many, cache, lengths),
-        compiler_params=params(28),
-        cost_estimate=cost(
-            8 * rows * many * slots * size, 4 * rows * slots * own * size, rows * many * slots * own
-        ),
+    heads = many // steps
+    half = (rows, slots, own, size)
+    scores = (chunk // 2, slots * own, 2 * many)
+    line = (rows // 2, 2 * many)
+    outs = (
+        pltpu.VMEM(half, jnp.bfloat16),
+        pltpu.VMEM(half, jnp.bfloat16),
+        pltpu.VMEM((rows, many, size), jnp.float32),
+        pltpu.VMEM(line, jnp.float32),
+        pltpu.VMEM(line, jnp.float32),
+    )
+    _, _, *state = pl.pallas_call(
+        functools.partial(cached_kernel, chunk, early, heads, size ** (-0.5)),
+        out_shape=outs,
+        in_specs=[pl.BlockSpec(memory_space=pltpu.HBM)] * 2 + [VMEM] * 3,
+        out_specs=(VMEM,) * len(outs),
+        scratch_shapes=[
+            pltpu.SMEM(lengths.shape, jnp.int32),
+            pltpu.VMEM(scores, jnp.float32),
+            pltpu.VMEM(scores, jnp.float32),
+            pltpu.VMEM(scores, jnp.bfloat16),
+            pltpu.VMEM(scores, jnp.bfloat16),
+            pltpu.SemaphoreType.DMA((rows // chunk, 2)),
+            pltpu.SemaphoreType.DMA,
+        ],
+        input_output_aliases={3: 0, 4: 1},
+        compiler_params=params(16),
+        cost_estimate=cost(8 * rows * many * slots * size, 4 * rows * slots * own * size, rows * many * slots * own),
         name="attend_cached",
-    )(*map(in_hbm, (lengths, queries.reshape(-1, many, size), cache)))
-
-
-def arrange_kernel(chunks, own, hidden_hbm, base_hbm, tokens_ref, base_ref, hidden, base, sems):
+    )(in_hbm(lengths), in_hbm(cache), in_vmem(queries), keys, values)
+    return [queries, *state]
+
+
+def arrange_kernel(chunks, chunk, early, *refs):
+    cache_hbm, hidden_hbm, base_hbm, tokens_ref, base_ref, k, v, hidden, base, base_sems, sems = refs
     width, two, kvh, size = base.shape
+    own = k.shape[2]
     groups = two * kvh
     some_width = width // chunks
-
-    def copy(i):
+    copies = [copy for i in range(early) for copy in cache_copies(cache_hbm, k, v, sems, i, chunk)]
+    get_hidden = pltpu.make_async_copy(hidden_hbm, hidden, base_sems.at[chunks])
+
+    def get_base(i):
         features = pl.ds(i * some_width, some_width)
-        return pltpu.make_async_copy(base_hbm.at[features], base.at[features], sems.at[i])
-
-    get_hidden = pltpu.make_async_copy(hidden_hbm, hidden, sems.at[chunks])
+        return pltpu.make_async_copy(base_hbm.at[features], base.at[features], base_sems.at[i])
+
     for i in range(chunks):
-        copy(i).start()
+        get_base(i).start()
     get_hidden.start()
+    for copy in copies:
+        copy.start()
 
     tile = 256
     some = tile // groups
@@ -244,35 +245,43 @@
 
     @pl.loop(0, chunks)
     def _(i):
-        copy(i).wait()
+        get_base(i).wait()
         for f in range(0, some_width, 2 * some):
             arrange(i * some_width + f)
 
     get_hidden.wait()
     tokens_ref[...] = hidden.reshape(tokens_ref.shape)[...]
-
-
-def arrange(hidden, base, own):
+    for copy in copies:
+        copy.wait()
+
+
+def arrange(hidden, base, cache, chunk, early):
     rows, steps, _ = hidden.shape
+    slots, own = cache.shape[1], cache.shape[3]
     width, two, kvh, size = base.shape
+    half = pltpu.VMEM((rows, slots, own, size), jnp.bfloat16)
     chunks = 4
+    outs = (
+        pltpu.VMEM((rows * steps, width), jnp.bfloat16),
+        pltpu.VMEM((two * kvh // own, width, own * size), jnp.bfloat16),
+        half,
+        half,
+    )
     return pl.pallas_call(
-        functools.partial(arrange_kernel, chunks, own),
-        out_shape=(
-            pltpu.VMEM((rows * steps, width), jnp.bfloat16),
-            pltpu.VMEM((two * kvh // own, width, own * size), jnp.bfloat16),
-        ),
-        in_specs=[pl.BlockSpec(memory_space=pltpu.HBM)] * 2,
-        out_specs=(VMEM, VMEM),
+        functools.partial(arrange_kernel, chunks, chunk, early),
+        out_shape=outs,
+        in_specs=[pl.BlockSpec(memory_space=pltpu.HBM)] * 3,
+        out_specs=(VMEM,) * len(outs),
         scratch_shapes=[
             pltpu.VMEM(hidden.shape, jnp.bfloat16),
             pltpu.VMEM(base.shape, jnp.bfloat16),
             pltpu.SemaphoreType.DMA((chunks + 1,)),
+            pltpu.SemaphoreType.DMA((early, 2)),
         ],
-        compiler_params=params(20),
+        compiler_params=params(16),
         cost_estimate=cost(512 * base.size, 4 * (base.size + hidden.size)),
         name="arrange",
-    )(in_hbm(hidden), in_hbm(base))
+    )(in_hbm(cache), in_hbm(hidden), in_hbm(base))
 
 
 def project_kernel(k, hidden_ref, base_ref, *refs):
@@ -450,11 +459,15 @@
     steps, own = queries.shape[1], cache.shape[3]
     assert dp % 2 == 0
     blocks = gather_second(factor_a, factor_b, dp)
-    tokens, base = arrange(hidden, base_weight, own)
-    blocks, tokens, base, cache = lax.optimization_barrier((blocks, tokens, base, cache))
+    rows, steps, heads, size = queries.shape
+    queries = queries.reshape(rows, steps * heads, size)
+    chunk, early = 6, 2
+    tokens, base, keys, values = arrange(hidden, base_weight, cache, chunk, early)
+    blocks, tokens, base, keys, values = lax.optimization_barrier((blocks, tokens, base, keys, values))
     gathered = join(blocks) if len(blocks) > 1 else blocks[0]
     gathered = [gathered, lax.ppermute(gathered, "dp", [(i, i ^ 1) for i in range(dp)])]
-    state = attend_cached(queries, cache, lengths)
+    state = attend_cached(queries, cache, lengths, keys, values, steps, chunk, early)
+    gathered, state, tokens, base = lax.optimization_barrier((gathered, state, tokens, base))
     received = []
     for k in range(1, tp):
         other = project(k, tokens, base, gathered)

time: 30.2 us -> 26.2 us (0.87)
  waiting for transfers between devices: 5.76 us -> 2.48 us
  Pallas kernels: 16 us -> 15.5 us
    ppermute x1, waiting for transfers between devices: 5.1 us -> 0.01 us  [shards(): lax.ppermute(gathered, 'dp', [(i, i ^ 1) for i in range(dp)])]
    ppermute x3, waiting for transfers between devices: 0.66 us -> 2.15 us  [gather_second(): lax.ppermute(payload, 'dp', [(i, i ^ 2 * k) for i in range(dp)])]
    pallas_call x2, Pallas kernels: 10.3 us -> 9.79 us  [the longest x1 6 us: attend_cached(): pl.pallas_call(functools.partial(cached_kernel, chunk, early, heads, size...]
    ppermute x1, waiting for transfers between devices: 0.01 us -> 0.33 us  [shards(): received.append(lax.ppermute(other, 'tp', [(i, i ^ k) for i in range(tp)]))]
  transfers between devices with their start and end apart: 5 -> 5, of which waited for: 2 -> 2; matrix products, arithmetic and copies ran while one was open for 0% -> 0% of each run, Pallas kernels for 39% -> 43%
where the time goes in v18:
time: 26.2 us; the launch traced here: 26 us
  Pallas kernels  15.5 us (59%)
  starting transfers between devices  7.34 us (28%)
  waiting for transfers between devices  2.48 us (9%)
  between operations  0.72 us (3%)
    pallas_call x1, Pallas kernels, attend_cached(): pl.pallas_call(functools.partial(cached_kernel, chunk, early, heads, size...  6 us
    ppermute x3, starting transfers between devices, gather_second(): lax.ppermute(payload, 'dp', [(i, i ^ 2 * k) for i in range(dp)])  5.68 us
    pallas_call x1, Pallas kernels, arrange(): pl.pallas_call(functools.partial(arrange_kernel, chunks, chunk, early), o...  3.8 us
    pallas_call x2, Pallas kernels, project(): pl.pallas_call(functools.partial(project_kernel, k), out_shape=pltpu.VMEM...  2.75 us
    ppermute x3, waiting for transfers between devices, gather_second(): lax.ppermute(payload, 'dp', [(i, i ^ 2 * k) for i in range(dp)])  2.15 us
    pallas_call x1, Pallas kernels, finish(): pl.pallas_call(functools.partial(finish_kernel, steps, heads, size ** (-0...  2.08 us
    ppermute x1, starting transfers between devices, shards(): lax.ppermute(gathered, 'dp', [(i, i ^ 1) for i in range(dp)])  1.58 us
    pallas_call x1, Pallas kernels, make_payload(): pl.pallas_call(payload_kernel, out_shape=pltpu.VMEM((ranks, width + group...  0.81 us
  transfers between devices with their start and end apart: 5, of which 2 were waited for; matrix products, arithmetic and copies ran while one was open for 0% of the time, Pallas kernels for 43%

profile of v18, /device:TPU:0, one launch (start us, length us, event | category | flops | bytes accessed | tf_op | source)
XLA Modules:
  0.0 26.0 jit_solution(14626948086779970238)
XLA Ops:
  0.6 0.8 %payload.1.refs_0_ = bf16[8,3584]{1,0:T(8,128)(2,1)S(1)} custom-call(bf16[8,2560]{1,0:T(8,128)(2,1)} %bitcast.5, bf16[8,2,4,128]{3,2,1,0:T(4,128)(2,1)} %up_hbm.1), custom_call_target="tpu_custom_call" | custom-call | tf_op jit(solution)/shard_map/payload/pallas_call | solution.py:51
  1.5 0.0 copy-start
  1.5 3.1 %collective-permute-start = (bf16[8,3584]{1,0:T(8,128)(2,1)S(1)}, bf16[8,3584]{1,0:T(8,128)(2,1)S(1)}, u32[]{:S(2)}, u32[]{:S(2)}) collective-permute-start(bf16[8,3584]{1,0:T(8,128)(2,1)S(1)} %payload.1.refs_0_), channel_id=1, source_target_pairs={{0,4},{2,6},{4,0},{6,2},{8,12},{10,14},{12,8},{14,10},{1,5},{3,7},... | collective-permute-start | bytes 172040 | tf_op jit(solution)/shard_map/ppermute | solution.py:450
  4.6 2.6 %collective-permute-start.1 = (bf16[8,3584]{1,0:T(8,128)(2,1)S(1)}, bf16[8,3584]{1,0:T(8,128)(2,1)S(1)}, u32[]{:S(2)}, u32[]{:S(2)}) collective-permute-start(bf16[8,3584]{1,0:T(8,128)(2,1)S(1)} %payload.1.refs_0_), channel_id=1, source_target_pairs={{0,8},{2,10},{4,12},{6,14},{8,0},{10,2},{12,4},{14,6},{1,9},{3,11}... | collective-permute-start | bytes 172040 | tf_op jit(solution)/shard_map/ppermute | solution.py:450
  7.1 0.0 collective-permute-start.2
  7.1 3.8 %arrange.1 = (bf16[192,2560]{1,0:T(8,128)(2,1)S(1)}, bf16[4,2560,256]{2,1,0:T(8,128)(2,1)S(1)}, bf16[48,128,2,128]{3,2,1,0:T(2,128)(2,1)S(1)}, bf16[48,128,2,128]{3,2,1,0:T(2,128)(2,1)S(1)}) custom-call(bf16[48,128,2,2,128]{4,3,2,1,0:T(2,128)(2,1)} %refs_1_.3, bf16[48,4,2560]{2,1,0:T(4,128)(2,1)} %refs_1_.2, bf16[2560,2,4,128]{3,2,1,0:T(4,128)(2,1)} %refs_2_.1), custom_call_target="tpu_custom_call" | custom-call | flops 1342177280 | bytes 12451840 | tf_op jit(solution)/shard_map/arrange/pallas_call | solution.py:270
  10.9 0.0 collective-permute-done.refs_1_
  11.0 0.0 collective-permute-done.1.refs_2_
  11.0 2.1 %collective-permute-done.2.refs_3_ = bf16[8,3584]{1,0:T(8,128)(2,1)S(1)} collective-permute-done((bf16[8,3584]{1,0:T(8,128)(2,1)S(1)}, bf16[8,3584]{1,0:T(8,128)(2,1)S(1)}, u32[]{:S(2)}, u32[]{:S(2)}) %collective-permute-start.2) | collective-permute-done | bytes 57376 | tf_op jit(solution)/shard_map/ppermute | solution.py:450
  13.1 1.6 %collective-permute-start.3 = (bf16[32,3584]{1,0:T(8,128)(2,1)S(1)}, bf16[32,3584]{1,0:T(8,128)(2,1)S(1)}, u32[]{:S(2)}, u32[]{:S(2)}) collective-permute-start(bf16[32,3584]{1,0:T(8,128)(2,1)S(1)} %join.1.refs_0_), channel_id=1, source_target_pairs={{0,2},{2,0},{4,6},{6,4},{8,10},{10,8},{12,14},{14,12},{1,3},{3,1},... | collective-permute-start | bytes 688136 | tf_op jit(solution)/shard_map/ppermute | solution.py:468
  14.7 0.0 copy-done
  14.7 6.0 %attend_cached.1 = (bf16[48,128,2,128]{3,2,1,0:T(2,128)(2,1)S(1)}, bf16[48,128,2,128]{3,2,1,0:T(2,128)(2,1)S(1)}, f32[48,64,128]{2,1,0:T(8,128)S(1)}, f32[24,128]{1,0:T(8,128)S(1)}, f32[24,128]{1,0:T(8,128)S(1)}) custom-call(s32[48]{0:T(128)} %refs_0_.3, bf16[48,128,2,2,128]{4,3,2,1,0:T(2,128)(2,1)} %refs_1_.3, ...), custom_call_target="tpu_custom_call", output_to_operand_aliasing={{0}: (3, {}), {1}: (4, {})} | custom-call | flops 402653184 | bytes 6291456 | tf_op jit(solution)/shard_map/attend_cached/pallas_call | solution.py:187
  20.7 0.0 collective-permute-done.3.refs_1_
  20.7 1.4 %project.3 = f32[192,512]{1,0:T(8,128)S(1)} custom-call(bf16[192,2560]{1,0:T(8,128)(2,1)S(1)} %get-tuple-element.42.hidden_ref, bf16[4,2560,256]{2,1,0:T(8,128)(2,1)S(1)} %get-tuple-element.43.base_ref, bf16[32,3584]{1,0:T(8,128)(2,1)S(1)} %join.1.refs_0_, bf16[32,3584]{1,0:T(8,128)(2,1)S(1)} %collective-permute-done.3.refs_1_), custom_call_target="tpu_custom_call" | custom-call | flops 671088640 | bytes 3604480 | tf_op jit(solution)/shard_map/project/pallas_call | solution.py:318
  22.1 0.1 collective-permute-start.4
  22.2 1.4 %project.2.refs_0_ = f32[192,512]{1,0:T(8,128)S(1)} custom-call(bf16[192,2560]{1,0:T(8,128)(2,1)S(1)} %get-tuple-element.42.hidden_ref, bf16[4,2560,256]{2,1,0:T(8,128)(2,1)S(1)} %get-tuple-element.43.base_ref, bf16[32,3584]{1,0:T(8,128)(2,1)S(1)} %join.1.refs_0_, bf16[32,3584]{1,0:T(8,128)(2,1)S(1)} %collective-permute-done.3.refs_1_), custom_call_target="tpu_custom_call" | custom-call | flops 671088640 | bytes 3604480 | tf_op jit(solution)/shard_map/project/pallas_call | solution.py:318
  23.6 0.3 %collective-permute-done.4.refs_1_ = f32[192,512]{1,0:T(8,128)S(1)} collective-permute-done((f32[192,512]{1,0:T(8,128)S(1)}, f32[192,512]{1,0:T(8,128)S(1)}, u32[]{:S(2)}, u32[]{:S(2)}) %collective-permute-start.4) | collective-permute-done | bytes 393248 | tf_op jit(solution)/shard_map/ppermute | solution.py:474
  23.9 2.1 %finish.1 = (bf16[48,4,2,2,128]{4,3,2,1,0:T(2,128)(2,1)}, bf16[48,64,128]{2,1,0:T(8,128)(2,1)}) custom-call(f32[192,512]{1,0:T(8,128)S(1)} %project.2.refs_0_, f32[192,512]{1,0:T(8,128)S(1)} %collective-permute-done.4.refs_1_, bf16[48,64,128]{2,1,0:T(8,128)(2,1)S(1)} %bitcast.4, f32[48,64,128]{2,1,0:T(8,128)S(1)} %get-tuple-element.47.refs_3_, ...), custom_call_target="tpu_custom_call" | custom-call | flops 301989888 | bytes 3145728 | tf_op jit(solution)/shard_map/finish/pallas_call | solution.py:404
  (1 shorter events, 0.0 us)
Async XLA Ops:
  1.5 13.3 %copy-start = (bf16[48,4,16,128]{3,2,1,0:T(8,128)(2,1)S(1)}, bf16[48,4,16,128]{3,2,1,0:T(8,128)(2,1)}, u32[]{:S(2)}) copy-start(bf16[48,4,16,128]{3,2,1,0:T(8,128)(2,1)} %param.11) | copy-start | bytes 2359300
  1.5 9.5 %collective-permute-start = (bf16[8,3584]{1,0:T(8,128)(2,1)S(1)}, bf16[8,3584]{1,0:T(8,128)(2,1)S(1)}, u32[]{:S(2)}, u32[]{:S(2)}) collective-permute-start(bf16[8,3584]{1,0:T(8,128)(2,1)S(1)} %payload.1.refs_0_), channel_id=1, source_target_pairs={{0,4},{2,6},{4,0},{6,2},{8,12},{10,14},{12,8},{14,10},{1,5},{3,7},... | collective-permute-start | bytes 172040 | tf_op jit(solution)/shard_map/ppermute | solution.py:450
  4.6 6.4 %collective-permute-start.1 = (bf16[8,3584]{1,0:T(8,128)(2,1)S(1)}, bf16[8,3584]{1,0:T(8,128)(2,1)S(1)}, u32[]{:S(2)}, u32[]{:S(2)}) collective-permute-start(bf16[8,3584]{1,0:T(8,128)(2,1)S(1)} %payload.1.refs_0_), channel_id=1, source_target_pairs={{0,8},{2,10},{4,12},{6,14},{8,0},{10,2},{12,4},{14,6},{1,9},{3,11}... | collective-permute-start | bytes 172040 | tf_op jit(solution)/shard_map/ppermute | solution.py:450
  7.1 6.0 %collective-permute-start.2 = (bf16[8,3584]{1,0:T(8,128)(2,1)S(1)}, bf16[8,3584]{1,0:T(8,128)(2,1)S(1)}, u32[]{:S(2)}, u32[]{:S(2)}) collective-permute-start(bf16[8,3584]{1,0:T(8,128)(2,1)S(1)} %payload.1.refs_0_), channel_id=1, source_target_pairs={{0,12},{2,14},{4,8},{6,10},{8,4},{10,6},{12,0},{14,2},{1,13},{3,15... | collective-permute-start | bytes 172040 | tf_op jit(solution)/shard_map/ppermute | solution.py:450
  13.1 7.6 %collective-permute-start.3 = (bf16[32,3584]{1,0:T(8,128)(2,1)S(1)}, bf16[32,3584]{1,0:T(8,128)(2,1)S(1)}, u32[]{:S(2)}, u32[]{:S(2)}) collective-permute-start(bf16[32,3584]{1,0:T(8,128)(2,1)S(1)} %join.1.refs_0_), channel_id=1, source_target_pairs={{0,2},{2,0},{4,6},{6,4},{8,10},{10,8},{12,14},{14,12},{1,3},{3,1},... | collective-permute-start | bytes 688136 | tf_op jit(solution)/shard_map/ppermute | solution.py:468
  22.1 1.8 %collective-permute-start.4 = (f32[192,512]{1,0:T(8,128)S(1)}, f32[192,512]{1,0:T(8,128)S(1)}, u32[]{:S(2)}, u32[]{:S(2)}) collective-permute-start(f32[192,512]{1,0:T(8,128)S(1)} %project.3), channel_id=1, source_target_pairs={{0,1},{1,0},{2,3},{3,2},{4,5},{5,4},{6,7},{7,6},{8,9},{9,8},{10,11... | collective-permute-start | bytes 1179656 | tf_op jit(solution)/shard_map/ppermute | solution.py:474

commit v19 on v18

--- a/solution.py
+++ b/solution.py
@@ -447,7 +447,7 @@
     ranks = factor_b.shape[0]
     if ranks % 8 == 0 and count in (1, 2, 4):
         payload = make_payload(factor_a.T, factor_b)
-        return [payload] + [lax.ppermute(payload, "dp", [(i, i ^ (2 * k)) for i in range(dp)]) for k in range(1, count)]
+        return [payload] + [lax.ppermute(payload, "dp", [(i, i ^ (2 * k)) for i in range(dp)]) for k in range(count - 1, 0, -1)]
     payload = jnp.concatenate([factor_a.T, factor_b.reshape(ranks, -1)], axis=1)
     groups = [[i for i in range(dp) if i % 2 == n] for n in range(2)]
     copies = jnp.broadcast_to(payload[None], (count,) + payload.shape)
@@ -461,7 +461,7 @@
     blocks = gather_second(factor_a, factor_b, dp)
     rows, steps, heads, size = queries.shape
     queries = queries.reshape(rows, steps * heads, size)
-    chunk, early = 6, 2
+    chunk, early = 6, 3
     tokens, base, keys, values = arrange(hidden, base_weight, cache, chunk, early)
     blocks, tokens, base, keys, values = lax.optimization_barrier((blocks, tokens, base, keys, values))
     gathered = join(blocks) if len(blocks) > 1 else blocks[0]

time: 26.2 us -> 24.8 us (0.947)
  waiting for transfers between devices: 2.48 us -> 0.8 us
    ppermute x3, waiting for transfers between devices: 2.15 us -> 0.47 us  [gather_second(): lax.ppermute(payload, 'dp', [(i, i ^ 2 * k) for i in range(dp)])]
  transfers between devices with their start and end apart: 5 -> 5, of which waited for: 2 -> 2; matrix products, arithmetic and copies ran while one was open for 0% -> 0% of each run, Pallas kernels for 43% -> 46%
where the time goes in v19:
time: 24.8 us; the launch traced here: 24.6 us
  Pallas kernels  15.6 us (63%)
  starting transfers between devices  7.44 us (30%)
  waiting for transfers between devices  0.8 us (3%)
  between operations  0.71 us (3%)
    pallas_call x1, Pallas kernels, attend_cached(): pl.pallas_call(functools.partial(cached_kernel, chunk, early, heads, size...  5.99 us
    ppermute x3, starting transfers between devices, gather_second(): lax.ppermute(payload, 'dp', [(i, i ^ 2 * k) for i in range(dp)])  5.76 us
    pallas_call x1, Pallas kernels, arrange(): pl.pallas_call(functools.partial(arrange_kernel, chunks, chunk, early), o...  3.95 us
    pallas_call x2, Pallas kernels, project(): pl.pallas_call(functools.partial(project_kernel, k), out_shape=pltpu.VMEM...  2.75 us
    pallas_call x1, Pallas kernels, finish(): pl.pallas_call(functools.partial(finish_kernel, steps, heads, size ** (-0...  2.08 us
    ppermute x1, starting transfers between devices, shards(): lax.ppermute(gathered, 'dp', [(i, i ^ 1) for i in range(dp)])  1.61 us
    pallas_call x1, Pallas kernels, make_payload(): pl.pallas_call(payload_kernel, out_shape=pltpu.VMEM((ranks, width + group...  0.81 us
  transfers between devices with their start and end apart: 5, of which 2 were waited for; matrix products, arithmetic and copies ran while one was open for 0% of the time, Pallas kernels for 46%

profile of v19, /device:TPU:0, one launch (start us, length us, event | category | flops | bytes accessed | tf_op | source)
XLA Modules:
  0.0 24.6 jit_solution(3466203961912971464)
XLA Ops:
  0.6 0.8 %payload.1.refs_0_ = bf16[8,3584]{1,0:T(8,128)(2,1)S(1)} custom-call(bf16[8,2560]{1,0:T(8,128)(2,1)} %bitcast.5, bf16[8,2,4,128]{3,2,1,0:T(4,128)(2,1)} %up_hbm.1), custom_call_target="tpu_custom_call" | custom-call | tf_op jit(solution)/shard_map/payload/pallas_call | solution.py:51
  1.5 0.0 copy-start
  1.5 5.1 %collective-permute-start = (bf16[8,3584]{1,0:T(8,128)(2,1)S(1)}, bf16[8,3584]{1,0:T(8,128)(2,1)S(1)}, u32[]{:S(2)}, u32[]{:S(2)}) collective-permute-start(bf16[8,3584]{1,0:T(8,128)(2,1)S(1)} %payload.1.refs_0_), channel_id=1, source_target_pairs={{0,12},{2,14},{4,8},{6,10},{8,4},{10,6},{12,0},{14,2},{1,13},{3,15... | collective-permute-start | bytes 172040 | tf_op jit(solution)/shard_map/ppermute | solution.py:450
  6.6 0.0 collective-permute-start.1
  6.6 0.6 %collective-permute-start.2 = (bf16[8,3584]{1,0:T(8,128)(2,1)S(1)}, bf16[8,3584]{1,0:T(8,128)(2,1)S(1)}, u32[]{:S(2)}, u32[]{:S(2)}) collective-permute-start(bf16[8,3584]{1,0:T(8,128)(2,1)S(1)} %payload.1.refs_0_), channel_id=1, source_target_pairs={{0,4},{2,6},{4,0},{6,2},{8,12},{10,14},{12,8},{14,10},{1,5},{3,7},... | collective-permute-start | bytes 172040 | tf_op jit(solution)/shard_map/ppermute | solution.py:450
  7.2 3.9 %arrange.1 = (bf16[192,2560]{1,0:T(8,128)(2,1)S(1)}, bf16[4,2560,256]{2,1,0:T(8,128)(2,1)S(1)}, bf16[48,128,2,128]{3,2,1,0:T(2,128)(2,1)S(1)}, bf16[48,128,2,128]{3,2,1,0:T(2,128)(2,1)S(1)}) custom-call(bf16[48,128,2,2,128]{4,3,2,1,0:T(2,128)(2,1)} %refs_1_.3, bf16[48,4,2560]{2,1,0:T(4,128)(2,1)} %refs_1_.2, bf16[2560,2,4,128]{3,2,1,0:T(4,128)(2,1)} %refs_2_.1), custom_call_target="tpu_custom_call" | custom-call | flops 1342177280 | bytes 12451840 | tf_op jit(solution)/shard_map/arrange/pallas_call | solution.py:270
  11.2 0.0 collective-permute-done.refs_1_
  11.2 0.5 %collective-permute-done.1.refs_2_ = bf16[8,3584]{1,0:T(8,128)(2,1)S(1)} collective-permute-done((bf16[8,3584]{1,0:T(8,128)(2,1)S(1)}, bf16[8,3584]{1,0:T(8,128)(2,1)S(1)}, u32[]{:S(2)}, u32[]{:S(2)}) %collective-permute-start.1) | collective-permute-done | bytes 57376 | tf_op jit(solution)/shard_map/ppermute | solution.py:450
  11.7 0.0 collective-permute-done.2.refs_3_
  11.7 1.6 %collective-permute-start.3 = (bf16[32,3584]{1,0:T(8,128)(2,1)S(1)}, bf16[32,3584]{1,0:T(8,128)(2,1)S(1)}, u32[]{:S(2)}, u32[]{:S(2)}) collective-permute-start(bf16[32,3584]{1,0:T(8,128)(2,1)S(1)} %join.1.refs_0_), channel_id=1, source_target_pairs={{0,2},{2,0},{4,6},{6,4},{8,10},{10,8},{12,14},{14,12},{1,3},{3,1},... | collective-permute-start | bytes 688136 | tf_op jit(solution)/shard_map/ppermute | solution.py:468
  13.3 0.0 copy-done
  13.3 6.0 %attend_cached.1 = (bf16[48,128,2,128]{3,2,1,0:T(2,128)(2,1)S(1)}, bf16[48,128,2,128]{3,2,1,0:T(2,128)(2,1)S(1)}, f32[48,64,128]{2,1,0:T(8,128)S(1)}, f32[24,128]{1,0:T(8,128)S(1)}, f32[24,128]{1,0:T(8,128)S(1)}) custom-call(s32[48]{0:T(128)} %refs_0_.3, bf16[48,128,2,2,128]{4,3,2,1,0:T(2,128)(2,1)} %refs_1_.3, ...), custom_call_target="tpu_custom_call", output_to_operand_aliasing={{0}: (3, {}), {1}: (4, {})} | custom-call | flops 402653184 | bytes 6291456 | tf_op jit(solution)/shard_map/attend_cached/pallas_call | solution.py:187
  19.3 0.0 collective-permute-done.3.refs_1_
  19.3 1.4 %project.3 = f32[192,512]{1,0:T(8,128)S(1)} custom-call(bf16[192,2560]{1,0:T(8,128)(2,1)S(1)} %get-tuple-element.42.hidden_ref, bf16[4,2560,256]{2,1,0:T(8,128)(2,1)S(1)} %get-tuple-element.43.base_ref, bf16[32,3584]{1,0:T(8,128)(2,1)S(1)} %join.1.refs_0_, bf16[32,3584]{1,0:T(8,128)(2,1)S(1)} %collective-permute-done.3.refs_1_), custom_call_target="tpu_custom_call" | custom-call | flops 671088640 | bytes 3604480 | tf_op jit(solution)/shard_map/project/pallas_call | solution.py:318
  20.7 0.1 collective-permute-start.4
  20.8 1.4 %project.2.refs_0_ = f32[192,512]{1,0:T(8,128)S(1)} custom-call(bf16[192,2560]{1,0:T(8,128)(2,1)S(1)} %get-tuple-element.42.hidden_ref, bf16[4,2560,256]{2,1,0:T(8,128)(2,1)S(1)} %get-tuple-element.43.base_ref, bf16[32,3584]{1,0:T(8,128)(2,1)S(1)} %join.1.refs_0_, bf16[32,3584]{1,0:T(8,128)(2,1)S(1)} %collective-permute-done.3.refs_1_), custom_call_target="tpu_custom_call" | custom-call | flops 671088640 | bytes 3604480 | tf_op jit(solution)/shard_map/project/pallas_call | solution.py:318
  22.1 0.3 %collective-permute-done.4.refs_1_ = f32[192,512]{1,0:T(8,128)S(1)} collective-permute-done((f32[192,512]{1,0:T(8,128)S(1)}, f32[192,512]{1,0:T(8,128)S(1)}, u32[]{:S(2)}, u32[]{:S(2)}) %collective-permute-start.4) | collective-permute-done | bytes 393248 | tf_op jit(solution)/shard_map/ppermute | solution.py:474
  22.5 2.1 %finish.1 = (bf16[48,4,2,2,128]{4,3,2,1,0:T(2,128)(2,1)}, bf16[48,64,128]{2,1,0:T(8,128)(2,1)}) custom-call(f32[192,512]{1,0:T(8,128)S(1)} %project.2.refs_0_, f32[192,512]{1,0:T(8,128)S(1)} %collective-permute-done.4.refs_1_, bf16[48,64,128]{2,1,0:T(8,128)(2,1)S(1)} %bitcast.4, f32[48,64,128]{2,1,0:T(8,128)S(1)} %get-tuple-element.47.refs_3_, ...), custom_call_target="tpu_custom_call" | custom-call | flops 301989888 | bytes 3145728 | tf_op jit(solution)/shard_map/finish/pallas_call | solution.py:404
  (1 shorter events, 0.0 us)
Async XLA Ops:
  1.5 11.8 %copy-start = (bf16[48,4,16,128]{3,2,1,0:T(8,128)(2,1)S(1)}, bf16[48,4,16,128]{3,2,1,0:T(8,128)(2,1)}, u32[]{:S(2)}) copy-start(bf16[48,4,16,128]{3,2,1,0:T(8,128)(2,1)} %param.11) | copy-start | bytes 2359300
  1.5 9.7 %collective-permute-start = (bf16[8,3584]{1,0:T(8,128)(2,1)S(1)}, bf16[8,3584]{1,0:T(8,128)(2,1)S(1)}, u32[]{:S(2)}, u32[]{:S(2)}) collective-permute-start(bf16[8,3584]{1,0:T(8,128)(2,1)S(1)} %payload.1.refs_0_), channel_id=1, source_target_pairs={{0,12},{2,14},{4,8},{6,10},{8,4},{10,6},{12,0},{14,2},{1,13},{3,15... | collective-permute-start | bytes 172040 | tf_op jit(solution)/shard_map/ppermute | solution.py:450
  6.6 5.1 %collective-permute-start.1 = (bf16[8,3584]{1,0:T(8,128)(2,1)S(1)}, bf16[8,3584]{1,0:T(8,128)(2,1)S(1)}, u32[]{:S(2)}, u32[]{:S(2)}) collective-permute-start(bf16[8,3584]{1,0:T(8,128)(2,1)S(1)} %payload.1.refs_0_), channel_id=1, source_target_pairs={{0,8},{2,10},{4,12},{6,14},{8,0},{10,2},{12,4},{14,6},{1,9},{3,11}... | collective-permute-start | bytes 172040 | tf_op jit(solution)/shard_map/ppermute | solution.py:450
  6.6 5.1 %collective-permute-start.2 = (bf16[8,3584]{1,0:T(8,128)(2,1)S(1)}, bf16[8,3584]{1,0:T(8,128)(2,1)S(1)}, u32[]{:S(2)}, u32[]{:S(2)}) collective-permute-start(bf16[8,3584]{1,0:T(8,128)(2,1)S(1)} %payload.1.refs_0_), channel_id=1, source_target_pairs={{0,4},{2,6},{4,0},{6,2},{8,12},{10,14},{12,8},{14,10},{1,5},{3,7},... | collective-permute-start | bytes 172040 | tf_op jit(solution)/shard_map/ppermute | solution.py:450
  11.7 7.6 %collective-permute-start.3 = (bf16[32,3584]{1,0:T(8,128)(2,1)S(1)}, bf16[32,3584]{1,0:T(8,128)(2,1)S(1)}, u32[]{:S(2)}, u32[]{:S(2)}) collective-permute-start(bf16[32,3584]{1,0:T(8,128)(2,1)S(1)} %join.1.refs_0_), channel_id=1, source_target_pairs={{0,2},{2,0},{4,6},{6,4},{8,10},{10,8},{12,14},{14,12},{1,3},{3,1},... | collective-permute-start | bytes 688136 | tf_op jit(solution)/shard_map/ppermute | solution.py:468
  20.7 1.8 %collective-permute-start.4 = (f32[192,512]{1,0:T(8,128)S(1)}, f32[192,512]{1,0:T(8,128)S(1)}, u32[]{:S(2)}, u32[]{:S(2)}) collective-permute-start(f32[192,512]{1,0:T(8,128)S(1)} %project.3), channel_id=1, source_target_pairs={{0,1},{1,0},{2,3},{3,2},{4,5},{5,4},{6,7},{7,6},{8,9},{9,8},{10,11... | collective-permute-start | bytes 1179656 | tf_op jit(solution)/shard_map/ppermute | solution.py:474

commit v20 on v19

--- a/solution.py
+++ b/solution.py
@@ -461,7 +461,7 @@
     blocks = gather_second(factor_a, factor_b, dp)
     rows, steps, heads, size = queries.shape
     queries = queries.reshape(rows, steps * heads, size)
-    chunk, early = 6, 3
+    chunk, early = 8, 3
     tokens, base, keys, values = arrange(hidden, base_weight, cache, chunk, early)
     blocks, tokens, base, keys, values = lax.optimization_barrier((blocks, tokens, base, keys, values))
     gathered = join(blocks) if len(blocks) > 1 else blocks[0]

time: 24.8 us -> 24.5 us (0.988)
    pallas_call x1, Pallas kernels: 5.99 us -> 5.73 us  [attend_cached(): pl.pallas_call(functools.partial(cached_kernel, chunk, early, heads, size...]
where the time goes in v20:
time: 24.5 us; the launch traced here: 24.3 us
  Pallas kernels  15.4 us (63%)
  starting transfers between devices  7.44 us (30%)
  waiting for transfers between devices  0.76 us (3%)
  between operations  0.71 us (3%)
    ppermute x3, starting transfers between devices, gather_second(): lax.ppermute(payload, 'dp', [(i, i ^ 2 * k) for i in range(dp)])  5.76 us
    pallas_call x1, Pallas kernels, attend_cached(): pl.pallas_call(functools.partial(cached_kernel, chunk, early, heads, size...  5.73 us
    pallas_call x1, Pallas kernels, arrange(): pl.pallas_call(functools.partial(arrange_kernel, chunks, chunk, early), o...  3.99 us
    pallas_call x2, Pallas kernels, project(): pl.pallas_call(functools.partial(project_kernel, k), out_shape=pltpu.VMEM...  2.75 us
    pallas_call x1, Pallas kernels, finish(): pl.pallas_call(functools.partial(finish_kernel, steps, heads, size ** (-0...  2.08 us
    ppermute x1, starting transfers between devices, shards(): lax.ppermute(gathered, 'dp', [(i, i ^ 1) for i in range(dp)])  1.61 us
    pallas_call x1, Pallas kernels, make_payload(): pl.pallas_call(payload_kernel, out_shape=pltpu.VMEM((ranks, width + group...  0.81 us
  transfers between devices with their start and end apart: 5, of which 2 were waited for; matrix products, arithmetic and copies ran while one was open for 0% of the time, Pallas kernels for 46%

profile of v20, /device:TPU:0, one launch (start us, length us, event | category | flops | bytes accessed | tf_op | source)
XLA Modules:
  0.0 24.3 jit_solution(7686891487654609589)
XLA Ops:
  0.6 0.8 %payload.1.refs_0_ = bf16[8,3584]{1,0:T(8,128)(2,1)S(1)} custom-call(bf16[8,2560]{1,0:T(8,128)(2,1)} %bitcast.5, bf16[8,2,4,128]{3,2,1,0:T(4,128)(2,1)} %up_hbm.1), custom_call_target="tpu_custom_call" | custom-call | tf_op jit(solution)/shard_map/payload/pallas_call | solution.py:51
  1.5 0.0 copy-start
  1.5 5.1 %collective-permute-start = (bf16[8,3584]{1,0:T(8,128)(2,1)S(1)}, bf16[8,3584]{1,0:T(8,128)(2,1)S(1)}, u32[]{:S(2)}, u32[]{:S(2)}) collective-permute-start(bf16[8,3584]{1,0:T(8,128)(2,1)S(1)} %payload.1.refs_0_), channel_id=1, source_target_pairs={{0,12},{2,14},{4,8},{6,10},{8,4},{10,6},{12,0},{14,2},{1,13},{3,15... | collective-permute-start | bytes 172040 | tf_op jit(solution)/shard_map/ppermute | solution.py:450
  6.6 0.0 collective-permute-start.1
  6.6 0.6 %collective-permute-start.2 = (bf16[8,3584]{1,0:T(8,128)(2,1)S(1)}, bf16[8,3584]{1,0:T(8,128)(2,1)S(1)}, u32[]{:S(2)}, u32[]{:S(2)}) collective-permute-start(bf16[8,3584]{1,0:T(8,128)(2,1)S(1)} %payload.1.refs_0_), channel_id=1, source_target_pairs={{0,4},{2,6},{4,0},{6,2},{8,12},{10,14},{12,8},{14,10},{1,5},{3,7},... | collective-permute-start | bytes 172040 | tf_op jit(solution)/shard_map/ppermute | solution.py:450
  7.2 4.0 %arrange.1 = (bf16[192,2560]{1,0:T(8,128)(2,1)S(1)}, bf16[4,2560,256]{2,1,0:T(8,128)(2,1)S(1)}, bf16[48,128,2,128]{3,2,1,0:T(2,128)(2,1)S(1)}, bf16[48,128,2,128]{3,2,1,0:T(2,128)(2,1)S(1)}) custom-call(bf16[48,128,2,2,128]{4,3,2,1,0:T(2,128)(2,1)} %refs_1_.3, bf16[48,4,2560]{2,1,0:T(4,128)(2,1)} %refs_1_.2, bf16[2560,2,4,128]{3,2,1,0:T(4,128)(2,1)} %refs_2_.1), custom_call_target="tpu_custom_call" | custom-call | flops 1342177280 | bytes 12451840 | tf_op jit(solution)/shard_map/arrange/pallas_call | solution.py:270
  11.2 0.0 collective-permute-done.refs_1_
  11.2 0.4 %collective-permute-done.1.refs_2_ = bf16[8,3584]{1,0:T(8,128)(2,1)S(1)} collective-permute-done((bf16[8,3584]{1,0:T(8,128)(2,1)S(1)}, bf16[8,3584]{1,0:T(8,128)(2,1)S(1)}, u32[]{:S(2)}, u32[]{:S(2)}) %collective-permute-start.1) | collective-permute-done | bytes 57376 | tf_op jit(solution)/shard_map/ppermute | solution.py:450
  11.7 0.0 collective-permute-done.2.refs_3_
  11.7 1.6 %collective-permute-start.3 = (bf16[32,3584]{1,0:T(8,128)(2,1)S(1)}, bf16[32,3584]{1,0:T(8,128)(2,1)S(1)}, u32[]{:S(2)}, u32[]{:S(2)}) collective-permute-start(bf16[32,3584]{1,0:T(8,128)(2,1)S(1)} %join.1.refs_0_), channel_id=1, source_target_pairs={{0,2},{2,0},{4,6},{6,4},{8,10},{10,8},{12,14},{14,12},{1,3},{3,1},... | collective-permute-start | bytes 688136 | tf_op jit(solution)/shard_map/ppermute | solution.py:468
  13.3 0.0 copy-done
  13.3 5.7 %attend_cached.1 = (bf16[48,128,2,128]{3,2,1,0:T(2,128)(2,1)S(1)}, bf16[48,128,2,128]{3,2,1,0:T(2,128)(2,1)S(1)}, f32[48,64,128]{2,1,0:T(8,128)S(1)}, f32[24,128]{1,0:T(8,128)S(1)}, f32[24,128]{1,0:T(8,128)S(1)}) custom-call(s32[48]{0:T(128)} %refs_0_.3, bf16[48,128,2,2,128]{4,3,2,1,0:T(2,128)(2,1)} %refs_1_.3, ...), custom_call_target="tpu_custom_call", output_to_operand_aliasing={{0}: (3, {}), {1}: (4, {})} | custom-call | flops 402653184 | bytes 6291456 | tf_op jit(solution)/shard_map/attend_cached/pallas_call | solution.py:187
  19.0 0.0 collective-permute-done.3.refs_1_
  19.0 1.4 %project.3 = f32[192,512]{1,0:T(8,128)S(1)} custom-call(bf16[192,2560]{1,0:T(8,128)(2,1)S(1)} %get-tuple-element.42.hidden_ref, bf16[4,2560,256]{2,1,0:T(8,128)(2,1)S(1)} %get-tuple-element.43.base_ref, bf16[32,3584]{1,0:T(8,128)(2,1)S(1)} %join.1.refs_0_, bf16[32,3584]{1,0:T(8,128)(2,1)S(1)} %collective-permute-done.3.refs_1_), custom_call_target="tpu_custom_call" | custom-call | flops 671088640 | bytes 3604480 | tf_op jit(solution)/shard_map/project/pallas_call | solution.py:318
  20.4 0.1 collective-permute-start.4
  20.5 1.4 %project.2.refs_0_ = f32[192,512]{1,0:T(8,128)S(1)} custom-call(bf16[192,2560]{1,0:T(8,128)(2,1)S(1)} %get-tuple-element.42.hidden_ref, bf16[4,2560,256]{2,1,0:T(8,128)(2,1)S(1)} %get-tuple-element.43.base_ref, bf16[32,3584]{1,0:T(8,128)(2,1)S(1)} %join.1.refs_0_, bf16[32,3584]{1,0:T(8,128)(2,1)S(1)} %collective-permute-done.3.refs_1_), custom_call_target="tpu_custom_call" | custom-call | flops 671088640 | bytes 3604480 | tf_op jit(solution)/shard_map/project/pallas_call | solution.py:318
  21.9 0.3 %collective-permute-done.4.refs_1_ = f32[192,512]{1,0:T(8,128)S(1)} collective-permute-done((f32[192,512]{1,0:T(8,128)S(1)}, f32[192,512]{1,0:T(8,128)S(1)}, u32[]{:S(2)}, u32[]{:S(2)}) %collective-permute-start.4) | collective-permute-done | bytes 393248 | tf_op jit(solution)/shard_map/ppermute | solution.py:474
  22.2 2.1 %finish.1 = (bf16[48,4,2,2,128]{4,3,2,1,0:T(2,128)(2,1)}, bf16[48,64,128]{2,1,0:T(8,128)(2,1)}) custom-call(f32[192,512]{1,0:T(8,128)S(1)} %project.2.refs_0_, f32[192,512]{1,0:T(8,128)S(1)} %collective-permute-done.4.refs_1_, bf16[48,64,128]{2,1,0:T(8,128)(2,1)S(1)} %bitcast.4, f32[48,64,128]{2,1,0:T(8,128)S(1)} %get-tuple-element.47.refs_3_, ...), custom_call_target="tpu_custom_call" | custom-call | flops 301989888 | bytes 3145728 | tf_op jit(solution)/shard_map/finish/pallas_call | solution.py:404
  (1 shorter events, 0.0 us)
Async XLA Ops:
  1.5 11.8 %copy-start = (bf16[48,4,16,128]{3,2,1,0:T(8,128)(2,1)S(1)}, bf16[48,4,16,128]{3,2,1,0:T(8,128)(2,1)}, u32[]{:S(2)}) copy-start(bf16[48,4,16,128]{3,2,1,0:T(8,128)(2,1)} %param.11) | copy-start | bytes 2359300
  1.5 9.8 %collective-permute-start = (bf16[8,3584]{1,0:T(8,128)(2,1)S(1)}, bf16[8,3584]{1,0:T(8,128)(2,1)S(1)}, u32[]{:S(2)}, u32[]{:S(2)}) collective-permute-start(bf16[8,3584]{1,0:T(8,128)(2,1)S(1)} %payload.1.refs_0_), channel_id=1, source_target_pairs={{0,12},{2,14},{4,8},{6,10},{8,4},{10,6},{12,0},{14,2},{1,13},{3,15... | collective-permute-start | bytes 172040 | tf_op jit(solution)/shard_map/ppermute | solution.py:450
  6.6 5.1 %collective-permute-start.1 = (bf16[8,3584]{1,0:T(8,128)(2,1)S(1)}, bf16[8,3584]{1,0:T(8,128)(2,1)S(1)}, u32[]{:S(2)}, u32[]{:S(2)}) collective-permute-start(bf16[8,3584]{1,0:T(8,128)(2,1)S(1)} %payload.1.refs_0_), channel_id=1, source_target_pairs={{0,8},{2,10},{4,12},{6,14},{8,0},{10,2},{12,4},{14,6},{1,9},{3,11}... | collective-permute-start | bytes 172040 | tf_op jit(solution)/shard_map/ppermute | solution.py:450
  6.6 5.1 %collective-permute-start.2 = (bf16[8,3584]{1,0:T(8,128)(2,1)S(1)}, bf16[8,3584]{1,0:T(8,128)(2,1)S(1)}, u32[]{:S(2)}, u32[]{:S(2)}) collective-permute-start(bf16[8,3584]{1,0:T(8,128)(2,1)S(1)} %payload.1.refs_0_), channel_id=1, source_target_pairs={{0,4},{2,6},{4,0},{6,2},{8,12},{10,14},{12,8},{14,10},{1,5},{3,7},... | collective-permute-start | bytes 172040 | tf_op jit(solution)/shard_map/ppermute | solution.py:450
  11.7 7.4 %collective-permute-start.3 = (bf16[32,3584]{1,0:T(8,128)(2,1)S(1)}, bf16[32,3584]{1,0:T(8,128)(2,1)S(1)}, u32[]{:S(2)}, u32[]{:S(2)}) collective-permute-start(bf16[32,3584]{1,0:T(8,128)(2,1)S(1)} %join.1.refs_0_), channel_id=1, source_target_pairs={{0,2},{2,0},{4,6},{6,4},{8,10},{10,8},{12,14},{14,12},{1,3},{3,1},... | collective-permute-start | bytes 688136 | tf_op jit(solution)/shard_map/ppermute | solution.py:468
  20.4 1.8 %collective-permute-start.4 = (f32[192,512]{1,0:T(8,128)S(1)}, f32[192,512]{1,0:T(8,128)S(1)}, u32[]{:S(2)}, u32[]{:S(2)}) collective-permute-start(f32[192,512]{1,0:T(8,128)S(1)} %project.3), channel_id=1, source_target_pairs={{0,1},{1,0},{2,3},{3,2},{4,5},{5,4},{6,7},{7,6},{8,9},{9,8},{10,11... | collective-permute-start | bytes 1179656 | tf_op jit(solution)/shard_map/ppermute | solution.py:474

commit v21 on v20

--- a/solution.py
+++ b/solution.py
@@ -299,16 +299,25 @@
         ],
         axis=1,
     )
-    step = 512
-    for f in range(0, width, step):
-        down = jnp.concatenate([ref[:, f : f + step] for ref in gathered], axis=0).T
-        low_rank = jnp.dot(down, up, preferred_element_type=jnp.float32)
-        for c in range(2):
-            base = base_ref[c * parts + part, f : f + step, :].astype(jnp.float32)
-            merged[f : f + step, c * half : (c + 1) * half] = (base + low_rank[:, c * half : (c + 1) * half]).astype(
-                jnp.bfloat16
-            )
-    out_ref[...] = jnp.dot(hidden_ref[...], merged[...], preferred_element_type=jnp.float32)
+    step = 256
+
+    def merge(first, last):
+        for f in range(first, last, step):
+            down = jnp.concatenate([ref[:, f : f + step] for ref in gathered], axis=0).T
+            low_rank = jnp.dot(down, up, preferred_element_type=jnp.float32)
+            for c in range(2):
+                base = base_ref[c * parts + part, f : f + step, :].astype(jnp.float32)
+                merged[f : f + step, c * half : (c + 1) * half] = (
+                    base + low_rank[:, c * half : (c + 1) * half]
+                ).astype(jnp.bfloat16)
+
+    cuts = [0, width // 2, width]
+    total = None
+    for first, last in zip(cuts, cuts[1:]):
+        merge(first, last)
+        product = jnp.dot(hidden_ref[:, first:last], merged[first:last, :], preferred_element_type=jnp.float32)
+        total = product if total is None else total + product
+    out_ref[...] = total
 
 
 def project(k, hidden, base, gathered):
@@ -354,11 +363,19 @@
     def rows_of(ref, pair):
         return ref[2 * pair : 2 * pair + 2].reshape(many, size)
 
-    scores = [
-        lax.dot_general(new_lines(0, p), rows_of(q_ref, p), NT, preferred_element_type=jnp.float32)
-        for p in range(rows // 2)
-    ]
-    scores = jnp.stack([jnp.where(live, s, LOW) for s in scores])
+    def two_scores(p):
+        lines = jnp.concatenate(
+            [
+                jnp.concatenate([new_lines(0, p), nothing], axis=1),
+                jnp.concatenate([nothing, new_lines(0, p + 1)], axis=1),
+            ],
+            axis=0,
+        )
+        both_q = jnp.concatenate([rows_of(q_ref, p), rows_of(q_ref, p + 1)], axis=1)
+        return lax.dot_general(lines, both_q, NT, preferred_element_type=jnp.float32).reshape(2, keys, many)
+
+    scores = jnp.concatenate([two_scores(p) for p in range(0, rows // 2, 2)], axis=0)
+    scores = jnp.where(live[None], scores, LOW)
     old_top = top_ref[...]
     top = jnp.maximum(old_top, jnp.max(scores, axis=1))
     expo = jnp.exp((scores - top[:, None, :]) * scale)
@@ -461,7 +478,7 @@
     blocks = gather_second(factor_a, factor_b, dp)
     rows, steps, heads, size = queries.shape
     queries = queries.reshape(rows, steps * heads, size)
-    chunk, early = 8, 3
+    chunk, early = 12, 2
     tokens, base, keys, values = arrange(hidden, base_weight, cache, chunk, early)
     blocks, tokens, base, keys, values = lax.optimization_barrier((blocks, tokens, base, keys, values))
     gathered = join(blocks) if len(blocks) > 1 else blocks[0]

time: 24.5 us -> 24.2 us (0.988)
  Pallas kernels: 15.4 us -> 14.8 us
    pallas_call x1, Pallas kernels: 5.73 us -> 5.32 us  [attend_cached(): pl.pallas_call(functools.partial(cached_kernel, chunk, early, heads, size...]
  transfers between devices with their start and end apart: 5 -> 5, of which waited for: 2 -> 2; matrix products, arithmetic and copies ran while one was open for 0% -> 0% of each run, Pallas kernels for 46% -> 44%
where the time goes in v21:
time: 24.2 us; the launch traced here: 24 us
  Pallas kernels  14.8 us (61%)
  starting transfers between devices  7.44 us (31%)
  waiting for transfers between devices  0.96 us (4%)
  between operations  0.71 us (3%)
    ppermute x3, starting transfers between devices, gather_second(): lax.ppermute(payload, 'dp', [(i, i ^ 2 * k) for i in range(dp)])  5.76 us
    pallas_call x1, Pallas kernels, attend_cached(): pl.pallas_call(functools.partial(cached_kernel, chunk, early, heads, size...  5.32 us
    pallas_call x1, Pallas kernels, arrange(): pl.pallas_call(functools.partial(arrange_kernel, chunks, chunk, early), o...  3.8 us
    pallas_call x2, Pallas kernels, project(): pl.pallas_call(functools.partial(project_kernel, k), out_shape=pltpu.VMEM...  2.75 us
    pallas_call x1, Pallas kernels, finish(): pl.pallas_call(functools.partial(finish_kernel, steps, heads, size ** (-0...  2.15 us
    ppermute x1, starting transfers between devices, shards(): lax.ppermute(gathered, 'dp', [(i, i ^ 1) for i in range(dp)])  1.61 us
    pallas_call x1, Pallas kernels, make_payload(): pl.pallas_call(payload_kernel, out_shape=pltpu.VMEM((ranks, width + group...  0.81 us
    ppermute x3, waiting for transfers between devices, gather_second(): lax.ppermute(payload, 'dp', [(i, i ^ 2 * k) for i in range(dp)])  0.62 us
  transfers between devices with their start and end apart: 5, of which 2 were waited for; matrix products, arithmetic and copies ran while one was open for 0% of the time, Pallas kernels for 44%

profile of v21, /device:TPU:0, one launch (start us, length us, event | category | flops | bytes accessed | tf_op | source)
XLA Modules:
  0.0 24.0 jit_solution(14230134750431014217)
XLA Ops:
  0.6 0.8 %payload.1.refs_0_ = bf16[8,3584]{1,0:T(8,128)(2,1)S(1)} custom-call(bf16[8,2560]{1,0:T(8,128)(2,1)} %bitcast.5, bf16[8,2,4,128]{3,2,1,0:T(4,128)(2,1)} %up_hbm.1), custom_call_target="tpu_custom_call" | custom-call | tf_op jit(solution)/shard_map/payload/pallas_call | solution.py:51
  1.5 0.0 copy-start
  1.5 5.1 %collective-permute-start = (bf16[8,3584]{1,0:T(8,128)(2,1)S(1)}, bf16[8,3584]{1,0:T(8,128)(2,1)S(1)}, u32[]{:S(2)}, u32[]{:S(2)}) collective-permute-start(bf16[8,3584]{1,0:T(8,128)(2,1)S(1)} %payload.1.refs_0_), channel_id=1, source_target_pairs={{0,12},{2,14},{4,8},{6,10},{8,4},{10,6},{12,0},{14,2},{1,13},{3,15... | collective-permute-start | bytes 172040 | tf_op jit(solution)/shard_map/ppermute | solution.py:467
  6.6 0.0 collective-permute-start.1
  6.6 0.6 %collective-permute-start.2 = (bf16[8,3584]{1,0:T(8,128)(2,1)S(1)}, bf16[8,3584]{1,0:T(8,128)(2,1)S(1)}, u32[]{:S(2)}, u32[]{:S(2)}) collective-permute-start(bf16[8,3584]{1,0:T(8,128)(2,1)S(1)} %payload.1.refs_0_), channel_id=1, source_target_pairs={{0,4},{2,6},{4,0},{6,2},{8,12},{10,14},{12,8},{14,10},{1,5},{3,7},... | collective-permute-start | bytes 172040 | tf_op jit(solution)/shard_map/ppermute | solution.py:467
  7.2 3.8 %arrange.1 = (bf16[192,2560]{1,0:T(8,128)(2,1)S(1)}, bf16[4,2560,256]{2,1,0:T(8,128)(2,1)S(1)}, bf16[48,128,2,128]{3,2,1,0:T(2,128)(2,1)S(1)}, bf16[48,128,2,128]{3,2,1,0:T(2,128)(2,1)S(1)}) custom-call(bf16[48,128,2,2,128]{4,3,2,1,0:T(2,128)(2,1)} %refs_1_.3, bf16[48,4,2560]{2,1,0:T(4,128)(2,1)} %refs_1_.2, bf16[2560,2,4,128]{3,2,1,0:T(4,128)(2,1)} %refs_2_.1), custom_call_target="tpu_custom_call" | custom-call | flops 1342177280 | bytes 12451840 | tf_op jit(solution)/shard_map/arrange/pallas_call | solution.py:270
  11.0 0.0 collective-permute-done.refs_1_
  11.0 0.6 %collective-permute-done.1.refs_2_ = bf16[8,3584]{1,0:T(8,128)(2,1)S(1)} collective-permute-done((bf16[8,3584]{1,0:T(8,128)(2,1)S(1)}, bf16[8,3584]{1,0:T(8,128)(2,1)S(1)}, u32[]{:S(2)}, u32[]{:S(2)}) %collective-permute-start.1) | collective-permute-done | bytes 57376 | tf_op jit(solution)/shard_map/ppermute | solution.py:467
  11.7 0.0 collective-permute-done.2.refs_3_
  11.7 1.6 %collective-permute-start.3 = (bf16[32,3584]{1,0:T(8,128)(2,1)S(1)}, bf16[32,3584]{1,0:T(8,128)(2,1)S(1)}, u32[]{:S(2)}, u32[]{:S(2)}) collective-permute-start(bf16[32,3584]{1,0:T(8,128)(2,1)S(1)} %join.1.refs_0_), channel_id=1, source_target_pairs={{0,2},{2,0},{4,6},{6,4},{8,10},{10,8},{12,14},{14,12},{1,3},{3,1},... | collective-permute-start | bytes 688136 | tf_op jit(solution)/shard_map/ppermute | solution.py:485
  13.3 0.0 copy-done
  13.3 5.3 %attend_cached.1 = (bf16[48,128,2,128]{3,2,1,0:T(2,128)(2,1)S(1)}, bf16[48,128,2,128]{3,2,1,0:T(2,128)(2,1)S(1)}, f32[48,64,128]{2,1,0:T(8,128)S(1)}, f32[24,128]{1,0:T(8,128)S(1)}, f32[24,128]{1,0:T(8,128)S(1)}) custom-call(s32[48]{0:T(128)} %refs_0_.3, bf16[48,128,2,2,128]{4,3,2,1,0:T(2,128)(2,1)} %refs_1_.3, ...), custom_call_target="tpu_custom_call", output_to_operand_aliasing={{0}: (3, {}), {1}: (4, {})} | custom-call | flops 402653184 | bytes 6291456 | tf_op jit(solution)/shard_map/attend_cached/pallas_call | solution.py:187
  18.6 0.0 collective-permute-done.3.refs_1_
  18.6 1.4 %project.3 = f32[192,512]{1,0:T(8,128)S(1)} custom-call(bf16[192,2560]{1,0:T(8,128)(2,1)S(1)} %get-tuple-element.42.hidden_ref, bf16[4,2560,256]{2,1,0:T(8,128)(2,1)S(1)} %get-tuple-element.43.base_ref, bf16[32,3584]{1,0:T(8,128)(2,1)S(1)} %join.1.refs_0_, bf16[32,3584]{1,0:T(8,128)(2,1)S(1)} %collective-permute-done.3.refs_1_), custom_call_target="tpu_custom_call" | custom-call | flops 671088640 | bytes 3604480 | tf_op jit(solution)/shard_map/project/pallas_call | solution.py:327
  20.0 0.1 collective-permute-start.4
  20.1 1.4 %project.2.refs_0_ = f32[192,512]{1,0:T(8,128)S(1)} custom-call(bf16[192,2560]{1,0:T(8,128)(2,1)S(1)} %get-tuple-element.42.hidden_ref, bf16[4,2560,256]{2,1,0:T(8,128)(2,1)S(1)} %get-tuple-element.43.base_ref, bf16[32,3584]{1,0:T(8,128)(2,1)S(1)} %join.1.refs_0_, bf16[32,3584]{1,0:T(8,128)(2,1)S(1)} %collective-permute-done.3.refs_1_), custom_call_target="tpu_custom_call" | custom-call | flops 671088640 | bytes 3604480 | tf_op jit(solution)/shard_map/project/pallas_call | solution.py:327
  21.5 0.3 %collective-permute-done.4.refs_1_ = f32[192,512]{1,0:T(8,128)S(1)} collective-permute-done((f32[192,512]{1,0:T(8,128)S(1)}, f32[192,512]{1,0:T(8,128)S(1)}, u32[]{:S(2)}, u32[]{:S(2)}) %collective-permute-start.4) | collective-permute-done | bytes 393248 | tf_op jit(solution)/shard_map/ppermute | solution.py:491
  21.8 2.1 %finish.1 = (bf16[48,4,2,2,128]{4,3,2,1,0:T(2,128)(2,1)}, bf16[48,64,128]{2,1,0:T(8,128)(2,1)}) custom-call(f32[192,512]{1,0:T(8,128)S(1)} %project.2.refs_0_, f32[192,512]{1,0:T(8,128)S(1)} %collective-permute-done.4.refs_1_, bf16[48,64,128]{2,1,0:T(8,128)(2,1)S(1)} %bitcast.4, f32[48,64,128]{2,1,0:T(8,128)S(1)} %get-tuple-element.47.refs_3_, ...), custom_call_target="tpu_custom_call" | custom-call | flops 301989888 | bytes 3145728 | tf_op jit(solution)/shard_map/finish/pallas_call | solution.py:421
  (1 shorter events, 0.0 us)
Async XLA Ops:
  1.5 11.8 %copy-start = (bf16[48,4,16,128]{3,2,1,0:T(8,128)(2,1)S(1)}, bf16[48,4,16,128]{3,2,1,0:T(8,128)(2,1)}, u32[]{:S(2)}) copy-start(bf16[48,4,16,128]{3,2,1,0:T(8,128)(2,1)} %param.11) | copy-start | bytes 2359300
  1.5 9.6 %collective-permute-start = (bf16[8,3584]{1,0:T(8,128)(2,1)S(1)}, bf16[8,3584]{1,0:T(8,128)(2,1)S(1)}, u32[]{:S(2)}, u32[]{:S(2)}) collective-permute-start(bf16[8,3584]{1,0:T(8,128)(2,1)S(1)} %payload.1.refs_0_), channel_id=1, source_target_pairs={{0,12},{2,14},{4,8},{6,10},{8,4},{10,6},{12,0},{14,2},{1,13},{3,15... | collective-permute-start | bytes 172040 | tf_op jit(solution)/shard_map/ppermute | solution.py:467
  6.6 5.1 %collective-permute-start.1 = (bf16[8,3584]{1,0:T(8,128)(2,1)S(1)}, bf16[8,3584]{1,0:T(8,128)(2,1)S(1)}, u32[]{:S(2)}, u32[]{:S(2)}) collective-permute-start(bf16[8,3584]{1,0:T(8,128)(2,1)S(1)} %payload.1.refs_0_), channel_id=1, source_target_pairs={{0,8},{2,10},{4,12},{6,14},{8,0},{10,2},{12,4},{14,6},{1,9},{3,11}... | collective-permute-start | bytes 172040 | tf_op jit(solution)/shard_map/ppermute | solution.py:467
  6.6 5.1 %collective-permute-start.2 = (bf16[8,3584]{1,0:T(8,128)(2,1)S(1)}, bf16[8,3584]{1,0:T(8,128)(2,1)S(1)}, u32[]{:S(2)}, u32[]{:S(2)}) collective-permute-start(bf16[8,3584]{1,0:T(8,128)(2,1)S(1)} %payload.1.refs_0_), channel_id=1, source_target_pairs={{0,4},{2,6},{4,0},{6,2},{8,12},{10,14},{12,8},{14,10},{1,5},{3,7},... | collective-permute-start | bytes 172040 | tf_op jit(solution)/shard_map/ppermute | solution.py:467
  11.7 6.9 %collective-permute-start.3 = (bf16[32,3584]{1,0:T(8,128)(2,1)S(1)}, bf16[32,3584]{1,0:T(8,128)(2,1)S(1)}, u32[]{:S(2)}, u32[]{:S(2)}) collective-permute-start(bf16[32,3584]{1,0:T(8,128)(2,1)S(1)} %join.1.refs_0_), channel_id=1, source_target_pairs={{0,2},{2,0},{4,6},{6,4},{8,10},{10,8},{12,14},{14,12},{1,3},{3,1},... | collective-permute-start | bytes 688136 | tf_op jit(solution)/shard_map/ppermute | solution.py:485
  20.0 1.8 %collective-permute-start.4 = (f32[192,512]{1,0:T(8,128)S(1)}, f32[192,512]{1,0:T(8,128)S(1)}, u32[]{:S(2)}, u32[]{:S(2)}) collective-permute-start(f32[192,512]{1,0:T(8,128)S(1)} %project.3), channel_id=1, source_target_pairs={{0,1},{1,0},{2,3},{3,2},{4,5},{5,4},{6,7},{7,6},{8,9},{9,8},{10,11... | collective-permute-start | bytes 1179656 | tf_op jit(solution)/shard_map/ppermute | solution.py:491

commit v22 on v21

--- a/solution.py
+++ b/solution.py
@@ -31,15 +31,18 @@
 
 def payload_kernel(down_hbm, up_hbm, out_ref, ups, wide, sems):
     ranks, width = down_hbm.shape
-    groups, size = ups.shape[1] * ups.shape[2], ups.shape[3]
+    _, two, kvh, size = ups.shape
+    groups, own = two * kvh, kvh // 2
     get_down = pltpu.make_async_copy(down_hbm, out_ref.at[:, pl.ds(0, width)], sems.at[0])
     get_up = pltpu.make_async_copy(up_hbm, ups, sems.at[1])
     get_up.start()
     get_down.start()
     get_up.wait()
     wide[...] = ups.reshape(ranks * groups, size)[...].astype(jnp.float32)
-    for n in range(groups):
-        out_ref[:, width + n * size : width + (n + 1) * size] = wide[pl.ds(n, ranks, stride=groups), :].astype(
+    other = 1 - lax.axis_index("tp")
+    for n in range(groups // 2):
+        head = n // own * kvh + other * own + n % own
+        out_ref[:, width + n * size : width + (n + 1) * size] = wide[pl.ds(head, ranks, stride=groups), :].astype(
             jnp.bfloat16
         )
     get_down.wait()
@@ -50,7 +53,7 @@
     groups, size = up.shape[1] * up.shape[2], up.shape[3]
     return pl.pallas_call(
         payload_kernel,
-        out_shape=pltpu.VMEM((ranks, width + groups * size), jnp.bfloat16),
+        out_shape=pltpu.VMEM((ranks, width + groups // 2 * size), jnp.bfloat16),
         in_specs=[pl.BlockSpec(memory_space=pltpu.HBM)] * 2,
         out_specs=VMEM,
         scratch_shapes=[
@@ -284,26 +287,18 @@
     )(in_hbm(cache), in_hbm(hidden), in_hbm(base))
 
 
-def project_kernel(k, hidden_ref, base_ref, *refs):
-    gathered, (out_ref, merged) = refs[:-2], refs[-2:]
+def project_kernel(k, at, count, hidden_ref, base_ref, *refs):
+    downs, ups, (out_ref, merged) = refs[:count], refs[count:-2], refs[-2:]
     width, columns = merged.shape
     part = lax.axis_index("tp") ^ k
     parts = base_ref.shape[0] // 2
     half = columns // 2
-    up = jnp.concatenate(
-        [
-            jnp.concatenate(
-                [ref[:, pl.ds(pl.multiple_of(width + (c * parts + part) * half, 128), half)] for ref in gathered], axis=0
-            )
-            for c in range(2)
-        ],
-        axis=1,
-    )
+    up = jnp.concatenate([ref[:, at : at + columns] for ref in ups], axis=0)
     step = 256
 
     def merge(first, last):
         for f in range(first, last, step):
-            down = jnp.concatenate([ref[:, f : f + step] for ref in gathered], axis=0).T
+            down = jnp.concatenate([ref[:, f : f + step] for ref in downs], axis=0).T
             low_rank = jnp.dot(down, up, preferred_element_type=jnp.float32)
             for c in range(2):
                 base = base_ref[c * parts + part, f : f + step, :].astype(jnp.float32)
@@ -320,20 +315,20 @@
     out_ref[...] = total
 
 
-def project(k, hidden, base, gathered):
+def project(k, hidden, base, downs, ups, at):
     tokens, width = hidden.shape
     columns = 2 * base.shape[2]
-    ranks = sum(g.shape[0] for g in gathered)
+    ranks = sum(g.shape[0] for g in downs)
     return pl.pallas_call(
-        functools.partial(project_kernel, k),
+        functools.partial(project_kernel, k, at, len(downs)),
         out_shape=pltpu.VMEM((tokens, columns), jnp.float32),
-        in_specs=[VMEM] * (2 + len(gathered)),
+        in_specs=[VMEM] * (2 + len(downs) + len(ups)),
         out_specs=VMEM,
         scratch_shapes=[pltpu.VMEM((width, columns), jnp.bfloat16)],
         compiler_params=params(24),
         cost_estimate=cost(2 * width * columns * (tokens + ranks), 2 * width * columns + 2 * width * tokens),
         name="project",
-    )(hidden, base, *gathered)
+    )(hidden, base, *downs, *ups)
 
 
 def finish_kernel(steps, heads, scale, terms, *refs):
@@ -363,19 +358,11 @@
     def rows_of(ref, pair):
         return ref[2 * pair : 2 * pair + 2].reshape(many, size)
 
-    def two_scores(p):
-        lines = jnp.concatenate(
-            [
-                jnp.concatenate([new_lines(0, p), nothing], axis=1),
-                jnp.concatenate([nothing, new_lines(0, p + 1)], axis=1),
-            ],
-            axis=0,
-        )
-        both_q = jnp.concatenate([rows_of(q_ref, p), rows_of(q_ref, p + 1)], axis=1)
-        return lax.dot_general(lines, both_q, NT, preferred_element_type=jnp.float32).reshape(2, keys, many)
-
-    scores = jnp.concatenate([two_scores(p) for p in range(0, rows // 2, 2)], axis=0)
-    scores = jnp.where(live[None], scores, LOW)
+    scores = [
+        lax.dot_general(new_lines(0, p), rows_of(q_ref, p), NT, preferred_element_type=jnp.float32)
+        for p in range(rows // 2)
+    ]
+    scores = jnp.stack([jnp.where(live, s, LOW) for s in scores])
     old_top = top_ref[...]
     top = jnp.maximum(old_top, jnp.max(scores, axis=1))
     expo = jnp.exp((scores - top[:, None, :]) * scale)
@@ -439,19 +426,19 @@
     return fresh, context.reshape(rows, steps, heads, size)
 
 
-def join_kernel(*refs):
+def join_kernel(first, *refs):
     blocks, out_ref = refs[:-1], refs[-1]
     at = 0
     for block in blocks:
-        out_ref[at : at + block.shape[0], :] = block[...]
+        out_ref[at : at + block.shape[0], :] = block[:, first:]
         at += block.shape[0]
 
 
-def join(blocks):
+def join(blocks, first=0):
     rows = sum(b.shape[0] for b in blocks)
     return pl.pallas_call(
-        join_kernel,
-        out_shape=pltpu.VMEM((rows, blocks[0].shape[1]), jnp.bfloat16),
+        functools.partial(join_kernel, first),
+        out_shape=pltpu.VMEM((rows, blocks[0].shape[1] - first), jnp.bfloat16),
         in_specs=[VMEM] * len(blocks),
         out_specs=VMEM,
         compiler_params=params(8),
@@ -459,37 +446,44 @@
     )(*blocks)
 
 
-def gather_second(factor_a, factor_b, dp):
-    count = dp // 2
-    ranks = factor_b.shape[0]
-    if ranks % 8 == 0 and count in (1, 2, 4):
-        payload = make_payload(factor_a.T, factor_b)
-        return [payload] + [lax.ppermute(payload, "dp", [(i, i ^ (2 * k)) for i in range(dp)]) for k in range(count - 1, 0, -1)]
-    payload = jnp.concatenate([factor_a.T, factor_b.reshape(ranks, -1)], axis=1)
-    groups = [[i for i in range(dp) if i % 2 == n] for n in range(2)]
-    copies = jnp.broadcast_to(payload[None], (count,) + payload.shape)
-    blocks = lax.all_to_all(copies, "dp", 0, 0, axis_index_groups=groups, tiled=True)
-    return [blocks.reshape(count * ranks, payload.shape[1])]
-
-
 def shards(dp, tp, hidden, base_weight, factor_a, factor_b, queries, cache, lengths):
-    steps, own = queries.shape[1], cache.shape[3]
-    assert dp % 2 == 0
-    blocks = gather_second(factor_a, factor_b, dp)
     rows, steps, heads, size = queries.shape
+    own = cache.shape[3]
+    ranks, width = factor_b.shape[0], factor_a.shape[0]
     queries = queries.reshape(rows, steps * heads, size)
     chunk, early = 12, 2
+
+    def swap(x, axis, count, k):
+        return lax.ppermute(x, axis, [(i, i ^ k) for i in range(count)])
+
+    short = dp == 8 and tp == 2 and ranks % 8 == 0
+    if short:
+        payload = make_payload(factor_a.T, factor_b)
+        blocks = [payload] + [swap(payload, "dp", dp, k) for k in (6, 4, 2)]
+    else:
+        payload = jnp.concatenate([factor_a.T, factor_b.reshape(ranks, -1)], axis=1)
+        copies = jnp.broadcast_to(payload[None], (dp,) + payload.shape)
+        blocks = [lax.all_to_all(copies, "dp", 0, 0, tiled=True).reshape(dp * ranks, payload.shape[1])]
     tokens, base, keys, values = arrange(hidden, base_weight, cache, chunk, early)
     blocks, tokens, base, keys, values = lax.optimization_barrier((blocks, tokens, base, keys, values))
-    gathered = join(blocks) if len(blocks) > 1 else blocks[0]
-    gathered = [gathered, lax.ppermute(gathered, "dp", [(i, i ^ 1) for i in range(dp)])]
+    if short:
+        block = join(blocks)
+        blocks = [block, swap(block, "dp", dp, 1)]
     state = attend_cached(queries, cache, lengths, keys, values, steps, chunk, early)
-    gathered, state, tokens, base = lax.optimization_barrier((gathered, state, tokens, base))
+    blocks, state, tokens, base = lax.optimization_barrier((blocks, state, tokens, base))
+    if short:
+        blocks, up = lax.optimization_barrier((blocks, join(blocks, width)))
+        ups = {1: (blocks, width), 0: ([swap(up, "tp", tp, 1)], 0)}
+    else:
+        by_part = blocks[0][:, width:].reshape(-1, 2, tp, own * size)
+        me = lax.axis_index("tp")
+        pick = [lax.dynamic_index_in_dim(by_part, me ^ k, 2, keepdims=False) for k in range(tp)]
+        ups = {k: ([pick[k].reshape(-1, 2 * own * size)], 0) for k in range(tp)}
     received = []
     for k in range(1, tp):
-        other = project(k, tokens, base, gathered)
-        received.append(lax.ppermute(other, "tp", [(i, i ^ k) for i in range(tp)]))
-    mine = project(0, tokens, base, gathered)
+        other = project(k, tokens, base, blocks, *ups[k])
+        received.append(swap(other, "tp", tp, k))
+    mine = project(0, tokens, base, blocks, *ups[0])
     return finish([mine] + received, state, steps, own)
 
 

time: 24.2 us -> 25.5 us (1.054)
  waiting for transfers between devices: 0.96 us -> 1.85 us
  starting transfers between devices: 7.44 us -> 7.91 us
    ppermute x5 -> x6, waiting for transfers between devices: 0.96 us -> 1.85 us  [swap(): return lax.ppermute(x, axis, [(i, i ^ k) for i in range(count)])]
    ppermute x5 -> x6, starting transfers between devices: 7.44 us -> 7.91 us  [swap(): return lax.ppermute(x, axis, [(i, i ^ k) for i in range(count)])]
    pallas_call x3 -> x4, Pallas kernels: 2.77 us -> 2.76 us  [the longest x2 2.74 us: project(): pl.pallas_call(functools.partial(project_kernel, k, at, len(downs)), out_...]
  transfers between devices with their start and end apart: 5 -> 6, of which waited for: 2 -> 2; matrix products, arithmetic and copies ran while one was open for 0% -> 0% of each run, Pallas kernels for 44% -> 42%
where the time goes in v22:
time: 25.5 us; the launch traced here: 25.2 us
  Pallas kernels  14.7 us (58%)
  starting transfers between devices  7.91 us (31%)
  waiting for transfers between devices  1.85 us (7%)
  between operations  0.73 us (3%)
    ppermute x6, starting transfers between devices, swap(): return lax.ppermute(x, axis, [(i, i ^ k) for i in range(count)])  7.91 us
    pallas_call x1, Pallas kernels, attend_cached(): pl.pallas_call(functools.partial(cached_kernel, chunk, early, heads, size...  5.33 us
    pallas_call x1, Pallas kernels, arrange(): pl.pallas_call(functools.partial(arrange_kernel, chunks, chunk, early), o...  3.8 us
    pallas_call x2, Pallas kernels, project(): pl.pallas_call(functools.partial(project_kernel, k, at, len(downs)), out_...  2.74 us
    pallas_call x1, Pallas kernels, finish(): pl.pallas_call(functools.partial(finish_kernel, steps, heads, size ** (-0...  2.05 us
    ppermute x6, waiting for transfers between devices, swap(): return lax.ppermute(x, axis, [(i, i ^ k) for i in range(count)])  1.85 us
    pallas_call x1, Pallas kernels, make_payload(): pl.pallas_call(payload_kernel, out_shape=pltpu.VMEM((ranks, width + group...  0.81 us
  transfers between devices with their start and end apart: 6, of which 2 were waited for; matrix products, arithmetic and copies ran while one was open for 0% of the time, Pallas kernels for 42%

profile of v22, /device:TPU:0, one launch (start us, length us, event | category | flops | bytes accessed | tf_op | source)
XLA Modules:
  0.0 25.2 jit_solution(11197781988595295681)
XLA Ops:
  0.6 0.8 %payload.1.refs_0_ = bf16[8,3072]{1,0:T(8,128)(2,1)S(1)} custom-call(bf16[8,2560]{1,0:T(8,128)(2,1)} %bitcast.5, bf16[8,2,4,128]{3,2,1,0:T(4,128)(2,1)} %up_hbm.1), custom_call_target="tpu_custom_call" | custom-call | tf_op jit(solution)/shard_map/payload/pallas_call | solution.py:54
  1.5 0.0 copy-start
  1.5 5.1 %collective-permute-start = (bf16[8,3072]{1,0:T(8,128)(2,1)S(1)}, bf16[8,3072]{1,0:T(8,128)(2,1)S(1)}, u32[]{:S(2)}, u32[]{:S(2)}) collective-permute-start(bf16[8,3072]{1,0:T(8,128)(2,1)S(1)} %payload.1.refs_0_), channel_id=1, source_target_pairs={{0,12},{2,14},{4,8},{6,10},{8,4},{10,6},{12,0},{14,2},{1,13},{3,15... | collective-permute-start | bytes 147464 | tf_op jit(solution)/shard_map/ppermute | solution.py:457
  6.6 0.0 collective-permute-start.1
  6.6 0.6 %collective-permute-start.2 = (bf16[8,3072]{1,0:T(8,128)(2,1)S(1)}, bf16[8,3072]{1,0:T(8,128)(2,1)S(1)}, u32[]{:S(2)}, u32[]{:S(2)}) collective-permute-start(bf16[8,3072]{1,0:T(8,128)(2,1)S(1)} %payload.1.refs_0_), channel_id=1, source_target_pairs={{0,4},{2,6},{4,0},{6,2},{8,12},{10,14},{12,8},{14,10},{1,5},{3,7},... | collective-permute-start | bytes 147464 | tf_op jit(solution)/shard_map/ppermute | solution.py:457
  7.2 3.8 %arrange.1 = (bf16[192,2560]{1,0:T(8,128)(2,1)S(1)}, bf16[4,2560,256]{2,1,0:T(8,128)(2,1)S(1)}, bf16[48,128,2,128]{3,2,1,0:T(2,128)(2,1)S(1)}, bf16[48,128,2,128]{3,2,1,0:T(2,128)(2,1)S(1)}) custom-call(bf16[48,128,2,2,128]{4,3,2,1,0:T(2,128)(2,1)} %refs_1_.3, bf16[48,4,2560]{2,1,0:T(4,128)(2,1)} %refs_1_.2, bf16[2560,2,4,128]{3,2,1,0:T(4,128)(2,1)} %refs_2_.1), custom_call_target="tpu_custom_call" | custom-call | flops 1342177280 | bytes 12451840 | tf_op jit(solution)/shard_map/arrange/pallas_call | solution.py:273
  11.0 0.0 collective-permute-done.refs_1_
  11.0 0.5 %collective-permute-done.1.refs_2_ = bf16[8,3072]{1,0:T(8,128)(2,1)S(1)} collective-permute-done((bf16[8,3072]{1,0:T(8,128)(2,1)S(1)}, bf16[8,3072]{1,0:T(8,128)(2,1)S(1)}, u32[]{:S(2)}, u32[]{:S(2)}) %collective-permute-start.1) | collective-permute-done | bytes 49184 | tf_op jit(solution)/shard_map/ppermute | solution.py:457
  11.6 0.0 collective-permute-done.2.refs_3_
  11.6 1.6 %collective-permute-start.3 = (bf16[32,3072]{1,0:T(8,128)(2,1)S(1)}, bf16[32,3072]{1,0:T(8,128)(2,1)S(1)}, u32[]{:S(2)}, u32[]{:S(2)}) collective-permute-start(bf16[32,3072]{1,0:T(8,128)(2,1)S(1)} %join.2.refs_0_.refs_2_), channel_id=1, source_target_pairs={{0,2},{2,0},{4,6},{6,4},{8,10},{10,8},{12,14},{14,12},{1,3},{3,1},... | collective-permute-start | bytes 589832 | tf_op jit(solution)/shard_map/ppermute | solution.py:457
  13.2 0.0 copy-done
  13.2 5.3 %attend_cached.1 = (bf16[48,128,2,128]{3,2,1,0:T(2,128)(2,1)S(1)}, bf16[48,128,2,128]{3,2,1,0:T(2,128)(2,1)S(1)}, f32[48,64,128]{2,1,0:T(8,128)S(1)}, f32[24,128]{1,0:T(8,128)S(1)}, f32[24,128]{1,0:T(8,128)S(1)}) custom-call(s32[48]{0:T(128)} %refs_0_.3, bf16[48,128,2,2,128]{4,3,2,1,0:T(2,128)(2,1)} %refs_1_.3, ...), custom_call_target="tpu_custom_call", output_to_operand_aliasing={{0}: (3, {}), {1}: (4, {})} | custom-call | flops 402653184 | bytes 6291456 | tf_op jit(solution)/shard_map/attend_cached/pallas_call | solution.py:190
  18.5 0.0 collective-permute-done.3.refs_1_.refs_3_
  18.5 1.4 %project.3 = f32[192,512]{1,0:T(8,128)S(1)} custom-call(bf16[192,2560]{1,0:T(8,128)(2,1)S(1)} %get-tuple-element.45.hidden_ref, bf16[4,2560,256]{2,1,0:T(8,128)(2,1)S(1)} %get-tuple-element.46.base_ref, bf16[32,3072]{1,0:T(8,128)(2,1)S(1)} %join.2.refs_0_.refs_2_, bf16[32,3072]{1,0:T(8,128)(2,1)S(1)} %collective-permute-done.3.refs_1_.refs_3_, ...), custom_call_target="tpu_custom_call" | custom-call | flops 671088640 | bytes 3604480 | tf_op jit(solution)/shard_map/project/pallas_call | solution.py:322
  19.9 0.1 collective-permute-start.5
  20.0 0.5 %collective-permute-start.4 = (bf16[64,512]{1,0:T(8,128)(2,1)S(1)}, bf16[64,512]{1,0:T(8,128)(2,1)S(1)}, u32[]{:S(2)}, u32[]{:S(2)}) collective-permute-start(bf16[64,512]{1,0:T(8,128)(2,1)S(1)} %join.3), channel_id=1, source_target_pairs={{0,1},{1,0},{2,3},{3,2},{4,5},{5,4},{6,7},{7,6},{8,9},{9,8},{10,11... | collective-permute-start | bytes 196616 | tf_op jit(solution)/shard_map/ppermute | solution.py:457
  20.5 1.3 %collective-permute-done.4.refs_2_ = bf16[64,512]{1,0:T(8,128)(2,1)S(1)} collective-permute-done((bf16[64,512]{1,0:T(8,128)(2,1)S(1)}, bf16[64,512]{1,0:T(8,128)(2,1)S(1)}, u32[]{:S(2)}, u32[]{:S(2)}) %collective-permute-start.4) | collective-permute-done | bytes 65568 | tf_op jit(solution)/shard_map/ppermute | solution.py:457
  21.8 1.4 %project.2.refs_0_ = f32[192,512]{1,0:T(8,128)S(1)} custom-call(bf16[192,2560]{1,0:T(8,128)(2,1)S(1)} %get-tuple-element.45.hidden_ref, bf16[4,2560,256]{2,1,0:T(8,128)(2,1)S(1)} %get-tuple-element.46.base_ref, bf16[32,3072]{1,0:T(8,128)(2,1)S(1)} %join.2.refs_0_.refs_2_, bf16[32,3072]{1,0:T(8,128)(2,1)S(1)} %collective-permute-done.3.refs_1_.refs_3_, ...), custom_call_target="tpu_custom_call" | custom-call | flops 671088640 | bytes 3604480 | tf_op jit(solution)/shard_map/project/pallas_call | solution.py:322
  23.2 0.0 collective-permute-done.5.refs_1_
  23.2 2.1 %finish.1 = (bf16[48,4,2,2,128]{4,3,2,1,0:T(2,128)(2,1)}, bf16[48,64,128]{2,1,0:T(8,128)(2,1)}) custom-call(f32[192,512]{1,0:T(8,128)S(1)} %project.2.refs_0_, f32[192,512]{1,0:T(8,128)S(1)} %collective-permute-done.5.refs_1_, bf16[48,64,128]{2,1,0:T(8,128)(2,1)S(1)} %bitcast.4, f32[48,64,128]{2,1,0:T(8,128)S(1)} %get-tuple-element.53.refs_3_, ...), custom_call_target="tpu_custom_call" | custom-call | flops 301989888 | bytes 3145728 | tf_op jit(solution)/shard_map/finish/pallas_call | solution.py:408
  (2 shorter events, 0.0 us)
Async XLA Ops:
  1.5 11.7 %copy-start = (bf16[48,4,16,128]{3,2,1,0:T(8,128)(2,1)S(1)}, bf16[48,4,16,128]{3,2,1,0:T(8,128)(2,1)}, u32[]{:S(2)}) copy-start(bf16[48,4,16,128]{3,2,1,0:T(8,128)(2,1)} %param.11) | copy-start | bytes 2359300
  1.5 9.6 %collective-permute-start = (bf16[8,3072]{1,0:T(8,128)(2,1)S(1)}, bf16[8,3072]{1,0:T(8,128)(2,1)S(1)}, u32[]{:S(2)}, u32[]{:S(2)}) collective-permute-start(bf16[8,3072]{1,0:T(8,128)(2,1)S(1)} %payload.1.refs_0_), channel_id=1, source_target_pairs={{0,12},{2,14},{4,8},{6,10},{8,4},{10,6},{12,0},{14,2},{1,13},{3,15... | collective-permute-start | bytes 147464 | tf_op jit(solution)/shard_map/ppermute | solution.py:457
  6.6 5.0 %collective-permute-start.1 = (bf16[8,3072]{1,0:T(8,128)(2,1)S(1)}, bf16[8,3072]{1,0:T(8,128)(2,1)S(1)}, u32[]{:S(2)}, u32[]{:S(2)}) collective-permute-start(bf16[8,3072]{1,0:T(8,128)(2,1)S(1)} %payload.1.refs_0_), channel_id=1, source_target_pairs={{0,8},{2,10},{4,12},{6,14},{8,0},{10,2},{12,4},{14,6},{1,9},{3,11}... | collective-permute-start | bytes 147464 | tf_op jit(solution)/shard_map/ppermute | solution.py:457
  6.6 5.0 %collective-permute-start.2 = (bf16[8,3072]{1,0:T(8,128)(2,1)S(1)}, bf16[8,3072]{1,0:T(8,128)(2,1)S(1)}, u32[]{:S(2)}, u32[]{:S(2)}) collective-permute-start(bf16[8,3072]{1,0:T(8,128)(2,1)S(1)} %payload.1.refs_0_), channel_id=1, source_target_pairs={{0,4},{2,6},{4,0},{6,2},{8,12},{10,14},{12,8},{14,10},{1,5},{3,7},... | collective-permute-start | bytes 147464 | tf_op jit(solution)/shard_map/ppermute | solution.py:457
  11.6 6.9 %collective-permute-start.3 = (bf16[32,3072]{1,0:T(8,128)(2,1)S(1)}, bf16[32,3072]{1,0:T(8,128)(2,1)S(1)}, u32[]{:S(2)}, u32[]{:S(2)}) collective-permute-start(bf16[32,3072]{1,0:T(8,128)(2,1)S(1)} %join.2.refs_0_.refs_2_), channel_id=1, source_target_pairs={{0,2},{2,0},{4,6},{6,4},{8,10},{10,8},{12,14},{14,12},{1,3},{3,1},... | collective-permute-start | bytes 589832 | tf_op jit(solution)/shard_map/ppermute | solution.py:457
  19.9 3.3 %collective-permute-start.5 = (f32[192,512]{1,0:T(8,128)S(1)}, f32[192,512]{1,0:T(8,128)S(1)}, u32[]{:S(2)}, u32[]{:S(2)}) collective-permute-start(f32[192,512]{1,0:T(8,128)S(1)} %project.3), channel_id=1, source_target_pairs={{0,1},{1,0},{2,3},{3,2},{4,5},{5,4},{6,7},{7,6},{8,9},{9,8},{10,11... | collective-permute-start | bytes 1179656 | tf_op jit(solution)/shard_map/ppermute | solution.py:457
  20.0 1.8 %collective-permute-start.4 = (bf16[64,512]{1,0:T(8,128)(2,1)S(1)}, bf16[64,512]{1,0:T(8,128)(2,1)S(1)}, u32[]{:S(2)}, u32[]{:S(2)}) collective-permute-start(bf16[64,512]{1,0:T(8,128)(2,1)S(1)} %join.3), channel_id=1, source_target_pairs={{0,1},{1,0},{2,3},{3,2},{4,5},{5,4},{6,7},{7,6},{8,9},{9,8},{10,11... | collective-permute-start | bytes 196616 | tf_op jit(solution)/shard_map/ppermute | solution.py:457

commit v23 on v21

--- a/solution.py
+++ b/solution.py
@@ -363,19 +363,11 @@
     def rows_of(ref, pair):
         return ref[2 * pair : 2 * pair + 2].reshape(many, size)
 
-    def two_scores(p):
-        lines = jnp.concatenate(
-            [
-                jnp.concatenate([new_lines(0, p), nothing], axis=1),
-                jnp.concatenate([nothing, new_lines(0, p + 1)], axis=1),
-            ],
-            axis=0,
-        )
-        both_q = jnp.concatenate([rows_of(q_ref, p), rows_of(q_ref, p + 1)], axis=1)
-        return lax.dot_general(lines, both_q, NT, preferred_element_type=jnp.float32).reshape(2, keys, many)
-
-    scores = jnp.concatenate([two_scores(p) for p in range(0, rows // 2, 2)], axis=0)
-    scores = jnp.where(live[None], scores, LOW)
+    scores = [
+        lax.dot_general(new_lines(0, p), rows_of(q_ref, p), NT, preferred_element_type=jnp.float32)
+        for p in range(rows // 2)
+    ]
+    scores = jnp.stack([jnp.where(live, s, LOW) for s in scores])
     old_top = top_ref[...]
     top = jnp.maximum(old_top, jnp.max(scores, axis=1))
     expo = jnp.exp((scores - top[:, None, :]) * scale)
@@ -463,8 +455,9 @@
     count = dp // 2
     ranks = factor_b.shape[0]
     if ranks % 8 == 0 and count in (1, 2, 4):
+        order = {1: (), 2: (1,), 4: (2, 3, 1)}[count]
         payload = make_payload(factor_a.T, factor_b)
-        return [payload] + [lax.ppermute(payload, "dp", [(i, i ^ (2 * k)) for i in range(dp)]) for k in range(count - 1, 0, -1)]
+        return [payload] + [lax.ppermute(payload, "dp", [(i, i ^ (2 * k)) for i in range(dp)]) for k in order]
     payload = jnp.concatenate([factor_a.T, factor_b.reshape(ranks, -1)], axis=1)
     groups = [[i for i in range(dp) if i % 2 == n] for n in range(2)]
     copies = jnp.broadcast_to(payload[None], (count,) + payload.shape)

time: 24.2 us -> 24.2 us (level)
  transfers between devices with their start and end apart: 5 -> 5, of which waited for: 2 -> 3; matrix products, arithmetic and copies ran while one was open for 0% -> 0% of each run, Pallas kernels for 44% -> 44%
where the time goes in v23:
time: 24.2 us; the launch traced here: 23.9 us
  Pallas kernels  14.8 us (61%)
  starting transfers between devices  7.34 us (30%)
  waiting for transfers between devices  1.08 us (4%)
  between operations  0.71 us (3%)
    ppermute x3, starting transfers between devices, gather_second(): lax.ppermute(payload, 'dp', [(i, i ^ 2 * k) for i in range(dp)])  5.68 us
    pallas_call x1, Pallas kernels, attend_cached(): pl.pallas_call(functools.partial(cached_kernel, chunk, early, heads, size...  5.33 us
    pallas_call x1, Pallas kernels, arrange(): pl.pallas_call(functools.partial(arrange_kernel, chunks, chunk, early), o...  3.8 us
    pallas_call x2, Pallas kernels, project(): pl.pallas_call(functools.partial(project_kernel, k), out_shape=pltpu.VMEM...  2.75 us
    pallas_call x1, Pallas kernels, finish(): pl.pallas_call(functools.partial(finish_kernel, steps, heads, size ** (-0...  2.08 us
    ppermute x1, starting transfers between devices, shards(): lax.ppermute(gathered, 'dp', [(i, i ^ 1) for i in range(dp)])  1.58 us
    pallas_call x1, Pallas kernels, make_payload(): pl.pallas_call(payload_kernel, out_shape=pltpu.VMEM((ranks, width + group...  0.81 us
    ppermute x3, waiting for transfers between devices, gather_second(): lax.ppermute(payload, 'dp', [(i, i ^ 2 * k) for i in range(dp)])  0.75 us
  transfers between devices with their start and end apart: 5, of which 3 were waited for; matrix products, arithmetic and copies ran while one was open for 0% of the time, Pallas kernels for 44%

profile of v23, /device:TPU:0, one launch (start us, length us, event | category | flops | bytes accessed | tf_op | source)
XLA Modules:
  0.0 23.9 jit_solution(7296453021109201443)
XLA Ops:
  0.6 0.8 %payload.1.refs_0_ = bf16[8,3584]{1,0:T(8,128)(2,1)S(1)} custom-call(bf16[8,2560]{1,0:T(8,128)(2,1)} %bitcast.5, bf16[8,2,4,128]{3,2,1,0:T(4,128)(2,1)} %up_hbm.1), custom_call_target="tpu_custom_call" | custom-call | tf_op jit(solution)/shard_map/payload/pallas_call | solution.py:51
  1.5 0.0 copy-start
  1.5 4.1 %collective-permute-start = (bf16[8,3584]{1,0:T(8,128)(2,1)S(1)}, bf16[8,3584]{1,0:T(8,128)(2,1)S(1)}, u32[]{:S(2)}, u32[]{:S(2)}) collective-permute-start(bf16[8,3584]{1,0:T(8,128)(2,1)S(1)} %payload.1.refs_0_), channel_id=1, source_target_pairs={{0,8},{2,10},{4,12},{6,14},{8,0},{10,2},{12,4},{14,6},{1,9},{3,11}... | collective-permute-start | bytes 172040 | tf_op jit(solution)/shard_map/ppermute | solution.py:460
  5.6 1.3 %collective-permute-start.1 = (bf16[8,3584]{1,0:T(8,128)(2,1)S(1)}, bf16[8,3584]{1,0:T(8,128)(2,1)S(1)}, u32[]{:S(2)}, u32[]{:S(2)}) collective-permute-start(bf16[8,3584]{1,0:T(8,128)(2,1)S(1)} %payload.1.refs_0_), channel_id=1, source_target_pairs={{0,12},{2,14},{4,8},{6,10},{8,4},{10,6},{12,0},{14,2},{1,13},{3,15... | collective-permute-start | bytes 172040 | tf_op jit(solution)/shard_map/ppermute | solution.py:460
  6.9 0.2 collective-permute-start.2
  7.1 3.8 %arrange.1 = (bf16[192,2560]{1,0:T(8,128)(2,1)S(1)}, bf16[4,2560,256]{2,1,0:T(8,128)(2,1)S(1)}, bf16[48,128,2,128]{3,2,1,0:T(2,128)(2,1)S(1)}, bf16[48,128,2,128]{3,2,1,0:T(2,128)(2,1)S(1)}) custom-call(bf16[48,128,2,2,128]{4,3,2,1,0:T(2,128)(2,1)} %refs_1_.3, bf16[48,4,2560]{2,1,0:T(4,128)(2,1)} %refs_1_.2, bf16[2560,2,4,128]{3,2,1,0:T(4,128)(2,1)} %refs_2_.1), custom_call_target="tpu_custom_call" | custom-call | flops 1342177280 | bytes 12451840 | tf_op jit(solution)/shard_map/arrange/pallas_call | solution.py:270
  10.9 0.0 collective-permute-done.refs_1_
  11.0 0.7 %collective-permute-done.1.refs_2_ = bf16[8,3584]{1,0:T(8,128)(2,1)S(1)} collective-permute-done((bf16[8,3584]{1,0:T(8,128)(2,1)S(1)}, bf16[8,3584]{1,0:T(8,128)(2,1)S(1)}, u32[]{:S(2)}, u32[]{:S(2)}) %collective-permute-start.1) | collective-permute-done | bytes 57376 | tf_op jit(solution)/shard_map/ppermute | solution.py:460
  11.6 0.1 collective-permute-done.2.refs_3_
  11.7 1.6 %collective-permute-start.3 = (bf16[32,3584]{1,0:T(8,128)(2,1)S(1)}, bf16[32,3584]{1,0:T(8,128)(2,1)S(1)}, u32[]{:S(2)}, u32[]{:S(2)}) collective-permute-start(bf16[32,3584]{1,0:T(8,128)(2,1)S(1)} %join.1.refs_0_), channel_id=1, source_target_pairs={{0,2},{2,0},{4,6},{6,4},{8,10},{10,8},{12,14},{14,12},{1,3},{3,1},... | collective-permute-start | bytes 688136 | tf_op jit(solution)/shard_map/ppermute | solution.py:478
  13.3 0.0 copy-done
  13.3 5.3 %attend_cached.1 = (bf16[48,128,2,128]{3,2,1,0:T(2,128)(2,1)S(1)}, bf16[48,128,2,128]{3,2,1,0:T(2,128)(2,1)S(1)}, f32[48,64,128]{2,1,0:T(8,128)S(1)}, f32[24,128]{1,0:T(8,128)S(1)}, f32[24,128]{1,0:T(8,128)S(1)}) custom-call(s32[48]{0:T(128)} %refs_0_.3, bf16[48,128,2,2,128]{4,3,2,1,0:T(2,128)(2,1)} %refs_1_.3, ...), custom_call_target="tpu_custom_call", output_to_operand_aliasing={{0}: (3, {}), {1}: (4, {})} | custom-call | flops 402653184 | bytes 6291456 | tf_op jit(solution)/shard_map/attend_cached/pallas_call | solution.py:187
  18.7 0.0 collective-permute-done.3.refs_1_
  18.7 1.4 %project.3 = f32[192,512]{1,0:T(8,128)S(1)} custom-call(bf16[192,2560]{1,0:T(8,128)(2,1)S(1)} %get-tuple-element.42.hidden_ref, bf16[4,2560,256]{2,1,0:T(8,128)(2,1)S(1)} %get-tuple-element.43.base_ref, bf16[32,3584]{1,0:T(8,128)(2,1)S(1)} %join.1.refs_0_, bf16[32,3584]{1,0:T(8,128)(2,1)S(1)} %collective-permute-done.3.refs_1_), custom_call_target="tpu_custom_call" | custom-call | flops 671088640 | bytes 3604480 | tf_op jit(solution)/shard_map/project/pallas_call | solution.py:327
  20.0 0.1 collective-permute-start.4
  20.1 1.4 %project.2.refs_0_ = f32[192,512]{1,0:T(8,128)S(1)} custom-call(bf16[192,2560]{1,0:T(8,128)(2,1)S(1)} %get-tuple-element.42.hidden_ref, bf16[4,2560,256]{2,1,0:T(8,128)(2,1)S(1)} %get-tuple-element.43.base_ref, bf16[32,3584]{1,0:T(8,128)(2,1)S(1)} %join.1.refs_0_, bf16[32,3584]{1,0:T(8,128)(2,1)S(1)} %collective-permute-done.3.refs_1_), custom_call_target="tpu_custom_call" | custom-call | flops 671088640 | bytes 3604480 | tf_op jit(solution)/shard_map/project/pallas_call | solution.py:327
  21.5 0.3 %collective-permute-done.4.refs_1_ = f32[192,512]{1,0:T(8,128)S(1)} collective-permute-done((f32[192,512]{1,0:T(8,128)S(1)}, f32[192,512]{1,0:T(8,128)S(1)}, u32[]{:S(2)}, u32[]{:S(2)}) %collective-permute-start.4) | collective-permute-done | bytes 393248 | tf_op jit(solution)/shard_map/ppermute | solution.py:484
  21.8 2.1 %finish.1 = (bf16[48,4,2,2,128]{4,3,2,1,0:T(2,128)(2,1)}, bf16[48,64,128]{2,1,0:T(8,128)(2,1)}) custom-call(f32[192,512]{1,0:T(8,128)S(1)} %project.2.refs_0_, f32[192,512]{1,0:T(8,128)S(1)} %collective-permute-done.4.refs_1_, bf16[48,64,128]{2,1,0:T(8,128)(2,1)S(1)} %bitcast.4, f32[48,64,128]{2,1,0:T(8,128)S(1)} %get-tuple-element.47.refs_3_, ...), custom_call_target="tpu_custom_call" | custom-call | flops 301989888 | bytes 3145728 | tf_op jit(solution)/shard_map/finish/pallas_call | solution.py:413
  (1 shorter events, 0.0 us)
Async XLA Ops:
  1.5 11.9 %copy-start = (bf16[48,4,16,128]{3,2,1,0:T(8,128)(2,1)S(1)}, bf16[48,4,16,128]{3,2,1,0:T(8,128)(2,1)}, u32[]{:S(2)}) copy-start(bf16[48,4,16,128]{3,2,1,0:T(8,128)(2,1)} %param.11) | copy-start | bytes 2359300
  1.5 9.5 %collective-permute-start = (bf16[8,3584]{1,0:T(8,128)(2,1)S(1)}, bf16[8,3584]{1,0:T(8,128)(2,1)S(1)}, u32[]{:S(2)}, u32[]{:S(2)}) collective-permute-start(bf16[8,3584]{1,0:T(8,128)(2,1)S(1)} %payload.1.refs_0_), channel_id=1, source_target_pairs={{0,8},{2,10},{4,12},{6,14},{8,0},{10,2},{12,4},{14,6},{1,9},{3,11}... | collective-permute-start | bytes 172040 | tf_op jit(solution)/shard_map/ppermute | solution.py:460
  5.6 6.1 %collective-permute-start.1 = (bf16[8,3584]{1,0:T(8,128)(2,1)S(1)}, bf16[8,3584]{1,0:T(8,128)(2,1)S(1)}, u32[]{:S(2)}, u32[]{:S(2)}) collective-permute-start(bf16[8,3584]{1,0:T(8,128)(2,1)S(1)} %payload.1.refs_0_), channel_id=1, source_target_pairs={{0,12},{2,14},{4,8},{6,10},{8,4},{10,6},{12,0},{14,2},{1,13},{3,15... | collective-permute-start | bytes 172040 | tf_op jit(solution)/shard_map/ppermute | solution.py:460
  6.9 4.8 %collective-permute-start.2 = (bf16[8,3584]{1,0:T(8,128)(2,1)S(1)}, bf16[8,3584]{1,0:T(8,128)(2,1)S(1)}, u32[]{:S(2)}, u32[]{:S(2)}) collective-permute-start(bf16[8,3584]{1,0:T(8,128)(2,1)S(1)} %payload.1.refs_0_), channel_id=1, source_target_pairs={{0,4},{2,6},{4,0},{6,2},{8,12},{10,14},{12,8},{14,10},{1,5},{3,7},... | collective-permute-start | bytes 172040 | tf_op jit(solution)/shard_map/ppermute | solution.py:460
  11.7 6.9 %collective-permute-start.3 = (bf16[32,3584]{1,0:T(8,128)(2,1)S(1)}, bf16[32,3584]{1,0:T(8,128)(2,1)S(1)}, u32[]{:S(2)}, u32[]{:S(2)}) collective-permute-start(bf16[32,3584]{1,0:T(8,128)(2,1)S(1)} %join.1.refs_0_), channel_id=1, source_target_pairs={{0,2},{2,0},{4,6},{6,4},{8,10},{10,8},{12,14},{14,12},{1,3},{3,1},... | collective-permute-start | bytes 688136 | tf_op jit(solution)/shard_map/ppermute | solution.py:478
  20.0 1.8 %collective-permute-start.4 = (f32[192,512]{1,0:T(8,128)S(1)}, f32[192,512]{1,0:T(8,128)S(1)}, u32[]{:S(2)}, u32[]{:S(2)}) collective-permute-start(f32[192,512]{1,0:T(8,128)S(1)} %project.3), channel_id=1, source_target_pairs={{0,1},{1,0},{2,3},{3,2},{4,5},{5,4},{6,7},{7,6},{8,9},{9,8},{10,11... | collective-permute-start | bytes 1179656 | tf_op jit(solution)/shard_map/ppermute | solution.py:484

commit v24 on v23

--- a/solution.py
+++ b/solution.py
@@ -68,14 +68,34 @@
     return [pltpu.make_async_copy(cache_hbm.at[mine, :, n], ref.at[mine], sems.at[i, n]) for n, ref in enumerate((k, v))]
 
 
+def two_rows(ref, r):
+    rows, slots, own, size = ref.shape
+    flat = ref.reshape(rows, slots * own, size)
+    return jnp.concatenate([flat[r], flat[r + 1]], axis=1)
+
+
+def score_chunk(q_ref, k_ref, scores_ref, i, chunk):
+    nothing = jnp.zeros(q_ref.shape[1:], jnp.bfloat16)
+    for p in range(chunk // 2):
+        r = i * chunk + 2 * p
+        both_q = jnp.concatenate(
+            [
+                jnp.concatenate([q_ref[r], nothing], axis=1),
+                jnp.concatenate([nothing, q_ref[r + 1]], axis=1),
+            ],
+            axis=0,
+        )
+        scores_ref[p] = lax.dot_general(two_rows(k_ref, r), both_q, NT, preferred_element_type=jnp.float32)
+
+
 class Cached:
     def __init__(self, chunk, heads, scale, inputs, outputs, scratch):
         self.chunk, self.heads, self.scale = chunk, heads, scale
         self.lengths_hbm, self.cache_hbm, self.q = inputs
-        self.k, self.v, self.sums, self.tops, self.totals = outputs
-        self.lengths, *rest = scratch
-        self.scores, self.weights = rest[0:2], rest[2:4]
-        self.sems, self.length_sem = rest[4:]
+        self.k, self.v, first_scores, self.sums, self.tops, self.totals = outputs
+        self.lengths, second_scores, *rest = scratch
+        self.scores, self.weights = (first_scores, second_scores), rest[0:2]
+        self.sems, self.length_sem = rest[2:]
         self.rows, self.queries, self.size = self.q.shape
         self.slots, self.own = self.k.shape[1:3]
         self.keys = self.slots * self.own
@@ -84,7 +104,6 @@
         query = lax.broadcasted_iota(jnp.int32, (self.keys, 2 * queries), 1)
         self.line = jnp.where(line % own == (query % heads) // (heads // own), line, self.keys)
         self.one = lax.broadcasted_iota(jnp.int32, (1, 2 * queries), 1) < queries
-        self.nothing = jnp.zeros((queries, self.size), jnp.bfloat16)
 
     def copies(self, i):
         return cache_copies(self.cache_hbm, self.k, self.v, self.sems, i, self.chunk)
@@ -101,22 +120,10 @@
             copy.wait()
 
     def lines(self, ref, r):
-        flat = ref.reshape(self.rows, self.keys, self.size)
-        return jnp.concatenate([flat[r], flat[r + 1]], axis=1)
+        return two_rows(ref, r)
 
     def score(self, i, slot):
-        for p in range(self.chunk // 2):
-            r = i * self.chunk + 2 * p
-            both_q = jnp.concatenate(
-                [
-                    jnp.concatenate([self.q[r], self.nothing], axis=1),
-                    jnp.concatenate([self.nothing, self.q[r + 1]], axis=1),
-                ],
-                axis=0,
-            )
-            self.scores[slot][p] = lax.dot_general(
-                self.lines(self.k, r), both_q, NT, preferred_element_type=jnp.float32
-            )
+        score_chunk(self.q, self.k, self.scores[slot], i, self.chunk)
 
     def soften(self, i, slot):
         for p in range(self.chunk // 2):
@@ -142,13 +149,12 @@
 
 
 def cached_kernel(chunk, early, heads, scale, *refs):
-    cached = Cached(chunk, heads, scale, refs[:3], refs[5:10], refs[10:])
+    cached = Cached(chunk, heads, scale, refs[:3], refs[6:12], refs[12:])
     chunks = cached.rows // chunk
     cached.lengths_copy().start()
     for i in range(early, chunks):
         cached.start(i)
     cached.lengths_copy().wait()
-    cached.score(0, 0)
     cached.score(1, 1)
     cached.soften(0, 0)
 
@@ -170,7 +176,7 @@
     cached.collect(chunks - 1, 1)
 
 
-def attend_cached(queries, cache, lengths, keys, values, steps, chunk, early):
+def attend_cached(queries, cache, lengths, keys, values, first_scores, steps, chunk, early):
     rows, many, size = queries.shape
     slots, own = cache.shape[1], cache.shape[3]
     heads = many // steps
@@ -180,34 +186,35 @@
     outs = (
         pltpu.VMEM(half, jnp.bfloat16),
         pltpu.VMEM(half, jnp.bfloat16),
+        pltpu.VMEM(scores, jnp.float32),
         pltpu.VMEM((rows, many, size), jnp.float32),
         pltpu.VMEM(line, jnp.float32),
         pltpu.VMEM(line, jnp.float32),
     )
-    _, _, *state = pl.pallas_call(
+    _, _, _, *state = pl.pallas_call(
         functools.partial(cached_kernel, chunk, early, heads, size ** (-0.5)),
         out_shape=outs,
-        in_specs=[pl.BlockSpec(memory_space=pltpu.HBM)] * 2 + [VMEM] * 3,
+        in_specs=[pl.BlockSpec(memory_space=pltpu.HBM)] * 2 + [VMEM] * 4,
         out_specs=(VMEM,) * len(outs),
         scratch_shapes=[
             pltpu.SMEM(lengths.shape, jnp.int32),
-            pltpu.VMEM(scores, jnp.float32),
             pltpu.VMEM(scores, jnp.float32),
             pltpu.VMEM(scores, jnp.bfloat16),
             pltpu.VMEM(scores, jnp.bfloat16),
             pltpu.SemaphoreType.DMA((rows // chunk, 2)),
             pltpu.SemaphoreType.DMA,
         ],
-        input_output_aliases={3: 0, 4: 1},
+        input_output_aliases={3: 0, 4: 1, 5: 2},
         compiler_params=params(16),
         cost_estimate=cost(8 * rows * many * slots * size, 4 * rows * slots * own * size, rows * many * slots * own),
         name="attend_cached",
-    )(in_hbm(lengths), in_hbm(cache), in_vmem(queries), keys, values)
+    )(in_hbm(lengths), in_hbm(cache), in_vmem(queries), keys, values, first_scores)
     return [queries, *state]
 
 
 def arrange_kernel(chunks, chunk, early, *refs):
-    cache_hbm, hidden_hbm, base_hbm, tokens_ref, base_ref, k, v, hidden, base, base_sems, sems = refs
+    cache_hbm, hidden_hbm, base_hbm, queries_hbm, tokens_ref, base_ref, k, v, scores_ref = refs[:9]
+    hidden, base, q, base_sems, sems = refs[9:]
     width, two, kvh, size = base.shape
     own = k.shape[2]
     groups = two * kvh
@@ -222,6 +229,8 @@
     for i in range(chunks):
         get_base(i).start()
     get_hidden.start()
+    get_queries = pltpu.make_async_copy(queries_hbm.at[pl.ds(0, chunk)], q, base_sems.at[chunks + 1])
+    get_queries.start()
     for copy in copies:
         copy.start()
 
@@ -251,11 +260,14 @@
 
     get_hidden.wait()
     tokens_ref[...] = hidden.reshape(tokens_ref.shape)[...]
-    for copy in copies:
+    get_queries.wait()
+    copies[0].wait()
+    score_chunk(q, k, scores_ref, 0, chunk)
+    for copy in copies[1:]:
         copy.wait()
 
 
-def arrange(hidden, base, cache, chunk, early):
+def arrange(hidden, base, cache, queries, chunk, early):
     rows, steps, _ = hidden.shape
     slots, own = cache.shape[1], cache.shape[3]
     width, two, kvh, size = base.shape
@@ -266,22 +278,24 @@
         pltpu.VMEM((two * kvh // own, width, own * size), jnp.bfloat16),
         half,
         half,
+        pltpu.VMEM((chunk // 2, slots * own, 2 * queries.shape[1]), jnp.float32),
     )
     return pl.pallas_call(
         functools.partial(arrange_kernel, chunks, chunk, early),
         out_shape=outs,
-        in_specs=[pl.BlockSpec(memory_space=pltpu.HBM)] * 3,
+        in_specs=[pl.BlockSpec(memory_space=pltpu.HBM)] * 4,
         out_specs=(VMEM,) * len(outs),
         scratch_shapes=[
             pltpu.VMEM(hidden.shape, jnp.bfloat16),
             pltpu.VMEM(base.shape, jnp.bfloat16),
-            pltpu.SemaphoreType.DMA((chunks + 1,)),
+            pltpu.VMEM((chunk,) + queries.shape[1:], jnp.bfloat16),
+            pltpu.SemaphoreType.DMA((chunks + 2,)),
             pltpu.SemaphoreType.DMA((early, 2)),
         ],
         compiler_params=params(16),
         cost_estimate=cost(512 * base.size, 4 * (base.size + hidden.size)),
         name="arrange",
-    )(in_hbm(cache), in_hbm(hidden), in_hbm(base))
+    )(in_hbm(cache), in_hbm(hidden), in_hbm(base), in_hbm(queries))
 
 
 def project_kernel(k, hidden_ref, base_ref, *refs):
@@ -472,11 +486,11 @@
     rows, steps, heads, size = queries.shape
     queries = queries.reshape(rows, steps * heads, size)
     chunk, early = 12, 2
-    tokens, base, keys, values = arrange(hidden, base_weight, cache, chunk, early)
-    blocks, tokens, base, keys, values = lax.optimization_barrier((blocks, tokens, base, keys, values))
+    tokens, base, keys, values, scores = arrange(hidden, base_weight, cache, queries, chunk, early)
+    blocks, tokens, base, keys, values, scores = lax.optimization_barrier((blocks, tokens, base, keys, values, scores))
     gathered = join(blocks) if len(blocks) > 1 else blocks[0]
     gathered = [gathered, lax.ppermute(gathered, "dp", [(i, i ^ 1) for i in range(dp)])]
-    state = attend_cached(queries, cache, lengths, keys, values, steps, chunk, early)
+    state = attend_cached(queries, cache, lengths, keys, values, scores, steps, chunk, early)
     gathered, state, tokens, base = lax.optimization_barrier((gathered, state, tokens, base))
     received = []
     for k in range(1, tp):

time: 24.2 us -> 23.9 us (0.988)
  waiting for transfers between devices: 1.08 us -> 0.75 us
    ppermute x3, waiting for transfers between devices: 0.75 us -> 0.18 us  [gather_second(): lax.ppermute(payload, 'dp', [(i, i ^ 2 * k) for i in range(dp)])]
    pallas_call x1, Pallas kernels: 3.8 us -> 4.36 us  [arrange(): pl.pallas_call(functools.partial(arrange_kernel, chunks, chunk, early), o...]
    pallas_call x1, Pallas kernels: 5.33 us -> 4.87 us  [attend_cached(): pl.pallas_call(functools.partial(cached_kernel, chunk, early, heads, size...]
  transfers between devices with their start and end apart: 5 -> 5, of which waited for: 3 -> 4; matrix products, arithmetic and copies ran while one was open for 0% -> 0% of each run, Pallas kernels for 44% -> 45%
where the time goes in v24:
time: 23.9 us; the launch traced here: 23.7 us
  Pallas kernels  14.9 us (62%)
  starting transfers between devices  7.34 us (31%)
  waiting for transfers between devices  0.75 us (3%)
  between operations  0.69 us (3%)
    ppermute x3, starting transfers between devices, gather_second(): lax.ppermute(payload, 'dp', [(i, i ^ 2 * k) for i in range(dp)])  5.68 us
    pallas_call x1, Pallas kernels, attend_cached(): pl.pallas_call(functools.partial(cached_kernel, chunk, early, heads, size...  4.87 us
    pallas_call x1, Pallas kernels, arrange(): pl.pallas_call(functools.partial(arrange_kernel, chunks, chunk, early), o...  4.36 us
    pallas_call x2, Pallas kernels, project(): pl.pallas_call(functools.partial(project_kernel, k), out_shape=pltpu.VMEM...  2.75 us
    pallas_call x1, Pallas kernels, finish(): pl.pallas_call(functools.partial(finish_kernel, steps, heads, size ** (-0...  2.07 us
    ppermute x1, starting transfers between devices, shards(): lax.ppermute(gathered, 'dp', [(i, i ^ 1) for i in range(dp)])  1.58 us
    pallas_call x1, Pallas kernels, make_payload(): pl.pallas_call(payload_kernel, out_shape=pltpu.VMEM((ranks, width + group...  0.81 us
  transfers between devices with their start and end apart: 5, of which 4 were waited for; matrix products, arithmetic and copies ran while one was open for 0% of the time, Pallas kernels for 45%

profile of v24, /device:TPU:0, one launch (start us, length us, event | category | flops | bytes accessed | tf_op | source)
XLA Modules:
  0.0 23.7 jit_solution(11913348065467539373)
XLA Ops:
  0.6 0.8 %payload.1.refs_0_ = bf16[8,3584]{1,0:T(8,128)(2,1)S(1)} custom-call(bf16[8,2560]{1,0:T(8,128)(2,1)} %bitcast.6, bf16[8,2,4,128]{3,2,1,0:T(4,128)(2,1)} %up_hbm.1), custom_call_target="tpu_custom_call" | custom-call | tf_op jit(solution)/shard_map/payload/pallas_call | solution.py:51
  1.5 4.1 %collective-permute-start = (bf16[8,3584]{1,0:T(8,128)(2,1)S(1)}, bf16[8,3584]{1,0:T(8,128)(2,1)S(1)}, u32[]{:S(2)}, u32[]{:S(2)}) collective-permute-start(bf16[8,3584]{1,0:T(8,128)(2,1)S(1)} %payload.1.refs_0_), channel_id=1, source_target_pairs={{0,8},{2,10},{4,12},{6,14},{8,0},{10,2},{12,4},{14,6},{1,9},{3,11}... | collective-permute-start | bytes 172040 | tf_op jit(solution)/shard_map/ppermute | solution.py:474
  5.6 1.3 %collective-permute-start.1 = (bf16[8,3584]{1,0:T(8,128)(2,1)S(1)}, bf16[8,3584]{1,0:T(8,128)(2,1)S(1)}, u32[]{:S(2)}, u32[]{:S(2)}) collective-permute-start(bf16[8,3584]{1,0:T(8,128)(2,1)S(1)} %payload.1.refs_0_), channel_id=1, source_target_pairs={{0,12},{2,14},{4,8},{6,10},{8,4},{10,6},{12,0},{14,2},{1,13},{3,15... | collective-permute-start | bytes 172040 | tf_op jit(solution)/shard_map/ppermute | solution.py:474
  6.9 0.2 collective-permute-start.2
  7.1 0.0 copy-start
  7.1 4.4 %arrange.1 = (bf16[192,2560]{1,0:T(8,128)(2,1)S(1)}, bf16[4,2560,256]{2,1,0:T(8,128)(2,1)S(1)}, bf16[48,128,2,128]{3,2,1,0:T(2,128)(2,1)S(1)}, bf16[48,128,2,128]{3,2,1,0:T(2,128)(2,1)S(1)}, f32[6,256,128]{2,1,0:T(8,128)S(1)}) custom-call(bf16[48,128,2,2,128]{4,3,2,1,0:T(2,128)(2,1)} %refs_1_.3, bf16[48,4,2560]{2,1,0:T(4,128)(2,1)} %refs_1_.2, ...), custom_call_target="tpu_custom_call" | custom-call | flops 1342177280 | bytes 12451840 | tf_op jit(solution)/shard_map/arrange/pallas_call | solution.py:283
  11.5 0.0 collective-permute-done.refs_1_
  11.5 0.1 collective-permute-done.1.refs_2_
  11.6 0.1 collective-permute-done.2.refs_3_
  11.7 1.6 %collective-permute-start.3 = (bf16[32,3584]{1,0:T(8,128)(2,1)S(1)}, bf16[32,3584]{1,0:T(8,128)(2,1)S(1)}, u32[]{:S(2)}, u32[]{:S(2)}) collective-permute-start(bf16[32,3584]{1,0:T(8,128)(2,1)S(1)} %join.1.refs_0_), channel_id=1, source_target_pairs={{0,2},{2,0},{4,6},{6,4},{8,10},{10,8},{12,14},{14,12},{1,3},{3,1},... | collective-permute-start | bytes 688136 | tf_op jit(solution)/shard_map/ppermute | solution.py:492
  13.3 0.0 copy-done
  13.3 4.9 %attend_cached.1 = (bf16[48,128,2,128]{3,2,1,0:T(2,128)(2,1)S(1)}, bf16[48,128,2,128]{3,2,1,0:T(2,128)(2,1)S(1)}, f32[6,256,128]{2,1,0:T(8,128)S(1)}, f32[48,64,...) custom-call(s32[48]{0:T(128)} %refs_0_.3, ...), custom_call_target="tpu_custom_call", output_to_operand_aliasing={{0}: (3, {}), {1}: (4, {}), {2}: (5, {})} | custom-call | flops 402653184 | bytes 6291456 | tf_op jit(solution)/shard_map/attend_cached/pallas_call | solution.py:194
  18.2 0.2 %collective-permute-done.3.refs_1_ = bf16[32,3584]{1,0:T(8,128)(2,1)S(1)} collective-permute-done((bf16[32,3584]{1,0:T(8,128)(2,1)S(1)}, bf16[32,3584]{1,0:T(8,128)(2,1)S(1)}, u32[]{:S(2)}, u32[]{:S(2)}) %collective-permute-start.3) | collective-permute-done | bytes 229408 | tf_op jit(solution)/shard_map/ppermute | solution.py:492
  18.4 1.4 %project.3 = f32[192,512]{1,0:T(8,128)S(1)} custom-call(bf16[192,2560]{1,0:T(8,128)(2,1)S(1)} %get-tuple-element.46.hidden_ref, bf16[4,2560,256]{2,1,0:T(8,128)(2,1)S(1)} %get-tuple-element.47.base_ref, bf16[32,3584]{1,0:T(8,128)(2,1)S(1)} %join.1.refs_0_, bf16[32,3584]{1,0:T(8,128)(2,1)S(1)} %collective-permute-done.3.refs_1_), custom_call_target="tpu_custom_call" | custom-call | flops 671088640 | bytes 3604480 | tf_op jit(solution)/shard_map/project/pallas_call | solution.py:341
  19.8 0.1 collective-permute-start.4
  19.9 1.4 %project.2.refs_0_ = f32[192,512]{1,0:T(8,128)S(1)} custom-call(bf16[192,2560]{1,0:T(8,128)(2,1)S(1)} %get-tuple-element.46.hidden_ref, bf16[4,2560,256]{2,1,0:T(8,128)(2,1)S(1)} %get-tuple-element.47.base_ref, bf16[32,3584]{1,0:T(8,128)(2,1)S(1)} %join.1.refs_0_, bf16[32,3584]{1,0:T(8,128)(2,1)S(1)} %collective-permute-done.3.refs_1_), custom_call_target="tpu_custom_call" | custom-call | flops 671088640 | bytes 3604480 | tf_op jit(solution)/shard_map/project/pallas_call | solution.py:341
  21.3 0.3 %collective-permute-done.4.refs_1_ = f32[192,512]{1,0:T(8,128)S(1)} collective-permute-done((f32[192,512]{1,0:T(8,128)S(1)}, f32[192,512]{1,0:T(8,128)S(1)}, u32[]{:S(2)}, u32[]{:S(2)}) %collective-permute-start.4) | collective-permute-done | bytes 393248 | tf_op jit(solution)/shard_map/ppermute | solution.py:498
  21.6 2.1 %finish.1 = (bf16[48,4,2,2,128]{4,3,2,1,0:T(2,128)(2,1)}, bf16[48,64,128]{2,1,0:T(8,128)(2,1)}) custom-call(f32[192,512]{1,0:T(8,128)S(1)} %project.2.refs_0_, f32[192,512]{1,0:T(8,128)S(1)} %collective-permute-done.4.refs_1_, bf16[48,64,128]{2,1,0:T(8,128)(2,1)S(1)} %bitcast.5, f32[48,64,128]{2,1,0:T(8,128)S(1)} %get-tuple-element.51.refs_3_, ...), custom_call_target="tpu_custom_call" | custom-call | flops 301989888 | bytes 3145728 | tf_op jit(solution)/shard_map/finish/pallas_call | solution.py:427
  (1 shorter events, 0.0 us)
Async XLA Ops:
  1.5 10.1 %collective-permute-start = (bf16[8,3584]{1,0:T(8,128)(2,1)S(1)}, bf16[8,3584]{1,0:T(8,128)(2,1)S(1)}, u32[]{:S(2)}, u32[]{:S(2)}) collective-permute-start(bf16[8,3584]{1,0:T(8,128)(2,1)S(1)} %payload.1.refs_0_), channel_id=1, source_target_pairs={{0,8},{2,10},{4,12},{6,14},{8,0},{10,2},{12,4},{14,6},{1,9},{3,11}... | collective-permute-start | bytes 172040 | tf_op jit(solution)/shard_map/ppermute | solution.py:474
  5.6 6.1 %collective-permute-start.1 = (bf16[8,3584]{1,0:T(8,128)(2,1)S(1)}, bf16[8,3584]{1,0:T(8,128)(2,1)S(1)}, u32[]{:S(2)}, u32[]{:S(2)}) collective-permute-start(bf16[8,3584]{1,0:T(8,128)(2,1)S(1)} %payload.1.refs_0_), channel_id=1, source_target_pairs={{0,12},{2,14},{4,8},{6,10},{8,4},{10,6},{12,0},{14,2},{1,13},{3,15... | collective-permute-start | bytes 172040 | tf_op jit(solution)/shard_map/ppermute | solution.py:474
  6.9 4.8 %collective-permute-start.2 = (bf16[8,3584]{1,0:T(8,128)(2,1)S(1)}, bf16[8,3584]{1,0:T(8,128)(2,1)S(1)}, u32[]{:S(2)}, u32[]{:S(2)}) collective-permute-start(bf16[8,3584]{1,0:T(8,128)(2,1)S(1)} %payload.1.refs_0_), channel_id=1, source_target_pairs={{0,4},{2,6},{4,0},{6,2},{8,12},{10,14},{12,8},{14,10},{1,5},{3,7},... | collective-permute-start | bytes 172040 | tf_op jit(solution)/shard_map/ppermute | solution.py:474
  7.1 6.2 %copy-start = (bf16[48,4,16,128]{3,2,1,0:T(8,128)(2,1)S(1)}, bf16[48,4,16,128]{3,2,1,0:T(8,128)(2,1)}, u32[]{:S(2)}) copy-start(bf16[48,4,16,128]{3,2,1,0:T(8,128)(2,1)} %param.11) | copy-start | bytes 2359300
  11.7 6.7 %collective-permute-start.3 = (bf16[32,3584]{1,0:T(8,128)(2,1)S(1)}, bf16[32,3584]{1,0:T(8,128)(2,1)S(1)}, u32[]{:S(2)}, u32[]{:S(2)}) collective-permute-start(bf16[32,3584]{1,0:T(8,128)(2,1)S(1)} %join.1.refs_0_), channel_id=1, source_target_pairs={{0,2},{2,0},{4,6},{6,4},{8,10},{10,8},{12,14},{14,12},{1,3},{3,1},... | collective-permute-start | bytes 688136 | tf_op jit(solution)/shard_map/ppermute | solution.py:492
  19.8 1.8 %collective-permute-start.4 = (f32[192,512]{1,0:T(8,128)S(1)}, f32[192,512]{1,0:T(8,128)S(1)}, u32[]{:S(2)}, u32[]{:S(2)}) collective-permute-start(f32[192,512]{1,0:T(8,128)S(1)} %project.3), channel_id=1, source_target_pairs={{0,1},{1,0},{2,3},{3,2},{4,5},{5,4},{6,7},{7,6},{8,9},{9,8},{10,11... | collective-permute-start | bytes 1179656 | tf_op jit(solution)/shard_map/ppermute | solution.py:498

commit v25 on v24

--- a/solution.py
+++ b/solution.py
@@ -393,10 +393,9 @@
     for n in range(2 * own):
         wide[pl.ds(n, rows * steps, stride=2 * own), :] = fresh[:, n * size : (n + 1) * size]
     fresh_ref.reshape(rows * steps * 2 * own, size)[...] = wide[...].astype(jnp.bfloat16)
-    puts = [pltpu.make_async_copy(fresh_ref, fresh_hbm, sems.at[0])]
-    puts[0].start()
-
-    for at in range(0, rows // 2, group):
+    starts = list(range(0, rows // 2, group))
+
+    def new_sums(at):
         pairs = range(at, at + group)
         values = jnp.concatenate(
             [
@@ -405,16 +404,25 @@
             ],
             axis=0,
         )
-        new = lax.dot_general(
+        return lax.dot_general(
             weights[at : at + group].reshape(group * keys, many), values, TN, preferred_element_type=jnp.float32
         )
+
+    puts = []
+    following = new_sums(starts[0])
+    for at in starts:
+        new = following
+        if at != starts[-1]:
+            following = new_sums(at + group)
         factors = back[at : at + group].T
-        for n, p in enumerate(pairs):
+        for n, p in enumerate(range(at, at + group)):
             both = new[:, n * size : (n + 1) * size] + factors[:, n : n + 1] * rows_of(old_ref, p)
             context_ref[2 * p : 2 * p + 2] = both.astype(jnp.bfloat16).reshape(2, queries, size)
         mine = pl.ds(2 * at, 2 * group)
         puts.append(pltpu.make_async_copy(context_ref.at[mine], context_hbm.at[mine], sems.at[1 + at // group]))
         puts[-1].start()
+    puts.append(pltpu.make_async_copy(fresh_ref, fresh_hbm, sems.at[0]))
+    puts[-1].start()
     for put in puts:
         put.wait()
 

time: 23.9 us -> 24 us (level)
  no operation moved by 1% of the time
where the time goes in v25:
time: 24 us; the launch traced here: 23.7 us
  Pallas kernels  14.9 us (62%)
  starting transfers between devices  7.34 us (31%)
  waiting for transfers between devices  0.75 us (3%)
  between operations  0.69 us (3%)
    ppermute x3, starting transfers between devices, gather_second(): lax.ppermute(payload, 'dp', [(i, i ^ 2 * k) for i in range(dp)])  5.68 us
    pallas_call x1, Pallas kernels, attend_cached(): pl.pallas_call(functools.partial(cached_kernel, chunk, early, heads, size...  4.87 us
    pallas_call x1, Pallas kernels, arrange(): pl.pallas_call(functools.partial(arrange_kernel, chunks, chunk, early), o...  4.36 us
    pallas_call x2, Pallas kernels, project(): pl.pallas_call(functools.partial(project_kernel, k), out_shape=pltpu.VMEM...  2.75 us
    pallas_call x1, Pallas kernels, finish(): pl.pallas_call(functools.partial(finish_kernel, steps, heads, size ** (-0...  2.12 us
    ppermute x1, starting transfers between devices, shards(): lax.ppermute(gathered, 'dp', [(i, i ^ 1) for i in range(dp)])  1.58 us
    pallas_call x1, Pallas kernels, make_payload(): pl.pallas_call(payload_kernel, out_shape=pltpu.VMEM((ranks, width + group...  0.81 us
  transfers between devices with their start and end apart: 5, of which 4 were waited for; matrix products, arithmetic and copies ran while one was open for 0% of the time, Pallas kernels for 45%

profile of v25, /device:TPU:0, one launch (start us, length us, event | category | flops | bytes accessed | tf_op | source)
XLA Modules:
  0.0 23.7 jit_solution(17308018741477219831)
XLA Ops:
  0.6 0.8 %payload.1.refs_0_ = bf16[8,3584]{1,0:T(8,128)(2,1)S(1)} custom-call(bf16[8,2560]{1,0:T(8,128)(2,1)} %bitcast.6, bf16[8,2,4,128]{3,2,1,0:T(4,128)(2,1)} %up_hbm.1), custom_call_target="tpu_custom_call" | custom-call | tf_op jit(solution)/shard_map/payload/pallas_call | solution.py:51
  1.5 4.1 %collective-permute-start = (bf16[8,3584]{1,0:T(8,128)(2,1)S(1)}, bf16[8,3584]{1,0:T(8,128)(2,1)S(1)}, u32[]{:S(2)}, u32[]{:S(2)}) collective-permute-start(bf16[8,3584]{1,0:T(8,128)(2,1)S(1)} %payload.1.refs_0_), channel_id=1, source_target_pairs={{0,8},{2,10},{4,12},{6,14},{8,0},{10,2},{12,4},{14,6},{1,9},{3,11}... | collective-permute-start | bytes 172040 | tf_op jit(solution)/shard_map/ppermute | solution.py:482
  5.6 1.3 %collective-permute-start.1 = (bf16[8,3584]{1,0:T(8,128)(2,1)S(1)}, bf16[8,3584]{1,0:T(8,128)(2,1)S(1)}, u32[]{:S(2)}, u32[]{:S(2)}) collective-permute-start(bf16[8,3584]{1,0:T(8,128)(2,1)S(1)} %payload.1.refs_0_), channel_id=1, source_target_pairs={{0,12},{2,14},{4,8},{6,10},{8,4},{10,6},{12,0},{14,2},{1,13},{3,15... | collective-permute-start | bytes 172040 | tf_op jit(solution)/shard_map/ppermute | solution.py:482
  6.9 0.2 collective-permute-start.2
  7.1 0.0 copy-start
  7.1 4.4 %arrange.1 = (bf16[192,2560]{1,0:T(8,128)(2,1)S(1)}, bf16[4,2560,256]{2,1,0:T(8,128)(2,1)S(1)}, bf16[48,128,2,128]{3,2,1,0:T(2,128)(2,1)S(1)}, bf16[48,128,2,128]{3,2,1,0:T(2,128)(2,1)S(1)}, f32[6,256,128]{2,1,0:T(8,128)S(1)}) custom-call(bf16[48,128,2,2,128]{4,3,2,1,0:T(2,128)(2,1)} %refs_1_.3, bf16[48,4,2560]{2,1,0:T(4,128)(2,1)} %refs_1_.2, ...), custom_call_target="tpu_custom_call" | custom-call | flops 1342177280 | bytes 12451840 | tf_op jit(solution)/shard_map/arrange/pallas_call | solution.py:283
  11.5 0.0 collective-permute-done.refs_1_
  11.5 0.1 collective-permute-done.1.refs_2_
  11.6 0.1 collective-permute-done.2.refs_3_
  11.7 1.6 %collective-permute-start.3 = (bf16[32,3584]{1,0:T(8,128)(2,1)S(1)}, bf16[32,3584]{1,0:T(8,128)(2,1)S(1)}, u32[]{:S(2)}, u32[]{:S(2)}) collective-permute-start(bf16[32,3584]{1,0:T(8,128)(2,1)S(1)} %join.1.refs_0_), channel_id=1, source_target_pairs={{0,2},{2,0},{4,6},{6,4},{8,10},{10,8},{12,14},{14,12},{1,3},{3,1},... | collective-permute-start | bytes 688136 | tf_op jit(solution)/shard_map/ppermute | solution.py:500
  13.3 0.0 copy-done
  13.3 4.9 %attend_cached.1 = (bf16[48,128,2,128]{3,2,1,0:T(2,128)(2,1)S(1)}, bf16[48,128,2,128]{3,2,1,0:T(2,128)(2,1)S(1)}, f32[6,256,128]{2,1,0:T(8,128)S(1)}, f32[48,64,...) custom-call(s32[48]{0:T(128)} %refs_0_.3, ...), custom_call_target="tpu_custom_call", output_to_operand_aliasing={{0}: (3, {}), {1}: (4, {}), {2}: (5, {})} | custom-call | flops 402653184 | bytes 6291456 | tf_op jit(solution)/shard_map/attend_cached/pallas_call | solution.py:194
  18.2 0.2 %collective-permute-done.3.refs_1_ = bf16[32,3584]{1,0:T(8,128)(2,1)S(1)} collective-permute-done((bf16[32,3584]{1,0:T(8,128)(2,1)S(1)}, bf16[32,3584]{1,0:T(8,128)(2,1)S(1)}, u32[]{:S(2)}, u32[]{:S(2)}) %collective-permute-start.3) | collective-permute-done | bytes 229408 | tf_op jit(solution)/shard_map/ppermute | solution.py:500
  18.4 1.4 %project.3 = f32[192,512]{1,0:T(8,128)S(1)} custom-call(bf16[192,2560]{1,0:T(8,128)(2,1)S(1)} %get-tuple-element.46.hidden_ref, bf16[4,2560,256]{2,1,0:T(8,128)(2,1)S(1)} %get-tuple-element.47.base_ref, bf16[32,3584]{1,0:T(8,128)(2,1)S(1)} %join.1.refs_0_, bf16[32,3584]{1,0:T(8,128)(2,1)S(1)} %collective-permute-done.3.refs_1_), custom_call_target="tpu_custom_call" | custom-call | flops 671088640 | bytes 3604480 | tf_op jit(solution)/shard_map/project/pallas_call | solution.py:341
  19.8 0.1 collective-permute-start.4
  19.9 1.4 %project.2.refs_0_ = f32[192,512]{1,0:T(8,128)S(1)} custom-call(bf16[192,2560]{1,0:T(8,128)(2,1)S(1)} %get-tuple-element.46.hidden_ref, bf16[4,2560,256]{2,1,0:T(8,128)(2,1)S(1)} %get-tuple-element.47.base_ref, bf16[32,3584]{1,0:T(8,128)(2,1)S(1)} %join.1.refs_0_, bf16[32,3584]{1,0:T(8,128)(2,1)S(1)} %collective-permute-done.3.refs_1_), custom_call_target="tpu_custom_call" | custom-call | flops 671088640 | bytes 3604480 | tf_op jit(solution)/shard_map/project/pallas_call | solution.py:341
  21.3 0.3 %collective-permute-done.4.refs_1_ = f32[192,512]{1,0:T(8,128)S(1)} collective-permute-done((f32[192,512]{1,0:T(8,128)S(1)}, f32[192,512]{1,0:T(8,128)S(1)}, u32[]{:S(2)}, u32[]{:S(2)}) %collective-permute-start.4) | collective-permute-done | bytes 393248 | tf_op jit(solution)/shard_map/ppermute | solution.py:506
  21.6 2.1 %finish.1 = (bf16[48,4,2,2,128]{4,3,2,1,0:T(2,128)(2,1)}, bf16[48,64,128]{2,1,0:T(8,128)(2,1)}) custom-call(f32[192,512]{1,0:T(8,128)S(1)} %project.2.refs_0_, f32[192,512]{1,0:T(8,128)S(1)} %collective-permute-done.4.refs_1_, bf16[48,64,128]{2,1,0:T(8,128)(2,1)S(1)} %bitcast.5, f32[48,64,128]{2,1,0:T(8,128)S(1)} %get-tuple-element.51.refs_3_, ...), custom_call_target="tpu_custom_call" | custom-call | flops 301989888 | bytes 3145728 | tf_op jit(solution)/shard_map/finish/pallas_call | solution.py:435
  (1 shorter events, 0.0 us)
Async XLA Ops:
  1.5 10.1 %collective-permute-start = (bf16[8,3584]{1,0:T(8,128)(2,1)S(1)}, bf16[8,3584]{1,0:T(8,128)(2,1)S(1)}, u32[]{:S(2)}, u32[]{:S(2)}) collective-permute-start(bf16[8,3584]{1,0:T(8,128)(2,1)S(1)} %payload.1.refs_0_), channel_id=1, source_target_pairs={{0,8},{2,10},{4,12},{6,14},{8,0},{10,2},{12,4},{14,6},{1,9},{3,11}... | collective-permute-start | bytes 172040 | tf_op jit(solution)/shard_map/ppermute | solution.py:482
  5.6 6.1 %collective-permute-start.1 = (bf16[8,3584]{1,0:T(8,128)(2,1)S(1)}, bf16[8,3584]{1,0:T(8,128)(2,1)S(1)}, u32[]{:S(2)}, u32[]{:S(2)}) collective-permute-start(bf16[8,3584]{1,0:T(8,128)(2,1)S(1)} %payload.1.refs_0_), channel_id=1, source_target_pairs={{0,12},{2,14},{4,8},{6,10},{8,4},{10,6},{12,0},{14,2},{1,13},{3,15... | collective-permute-start | bytes 172040 | tf_op jit(solution)/shard_map/ppermute | solution.py:482
  6.9 4.8 %collective-permute-start.2 = (bf16[8,3584]{1,0:T(8,128)(2,1)S(1)}, bf16[8,3584]{1,0:T(8,128)(2,1)S(1)}, u32[]{:S(2)}, u32[]{:S(2)}) collective-permute-start(bf16[8,3584]{1,0:T(8,128)(2,1)S(1)} %payload.1.refs_0_), channel_id=1, source_target_pairs={{0,4},{2,6},{4,0},{6,2},{8,12},{10,14},{12,8},{14,10},{1,5},{3,7},... | collective-permute-start | bytes 172040 | tf_op jit(solution)/shard_map/ppermute | solution.py:482
  7.1 6.2 %copy-start = (bf16[48,4,16,128]{3,2,1,0:T(8,128)(2,1)S(1)}, bf16[48,4,16,128]{3,2,1,0:T(8,128)(2,1)}, u32[]{:S(2)}) copy-start(bf16[48,4,16,128]{3,2,1,0:T(8,128)(2,1)} %param.11) | copy-start | bytes 2359300
  11.7 6.7 %collective-permute-start.3 = (bf16[32,3584]{1,0:T(8,128)(2,1)S(1)}, bf16[32,3584]{1,0:T(8,128)(2,1)S(1)}, u32[]{:S(2)}, u32[]{:S(2)}) collective-permute-start(bf16[32,3584]{1,0:T(8,128)(2,1)S(1)} %join.1.refs_0_), channel_id=1, source_target_pairs={{0,2},{2,0},{4,6},{6,4},{8,10},{10,8},{12,14},{14,12},{1,3},{3,1},... | collective-permute-start | bytes 688136 | tf_op jit(solution)/shard_map/ppermute | solution.py:500
  19.8 1.8 %collective-permute-start.4 = (f32[192,512]{1,0:T(8,128)S(1)}, f32[192,512]{1,0:T(8,128)S(1)}, u32[]{:S(2)}, u32[]{:S(2)}) collective-permute-start(f32[192,512]{1,0:T(8,128)S(1)} %project.3), channel_id=1, source_target_pairs={{0,1},{1,0},{2,3},{3,2},{4,5},{5,4},{6,7},{7,6},{8,9},{9,8},{10,11... | collective-permute-start | bytes 1179656 | tf_op jit(solution)/shard_map/ppermute | solution.py:506

commit v26 on v24

--- a/solution.py
+++ b/solution.py
@@ -360,6 +360,11 @@
     fresh = parts[0][...]
     for part in parts[1:]:
         fresh = fresh + part[...]
+    for n in range(2 * own):
+        wide[pl.ds(n, rows * steps, stride=2 * own), :] = fresh[:, n * size : (n + 1) * size]
+    fresh_ref.reshape(rows * steps * 2 * own, size)[...] = wide[...].astype(jnp.bfloat16)
+    puts = [pltpu.make_async_copy(fresh_ref, fresh_hbm, sems.at[0])]
+    puts[0].start()
     keys, many = 2 * own * steps, 2 * queries
     group = size // keys
     key = lax.broadcasted_iota(jnp.int32, (keys, many), 0)
@@ -389,12 +394,6 @@
     inverse = 1.0 / (back * total_ref[...] + jnp.sum(expo, axis=1))
     weights = (expo * inverse[:, None, :]).astype(jnp.bfloat16)
     back = back * inverse
-
-    for n in range(2 * own):
-        wide[pl.ds(n, rows * steps, stride=2 * own), :] = fresh[:, n * size : (n + 1) * size]
-    fresh_ref.reshape(rows * steps * 2 * own, size)[...] = wide[...].astype(jnp.bfloat16)
-    puts = [pltpu.make_async_copy(fresh_ref, fresh_hbm, sems.at[0])]
-    puts[0].start()
 
     for at in range(0, rows // 2, group):
         pairs = range(at, at + group)

time: 23.9 us -> 23.9 us (level)
  no operation moved by 1% of the time
where the time goes in v26:
time: 23.9 us; the launch traced here: 23.7 us
  Pallas kernels  14.9 us (62%)
  starting transfers between devices  7.34 us (31%)
  waiting for transfers between devices  0.75 us (3%)
  between operations  0.69 us (3%)
    ppermute x3, starting transfers between devices, gather_second(): lax.ppermute(payload, 'dp', [(i, i ^ 2 * k) for i in range(dp)])  5.68 us
    pallas_call x1, Pallas kernels, attend_cached(): pl.pallas_call(functools.partial(cached_kernel, chunk, early, heads, size...  4.87 us
    pallas_call x1, Pallas kernels, arrange(): pl.pallas_call(functools.partial(arrange_kernel, chunks, chunk, early), o...  4.36 us
    pallas_call x2, Pallas kernels, project(): pl.pallas_call(functools.partial(project_kernel, k), out_shape=pltpu.VMEM...  2.75 us
    pallas_call x1, Pallas kernels, finish(): pl.pallas_call(functools.partial(finish_kernel, steps, heads, size ** (-0...  2.07 us
    ppermute x1, starting transfers between devices, shards(): lax.ppermute(gathered, 'dp', [(i, i ^ 1) for i in range(dp)])  1.58 us
    pallas_call x1, Pallas kernels, make_payload(): pl.pallas_call(payload_kernel, out_shape=pltpu.VMEM((ranks, width + group...  0.81 us
  transfers between devices with their start and end apart: 5, of which 4 were waited for; matrix products, arithmetic and copies ran while one was open for 0% of the time, Pallas kernels for 45%

profile of v26, /device:TPU:0, one launch (start us, length us, event | category | flops | bytes accessed | tf_op | source)
XLA Modules:
  0.0 23.7 jit_solution(11913348065467539373)
XLA Ops:
  0.6 0.8 %payload.1.refs_0_ = bf16[8,3584]{1,0:T(8,128)(2,1)S(1)} custom-call(bf16[8,2560]{1,0:T(8,128)(2,1)} %bitcast.6, bf16[8,2,4,128]{3,2,1,0:T(4,128)(2,1)} %up_hbm.1), custom_call_target="tpu_custom_call" | custom-call | tf_op jit(solution)/shard_map/payload/pallas_call | solution.py:51
  1.5 4.1 %collective-permute-start = (bf16[8,3584]{1,0:T(8,128)(2,1)S(1)}, bf16[8,3584]{1,0:T(8,128)(2,1)S(1)}, u32[]{:S(2)}, u32[]{:S(2)}) collective-permute-start(bf16[8,3584]{1,0:T(8,128)(2,1)S(1)} %payload.1.refs_0_), channel_id=1, source_target_pairs={{0,8},{2,10},{4,12},{6,14},{8,0},{10,2},{12,4},{14,6},{1,9},{3,11}... | collective-permute-start | bytes 172040 | tf_op jit(solution)/shard_map/ppermute | solution.py:473
  5.6 1.3 %collective-permute-start.1 = (bf16[8,3584]{1,0:T(8,128)(2,1)S(1)}, bf16[8,3584]{1,0:T(8,128)(2,1)S(1)}, u32[]{:S(2)}, u32[]{:S(2)}) collective-permute-start(bf16[8,3584]{1,0:T(8,128)(2,1)S(1)} %payload.1.refs_0_), channel_id=1, source_target_pairs={{0,12},{2,14},{4,8},{6,10},{8,4},{10,6},{12,0},{14,2},{1,13},{3,15... | collective-permute-start | bytes 172040 | tf_op jit(solution)/shard_map/ppermute | solution.py:473
  6.9 0.2 collective-permute-start.2
  7.1 0.0 copy-start
  7.1 4.4 %arrange.1 = (bf16[192,2560]{1,0:T(8,128)(2,1)S(1)}, bf16[4,2560,256]{2,1,0:T(8,128)(2,1)S(1)}, bf16[48,128,2,128]{3,2,1,0:T(2,128)(2,1)S(1)}, bf16[48,128,2,128]{3,2,1,0:T(2,128)(2,1)S(1)}, f32[6,256,128]{2,1,0:T(8,128)S(1)}) custom-call(bf16[48,128,2,2,128]{4,3,2,1,0:T(2,128)(2,1)} %refs_1_.3, bf16[48,4,2560]{2,1,0:T(4,128)(2,1)} %refs_1_.2, ...), custom_call_target="tpu_custom_call" | custom-call | flops 1342177280 | bytes 12451840 | tf_op jit(solution)/shard_map/arrange/pallas_call | solution.py:283
  11.5 0.0 collective-permute-done.refs_1_
  11.5 0.1 collective-permute-done.1.refs_2_
  11.6 0.1 collective-permute-done.2.refs_3_
  11.7 1.6 %collective-permute-start.3 = (bf16[32,3584]{1,0:T(8,128)(2,1)S(1)}, bf16[32,3584]{1,0:T(8,128)(2,1)S(1)}, u32[]{:S(2)}, u32[]{:S(2)}) collective-permute-start(bf16[32,3584]{1,0:T(8,128)(2,1)S(1)} %join.1.refs_0_), channel_id=1, source_target_pairs={{0,2},{2,0},{4,6},{6,4},{8,10},{10,8},{12,14},{14,12},{1,3},{3,1},... | collective-permute-start | bytes 688136 | tf_op jit(solution)/shard_map/ppermute | solution.py:491
  13.3 0.0 copy-done
  13.3 4.9 %attend_cached.1 = (bf16[48,128,2,128]{3,2,1,0:T(2,128)(2,1)S(1)}, bf16[48,128,2,128]{3,2,1,0:T(2,128)(2,1)S(1)}, f32[6,256,128]{2,1,0:T(8,128)S(1)}, f32[48,64,...) custom-call(s32[48]{0:T(128)} %refs_0_.3, ...), custom_call_target="tpu_custom_call", output_to_operand_aliasing={{0}: (3, {}), {1}: (4, {}), {2}: (5, {})} | custom-call | flops 402653184 | bytes 6291456 | tf_op jit(solution)/shard_map/attend_cached/pallas_call | solution.py:194
  18.2 0.2 %collective-permute-done.3.refs_1_ = bf16[32,3584]{1,0:T(8,128)(2,1)S(1)} collective-permute-done((bf16[32,3584]{1,0:T(8,128)(2,1)S(1)}, bf16[32,3584]{1,0:T(8,128)(2,1)S(1)}, u32[]{:S(2)}, u32[]{:S(2)}) %collective-permute-start.3) | collective-permute-done | bytes 229408 | tf_op jit(solution)/shard_map/ppermute | solution.py:491
  18.4 1.4 %project.3 = f32[192,512]{1,0:T(8,128)S(1)} custom-call(bf16[192,2560]{1,0:T(8,128)(2,1)S(1)} %get-tuple-element.46.hidden_ref, bf16[4,2560,256]{2,1,0:T(8,128)(2,1)S(1)} %get-tuple-element.47.base_ref, bf16[32,3584]{1,0:T(8,128)(2,1)S(1)} %join.1.refs_0_, bf16[32,3584]{1,0:T(8,128)(2,1)S(1)} %collective-permute-done.3.refs_1_), custom_call_target="tpu_custom_call" | custom-call | flops 671088640 | bytes 3604480 | tf_op jit(solution)/shard_map/project/pallas_call | solution.py:341
  19.8 0.1 collective-permute-start.4
  19.9 1.4 %project.2.refs_0_ = f32[192,512]{1,0:T(8,128)S(1)} custom-call(bf16[192,2560]{1,0:T(8,128)(2,1)S(1)} %get-tuple-element.46.hidden_ref, bf16[4,2560,256]{2,1,0:T(8,128)(2,1)S(1)} %get-tuple-element.47.base_ref, bf16[32,3584]{1,0:T(8,128)(2,1)S(1)} %join.1.refs_0_, bf16[32,3584]{1,0:T(8,128)(2,1)S(1)} %collective-permute-done.3.refs_1_), custom_call_target="tpu_custom_call" | custom-call | flops 671088640 | bytes 3604480 | tf_op jit(solution)/shard_map/project/pallas_call | solution.py:341
  21.3 0.3 %collective-permute-done.4.refs_1_ = f32[192,512]{1,0:T(8,128)S(1)} collective-permute-done((f32[192,512]{1,0:T(8,128)S(1)}, f32[192,512]{1,0:T(8,128)S(1)}, u32[]{:S(2)}, u32[]{:S(2)}) %collective-permute-start.4) | collective-permute-done | bytes 393248 | tf_op jit(solution)/shard_map/ppermute | solution.py:497
  21.6 2.1 %finish.1 = (bf16[48,4,2,2,128]{4,3,2,1,0:T(2,128)(2,1)}, bf16[48,64,128]{2,1,0:T(8,128)(2,1)}) custom-call(f32[192,512]{1,0:T(8,128)S(1)} %project.2.refs_0_, f32[192,512]{1,0:T(8,128)S(1)} %collective-permute-done.4.refs_1_, bf16[48,64,128]{2,1,0:T(8,128)(2,1)S(1)} %bitcast.5, f32[48,64,128]{2,1,0:T(8,128)S(1)} %get-tuple-element.51.refs_3_, ...), custom_call_target="tpu_custom_call" | custom-call | flops 301989888 | bytes 3145728 | tf_op jit(solution)/shard_map/finish/pallas_call | solution.py:426
  (1 shorter events, 0.0 us)
Async XLA Ops:
  1.5 10.1 %collective-permute-start = (bf16[8,3584]{1,0:T(8,128)(2,1)S(1)}, bf16[8,3584]{1,0:T(8,128)(2,1)S(1)}, u32[]{:S(2)}, u32[]{:S(2)}) collective-permute-start(bf16[8,3584]{1,0:T(8,128)(2,1)S(1)} %payload.1.refs_0_), channel_id=1, source_target_pairs={{0,8},{2,10},{4,12},{6,14},{8,0},{10,2},{12,4},{14,6},{1,9},{3,11}... | collective-permute-start | bytes 172040 | tf_op jit(solution)/shard_map/ppermute | solution.py:473
  5.6 6.1 %collective-permute-start.1 = (bf16[8,3584]{1,0:T(8,128)(2,1)S(1)}, bf16[8,3584]{1,0:T(8,128)(2,1)S(1)}, u32[]{:S(2)}, u32[]{:S(2)}) collective-permute-start(bf16[8,3584]{1,0:T(8,128)(2,1)S(1)} %payload.1.refs_0_), channel_id=1, source_target_pairs={{0,12},{2,14},{4,8},{6,10},{8,4},{10,6},{12,0},{14,2},{1,13},{3,15... | collective-permute-start | bytes 172040 | tf_op jit(solution)/shard_map/ppermute | solution.py:473
  6.9 4.8 %collective-permute-start.2 = (bf16[8,3584]{1,0:T(8,128)(2,1)S(1)}, bf16[8,3584]{1,0:T(8,128)(2,1)S(1)}, u32[]{:S(2)}, u32[]{:S(2)}) collective-permute-start(bf16[8,3584]{1,0:T(8,128)(2,1)S(1)} %payload.1.refs_0_), channel_id=1, source_target_pairs={{0,4},{2,6},{4,0},{6,2},{8,12},{10,14},{12,8},{14,10},{1,5},{3,7},... | collective-permute-start | bytes 172040 | tf_op jit(solution)/shard_map/ppermute | solution.py:473
  7.1 6.2 %copy-start = (bf16[48,4,16,128]{3,2,1,0:T(8,128)(2,1)S(1)}, bf16[48,4,16,128]{3,2,1,0:T(8,128)(2,1)}, u32[]{:S(2)}) copy-start(bf16[48,4,16,128]{3,2,1,0:T(8,128)(2,1)} %param.11) | copy-start | bytes 2359300
  11.7 6.7 %collective-permute-start.3 = (bf16[32,3584]{1,0:T(8,128)(2,1)S(1)}, bf16[32,3584]{1,0:T(8,128)(2,1)S(1)}, u32[]{:S(2)}, u32[]{:S(2)}) collective-permute-start(bf16[32,3584]{1,0:T(8,128)(2,1)S(1)} %join.1.refs_0_), channel_id=1, source_target_pairs={{0,2},{2,0},{4,6},{6,4},{8,10},{10,8},{12,14},{14,12},{1,3},{3,1},... | collective-permute-start | bytes 688136 | tf_op jit(solution)/shard_map/ppermute | solution.py:491
  19.8 1.8 %collective-permute-start.4 = (f32[192,512]{1,0:T(8,128)S(1)}, f32[192,512]{1,0:T(8,128)S(1)}, u32[]{:S(2)}, u32[]{:S(2)}) collective-permute-start(f32[192,512]{1,0:T(8,128)S(1)} %project.3), channel_id=1, source_target_pairs={{0,1},{1,0},{2,3},{3,2},{4,5},{5,4},{6,7},{7,6},{8,9},{9,8},{10,11... | collective-permute-start | bytes 1179656 | tf_op jit(solution)/shard_map/ppermute | solution.py:497

commit v27 on v26

--- a/solution.py
+++ b/solution.py
@@ -313,7 +313,7 @@
         ],
         axis=1,
     )
-    step = 256
+    step = 640
 
     def merge(first, last):
         for f in range(first, last, step):

time: 23.9 us -> 23.9 us (level)
  no operation moved by 1% of the time
where the time goes in v27:
time: 23.9 us; the launch traced here: 23.7 us
  Pallas kernels  14.9 us (62%)
  starting transfers between devices  7.34 us (31%)
  waiting for transfers between devices  0.75 us (3%)
  between operations  0.69 us (3%)
    ppermute x3, starting transfers between devices, gather_second(): lax.ppermute(payload, 'dp', [(i, i ^ 2 * k) for i in range(dp)])  5.68 us
    pallas_call x1, Pallas kernels, attend_cached(): pl.pallas_call(functools.partial(cached_kernel, chunk, early, heads, size...  4.87 us
    pallas_call x1, Pallas kernels, arrange(): pl.pallas_call(functools.partial(arrange_kernel, chunks, chunk, early), o...  4.36 us
    pallas_call x2, Pallas kernels, project(): pl.pallas_call(functools.partial(project_kernel, k), out_shape=pltpu.VMEM...  2.75 us
    pallas_call x1, Pallas kernels, finish(): pl.pallas_call(functools.partial(finish_kernel, steps, heads, size ** (-0...  2.07 us
    ppermute x1, starting transfers between devices, shards(): lax.ppermute(gathered, 'dp', [(i, i ^ 1) for i in range(dp)])  1.58 us
    pallas_call x1, Pallas kernels, make_payload(): pl.pallas_call(payload_kernel, out_shape=pltpu.VMEM((ranks, width + group...  0.81 us
  transfers between devices with their start and end apart: 5, of which 4 were waited for; matrix products, arithmetic and copies ran while one was open for 0% of the time, Pallas kernels for 45%

profile of v27, /device:TPU:0, one launch (start us, length us, event | category | flops | bytes accessed | tf_op | source)
XLA Modules:
  0.0 23.7 jit_solution(8778814861968547937)
XLA Ops:
  0.6 0.8 %payload.1.refs_0_ = bf16[8,3584]{1,0:T(8,128)(2,1)S(1)} custom-call(bf16[8,2560]{1,0:T(8,128)(2,1)} %bitcast.6, bf16[8,2,4,128]{3,2,1,0:T(4,128)(2,1)} %up_hbm.1), custom_call_target="tpu_custom_call" | custom-call | tf_op jit(solution)/shard_map/payload/pallas_call | solution.py:51
  1.5 4.1 %collective-permute-start = (bf16[8,3584]{1,0:T(8,128)(2,1)S(1)}, bf16[8,3584]{1,0:T(8,128)(2,1)S(1)}, u32[]{:S(2)}, u32[]{:S(2)}) collective-permute-start(bf16[8,3584]{1,0:T(8,128)(2,1)S(1)} %payload.1.refs_0_), channel_id=1, source_target_pairs={{0,8},{2,10},{4,12},{6,14},{8,0},{10,2},{12,4},{14,6},{1,9},{3,11}... | collective-permute-start | bytes 172040 | tf_op jit(solution)/shard_map/ppermute | solution.py:473
  5.6 1.3 %collective-permute-start.1 = (bf16[8,3584]{1,0:T(8,128)(2,1)S(1)}, bf16[8,3584]{1,0:T(8,128)(2,1)S(1)}, u32[]{:S(2)}, u32[]{:S(2)}) collective-permute-start(bf16[8,3584]{1,0:T(8,128)(2,1)S(1)} %payload.1.refs_0_), channel_id=1, source_target_pairs={{0,12},{2,14},{4,8},{6,10},{8,4},{10,6},{12,0},{14,2},{1,13},{3,15... | collective-permute-start | bytes 172040 | tf_op jit(solution)/shard_map/ppermute | solution.py:473
  6.9 0.2 collective-permute-start.2
  7.1 0.0 copy-start
  7.1 4.4 %arrange.1 = (bf16[192,2560]{1,0:T(8,128)(2,1)S(1)}, bf16[4,2560,256]{2,1,0:T(8,128)(2,1)S(1)}, bf16[48,128,2,128]{3,2,1,0:T(2,128)(2,1)S(1)}, bf16[48,128,2,128]{3,2,1,0:T(2,128)(2,1)S(1)}, f32[6,256,128]{2,1,0:T(8,128)S(1)}) custom-call(bf16[48,128,2,2,128]{4,3,2,1,0:T(2,128)(2,1)} %refs_1_.3, bf16[48,4,2560]{2,1,0:T(4,128)(2,1)} %refs_1_.2, ...), custom_call_target="tpu_custom_call" | custom-call | flops 1342177280 | bytes 12451840 | tf_op jit(solution)/shard_map/arrange/pallas_call | solution.py:283
  11.5 0.0 collective-permute-done.refs_1_
  11.5 0.1 collective-permute-done.1.refs_2_
  11.6 0.1 collective-permute-done.2.refs_3_
  11.7 1.6 %collective-permute-start.3 = (bf16[32,3584]{1,0:T(8,128)(2,1)S(1)}, bf16[32,3584]{1,0:T(8,128)(2,1)S(1)}, u32[]{:S(2)}, u32[]{:S(2)}) collective-permute-start(bf16[32,3584]{1,0:T(8,128)(2,1)S(1)} %join.1.refs_0_), channel_id=1, source_target_pairs={{0,2},{2,0},{4,6},{6,4},{8,10},{10,8},{12,14},{14,12},{1,3},{3,1},... | collective-permute-start | bytes 688136 | tf_op jit(solution)/shard_map/ppermute | solution.py:491
  13.3 0.0 copy-done
  13.3 4.9 %attend_cached.1 = (bf16[48,128,2,128]{3,2,1,0:T(2,128)(2,1)S(1)}, bf16[48,128,2,128]{3,2,1,0:T(2,128)(2,1)S(1)}, f32[6,256,128]{2,1,0:T(8,128)S(1)}, f32[48,64,...) custom-call(s32[48]{0:T(128)} %refs_0_.3, ...), custom_call_target="tpu_custom_call", output_to_operand_aliasing={{0}: (3, {}), {1}: (4, {}), {2}: (5, {})} | custom-call | flops 402653184 | bytes 6291456 | tf_op jit(solution)/shard_map/attend_cached/pallas_call | solution.py:194
  18.2 0.2 %collective-permute-done.3.refs_1_ = bf16[32,3584]{1,0:T(8,128)(2,1)S(1)} collective-permute-done((bf16[32,3584]{1,0:T(8,128)(2,1)S(1)}, bf16[32,3584]{1,0:T(8,128)(2,1)S(1)}, u32[]{:S(2)}, u32[]{:S(2)}) %collective-permute-start.3) | collective-permute-done | bytes 229408 | tf_op jit(solution)/shard_map/ppermute | solution.py:491
  18.4 1.4 %project.3 = f32[192,512]{1,0:T(8,128)S(1)} custom-call(bf16[192,2560]{1,0:T(8,128)(2,1)S(1)} %get-tuple-element.46.hidden_ref, bf16[4,2560,256]{2,1,0:T(8,128)(2,1)S(1)} %get-tuple-element.47.base_ref, bf16[32,3584]{1,0:T(8,128)(2,1)S(1)} %join.1.refs_0_, bf16[32,3584]{1,0:T(8,128)(2,1)S(1)} %collective-permute-done.3.refs_1_), custom_call_target="tpu_custom_call" | custom-call | flops 671088640 | bytes 3604480 | tf_op jit(solution)/shard_map/project/pallas_call | solution.py:341
  19.8 0.1 collective-permute-start.4
  19.9 1.4 %project.2.refs_0_ = f32[192,512]{1,0:T(8,128)S(1)} custom-call(bf16[192,2560]{1,0:T(8,128)(2,1)S(1)} %get-tuple-element.46.hidden_ref, bf16[4,2560,256]{2,1,0:T(8,128)(2,1)S(1)} %get-tuple-element.47.base_ref, bf16[32,3584]{1,0:T(8,128)(2,1)S(1)} %join.1.refs_0_, bf16[32,3584]{1,0:T(8,128)(2,1)S(1)} %collective-permute-done.3.refs_1_), custom_call_target="tpu_custom_call" | custom-call | flops 671088640 | bytes 3604480 | tf_op jit(solution)/shard_map/project/pallas_call | solution.py:341
  21.3 0.3 %collective-permute-done.4.refs_1_ = f32[192,512]{1,0:T(8,128)S(1)} collective-permute-done((f32[192,512]{1,0:T(8,128)S(1)}, f32[192,512]{1,0:T(8,128)S(1)}, u32[]{:S(2)}, u32[]{:S(2)}) %collective-permute-start.4) | collective-permute-done | bytes 393248 | tf_op jit(solution)/shard_map/ppermute | solution.py:497
  21.6 2.1 %finish.1 = (bf16[48,4,2,2,128]{4,3,2,1,0:T(2,128)(2,1)}, bf16[48,64,128]{2,1,0:T(8,128)(2,1)}) custom-call(f32[192,512]{1,0:T(8,128)S(1)} %project.2.refs_0_, f32[192,512]{1,0:T(8,128)S(1)} %collective-permute-done.4.refs_1_, bf16[48,64,128]{2,1,0:T(8,128)(2,1)S(1)} %bitcast.5, f32[48,64,128]{2,1,0:T(8,128)S(1)} %get-tuple-element.51.refs_3_, ...), custom_call_target="tpu_custom_call" | custom-call | flops 301989888 | bytes 3145728 | tf_op jit(solution)/shard_map/finish/pallas_call | solution.py:426
  (1 shorter events, 0.0 us)
Async XLA Ops:
  1.5 10.1 %collective-permute-start = (bf16[8,3584]{1,0:T(8,128)(2,1)S(1)}, bf16[8,3584]{1,0:T(8,128)(2,1)S(1)}, u32[]{:S(2)}, u32[]{:S(2)}) collective-permute-start(bf16[8,3584]{1,0:T(8,128)(2,1)S(1)} %payload.1.refs_0_), channel_id=1, source_target_pairs={{0,8},{2,10},{4,12},{6,14},{8,0},{10,2},{12,4},{14,6},{1,9},{3,11}... | collective-permute-start | bytes 172040 | tf_op jit(solution)/shard_map/ppermute | solution.py:473
  5.6 6.1 %collective-permute-start.1 = (bf16[8,3584]{1,0:T(8,128)(2,1)S(1)}, bf16[8,3584]{1,0:T(8,128)(2,1)S(1)}, u32[]{:S(2)}, u32[]{:S(2)}) collective-permute-start(bf16[8,3584]{1,0:T(8,128)(2,1)S(1)} %payload.1.refs_0_), channel_id=1, source_target_pairs={{0,12},{2,14},{4,8},{6,10},{8,4},{10,6},{12,0},{14,2},{1,13},{3,15... | collective-permute-start | bytes 172040 | tf_op jit(solution)/shard_map/ppermute | solution.py:473
  6.9 4.8 %collective-permute-start.2 = (bf16[8,3584]{1,0:T(8,128)(2,1)S(1)}, bf16[8,3584]{1,0:T(8,128)(2,1)S(1)}, u32[]{:S(2)}, u32[]{:S(2)}) collective-permute-start(bf16[8,3584]{1,0:T(8,128)(2,1)S(1)} %payload.1.refs_0_), channel_id=1, source_target_pairs={{0,4},{2,6},{4,0},{6,2},{8,12},{10,14},{12,8},{14,10},{1,5},{3,7},... | collective-permute-start | bytes 172040 | tf_op jit(solution)/shard_map/ppermute | solution.py:473
  7.1 6.2 %copy-start = (bf16[48,4,16,128]{3,2,1,0:T(8,128)(2,1)S(1)}, bf16[48,4,16,128]{3,2,1,0:T(8,128)(2,1)}, u32[]{:S(2)}) copy-start(bf16[48,4,16,128]{3,2,1,0:T(8,128)(2,1)} %param.11) | copy-start | bytes 2359300
  11.7 6.7 %collective-permute-start.3 = (bf16[32,3584]{1,0:T(8,128)(2,1)S(1)}, bf16[32,3584]{1,0:T(8,128)(2,1)S(1)}, u32[]{:S(2)}, u32[]{:S(2)}) collective-permute-start(bf16[32,3584]{1,0:T(8,128)(2,1)S(1)} %join.1.refs_0_), channel_id=1, source_target_pairs={{0,2},{2,0},{4,6},{6,4},{8,10},{10,8},{12,14},{14,12},{1,3},{3,1},... | collective-permute-start | bytes 688136 | tf_op jit(solution)/shard_map/ppermute | solution.py:491
  19.8 1.8 %collective-permute-start.4 = (f32[192,512]{1,0:T(8,128)S(1)}, f32[192,512]{1,0:T(8,128)S(1)}, u32[]{:S(2)}, u32[]{:S(2)}) collective-permute-start(f32[192,512]{1,0:T(8,128)S(1)} %project.3), channel_id=1, source_target_pairs={{0,1},{1,0},{2,3},{3,2},{4,5},{5,4},{6,7},{7,6},{8,9},{9,8},{10,11... | collective-permute-start | bytes 1179656 | tf_op jit(solution)/shard_map/ppermute | solution.py:497
